TPU v7x, 32 devices: a whole 2x2x4 slice. The times are simulated.
32 devices in a mesh: dp: 2 (over y), pipe: 4 (over x, core), tensor: 4 (over z).
Axes of the slice: x: 2, y: 2, z: 4, core: 2. Of those that a mesh axis runs over, the one named last changes fastest.
Arguments:
- tokens: bfloat16 [1024, 8192], P(('dp', 'tensor'), 'pipe'), parts along dimension 0, may hold values from -6 to 6
- gate_weight: bfloat16 [8192, 28672], P('pipe', 'tensor'), may hold values from -0.0625 to 0.0625
- up_weight: bfloat16 [8192, 28672], P('pipe', 'tensor'), may hold values from -0.0625 to 0.0625
- down_weight: bfloat16 [28672, 8192], P('tensor', 'pipe'), may hold values from -0.03125 to 0.03125
Outputs:
- mixed: bfloat16 [1024, 8192], P(('dp', 'tensor'), 'pipe'), parts along dimension 0
There are 2 independent parts, one for each index of `dp`. A program takes and returns all parts, laid end to end along the dimension named above; an argument that names none is the same for every part. Nothing has to cross between parts.
All inputs are finite; a program needn't handle non-finite values.
Results may differ from a plain program's by a relative error of at most 0.015.
Values may be sent and summed in bfloat16 or wider, within the bound.
No kernel may reach another device: no remote copies, remote signals or barrier semaphores. Data moves between devices by JAX's collectives and lax.ppermute only.
A program may use at most 256 MiB of HBM per device.

v0:
```python
import jax
import jax.numpy as jnp
from jax import lax
from jax.experimental import pallas as pl
from jax.experimental.pallas import tpu as pltpu
from jax.sharding import PartitionSpec as P

BF16, F32 = jnp.bfloat16, jnp.float32
MIB = 1 << 20
ANY = pl.BlockSpec(memory_space=pl.ANY)
HBM = pl.BlockSpec(memory_space=pltpu.HBM)


def block_of(size, most):
    return max(b for b in range(128, most + 1, 128) if size % b == 0)


def params(mib):
    return pltpu.CompilerParams(vmem_limit_bytes=mib * MIB, dimension_semantics=("arbitrary",))


def cost(flops, moved, exps=0):
    return pl.CostEstimate(flops=int(flops * 10), bytes_accessed=int(moved * 10), transcendentals=int(exps * 10))


def cut_order(bits):
    order = [0]
    for bit in reversed(range(bits)):
        order = order + [j | 1 << bit for j in order]
    return order


def first_dot(shards, weight, columns, bits, after):
    rows, depth = shards[0].shape
    at, width = columns
    n, g = 1 << bits, len(shards)
    r, m = rows // n, g * rows
    step = block_of(width, 512)
    steps = width // step
    slots = min(4, steps)
    order = cut_order(bits)

    def kernel(*refs):
        x, w = refs[:g], refs[g]
        keep, send, held, buf, x_sem, w_sem = refs[-6:]
        c = pl.program_id(0)

        def load(block):
            start = pl.multiple_of(at + block * step, 128)
            return pltpu.make_async_copy(w.at[:, pl.ds(start, step)], buf.at[block % slots], w_sem.at[block % slots])

        @pl.when(c == 0)
        def _():
            for block in range(slots):
                load(block).start()
            me = lax.axis_index("pipe")
            copies = []
            for spot, j in enumerate(order):
                start = pl.multiple_of((me ^ j) * r, r)
                for i in range(g):
                    to = spot * g + i
                    copies.append(
                        pltpu.make_async_copy(
                            x[i].at[pl.ds(start, r), :], held.at[pl.ds(to * r, r), :], x_sem.at[to]
                        )
                    )
            for copy in copies:
                copy.start()
            for copy in copies:
                copy.wait()

        load(c).wait()
        part = jnp.dot(held[...], buf[c % slots], preferred_element_type=F32).astype(BF16)
        keep[...] = part[: m // 2]
        send[...] = part[m // 2 :]

        @pl.when(c + slots < steps)
        def _():
            load(c + slots).start()

    out = jax.ShapeDtypeStruct((m // 2, width), BF16)
    return pl.pallas_call(
        kernel,
        grid=(steps,),
        in_specs=[ANY] * g + [HBM] + [ANY] * len(after),
        out_specs=[pl.BlockSpec((m // 2, step), lambda c: (0, c))] * 2,
        out_shape=[out, out],
        scratch_shapes=[
            pltpu.VMEM((m, depth), BF16),
            pltpu.VMEM((slots, depth, step), BF16),
            pltpu.SemaphoreType.DMA((n * g,)),
            pltpu.SemaphoreType.DMA((slots,)),
        ],
        compiler_params=params(40),
        cost_estimate=cost(2 * m * depth * width, 2 * depth * width),
        name="first_dot",
    )(*shards, weight, *after)


def fold(keep, got, after):
    m, width = keep.shape
    step = block_of(width, 1792)

    def kernel(*refs):
        stay, send = refs[-2:]
        total = (refs[0][...].astype(F32) + refs[1][...].astype(F32)).astype(BF16)
        stay[...] = total[: m // 2]
        send[...] = total[m // 2 :]

    out = jax.ShapeDtypeStruct((m // 2, width), BF16)
    return pl.pallas_call(
        kernel,
        grid=(width // step,),
        in_specs=[pl.BlockSpec((m, step), lambda c: (0, c))] * 2 + [ANY] * len(after),
        out_specs=[pl.BlockSpec((m // 2, step), lambda c: (0, c))] * 2,
        out_shape=[out, out],
        compiler_params=params(40),
        cost_estimate=cost(m * width, 6 * m * width),
        name="fold",
    )(keep, got, *after)


def activate(gate, up, after):
    m, width = gate[0].shape
    step = block_of(width, 1792)

    def kernel(*refs):
        g = refs[0][...].astype(F32) + refs[1][...].astype(F32)
        u = refs[2][...].astype(F32) + refs[3][...].astype(F32)
        refs[-1][...] = (g / (1.0 + jnp.exp(-g)) * u).astype(BF16)

    return pl.pallas_call(
        kernel,
        grid=(width // step,),
        in_specs=[pl.BlockSpec((m, step), lambda c: (0, c))] * 4 + [ANY] * len(after),
        out_specs=pl.BlockSpec((m, step), lambda c: (0, c)),
        out_shape=jax.ShapeDtypeStruct((m, width), BF16),
        compiler_params=params(40),
        cost_estimate=cost(8 * m * width, 10 * m * width, m * width),
        name="activate",
    )(*gate, *up, *after)


def last_dot(pieces, weight, at, carries, finals, after):
    n, g = len(pieces), len(carries)
    m1, depth = pieces[0].shape
    width = weight.shape[1]
    r, m = m1 // g, n * m1
    step = block_of(depth, 512)
    steps = depth // step
    slots = min(4, steps)
    given = [c for c in carries if c is not None]

    def kernel(*refs):
        h, w = refs[:n], refs[n]
        outs = refs[-5 - g : -5]
        total, rows, buf, h_sem, w_sem = refs[-5:]
        c = pl.program_id(0)

        def load(block):
            start = pl.multiple_of(at + block * step, 128)
            return pltpu.make_async_copy(w.at[pl.ds(start, step), :], buf.at[block % slots], w_sem.at[block % slots])

        @pl.when(c == 0)
        def _():
            for block in range(slots):
                load(block).start()
            copies = [pltpu.make_async_copy(h[j], rows.at[j], h_sem.at[j]) for j in range(n)]
            for copy in copies:
                copy.start()
            total[...] = jnp.zeros_like(total)
            for copy in copies:
                copy.wait()

        load(c).wait()
        part = rows[:, :, pl.ds(pl.multiple_of(c * step, 128), step)].reshape(m, step)
        total[...] += jnp.dot(part, buf[c % slots], preferred_element_type=F32)

        @pl.when(c + slots < steps)
        def _():
            load(c + slots).start()

        @pl.when(c == steps - 1)
        def _():
            me = lax.axis_index("pipe")
            for j in range(n):
                here = pl.ds(pl.multiple_of((me ^ j) * r, r), r)
                carry_at = n + 1
                for i in range(g):
                    spot = (j * g + i) * r
                    value = total[spot : spot + r, :]
                    if carries[i] is not None:
                        value = value + refs[carry_at][here, :]
                        carry_at += 1
                    outs[i][here, :] = value.astype(outs[i].dtype)

    return pl.pallas_call(
        kernel,
        grid=(steps,),
        in_specs=[ANY] * n + [HBM] + [pl.BlockSpec((n * r, width), lambda c: (0, 0))] * len(given) + [ANY] * len(after),
        out_specs=[pl.BlockSpec((n * r, width), lambda c: (0, 0))] * g,
        out_shape=[jax.ShapeDtypeStruct((n * r, width), BF16 if final else F32) for final in finals],
        scratch_shapes=[
            pltpu.VMEM((m, width), F32),
            pltpu.VMEM((n, m1, depth), BF16),
            pltpu.VMEM((slots, step, width), BF16),
            pltpu.SemaphoreType.DMA((n,)),
            pltpu.SemaphoreType.DMA((slots,)),
        ],
        compiler_params=params(40),
        cost_estimate=cost(2 * m * depth * width, 2 * depth * width),
        name="last_dot",
    )(*pieces, weight, *given, *after)


def add(values, after):
    m, width = values[0].shape
    step = block_of(width, 1024)

    def kernel(*refs):
        total = refs[0][...].astype(F32)
        for ref in refs[1 : len(values)]:
            total = total + ref[...].astype(F32)
        refs[-1][...] = total.astype(BF16)

    return pl.pallas_call(
        kernel,
        grid=(width // step,),
        in_specs=[pl.BlockSpec((m, step), lambda c: (0, c))] * len(values) + [ANY] * len(after),
        out_specs=pl.BlockSpec((m, step), lambda c: (0, c)),
        out_shape=jax.ShapeDtypeStruct((m, width), BF16),
        compiler_params=params(40),
        cost_estimate=cost(m * width * len(values), 2 * m * width * (len(values) + 1)),
        name="add",
    )(*values, *after)


def rectangles(n, width):
    block = block_of(width, 512)
    cut = width // block // 2 * block
    low, high = (0, cut), (cut, width - cut)
    if n != 4:
        mid = list(range(1, n - 1))
        rows = [[0]] + [mid[i : i + 2] for i in range(0, len(mid), 2)] + [[n - 1]]
        return [(s, c) for s in rows for c in (low, high)]
    return [([0], low), ([0, 1], high), ([1, 2], low), ([2, 3], high), ([3], low)]


def solution(mesh):
    n_pipe, n_tensor = mesh.shape["pipe"], mesh.shape["tensor"]
    bits = n_pipe.bit_length() - 1
    assert n_pipe == 1 << bits and bits >= 1 and n_tensor >= 3
    ring = [(i, (i + 1) % n_tensor) for i in range(n_tensor)]

    def hop(value):
        return lax.ppermute(value, "tensor", ring)

    def swap(value, bit):
        return lax.ppermute(value, "pipe", [(i, i ^ (1 << bit)) for i in range(n_pipe)])

    def shards(tokens, gate_weight, up_weight, down_weight):
        held = [tokens]
        for _ in range(n_tensor - 1):
            held.append(hop(held[-1]))
        rects = rectangles(n_tensor, gate_weight.shape[1])
        left = {i: sum(i in s for s, _ in rects) for i in range(n_tensor)}
        weights = (gate_weight, up_weight)
        last, dotted, folded, hidden, sums = [], {}, {}, {}, {}

        def dot(k, w):
            rows, columns = rects[k]
            keep, send = first_dot([held[i] for i in rows], weights[w], columns, bits, last)
            last[:] = [send]
            dotted[k, w] = keep, swap(send, 0)

        def sum_core(k, w):
            keep, got = dotted[k, w]
            for bit in range(1, bits):
                keep, send = fold(keep, got, last)
                last[:] = [send]
                got = swap(send, bit)
            folded[k, w] = keep, got

        def act(k):
            own = activate(folded[k, 0], folded[k, 1], last)
            last[:] = [own]
            pieces = {0: own}
            for bit in reversed(range(bits)):
                for j in list(pieces):
                    pieces[j | 1 << bit] = swap(pieces[j], bit)
            hidden[k] = [pieces[j] for j in range(n_pipe)]

        def down(k):
            rows, columns = rects[k]
            for i in rows:
                left[i] -= 1
            out = last_dot(
                hidden[k], down_weight, columns[0], [sums.get(i) for i in rows], [not left[i] for i in rows], last
            )
            last[:] = out[:1]
            sums.update(zip(rows, out))

        total = {}

        def pass_on(i):
            value = sums[i] if i == 1 else add([total[i - 1], sums[i]], last)
            if i > 1:
                last[:] = [value]
            total[i] = hop(value)

        if n_tensor == 4:
            plan = [
                (dot, 0, 0), (dot, 0, 1), (sum_core, 0, 0), (dot, 1, 0), (sum_core, 0, 1), (dot, 1, 1),
                (act, 0), (sum_core, 1, 0), (dot, 2, 0), (sum_core, 1, 1), (dot, 2, 1), (sum_core, 2, 0),
                (dot, 3, 0), (sum_core, 2, 1), (act, 1), (dot, 3, 1), (sum_core, 3, 0), (dot, 4, 0),
                (sum_core, 3, 1), (act, 2), (dot, 4, 1), (sum_core, 4, 0), (down, 0), (sum_core, 4, 1),
                (down, 1), (act, 3), (down, 2), (pass_on, 1), (act, 4), (down, 3), (pass_on, 2), (down, 4),
                (pass_on, 3),
            ]
        else:
            plan = []
            for k in range(len(rects)):
                plan += [(dot, k, 0), (dot, k, 1), (sum_core, k, 0), (sum_core, k, 1), (act, k), (down, k)]
            plan += [(pass_on, i) for i in range(1, n_tensor)]
        for task, *which in plan:
            task(*which)
        return add([tokens, total[n_tensor - 1], sums[0]], last)

    return jax.shard_map(
        shards,
        mesh=mesh,
        in_specs=(
            P(("dp", "tensor"), "pipe"),
            P("pipe", "tensor"),
            P("pipe", "tensor"),
            P("tensor", "pipe"),
        ),
        out_specs=P(("dp", "tensor"), "pipe"),
        check_vma=False,
    )
```

profile of v0, /device:TPU:0, one launch (start us, length us, event | category | flops | bytes accessed | tf_op | source)
XLA Modules:
  0.0 200.3 jit_solution(7915120335741291844)
XLA Ops:
  0.0 3.0 %collective-permute-start = (bf16[128,2048]{1,0:T(8,128)(2,1)}, bf16[128,2048]{1,0:T(8,128)(2,1)S(1)}, u32[]{:S(2)}, u32[]{:S(2)}) collective-permute-start(bf16[128,2048]{1,0:T(8,128)(2,1)} %refs_0_.9), channel_id=1, source_target_pairs={{0,1},{1,2},{2,3},{3,0},{4,5},{5,6},{6,7},{7,4},{8,9},{9,10},{10,1... | collective-permute-start | bytes 1572872 | tf_op jit(solution)/shard_map/ppermute | solution.py:256
  3.0 1.1 copy-done
  4.1 6.1 %first_dot.10 = (bf16[64,3584]{1,0:T(8,128)(2,1)S(1)}, bf16[64,3584]{1,0:T(8,128)(2,1)S(1)}) custom-call(bf16[128,2048]{1,0:T(8,128)(2,1)S(1)} %copy-done, bf16[2048,7168]{1,0:T(8,128)(2,1)} %refs_1_.6), custom_call_target="tpu_custom_call" | custom-call | flops 18790481920 | bytes 146800640 | tf_op jit(solution)/shard_map/first_dot/pallas_call | solution.py:82
  10.3 6.1 %first_dot.11 = (bf16[64,3584]{1,0:T(8,128)(2,1)S(1)}, bf16[64,3584]{1,0:T(8,128)(2,1)S(1)}) custom-call(bf16[128,2048]{1,0:T(8,128)(2,1)S(1)} %copy-done, bf16[2048,7168]{1,0:T(8,128)(2,1)} %refs_1_.7, bf16[64,3584]{1,0:T(8,128)(2,1)S(1)} %get-tuple-element.52.refs_2_), custom_call_target="tpu_custom_call" | custom-call | flops 18790481920 | bytes 146800640 | tf_op jit(solution)/shard_map/first_dot/pallas_call | solution.py:82
  16.4 0.5 collective-permute-start.5
  17.2 1.6 collective-permute-start.4
  18.7 6.8 %first_dot.12 = (bf16[128,3584]{1,0:T(8,128)(2,1)S(1)}, bf16[128,3584]{1,0:T(8,128)(2,1)S(1)}) custom-call(bf16[128,2048]{1,0:T(8,128)(2,1)S(1)} %copy-done.1, bf16[128,2048]{1,0:T(8,128)(2,1)S(1)} %collective-permute-done.refs_1_.refs_0_, bf16[2048,7168]{1,0:T(8,128)(2,1)} %refs_1_.6, bf16[32,3584]{1,0:T(8,128)(2,1)S(1)} %get-tuple-element.54.refs_3_), custom_call_target="tpu_custom_call" | custom-call | flops 37580963840 | bytes 146800640 | tf_op jit(solution)/shard_map/first_dot/pallas_call | solution.py:82
  25.7 0.3 fold.11
  25.9 0.6 collective-permute-start.6
  26.5 1.6 collective-permute-start.1
  28.1 6.8 %first_dot.13 = (bf16[128,3584]{1,0:T(8,128)(2,1)S(1)}, bf16[128,3584]{1,0:T(8,128)(2,1)S(1)}) custom-call(bf16[128,2048]{1,0:T(8,128)(2,1)S(1)} %copy-done.1, bf16[128,2048]{1,0:T(8,128)(2,1)S(1)} %collective-permute-done.refs_1_.refs_0_, bf16[2048,7168]{1,0:T(8,128)(2,1)} %refs_1_.7, bf16[32,3584]{1,0:T(8,128)(2,1)S(1)} %get-tuple-element.60.refs_3_), custom_call_target="tpu_custom_call" | custom-call | flops 37580963840 | bytes 146800640 | tf_op jit(solution)/shard_map/first_dot/pallas_call | solution.py:82
  35.0 1.0 activate.5.refs_2_.refs_0_
  36.0 1.5 collective-permute-start.24
  37.5 4.8 %collective-permute-done.1.refs_1_.refs_0_ = bf16[128,2048]{1,0:T(8,128)(2,1)S(1)} collective-permute-done((bf16[128,2048]{1,0:T(8,128)(2,1)S(1)}, bf16[128,2048]{1,0:T(8,128)(2,1)S(1)}, u32[]{:S(2)}, u32[]{:S(2)}) %collective-permute-start.1) | collective-permute-done | bytes 524320 | tf_op jit(solution)/shard_map/ppermute | solution.py:256
  42.4 0.5 fold.12
  42.8 1.6 collective-permute-start.13
  44.4 6.8 %first_dot.14 = (bf16[128,3584]{1,0:T(8,128)(2,1)S(1)}, bf16[128,3584]{1,0:T(8,128)(2,1)S(1)}) custom-call(bf16[128,2048]{1,0:T(8,128)(2,1)S(1)} %collective-permute-done.refs_1_.refs_0_, bf16[128,2048]{1,0:T(8,128)(2,1)S(1)} %collective-permute-done.1.refs_1_.refs_0_, bf16[2048,7168]{1,0:T(8,128)(2,1)} %refs_1_.6, ...), custom_call_target="tpu_custom_call" | custom-call | flops 37580963840 | bytes 146800640 | tf_op jit(solution)/shard_map/first_dot/pallas_call | solution.py:82
  51.3 0.5 fold.13
  51.8 0.6 collective-permute-start.14
  52.4 6.8 %first_dot.15 = (bf16[128,3584]{1,0:T(8,128)(2,1)S(1)}, bf16[128,3584]{1,0:T(8,128)(2,1)S(1)}) custom-call(bf16[128,2048]{1,0:T(8,128)(2,1)S(1)} %collective-permute-done.refs_1_.refs_0_, bf16[128,2048]{1,0:T(8,128)(2,1)S(1)} %collective-permute-done.1.refs_1_.refs_0_, bf16[2048,7168]{1,0:T(8,128)(2,1)} %refs_1_.7, ...), custom_call_target="tpu_custom_call" | custom-call | flops 37580963840 | bytes 146800640 | tf_op jit(solution)/shard_map/first_dot/pallas_call | solution.py:82
  59.4 0.4 fold.14
  59.9 1.6 collective-permute-start.9
  61.5 6.8 %first_dot.16 = (bf16[128,3584]{1,0:T(8,128)(2,1)S(1)}, bf16[128,3584]{1,0:T(8,128)(2,1)S(1)}) custom-call(bf16[128,2048]{1,0:T(8,128)(2,1)S(1)} %collective-permute-done.1.refs_1_.refs_0_, bf16[128,2048]{1,0:T(8,128)(2,1)S(1)} %collective-permute-done.11.refs_1_.refs_0_, bf16[2048,7168]{1,0:T(8,128)(2,1)} %refs_1_.6, ...), custom_call_target="tpu_custom_call" | custom-call | flops 37580963840 | bytes 146800640 | tf_op jit(solution)/shard_map/first_dot/pallas_call | solution.py:82
  68.4 0.4 fold.15
  68.9 0.6 collective-permute-start.12
  69.5 0.6 activate.6.refs_3_.refs_0_
  70.1 1.6 collective-permute-start.21
  71.7 6.8 %first_dot.17 = (bf16[128,3584]{1,0:T(8,128)(2,1)S(1)}, bf16[128,3584]{1,0:T(8,128)(2,1)S(1)}) custom-call(bf16[128,2048]{1,0:T(8,128)(2,1)S(1)} %collective-permute-done.1.refs_1_.refs_0_, bf16[128,2048]{1,0:T(8,128)(2,1)S(1)} %collective-permute-done.11.refs_1_.refs_0_, bf16[2048,7168]{1,0:T(8,128)(2,1)} %refs_1_.7, ...), custom_call_target="tpu_custom_call" | custom-call | flops 37580963840 | bytes 146800640 | tf_op jit(solution)/shard_map/first_dot/pallas_call | solution.py:82
  78.6 0.5 fold.16
  79.1 6.1 %first_dot.18 = (bf16[64,3584]{1,0:T(8,128)(2,1)S(1)}, bf16[64,3584]{1,0:T(8,128)(2,1)S(1)}) custom-call(bf16[128,2048]{1,0:T(8,128)(2,1)S(1)} %collective-permute-done.11.refs_1_.refs_0_, bf16[2048,7168]{1,0:T(8,128)(2,1)} %refs_1_.6, bf16[64,3584]{1,0:T(8,128)(2,1)S(1)} %get-tuple-element.79.refs_2_), custom_call_target="tpu_custom_call" | custom-call | flops 18790481920 | bytes 146800640 | tf_op jit(solution)/shard_map/first_dot/pallas_call | solution.py:82
  85.2 0.5 collective-permute-start.23
  85.8 0.4 fold.17
  86.3 0.5 collective-permute-start.20
  86.7 7.5 %collective-permute-done.21.refs_2_ = bf16[64,3584]{1,0:T(8,128)(2,1)S(1)} collective-permute-done((bf16[64,3584]{1,0:T(8,128)(2,1)S(1)}, bf16[64,3584]{1,0:T(8,128)(2,1)S(1)}, u32[]{:S(2)}, u32[]{:S(2)}) %collective-permute-start.21) | collective-permute-done | bytes 458784 | tf_op jit(solution)/shard_map/ppermute | solution.py:259
  94.2 0.5 collective-permute-start.26
  94.7 0.6 activate.7.refs_2_.refs_0_
  95.4 6.1 %first_dot.19 = (bf16[64,3584]{1,0:T(8,128)(2,1)S(1)}, bf16[64,3584]{1,0:T(8,128)(2,1)S(1)}) custom-call(bf16[128,2048]{1,0:T(8,128)(2,1)S(1)} %collective-permute-done.11.refs_1_.refs_0_, bf16[2048,7168]{1,0:T(8,128)(2,1)} %refs_1_.7, bf16[64,3584]{1,0:T(8,128)(2,1)S(1)} %activate.7.refs_2_.refs_0_), custom_call_target="tpu_custom_call" | custom-call | flops 18790481920 | bytes 146800640 | tf_op jit(solution)/shard_map/first_dot/pallas_call | solution.py:82
  101.5 0.3 fold.18
  101.8 1.3 collective-permute-start.29
  103.2 0.8 collective-permute-start.28
  103.9 7.5 %last_dot.5.refs_2_.refs_5_ = f32[128,2048]{1,0:T(8,128)S(1)} custom-call(bf16[32,3584]{1,0:T(8,128)(2,1)} %activate.5.refs_2_.refs_0_, bf16[32,3584]{1,0:T(8,128)(2,1)S(1)} %collective-permute-done.23.refs_1_, bf16[32,3584]{1,0:T(8,128)(2,1)} %collective-permute-done.24.refs_2_, bf16[32,3584]{1,0:T(8,128)(2,1)S(1)} %collective-permute-done.25.refs_3_, ...), custom_call_target="tpu_custom_call" | custom-call | flops 18790481920 | bytes 146800640 | tf_op jit(solution)/shard_map/last_dot/pallas_call | solution.py:197
  111.4 1.3 collective-permute-start.18
  113.1 6.9 %last_dot.6 = (bf16[128,2048]{1,0:T(8,128)(2,1)S(1)}, f32[128,2048]{1,0:T(8,128)S(1)}) custom-call(bf16[64,3584]{1,0:T(8,128)(2,1)S(1)} %activate.6.refs_3_.refs_0_, bf16[64,3584]{1,0:T(8,128)(2,1)S(1)} %collective-permute-done.20.refs_1_, bf16[64,3584]{1,0:T(8,128)(2,1)S(1)} %collective-permute-done.21.refs_2_, ...), custom_call_target="tpu_custom_call" | custom-call | flops 37580963840 | bytes 146800640 | tf_op jit(solution)/shard_map/last_dot/pallas_call | solution.py:197
  120.1 5.0 %collective-permute-done.28.refs_1_ = bf16[64,3584]{1,0:T(8,128)(2,1)S(1)} collective-permute-done((bf16[64,3584]{1,0:T(8,128)(2,1)S(1)}, bf16[64,3584]{1,0:T(8,128)(2,1)S(1)}, u32[]{:S(2)}, u32[]{:S(2)}) %collective-permute-start.28) | collective-permute-done | bytes 458784 | tf_op jit(solution)/shard_map/ppermute | solution.py:259
  125.0 0.6 activate.8.refs_6_.refs_0_
  125.7 1.3 collective-permute-start.32
  127.0 7.9 %collective-permute-done.18.refs_2_ = bf16[64,3584]{1,0:T(8,128)(2,1)S(1)} collective-permute-done((bf16[64,3584]{1,0:T(8,128)(2,1)S(1)}, bf16[64,3584]{1,0:T(8,128)(2,1)S(1)}, u32[]{:S(2)}, u32[]{:S(2)}) %collective-permute-start.18) | collective-permute-done | bytes 458784 | tf_op jit(solution)/shard_map/ppermute | solution.py:259
  134.9 1.3 collective-permute-start.35
  136.2 0.8 collective-permute-start.34
  136.9 7.8 %collective-permute-done.32.refs_2_ = bf16[64,3584]{1,0:T(8,128)(2,1)S(1)} collective-permute-done((bf16[64,3584]{1,0:T(8,128)(2,1)S(1)}, bf16[64,3584]{1,0:T(8,128)(2,1)S(1)}, u32[]{:S(2)}, u32[]{:S(2)}) %collective-permute-start.32) | collective-permute-done | bytes 458784 | tf_op jit(solution)/shard_map/ppermute | solution.py:259
  144.7 6.9 %last_dot.7 = (bf16[128,2048]{1,0:T(8,128)(2,1)S(1)}, f32[128,2048]{1,0:T(8,128)S(1)}) custom-call(bf16[64,3584]{1,0:T(8,128)(2,1)S(1)} %activate.7.refs_2_.refs_0_, bf16[64,3584]{1,0:T(8,128)(2,1)S(1)} %collective-permute-done.17.refs_1_, bf16[64,3584]{1,0:T(8,128)(2,1)S(1)} %collective-permute-done.18.refs_2_, ...), custom_call_target="tpu_custom_call" | custom-call | flops 37580963840 | bytes 146800640 | tf_op jit(solution)/shard_map/last_dot/pallas_call | solution.py:197
  151.6 2.5 %collective-permute-done.34.refs_1_ = bf16[32,3584]{1,0:T(8,128)(2,1)S(1)} collective-permute-done((bf16[32,3584]{1,0:T(8,128)(2,1)S(1)}, bf16[32,3584]{1,0:T(8,128)(2,1)S(1)}, u32[]{:S(2)}, u32[]{:S(2)}) %collective-permute-start.34) | collective-permute-done | bytes 229408 | tf_op jit(solution)/shard_map/ppermute | solution.py:259
  154.1 0.4 activate.9.refs_6_.refs_0_
  154.5 1.3 collective-permute-start.38
  155.8 1.2 collective-permute-start.30
  157.0 4.8 %collective-permute-done.38.refs_2_ = bf16[32,3584]{1,0:T(8,128)(2,1)S(1)} collective-permute-done((bf16[32,3584]{1,0:T(8,128)(2,1)S(1)}, bf16[32,3584]{1,0:T(8,128)(2,1)S(1)}, u32[]{:S(2)}, u32[]{:S(2)}) %collective-permute-start.38) | collective-permute-done | bytes 229408 | tf_op jit(solution)/shard_map/ppermute | solution.py:259
  161.8 6.9 %last_dot.8 = (bf16[128,2048]{1,0:T(8,128)(2,1)S(1)}, f32[128,2048]{1,0:T(8,128)S(1)}) custom-call(bf16[64,3584]{1,0:T(8,128)(2,1)S(1)} %activate.8.refs_6_.refs_0_, bf16[64,3584]{1,0:T(8,128)(2,1)S(1)} %collective-permute-done.31.refs_1_, bf16[64,3584]{1,0:T(8,128)(2,1)S(1)} %collective-permute-done.32.refs_2_, ...), custom_call_target="tpu_custom_call" | custom-call | flops 37580963840 | bytes 146800640 | tf_op jit(solution)/shard_map/last_dot/pallas_call | solution.py:197
  168.7 2.2 %collective-permute-done.30.refs_0_ = bf16[128,2048]{1,0:T(8,128)(2,1)S(1)} collective-permute-done((bf16[128,2048]{1,0:T(8,128)(2,1)S(1)}, bf16[128,2048]{1,0:T(8,128)(2,1)S(1)}, u32[]{:S(2)}, u32[]{:S(2)}) %collective-permute-start.30) | collective-permute-done | bytes 524320 | tf_op jit(solution)/shard_map/ppermute | solution.py:256
  170.9 0.3 add.3.refs_6_
  171.3 6.1 %last_dot.9.refs_1_.refs_2_ = bf16[128,2048]{1,0:T(8,128)(2,1)S(1)} custom-call(bf16[32,3584]{1,0:T(8,128)(2,1)S(1)} %activate.9.refs_6_.refs_0_, bf16[32,3584]{1,0:T(8,128)(2,1)S(1)} %collective-permute-done.37.refs_1_, bf16[32,3584]{1,0:T(8,128)(2,1)S(1)} %collective-permute-done.38.refs_2_, bf16[32,3584]{1,0:T(8,128)(2,1)S(1)} %collective-permute-done.39.refs_3_, ...), custom_call_target="tpu_custom_call" | custom-call | flops 18790481920 | bytes 146800640 | tf_op jit(solution)/shard_map/last_dot/pallas_call | solution.py:197
  177.4 8.1 %collective-permute-done.36.refs_0_ = bf16[128,2048]{1,0:T(8,128)(2,1)S(1)} collective-permute-done((bf16[128,2048]{1,0:T(8,128)(2,1)S(1)}, bf16[128,2048]{1,0:T(8,128)(2,1)S(1)}, u32[]{:S(2)}, u32[]{:S(2)}) %collective-permute-start.36) | collective-permute-done | bytes 524320 | tf_op jit(solution)/shard_map/ppermute | solution.py:256
  185.5 0.3 add.4.refs_3_
  185.8 13.5 %collective-permute-done.40.refs_1_ = bf16[128,2048]{1,0:T(8,128)(2,1)S(1)} collective-permute-done((bf16[128,2048]{1,0:T(8,128)(2,1)S(1)}, bf16[128,2048]{1,0:T(8,128)(2,1)S(1)}, u32[]{:S(2)}, u32[]{:S(2)}) %collective-permute-start.40) | collective-permute-done | bytes 524320 | tf_op jit(solution)/shard_map/ppermute | solution.py:256
  199.3 1.0 add.5
  (57 shorter events, 1.7 us)
Async XLA Ops:
  0.0 18.7 %collective-permute-start = (bf16[128,2048]{1,0:T(8,128)(2,1)}, bf16[128,2048]{1,0:T(8,128)(2,1)S(1)}, u32[]{:S(2)}, u32[]{:S(2)}) collective-permute-start(bf16[128,2048]{1,0:T(8,128)(2,1)} %refs_0_.9), channel_id=1, source_target_pairs={{0,1},{1,2},{2,3},{3,0},{4,5},{5,6},{6,7},{7,4},{8,9},{9,10},{10,1... | collective-permute-start | bytes 1572872 | tf_op jit(solution)/shard_map/ppermute | solution.py:256
  3.0 1.1 copy-start
  10.2 8.6 %copy-start.1 = (bf16[128,2048]{1,0:T(8,128)(2,1)S(1)}, bf16[128,2048]{1,0:T(8,128)(2,1)}, u32[]{:S(2)}) copy-start(bf16[128,2048]{1,0:T(8,128)(2,1)} %refs_0_.9) | copy-start | bytes 1572868
  10.2 6.7 %collective-permute-start.2 = (bf16[64,3584]{1,0:T(8,128)(2,1)S(1)}, bf16[64,3584]{1,0:T(8,128)(2,1)S(1)}, u32[]{:S(2)}, u32[]{:S(2)}) collective-permute-start(bf16[64,3584]{1,0:T(8,128)(2,1)S(1)} %get-tuple-element.52.refs_2_), channel_id=1, source_target_pairs={{0,4},{4,0},{8,12},{12,8},{1,5},{5,1},{9,13},{13,9},{2,6},{6,2},{1... | collective-permute-start | bytes 1376264 | tf_op jit(solution)/shard_map/ppermute | solution.py:259
  16.4 9.2 %collective-permute-start.5 = (bf16[64,3584]{1,0:T(8,128)(2,1)S(1)}, bf16[64,3584]{1,0:T(8,128)(2,1)S(1)}, u32[]{:S(2)}, u32[]{:S(2)}) collective-permute-start(bf16[64,3584]{1,0:T(8,128)(2,1)S(1)} %get-tuple-element.53.refs_2_), channel_id=1, source_target_pairs={{0,4},{4,0},{8,12},{12,8},{1,5},{5,1},{9,13},{13,9},{2,6},{6,2},{1... | collective-permute-start | bytes 1376264 | tf_op jit(solution)/shard_map/ppermute | solution.py:259
  17.2 17.8 %collective-permute-start.4 = (bf16[32,3584]{1,0:T(8,128)(2,1)S(1)}, bf16[32,3584]{1,0:T(8,128)(2,1)S(1)}, u32[]{:S(2)}, u32[]{:S(2)}) collective-permute-start(bf16[32,3584]{1,0:T(8,128)(2,1)S(1)} %get-tuple-element.54.refs_3_), channel_id=1, source_target_pairs={{0,8},{4,12},{8,0},{12,4},{1,9},{5,13},{9,1},{13,5},{2,10},{6,14},... | collective-permute-start | bytes 688136 | tf_op jit(solution)/shard_map/ppermute | solution.py:259
  25.6 16.8 %collective-permute-start.3 = (bf16[128,3584]{1,0:T(8,128)(2,1)S(1)}, bf16[128,3584]{1,0:T(8,128)(2,1)S(1)}, u32[]{:S(2)}, u32[]{:S(2)}) collective-permute-start(bf16[128,3584]{1,0:T(8,128)(2,1)S(1)} %get-tuple-element.56.refs_2_), channel_id=1, source_target_pairs={{0,4},{4,0},{8,12},{12,8},{1,5},{5,1},{9,13},{13,9},{2,6},{6,2},{1... | collective-permute-start | bytes 2752520 | tf_op jit(solution)/shard_map/ppermute | solution.py:259
  25.9 9.1 %collective-permute-start.6 = (bf16[32,3584]{1,0:T(8,128)(2,1)S(1)}, bf16[32,3584]{1,0:T(8,128)(2,1)S(1)}, u32[]{:S(2)}, u32[]{:S(2)}) collective-permute-start(bf16[32,3584]{1,0:T(8,128)(2,1)S(1)} %get-tuple-element.60.refs_3_), channel_id=1, source_target_pairs={{0,8},{4,12},{8,0},{12,4},{1,9},{5,13},{9,1},{13,5},{2,10},{6,14},... | collective-permute-start | bytes 688136 | tf_op jit(solution)/shard_map/ppermute | solution.py:259
  26.5 15.8 %collective-permute-start.1 = (bf16[128,2048]{1,0:T(8,128)(2,1)S(1)}, bf16[128,2048]{1,0:T(8,128)(2,1)S(1)}, u32[]{:S(2)}, u32[]{:S(2)}) collective-permute-start(bf16[128,2048]{1,0:T(8,128)(2,1)S(1)} %collective-permute-done.refs_1_.refs_0_), channel_id=1, source_target_pairs={{0,1},{1,2},{2,3},{3,0},{4,5},{5,6},{6,7},{7,4},{8,9},{9,10},{10,1... | collective-permute-start | bytes 1572872 | tf_op jit(solution)/shard_map/ppermute | solution.py:256
  34.9 16.4 %collective-permute-start.8 = (bf16[128,3584]{1,0:T(8,128)(2,1)S(1)}, bf16[128,3584]{1,0:T(8,128)(2,1)S(1)}, u32[]{:S(2)}, u32[]{:S(2)}) collective-permute-start(bf16[128,3584]{1,0:T(8,128)(2,1)S(1)} %get-tuple-element.61.refs_4_), channel_id=1, source_target_pairs={{0,4},{4,0},{8,12},{12,8},{1,5},{5,1},{9,13},{13,9},{2,6},{6,2},{1... | collective-permute-start | bytes 2752520 | tf_op jit(solution)/shard_map/ppermute | solution.py:259
  36.0 49.1 %collective-permute-start.24 = (bf16[32,3584]{1,0:T(8,128)(2,1)}, bf16[32,3584]{1,0:T(8,128)(2,1)}, u32[]{:S(2)}, u32[]{:S(2)}) collective-permute-start(bf16[32,3584]{1,0:T(8,128)(2,1)} %activate.5.refs_2_.refs_0_), channel_id=1, source_target_pairs={{0,8},{4,12},{8,0},{12,4},{1,9},{5,13},{9,1},{13,5},{2,10},{6,14},... | collective-permute-start | bytes 688136 | tf_op jit(solution)/shard_map/ppermute | solution.py:259
  42.4 17.6 %collective-permute-start.11 = (bf16[128,2048]{1,0:T(8,128)(2,1)S(1)}, bf16[128,2048]{1,0:T(8,128)(2,1)S(1)}, u32[]{:S(2)}, u32[]{:S(2)}) collective-permute-start(bf16[128,2048]{1,0:T(8,128)(2,1)S(1)} %collective-permute-done.1.refs_1_.refs_0_), channel_id=1, source_target_pairs={{0,1},{1,2},{2,3},{3,0},{4,5},{5,6},{6,7},{7,4},{8,9},{9,10},{10,1... | collective-permute-start | bytes 1572872 | tf_op jit(solution)/shard_map/ppermute | solution.py:256
  42.8 26.7 %collective-permute-start.13 = (bf16[64,3584]{1,0:T(8,128)(2,1)S(1)}, bf16[64,3584]{1,0:T(8,128)(2,1)S(1)}, u32[]{:S(2)}, u32[]{:S(2)}) collective-permute-start(bf16[64,3584]{1,0:T(8,128)(2,1)S(1)} %get-tuple-element.62.refs_3_), channel_id=1, source_target_pairs={{0,8},{4,12},{8,0},{12,4},{1,9},{5,13},{9,1},{13,5},{2,10},{6,14},... | collective-permute-start | bytes 1376264 | tf_op jit(solution)/shard_map/ppermute | solution.py:259
  51.2 8.0 %collective-permute-start.7 = (bf16[128,3584]{1,0:T(8,128)(2,1)S(1)}, bf16[128,3584]{1,0:T(8,128)(2,1)S(1)}, u32[]{:S(2)}, u32[]{:S(2)}) collective-permute-start(bf16[128,3584]{1,0:T(8,128)(2,1)S(1)} %get-tuple-element.64.refs_2_), channel_id=1, source_target_pairs={{0,4},{4,0},{8,12},{12,8},{1,5},{5,1},{9,13},{13,9},{2,6},{6,2},{1... | collective-permute-start | bytes 2752520 | tf_op jit(solution)/shard_map/ppermute | solution.py:259
  51.8 17.1 %collective-permute-start.14 = (bf16[64,3584]{1,0:T(8,128)(2,1)S(1)}, bf16[64,3584]{1,0:T(8,128)(2,1)S(1)}, u32[]{:S(2)}, u32[]{:S(2)}) collective-permute-start(bf16[64,3584]{1,0:T(8,128)(2,1)S(1)} %get-tuple-element.66.refs_3_), channel_id=1, source_target_pairs={{0,8},{4,12},{8,0},{12,4},{1,9},{5,13},{9,1},{13,5},{2,10},{6,14},... | collective-permute-start | bytes 1376264 | tf_op jit(solution)/shard_map/ppermute | solution.py:259
  59.2 9.1 %collective-permute-start.10 = (bf16[128,3584]{1,0:T(8,128)(2,1)S(1)}, bf16[128,3584]{1,0:T(8,128)(2,1)S(1)}, u32[]{:S(2)}, u32[]{:S(2)}) collective-permute-start(bf16[128,3584]{1,0:T(8,128)(2,1)S(1)} %get-tuple-element.67.refs_2_), channel_id=1, source_target_pairs={{0,4},{4,0},{8,12},{12,8},{1,5},{5,1},{9,13},{13,9},{2,6},{6,2},{1... | collective-permute-start | bytes 2752520 | tf_op jit(solution)/shard_map/ppermute | solution.py:259
  59.9 34.3 %collective-permute-start.9 = (bf16[64,3584]{1,0:T(8,128)(2,1)S(1)}, bf16[64,3584]{1,0:T(8,128)(2,1)S(1)}, u32[]{:S(2)}, u32[]{:S(2)}) collective-permute-start(bf16[64,3584]{1,0:T(8,128)(2,1)S(1)} %get-tuple-element.69.refs_3_), channel_id=1, source_target_pairs={{0,8},{4,12},{8,0},{12,4},{1,9},{5,13},{9,1},{13,5},{2,10},{6,14},... | collective-permute-start | bytes 1376264 | tf_op jit(solution)/shard_map/ppermute | solution.py:259
  68.3 10.2 %collective-permute-start.16 = (bf16[128,3584]{1,0:T(8,128)(2,1)S(1)}, bf16[128,3584]{1,0:T(8,128)(2,1)S(1)}, u32[]{:S(2)}, u32[]{:S(2)}) collective-permute-start(bf16[128,3584]{1,0:T(8,128)(2,1)S(1)} %get-tuple-element.71.refs_2_), channel_id=1, source_target_pairs={{0,4},{4,0},{8,12},{12,8},{1,5},{5,1},{9,13},{13,9},{2,6},{6,2},{1... | collective-permute-start | bytes 2752520 | tf_op jit(solution)/shard_map/ppermute | solution.py:259
  68.9 17.4 %collective-permute-start.12 = (bf16[64,3584]{1,0:T(8,128)(2,1)S(1)}, bf16[64,3584]{1,0:T(8,128)(2,1)S(1)}, u32[]{:S(2)}, u32[]{:S(2)}) collective-permute-start(bf16[64,3584]{1,0:T(8,128)(2,1)S(1)} %get-tuple-element.73.refs_4_), channel_id=1, source_target_pairs={{0,8},{4,12},{8,0},{12,4},{1,9},{5,13},{9,1},{13,5},{2,10},{6,14},... | collective-permute-start | bytes 1376264 | tf_op jit(solution)/shard_map/ppermute | solution.py:259
  70.1 24.1 %collective-permute-start.21 = (bf16[64,3584]{1,0:T(8,128)(2,1)S(1)}, bf16[64,3584]{1,0:T(8,128)(2,1)S(1)}, u32[]{:S(2)}, u32[]{:S(2)}) collective-permute-start(bf16[64,3584]{1,0:T(8,128)(2,1)S(1)} %activate.6.refs_3_.refs_0_), channel_id=1, source_target_pairs={{0,8},{4,12},{8,0},{12,4},{1,9},{5,13},{9,1},{13,5},{2,10},{6,14},... | collective-permute-start | bytes 1376264 | tf_op jit(solution)/shard_map/ppermute | solution.py:259
  78.5 7.2 %collective-permute-start.15 = (bf16[128,3584]{1,0:T(8,128)(2,1)S(1)}, bf16[128,3584]{1,0:T(8,128)(2,1)S(1)}, u32[]{:S(2)}, u32[]{:S(2)}) collective-permute-start(bf16[128,3584]{1,0:T(8,128)(2,1)S(1)} %get-tuple-element.77.refs_2_), channel_id=1, source_target_pairs={{0,4},{4,0},{8,12},{12,8},{1,5},{5,1},{9,13},{13,9},{2,6},{6,2},{1... | collective-permute-start | bytes 2752520 | tf_op jit(solution)/shard_map/ppermute | solution.py:259
  85.2 16.7 %collective-permute-start.23 = (bf16[32,3584]{1,0:T(8,128)(2,1)}, bf16[32,3584]{1,0:T(8,128)(2,1)S(1)}, u32[]{:S(2)}, u32[]{:S(2)}) collective-permute-start(bf16[32,3584]{1,0:T(8,128)(2,1)} %activate.5.refs_2_.refs_0_), channel_id=1, source_target_pairs={{0,4},{4,0},{8,12},{12,8},{1,5},{5,1},{9,13},{13,9},{2,6},{6,2},{1... | collective-permute-start | bytes 688136 | tf_op jit(solution)/shard_map/ppermute | solution.py:259
  85.7 17.5 %collective-permute-start.25 = (bf16[32,3584]{1,0:T(8,128)(2,1)}, bf16[32,3584]{1,0:T(8,128)(2,1)S(1)}, u32[]{:S(2)}, u32[]{:S(2)}) collective-permute-start(bf16[32,3584]{1,0:T(8,128)(2,1)} %collective-permute-done.24.refs_2_), channel_id=1, source_target_pairs={{0,4},{4,0},{8,12},{12,8},{1,5},{5,1},{9,13},{13,9},{2,6},{6,2},{1... | collective-permute-start | bytes 688136 | tf_op jit(solution)/shard_map/ppermute | solution.py:259
  86.3 26.8 %collective-permute-start.20 = (bf16[64,3584]{1,0:T(8,128)(2,1)S(1)}, bf16[64,3584]{1,0:T(8,128)(2,1)S(1)}, u32[]{:S(2)}, u32[]{:S(2)}) collective-permute-start(bf16[64,3584]{1,0:T(8,128)(2,1)S(1)} %activate.6.refs_3_.refs_0_), channel_id=1, source_target_pairs={{0,4},{4,0},{8,12},{12,8},{1,5},{5,1},{9,13},{13,9},{2,6},{6,2},{1... | collective-permute-start | bytes 1376264 | tf_op jit(solution)/shard_map/ppermute | solution.py:259
  94.2 18.9 %collective-permute-start.22 = (bf16[64,3584]{1,0:T(8,128)(2,1)S(1)}, bf16[64,3584]{1,0:T(8,128)(2,1)S(1)}, u32[]{:S(2)}, u32[]{:S(2)}) collective-permute-start(bf16[64,3584]{1,0:T(8,128)(2,1)S(1)} %collective-permute-done.21.refs_2_), channel_id=1, source_target_pairs={{0,4},{4,0},{8,12},{12,8},{1,5},{5,1},{9,13},{13,9},{2,6},{6,2},{1... | collective-permute-start | bytes 1376264 | tf_op jit(solution)/shard_map/ppermute | solution.py:259
  94.2 7.2 %collective-permute-start.26 = (bf16[64,3584]{1,0:T(8,128)(2,1)S(1)}, bf16[64,3584]{1,0:T(8,128)(2,1)S(1)}, u32[]{:S(2)}, u32[]{:S(2)}) collective-permute-start(bf16[64,3584]{1,0:T(8,128)(2,1)S(1)} %get-tuple-element.80.refs_2_), channel_id=1, source_target_pairs={{0,4},{4,0},{8,12},{12,8},{1,5},{5,1},{9,13},{13,9},{2,6},{6,2},{1... | collective-permute-start | bytes 1376264 | tf_op jit(solution)/shard_map/ppermute | solution.py:259
  101.5 10.0 %collective-permute-start.27 = (bf16[64,3584]{1,0:T(8,128)(2,1)S(1)}, bf16[64,3584]{1,0:T(8,128)(2,1)S(1)}, u32[]{:S(2)}, u32[]{:S(2)}) collective-permute-start(bf16[64,3584]{1,0:T(8,128)(2,1)S(1)} %get-tuple-element.83.refs_2_), channel_id=1, source_target_pairs={{0,4},{4,0},{8,12},{12,8},{1,5},{5,1},{9,13},{13,9},{2,6},{6,2},{1... | collective-permute-start | bytes 1376264 | tf_op jit(solution)/shard_map/ppermute | solution.py:259
  101.8 18.3 %collective-permute-start.29 = (bf16[64,3584]{1,0:T(8,128)(2,1)S(1)}, bf16[64,3584]{1,0:T(8,128)(2,1)S(1)}, u32[]{:S(2)}, u32[]{:S(2)}) collective-permute-start(bf16[64,3584]{1,0:T(8,128)(2,1)S(1)} %get-tuple-element.81.refs_4_), channel_id=1, source_target_pairs={{0,8},{4,12},{8,0},{12,4},{1,9},{5,13},{9,1},{13,5},{2,10},{6,14},... | collective-permute-start | bytes 1376264 | tf_op jit(solution)/shard_map/ppermute | solution.py:259
  103.2 21.9 %collective-permute-start.28 = (bf16[64,3584]{1,0:T(8,128)(2,1)S(1)}, bf16[64,3584]{1,0:T(8,128)(2,1)S(1)}, u32[]{:S(2)}, u32[]{:S(2)}) collective-permute-start(bf16[64,3584]{1,0:T(8,128)(2,1)S(1)} %get-tuple-element.79.refs_2_), channel_id=1, source_target_pairs={{0,8},{4,12},{8,0},{12,4},{1,9},{5,13},{9,1},{13,5},{2,10},{6,14},... | collective-permute-start | bytes 1376264 | tf_op jit(solution)/shard_map/ppermute | solution.py:259
  111.4 23.4 %collective-permute-start.18 = (bf16[64,3584]{1,0:T(8,128)(2,1)S(1)}, bf16[64,3584]{1,0:T(8,128)(2,1)S(1)}, u32[]{:S(2)}, u32[]{:S(2)}) collective-permute-start(bf16[64,3584]{1,0:T(8,128)(2,1)S(1)} %activate.7.refs_2_.refs_0_), channel_id=1, source_target_pairs={{0,8},{4,12},{8,0},{12,4},{1,9},{5,13},{9,1},{13,5},{2,10},{6,14},... | collective-permute-start | bytes 1376264 | tf_op jit(solution)/shard_map/ppermute | solution.py:259
  113.0 23.9 %collective-permute-start.17 = (bf16[64,3584]{1,0:T(8,128)(2,1)S(1)}, bf16[64,3584]{1,0:T(8,128)(2,1)S(1)}, u32[]{:S(2)}, u32[]{:S(2)}) collective-permute-start(bf16[64,3584]{1,0:T(8,128)(2,1)S(1)} %activate.7.refs_2_.refs_0_), channel_id=1, source_target_pairs={{0,4},{4,0},{8,12},{12,8},{1,5},{5,1},{9,13},{13,9},{2,6},{6,2},{1... | collective-permute-start | bytes 1376264 | tf_op jit(solution)/shard_map/ppermute | solution.py:259
  125.7 19.0 %collective-permute-start.32 = (bf16[64,3584]{1,0:T(8,128)(2,1)S(1)}, bf16[64,3584]{1,0:T(8,128)(2,1)S(1)}, u32[]{:S(2)}, u32[]{:S(2)}) collective-permute-start(bf16[64,3584]{1,0:T(8,128)(2,1)S(1)} %activate.8.refs_6_.refs_0_), channel_id=1, source_target_pairs={{0,8},{4,12},{8,0},{12,4},{1,9},{5,13},{9,1},{13,5},{2,10},{6,14},... | collective-permute-start | bytes 1376264 | tf_op jit(solution)/shard_map/ppermute | solution.py:259
  134.9 9.8 %collective-permute-start.19 = (bf16[64,3584]{1,0:T(8,128)(2,1)S(1)}, bf16[64,3584]{1,0:T(8,128)(2,1)S(1)}, u32[]{:S(2)}, u32[]{:S(2)}) collective-permute-start(bf16[64,3584]{1,0:T(8,128)(2,1)S(1)} %collective-permute-done.18.refs_2_), channel_id=1, source_target_pairs={{0,4},{4,0},{8,12},{12,8},{1,5},{5,1},{9,13},{13,9},{2,6},{6,2},{1... | collective-permute-start | bytes 1376264 | tf_op jit(solution)/shard_map/ppermute | solution.py:259
  134.9 16.8 %collective-permute-start.35 = (bf16[32,3584]{1,0:T(8,128)(2,1)S(1)}, bf16[32,3584]{1,0:T(8,128)(2,1)S(1)}, u32[]{:S(2)}, u32[]{:S(2)}) collective-permute-start(bf16[32,3584]{1,0:T(8,128)(2,1)S(1)} %get-tuple-element.86.refs_6_), channel_id=1, source_target_pairs={{0,8},{4,12},{8,0},{12,4},{1,9},{5,13},{9,1},{13,5},{2,10},{6,14},... | collective-permute-start | bytes 688136 | tf_op jit(solution)/shard_map/ppermute | solution.py:259
  136.2 18.0 %collective-permute-start.34 = (bf16[32,3584]{1,0:T(8,128)(2,1)S(1)}, bf16[32,3584]{1,0:T(8,128)(2,1)S(1)}, u32[]{:S(2)}, u32[]{:S(2)}) collective-permute-start(bf16[32,3584]{1,0:T(8,128)(2,1)S(1)} %get-tuple-element.84.refs_5_), channel_id=1, source_target_pairs={{0,8},{4,12},{8,0},{12,4},{1,9},{5,13},{9,1},{13,5},{2,10},{6,14},... | collective-permute-start | bytes 688136 | tf_op jit(solution)/shard_map/ppermute | solution.py:259
  136.9 24.9 %collective-permute-start.31 = (bf16[64,3584]{1,0:T(8,128)(2,1)S(1)}, bf16[64,3584]{1,0:T(8,128)(2,1)S(1)}, u32[]{:S(2)}, u32[]{:S(2)}) collective-permute-start(bf16[64,3584]{1,0:T(8,128)(2,1)S(1)} %activate.8.refs_6_.refs_0_), channel_id=1, source_target_pairs={{0,4},{4,0},{8,12},{12,8},{1,5},{5,1},{9,13},{13,9},{2,6},{6,2},{1... | collective-permute-start | bytes 1376264 | tf_op jit(solution)/shard_map/ppermute | solution.py:259
  144.7 17.1 %collective-permute-start.33 = (bf16[64,3584]{1,0:T(8,128)(2,1)S(1)}, bf16[64,3584]{1,0:T(8,128)(2,1)S(1)}, u32[]{:S(2)}, u32[]{:S(2)}) collective-permute-start(bf16[64,3584]{1,0:T(8,128)(2,1)S(1)} %collective-permute-done.32.refs_2_), channel_id=1, source_target_pairs={{0,4},{4,0},{8,12},{12,8},{1,5},{5,1},{9,13},{13,9},{2,6},{6,2},{1... | collective-permute-start | bytes 1376264 | tf_op jit(solution)/shard_map/ppermute | solution.py:259
  154.5 7.3 %collective-permute-start.38 = (bf16[32,3584]{1,0:T(8,128)(2,1)S(1)}, bf16[32,3584]{1,0:T(8,128)(2,1)S(1)}, u32[]{:S(2)}, u32[]{:S(2)}) collective-permute-start(bf16[32,3584]{1,0:T(8,128)(2,1)S(1)} %activate.9.refs_6_.refs_0_), channel_id=1, source_target_pairs={{0,8},{4,12},{8,0},{12,4},{1,9},{5,13},{9,1},{13,5},{2,10},{6,14},... | collective-permute-start | bytes 688136 | tf_op jit(solution)/shard_map/ppermute | solution.py:259
  155.8 15.0 %collective-permute-start.30 = (bf16[128,2048]{1,0:T(8,128)(2,1)S(1)}, bf16[128,2048]{1,0:T(8,128)(2,1)S(1)}, u32[]{:S(2)}, u32[]{:S(2)}) collective-permute-start(bf16[128,2048]{1,0:T(8,128)(2,1)S(1)} %get-tuple-element.91.refs_4_), channel_id=1, source_target_pairs={{0,1},{1,2},{2,3},{3,0},{4,5},{5,6},{6,7},{7,4},{8,9},{9,10},{10,1... | collective-permute-start | bytes 1572872 | tf_op jit(solution)/shard_map/ppermute | solution.py:256
  157.0 14.2 %collective-permute-start.37 = (bf16[32,3584]{1,0:T(8,128)(2,1)S(1)}, bf16[32,3584]{1,0:T(8,128)(2,1)S(1)}, u32[]{:S(2)}, u32[]{:S(2)}) collective-permute-start(bf16[32,3584]{1,0:T(8,128)(2,1)S(1)} %activate.9.refs_6_.refs_0_), channel_id=1, source_target_pairs={{0,4},{4,0},{8,12},{12,8},{1,5},{5,1},{9,13},{13,9},{2,6},{6,2},{1... | collective-permute-start | bytes 688136 | tf_op jit(solution)/shard_map/ppermute | solution.py:259
  161.8 9.5 %collective-permute-start.39 = (bf16[32,3584]{1,0:T(8,128)(2,1)S(1)}, bf16[32,3584]{1,0:T(8,128)(2,1)S(1)}, u32[]{:S(2)}, u32[]{:S(2)}) collective-permute-start(bf16[32,3584]{1,0:T(8,128)(2,1)S(1)} %collective-permute-done.38.refs_2_), channel_id=1, source_target_pairs={{0,4},{4,0},{8,12},{12,8},{1,5},{5,1},{9,13},{13,9},{2,6},{6,2},{1... | collective-permute-start | bytes 688136 | tf_op jit(solution)/shard_map/ppermute | solution.py:259
  171.2 14.3 %collective-permute-start.36 = (bf16[128,2048]{1,0:T(8,128)(2,1)S(1)}, bf16[128,2048]{1,0:T(8,128)(2,1)S(1)}, u32[]{:S(2)}, u32[]{:S(2)}) collective-permute-start(bf16[128,2048]{1,0:T(8,128)(2,1)S(1)} %add.3.refs_6_), channel_id=1, source_target_pairs={{0,1},{1,2},{2,3},{3,0},{4,5},{5,6},{6,7},{7,4},{8,9},{9,10},{10,1... | collective-permute-start | bytes 1572872 | tf_op jit(solution)/shard_map/ppermute | solution.py:256
  171.3 28.1 %copy-start.2 = (bf16[128,2048]{1,0:T(8,128)(2,1)S(1)}, bf16[128,2048]{1,0:T(8,128)(2,1)}, u32[]{:S(2)}) copy-start(bf16[128,2048]{1,0:T(8,128)(2,1)} %refs_0_.9) | copy-start | bytes 1572868
  185.8 13.5 %collective-permute-start.40 = (bf16[128,2048]{1,0:T(8,128)(2,1)S(1)}, bf16[128,2048]{1,0:T(8,128)(2,1)S(1)}, u32[]{:S(2)}, u32[]{:S(2)}) collective-permute-start(bf16[128,2048]{1,0:T(8,128)(2,1)S(1)} %add.4.refs_3_), channel_id=1, source_target_pairs={{0,1},{1,2},{2,3},{3,0},{4,5},{5,6},{6,7},{7,4},{8,9},{9,10},{10,1... | collective-permute-start | bytes 1572872 | tf_op jit(solution)/shard_map/ppermute | solution.py:256
where the time goes:
time: 201 us; the launch traced here: 200 us
  Pallas kernels  108 us (54%)
  waiting for transfers between devices  63.9 us (32%)
  starting transfers between devices  26.5 us (13%)
    pallas_call x10, Pallas kernels, first_dot(): pl.pallas_call(kernel, grid=(steps,), in_specs=[ANY] * g + [HBM] + [ANY]...  65.2 us
    ppermute x35, waiting for transfers between devices, swap(): lax.ppermute(value, 'pipe', [(i, i ^ 1 << bit) for i in range(n_pipe)])  35.4 us
    pallas_call x5, Pallas kernels, last_dot(): pl.pallas_call(kernel, grid=(steps,), in_specs=[ANY] * n + [HBM] + [pl.Bl...  34.4 us
    ppermute x6, waiting for transfers between devices, hop(): return lax.ppermute(value, 'tensor', ring)  28.5 us
    ppermute x35, starting transfers between devices, swap(): lax.ppermute(value, 'pipe', [(i, i ^ 1 << bit) for i in range(n_pipe)])  20.7 us
    ppermute x6, starting transfers between devices, hop(): return lax.ppermute(value, 'tensor', ring)  5.88 us
  transfers between devices with their start and end apart: 41, of which 10 were waited for; matrix products, arithmetic and copies ran while one was open for 0% of the time, Pallas kernels for 53%

commit v1 on v0

--- a/solution.py
+++ b/solution.py
@@ -30,7 +30,7 @@
     return order
 
 
-def first_dot(shards, weight, columns, bits, after):
+def first_dot(shards, weight, columns, bits, fixed, after):
     rows, depth = shards[0].shape
     at, width = columns
     n, g = 1 << bits, len(shards)
@@ -82,7 +82,7 @@
     return pl.pallas_call(
         kernel,
         grid=(steps,),
-        in_specs=[ANY] * g + [HBM] + [ANY] * len(after),
+        in_specs=[HBM if i in fixed else ANY for i in range(g)] + [HBM] + [ANY] * len(after),
         out_specs=[pl.BlockSpec((m // 2, step), lambda c: (0, c))] * 2,
         out_shape=[out, out],
         scratch_shapes=[
@@ -269,7 +269,9 @@
 
         def dot(k, w):
             rows, columns = rects[k]
-            keep, send = first_dot([held[i] for i in rows], weights[w], columns, bits, last)
+            keep, send = first_dot(
+                [held[i] for i in rows], weights[w], columns, bits, [j for j, i in enumerate(rows) if i == 0], last
+            )
             last[:] = [send]
             dotted[k, w] = keep, swap(send, 0)
 
@@ -285,22 +287,38 @@
             own = activate(folded[k, 0], folded[k, 1], last)
             last[:] = [own]
             pieces = {0: own}
-            for bit in reversed(range(bits)):
+            for bit in reversed(range(1, bits)):
                 for j in list(pieces):
                     pieces[j | 1 << bit] = swap(pieces[j], bit)
-            hidden[k] = [pieces[j] for j in range(n_pipe)]
+            pieces[1] = swap(own, 0)
+            hidden[k] = pieces
+
+        def forward(k):
+            pieces = hidden[k]
+            for j in range(2, n_pipe, 2):
+                piece, _ = lax.optimization_barrier((pieces[j], last[0]))
+                pieces[j + 1] = swap(piece, 0)
+
+        def need_partial(k, w):
+            last.append(folded[k, w][1])
+
+        def need_hidden(k):
+            last.extend(hidden[k][j] for j in range(1, n_pipe))
 
         def down(k):
             rows, columns = rects[k]
             for i in rows:
                 left[i] -= 1
             out = last_dot(
-                hidden[k], down_weight, columns[0], [sums.get(i) for i in rows], [not left[i] for i in rows], last
+                [hidden[k][j] for j in range(n_pipe)], down_weight, columns[0], [sums.get(i) for i in rows], [not left[i] for i in rows], last
             )
             last[:] = out[:1]
             sums.update(zip(rows, out))
 
         total = {}
+
+        def need(i):
+            last.append(held[i])
 
         def pass_on(i):
             value = sums[i] if i == 1 else add([total[i - 1], sums[i]], last)
@@ -310,17 +328,19 @@
 
         if n_tensor == 4:
             plan = [
-                (dot, 0, 0), (dot, 0, 1), (sum_core, 0, 0), (dot, 1, 0), (sum_core, 0, 1), (dot, 1, 1),
-                (act, 0), (sum_core, 1, 0), (dot, 2, 0), (sum_core, 1, 1), (dot, 2, 1), (sum_core, 2, 0),
-                (dot, 3, 0), (sum_core, 2, 1), (act, 1), (dot, 3, 1), (sum_core, 3, 0), (dot, 4, 0),
-                (sum_core, 3, 1), (act, 2), (dot, 4, 1), (sum_core, 4, 0), (down, 0), (sum_core, 4, 1),
-                (down, 1), (act, 3), (down, 2), (pass_on, 1), (act, 4), (down, 3), (pass_on, 2), (down, 4),
+                (dot, 0, 0), (dot, 0, 1), (sum_core, 0, 0), (dot, 1, 0), (sum_core, 0, 1), (need, 2),
+                (dot, 1, 1), (act, 0), (sum_core, 1, 0), (dot, 2, 0), (sum_core, 1, 1), (need_partial, 1, 0),
+                (dot, 2, 1), (sum_core, 2, 0), (forward, 0), (need_partial, 1, 1), (dot, 3, 0),
+                (sum_core, 2, 1), (act, 1), (need_hidden, 0), (need_partial, 2, 0), (dot, 3, 1),
+                (sum_core, 3, 0), (dot, 4, 0), (act, 2), (sum_core, 3, 1), (forward, 1), (dot, 4, 1),
+                (down, 1), (forward, 2), (act, 3), (down, 2), (pass_on, 1), (sum_core, 4, 0), (sum_core, 4, 1),
+                (forward, 3), (down, 0), (act, 4), (down, 3), (pass_on, 2), (forward, 4), (down, 4),
                 (pass_on, 3),
             ]
         else:
             plan = []
             for k in range(len(rects)):
-                plan += [(dot, k, 0), (dot, k, 1), (sum_core, k, 0), (sum_core, k, 1), (act, k), (down, k)]
+                plan += [(dot, k, 0), (dot, k, 1), (sum_core, k, 0), (sum_core, k, 1), (act, k), (forward, k), (down, k)]
             plan += [(pass_on, i) for i in range(1, n_tensor)]
         for task, *which in plan:
             task(*which)

time: 201 us -> 196 us (0.975)
  starting transfers between devices: 26.5 us -> 22.5 us
    ppermute x35, starting transfers between devices: 20.7 us -> 16.9 us  [swap(): lax.ppermute(value, 'pipe', [(i, i ^ 1 << bit) for i in range(n_pipe)])]
  transfers between devices with their start and end apart: 41 -> 41, of which waited for: 10 -> 11; matrix products, arithmetic and copies ran while one was open for 0% -> 0% of each run, Pallas kernels for 53% -> 54%
where the time goes in v1:
time: 196 us; the launch traced here: 195 us
  Pallas kernels  106 us (54%)
  waiting for transfers between devices  65.1 us (33%)
  starting transfers between devices  22.5 us (11%)
    pallas_call x10, Pallas kernels, first_dot(): pl.pallas_call(kernel, grid=(steps,), in_specs=[HBM if i in fixed else AN...  65.2 us
    ppermute x35, waiting for transfers between devices, swap(): lax.ppermute(value, 'pipe', [(i, i ^ 1 << bit) for i in range(n_pipe)])  35.8 us
    pallas_call x5, Pallas kernels, last_dot(): pl.pallas_call(kernel, grid=(steps,), in_specs=[ANY] * n + [HBM] + [pl.Bl...  32.9 us
    ppermute x6, waiting for transfers between devices, hop(): return lax.ppermute(value, 'tensor', ring)  29.3 us
    ppermute x35, starting transfers between devices, swap(): lax.ppermute(value, 'pipe', [(i, i ^ 1 << bit) for i in range(n_pipe)])  16.9 us
    ppermute x6, starting transfers between devices, hop(): return lax.ppermute(value, 'tensor', ring)  5.63 us
  transfers between devices with their start and end apart: 41, of which 11 were waited for; matrix products, arithmetic and copies ran while one was open for 0% of the time, Pallas kernels for 54%

profile of v1, /device:TPU:0, one launch (start us, length us, event | category | flops | bytes accessed | tf_op | source)
XLA Modules:
  0.0 195.4 jit_solution(9728553336113931502)
XLA Ops:
  0.0 3.0 %collective-permute-start = (bf16[128,2048]{1,0:T(8,128)(2,1)}, bf16[128,2048]{1,0:T(8,128)(2,1)S(1)}, u32[]{:S(2)}, u32[]{:S(2)}) collective-permute-start(bf16[128,2048]{1,0:T(8,128)(2,1)} %refs_0_.9), channel_id=1, source_target_pairs={{0,1},{1,2},{2,3},{3,0},{4,5},{5,6},{6,7},{7,4},{8,9},{9,10},{10,1... | collective-permute-start | bytes 1572872 | tf_op jit(solution)/shard_map/ppermute | solution.py:256
  3.0 1.1 copy-done
  4.1 6.1 %first_dot.10 = (bf16[64,3584]{1,0:T(8,128)(2,1)S(1)}, bf16[64,3584]{1,0:T(8,128)(2,1)S(1)}) custom-call(bf16[128,2048]{1,0:T(8,128)(2,1)S(1)} %copy-done, bf16[2048,7168]{1,0:T(8,128)(2,1)} %refs_1_.6), custom_call_target="tpu_custom_call" | custom-call | flops 18790481920 | bytes 146800640 | tf_op jit(solution)/shard_map/first_dot/pallas_call | solution.py:82
  10.3 6.1 %first_dot.11 = (bf16[64,3584]{1,0:T(8,128)(2,1)S(1)}, bf16[64,3584]{1,0:T(8,128)(2,1)S(1)}) custom-call(bf16[128,2048]{1,0:T(8,128)(2,1)S(1)} %copy-done, bf16[2048,7168]{1,0:T(8,128)(2,1)} %refs_1_.7, bf16[64,3584]{1,0:T(8,128)(2,1)S(1)} %get-tuple-element.57.refs_2_), custom_call_target="tpu_custom_call" | custom-call | flops 18790481920 | bytes 146800640 | tf_op jit(solution)/shard_map/first_dot/pallas_call | solution.py:82
  16.4 0.5 collective-permute-start.5
  16.9 0.3 fold.10
  17.2 1.6 collective-permute-start.4
  18.7 1.6 collective-permute-start.1
  20.3 6.8 %first_dot.12 = (bf16[128,3584]{1,0:T(8,128)(2,1)S(1)}, bf16[128,3584]{1,0:T(8,128)(2,1)S(1)}) custom-call(bf16[128,2048]{1,0:T(8,128)(2,1)S(1)} %copy-done.1, bf16[128,2048]{1,0:T(8,128)(2,1)S(1)} %collective-permute-done.refs_1_.refs_0_, bf16[2048,7168]{1,0:T(8,128)(2,1)} %refs_1_.6, bf16[32,3584]{1,0:T(8,128)(2,1)S(1)} %get-tuple-element.59.refs_3_), custom_call_target="tpu_custom_call" | custom-call | flops 37580963840 | bytes 146800640 | tf_op jit(solution)/shard_map/first_dot/pallas_call | solution.py:82
  27.2 0.3 fold.11
  27.5 0.6 collective-permute-start.6
  28.1 6.1 %collective-permute-done.1.refs_4_.refs_1_.refs_0_ = bf16[128,2048]{1,0:T(8,128)(2,1)S(1)} collective-permute-done((bf16[128,2048]{1,0:T(8,128)(2,1)S(1)}, bf16[128,2048]{1,0:T(8,128)(2,1)S(1)}, u32[]{:S(2)}, u32[]{:S(2)}) %collective-permute-start.1) | collective-permute-done | bytes 524320 | tf_op jit(solution)/shard_map/ppermute | solution.py:256
  34.2 6.8 %first_dot.13 = (bf16[128,3584]{1,0:T(8,128)(2,1)S(1)}, bf16[128,3584]{1,0:T(8,128)(2,1)S(1)}) custom-call(bf16[128,2048]{1,0:T(8,128)(2,1)S(1)} %copy-done.1, bf16[128,2048]{1,0:T(8,128)(2,1)S(1)} %collective-permute-done.refs_1_.refs_0_, bf16[2048,7168]{1,0:T(8,128)(2,1)} %refs_1_.7, bf16[32,3584]{1,0:T(8,128)(2,1)S(1)} %get-tuple-element.65.refs_3_, ...), custom_call_target="tpu_custom_call" | custom-call | flops 37580963840 | bytes 146800640 | tf_op jit(solution)/shard_map/first_dot/pallas_call | solution.py:82
  41.1 0.4 activate.5.refs_2_.refs_0_
  41.5 0.6 collective-permute-start.17
  42.3 0.5 fold.12
  42.7 1.6 collective-permute-start.9
  44.3 6.8 %first_dot.14 = (bf16[128,3584]{1,0:T(8,128)(2,1)S(1)}, bf16[128,3584]{1,0:T(8,128)(2,1)S(1)}) custom-call(bf16[128,2048]{1,0:T(8,128)(2,1)S(1)} %collective-permute-done.refs_1_.refs_0_, bf16[128,2048]{1,0:T(8,128)(2,1)S(1)} %collective-permute-done.1.refs_4_.refs_1_.refs_0_, bf16[2048,7168]{1,0:T(8,128)(2,1)} %refs_1_.6, ...), custom_call_target="tpu_custom_call" | custom-call | flops 37580963840 | bytes 146800640 | tf_op jit(solution)/shard_map/first_dot/pallas_call | solution.py:82
  51.2 0.4 fold.13
  51.7 7.7 %collective-permute-done.9.refs_4_.refs_1_ = bf16[64,3584]{1,0:T(8,128)(2,1)S(1)} collective-permute-done((bf16[64,3584]{1,0:T(8,128)(2,1)S(1)}, bf16[64,3584]{1,0:T(8,128)(2,1)S(1)}, u32[]{:S(2)}, u32[]{:S(2)}) %collective-permute-start.9) | collective-permute-done | bytes 458784 | tf_op jit(solution)/shard_map/ppermute | solution.py:259
  59.3 0.5 collective-permute-start.13
  59.9 6.8 %first_dot.15 = (bf16[128,3584]{1,0:T(8,128)(2,1)S(1)}, bf16[128,3584]{1,0:T(8,128)(2,1)S(1)}) custom-call(bf16[128,2048]{1,0:T(8,128)(2,1)S(1)} %collective-permute-done.refs_1_.refs_0_, bf16[128,2048]{1,0:T(8,128)(2,1)S(1)} %collective-permute-done.1.refs_4_.refs_1_.refs_0_, bf16[2048,7168]{1,0:T(8,128)(2,1)} %refs_1_.7, ...), custom_call_target="tpu_custom_call" | custom-call | flops 37580963840 | bytes 146800640 | tf_op jit(solution)/shard_map/first_dot/pallas_call | solution.py:82
  66.8 0.5 fold.14
  67.3 1.6 collective-permute-start.10
  68.8 0.2 collective-permute-start.18
  69.0 3.4 %collective-permute-done.13.refs_4_.refs_3_ = bf16[64,3584]{1,0:T(8,128)(2,1)S(1)} collective-permute-done((bf16[64,3584]{1,0:T(8,128)(2,1)S(1)}, bf16[64,3584]{1,0:T(8,128)(2,1)S(1)}, u32[]{:S(2)}, u32[]{:S(2)}) %collective-permute-start.13) | collective-permute-done | bytes 458784 | tf_op jit(solution)/shard_map/ppermute | solution.py:259
  72.4 6.8 %first_dot.16 = (bf16[128,3584]{1,0:T(8,128)(2,1)S(1)}, bf16[128,3584]{1,0:T(8,128)(2,1)S(1)}) custom-call(bf16[128,2048]{1,0:T(8,128)(2,1)S(1)} %collective-permute-done.1.refs_4_.refs_1_.refs_0_, bf16[128,2048]{1,0:T(8,128)(2,1)S(1)} %collective-permute-done.12.refs_1_.refs_0_, bf16[2048,7168]{1,0:T(8,128)(2,1)} %refs_1_.6, ...), custom_call_target="tpu_custom_call" | custom-call | flops 37580963840 | bytes 146800640 | tf_op jit(solution)/shard_map/first_dot/pallas_call | solution.py:82
  79.3 0.5 fold.15
  79.9 0.6 activate.6.refs_3_.refs_0_
  80.5 2.1 %collective-permute-start.22 = (bf16[64,3584]{1,0:T(8,128)(2,1)S(1)}, bf16[64,3584]{1,0:T(8,128)(2,1)S(1)}, u32[]{:S(2)}, u32[]{:S(2)}) collective-permute-start(bf16[64,3584]{1,0:T(8,128)(2,1)S(1)} %activate.6.refs_3_.refs_0_), channel_id=1, source_target_pairs={{0,8},{4,12},{8,0},{12,4},{1,9},{5,13},{9,1},{13,5},{2,10},{6,14},... | collective-permute-start | bytes 1376264 | tf_op jit(solution)/shard_map/ppermute | solution.py:259
  82.6 6.8 %first_dot.17 = (bf16[128,3584]{1,0:T(8,128)(2,1)S(1)}, bf16[128,3584]{1,0:T(8,128)(2,1)S(1)}) custom-call(bf16[128,2048]{1,0:T(8,128)(2,1)S(1)} %collective-permute-done.1.refs_4_.refs_1_.refs_0_, bf16[128,2048]{1,0:T(8,128)(2,1)S(1)} %collective-permute-done.12.refs_1_.refs_0_, bf16[2048,7168]{1,0:T(8,128)(2,1)} %refs_1_.7, ...), custom_call_target="tpu_custom_call" | custom-call | flops 37580963840 | bytes 146800640 | tf_op jit(solution)/shard_map/first_dot/pallas_call | solution.py:82
  89.5 0.6 collective-permute-start.23
  90.0 0.5 fold.16
  90.6 6.1 %first_dot.18 = (bf16[64,3584]{1,0:T(8,128)(2,1)S(1)}, bf16[64,3584]{1,0:T(8,128)(2,1)S(1)}) custom-call(bf16[128,2048]{1,0:T(8,128)(2,1)S(1)} %collective-permute-done.12.refs_1_.refs_0_, bf16[2048,7168]{1,0:T(8,128)(2,1)} %refs_1_.6, bf16[64,3584]{1,0:T(8,128)(2,1)S(1)} %get-tuple-element.84.refs_2_), custom_call_target="tpu_custom_call" | custom-call | flops 18790481920 | bytes 146800640 | tf_op jit(solution)/shard_map/first_dot/pallas_call | solution.py:82
  96.7 0.6 activate.7.refs_2_.refs_0_
  97.4 2.0 %collective-permute-start.20 = (bf16[64,3584]{1,0:T(8,128)(2,1)S(1)}, bf16[64,3584]{1,0:T(8,128)(2,1)S(1)}, u32[]{:S(2)}, u32[]{:S(2)}) collective-permute-start(bf16[64,3584]{1,0:T(8,128)(2,1)S(1)} %activate.7.refs_2_.refs_0_), channel_id=1, source_target_pairs={{0,8},{4,12},{8,0},{12,4},{1,9},{5,13},{9,1},{13,5},{2,10},{6,14},... | collective-permute-start | bytes 1376264 | tf_op jit(solution)/shard_map/ppermute | solution.py:259
  99.4 0.5 fold.17
  99.8 3.2 %collective-permute-done.22.refs_2_ = bf16[64,3584]{1,0:T(8,128)(2,1)S(1)} collective-permute-done((bf16[64,3584]{1,0:T(8,128)(2,1)S(1)}, bf16[64,3584]{1,0:T(8,128)(2,1)S(1)}, u32[]{:S(2)}, u32[]{:S(2)}) %collective-permute-start.22) | collective-permute-done | bytes 458784 | tf_op jit(solution)/shard_map/ppermute | solution.py:259
  103.0 6.1 %first_dot.19 = (bf16[64,3584]{1,0:T(8,128)(2,1)S(1)}, bf16[64,3584]{1,0:T(8,128)(2,1)S(1)}) custom-call(bf16[128,2048]{1,0:T(8,128)(2,1)S(1)} %collective-permute-done.12.refs_1_.refs_0_, bf16[2048,7168]{1,0:T(8,128)(2,1)} %refs_1_.7, bf16[64,3584]{1,0:T(8,128)(2,1)S(1)} %get-tuple-element.87.refs_2_), custom_call_target="tpu_custom_call" | custom-call | flops 18790481920 | bytes 146800640 | tf_op jit(solution)/shard_map/first_dot/pallas_call | solution.py:82
  109.3 6.9 %last_dot.5 = (f32[128,2048]{1,0:T(8,128)S(1)}, f32[128,2048]{1,0:T(8,128)S(1)}) custom-call(bf16[64,3584]{1,0:T(8,128)(2,1)S(1)} %activate.6.refs_3_.refs_0_, bf16[64,3584]{1,0:T(8,128)(2,1)S(1)} %collective-permute-done.21.refs_1_, bf16[64,3584]{1,0:T(8,128)(2,1)S(1)} %collective-permute-done.22.refs_2_, ...), custom_call_target="tpu_custom_call" | custom-call | flops 37580963840 | bytes 146800640 | tf_op jit(solution)/shard_map/last_dot/pallas_call | solution.py:197
  116.2 6.5 %collective-permute-done.20.refs_2_ = bf16[64,3584]{1,0:T(8,128)(2,1)S(1)} collective-permute-done((bf16[64,3584]{1,0:T(8,128)(2,1)S(1)}, bf16[64,3584]{1,0:T(8,128)(2,1)S(1)}, u32[]{:S(2)}, u32[]{:S(2)}) %collective-permute-start.20) | collective-permute-done | bytes 458784 | tf_op jit(solution)/shard_map/ppermute | solution.py:259
  122.7 0.5 collective-permute-start.32
  123.2 8.9 %collective-permute-done.27.refs_3_ = bf16[64,3584]{1,0:T(8,128)(2,1)S(1)} collective-permute-done((bf16[64,3584]{1,0:T(8,128)(2,1)S(1)}, bf16[64,3584]{1,0:T(8,128)(2,1)S(1)}, u32[]{:S(2)}, u32[]{:S(2)}) %collective-permute-start.27) | collective-permute-done | bytes 458784 | tf_op jit(solution)/shard_map/ppermute | solution.py:259
  132.1 0.6 activate.8.refs_6_.refs_0_
  132.7 0.4 collective-permute-start.30
  133.1 6.9 %last_dot.6 = (bf16[128,2048]{1,0:T(8,128)(2,1)S(1)}, f32[128,2048]{1,0:T(8,128)S(1)}) custom-call(bf16[64,3584]{1,0:T(8,128)(2,1)S(1)} %activate.7.refs_2_.refs_0_, bf16[64,3584]{1,0:T(8,128)(2,1)S(1)} %collective-permute-done.19.refs_1_, bf16[64,3584]{1,0:T(8,128)(2,1)S(1)} %collective-permute-done.20.refs_2_, ...), custom_call_target="tpu_custom_call" | custom-call | flops 37580963840 | bytes 146800640 | tf_op jit(solution)/shard_map/last_dot/pallas_call | solution.py:197
  140.1 0.3 fold.18
  140.4 1.8 collective-permute-start.34
  142.2 0.3 fold.19
  142.5 0.4 collective-permute-start.35
  142.8 3.4 %collective-permute-done.30.refs_2_ = bf16[64,3584]{1,0:T(8,128)(2,1)S(1)} collective-permute-done((bf16[64,3584]{1,0:T(8,128)(2,1)S(1)}, bf16[64,3584]{1,0:T(8,128)(2,1)S(1)}, u32[]{:S(2)}, u32[]{:S(2)}) %collective-permute-start.30) | collective-permute-done | bytes 458784 | tf_op jit(solution)/shard_map/ppermute | solution.py:259
  146.2 6.1 %last_dot.7.refs_4_.refs_2_ = bf16[128,2048]{1,0:T(8,128)(2,1)S(1)} custom-call(bf16[32,3584]{1,0:T(8,128)(2,1)S(1)} %activate.5.refs_2_.refs_0_, bf16[32,3584]{1,0:T(8,128)(2,1)S(1)} %collective-permute-done.16.refs_4_.refs_1_, bf16[32,3584]{1,0:T(8,128)(2,1)S(1)} %collective-permute-done.17.refs_5_.refs_2_, ...), custom_call_target="tpu_custom_call" | custom-call | flops 18790481920 | bytes 146800640 | tf_op jit(solution)/shard_map/last_dot/pallas_call | solution.py:197
  152.3 2.4 %collective-permute-done.35.refs_3_ = bf16[32,3584]{1,0:T(8,128)(2,1)S(1)} collective-permute-done((bf16[32,3584]{1,0:T(8,128)(2,1)S(1)}, bf16[32,3584]{1,0:T(8,128)(2,1)S(1)}, u32[]{:S(2)}, u32[]{:S(2)}) %collective-permute-start.35) | collective-permute-done | bytes 229408 | tf_op jit(solution)/shard_map/ppermute | solution.py:259
  154.7 0.4 activate.9.refs_6_.refs_0_
  155.1 0.6 collective-permute-start.38
  155.7 6.9 %last_dot.8 = (bf16[128,2048]{1,0:T(8,128)(2,1)S(1)}, f32[128,2048]{1,0:T(8,128)S(1)}) custom-call(bf16[64,3584]{1,0:T(8,128)(2,1)S(1)} %activate.8.refs_6_.refs_0_, bf16[64,3584]{1,0:T(8,128)(2,1)S(1)} %collective-permute-done.29.refs_1_, bf16[64,3584]{1,0:T(8,128)(2,1)S(1)} %collective-permute-done.30.refs_2_, ...), custom_call_target="tpu_custom_call" | custom-call | flops 37580963840 | bytes 146800640 | tf_op jit(solution)/shard_map/last_dot/pallas_call | solution.py:197
  162.6 0.3 add.3.refs_6_
  162.9 0.6 collective-permute-start.39
  163.5 0.9 collective-permute-start.36
  164.6 6.1 %last_dot.9.refs_1_.refs_2_ = bf16[128,2048]{1,0:T(8,128)(2,1)S(1)} custom-call(bf16[32,3584]{1,0:T(8,128)(2,1)S(1)} %activate.9.refs_6_.refs_0_, bf16[32,3584]{1,0:T(8,128)(2,1)S(1)} %collective-permute-done.37.refs_1_, bf16[32,3584]{1,0:T(8,128)(2,1)S(1)} %collective-permute-done.38.refs_2_, bf16[32,3584]{1,0:T(8,128)(2,1)S(1)} %collective-permute-done.39.refs_3_, ...), custom_call_target="tpu_custom_call" | custom-call | flops 18790481920 | bytes 146800640 | tf_op jit(solution)/shard_map/last_dot/pallas_call | solution.py:197
  170.7 8.4 %collective-permute-done.36.refs_0_ = bf16[128,2048]{1,0:T(8,128)(2,1)S(1)} collective-permute-done((bf16[128,2048]{1,0:T(8,128)(2,1)S(1)}, bf16[128,2048]{1,0:T(8,128)(2,1)S(1)}, u32[]{:S(2)}, u32[]{:S(2)}) %collective-permute-start.36) | collective-permute-done | bytes 524320 | tf_op jit(solution)/shard_map/ppermute | solution.py:256
  179.2 0.3 add.4.refs_3_
  179.5 14.8 %collective-permute-done.40.refs_1_ = bf16[128,2048]{1,0:T(8,128)(2,1)S(1)} collective-permute-done((bf16[128,2048]{1,0:T(8,128)(2,1)S(1)}, bf16[128,2048]{1,0:T(8,128)(2,1)S(1)}, u32[]{:S(2)}, u32[]{:S(2)}) %collective-permute-start.40) | collective-permute-done | bytes 524320 | tf_op jit(solution)/shard_map/ppermute | solution.py:256
  194.4 1.0 add.5
  (57 shorter events, 1.4 us)
Async XLA Ops:
  0.0 18.7 %collective-permute-start = (bf16[128,2048]{1,0:T(8,128)(2,1)}, bf16[128,2048]{1,0:T(8,128)(2,1)S(1)}, u32[]{:S(2)}, u32[]{:S(2)}) collective-permute-start(bf16[128,2048]{1,0:T(8,128)(2,1)} %refs_0_.9), channel_id=1, source_target_pairs={{0,1},{1,2},{2,3},{3,0},{4,5},{5,6},{6,7},{7,4},{8,9},{9,10},{10,1... | collective-permute-start | bytes 1572872 | tf_op jit(solution)/shard_map/ppermute | solution.py:256
  3.0 1.1 copy-start
  10.2 10.1 %copy-start.1 = (bf16[128,2048]{1,0:T(8,128)(2,1)S(1)}, bf16[128,2048]{1,0:T(8,128)(2,1)}, u32[]{:S(2)}) copy-start(bf16[128,2048]{1,0:T(8,128)(2,1)} %refs_0_.9) | copy-start | bytes 1572868
  10.2 6.7 %collective-permute-start.2 = (bf16[64,3584]{1,0:T(8,128)(2,1)S(1)}, bf16[64,3584]{1,0:T(8,128)(2,1)S(1)}, u32[]{:S(2)}, u32[]{:S(2)}) collective-permute-start(bf16[64,3584]{1,0:T(8,128)(2,1)S(1)} %get-tuple-element.57.refs_2_), channel_id=1, source_target_pairs={{0,4},{4,0},{8,12},{12,8},{1,5},{5,1},{9,13},{13,9},{2,6},{6,2},{1... | collective-permute-start | bytes 1376264 | tf_op jit(solution)/shard_map/ppermute | solution.py:259
  16.4 10.8 %collective-permute-start.5 = (bf16[64,3584]{1,0:T(8,128)(2,1)S(1)}, bf16[64,3584]{1,0:T(8,128)(2,1)S(1)}, u32[]{:S(2)}, u32[]{:S(2)}) collective-permute-start(bf16[64,3584]{1,0:T(8,128)(2,1)S(1)} %get-tuple-element.58.refs_2_), channel_id=1, source_target_pairs={{0,4},{4,0},{8,12},{12,8},{1,5},{5,1},{9,13},{13,9},{2,6},{6,2},{1... | collective-permute-start | bytes 1376264 | tf_op jit(solution)/shard_map/ppermute | solution.py:259
  17.2 23.9 %collective-permute-start.4 = (bf16[32,3584]{1,0:T(8,128)(2,1)S(1)}, bf16[32,3584]{1,0:T(8,128)(2,1)S(1)}, u32[]{:S(2)}, u32[]{:S(2)}) collective-permute-start(bf16[32,3584]{1,0:T(8,128)(2,1)S(1)} %get-tuple-element.59.refs_3_), channel_id=1, source_target_pairs={{0,8},{4,12},{8,0},{12,4},{1,9},{5,13},{9,1},{13,5},{2,10},{6,14},... | collective-permute-start | bytes 688136 | tf_op jit(solution)/shard_map/ppermute | solution.py:259
  18.7 15.4 %collective-permute-start.1 = (bf16[128,2048]{1,0:T(8,128)(2,1)S(1)}, bf16[128,2048]{1,0:T(8,128)(2,1)S(1)}, u32[]{:S(2)}, u32[]{:S(2)}) collective-permute-start(bf16[128,2048]{1,0:T(8,128)(2,1)S(1)} %collective-permute-done.refs_1_.refs_0_), channel_id=1, source_target_pairs={{0,1},{1,2},{2,3},{3,0},{4,5},{5,6},{6,7},{7,4},{8,9},{9,10},{10,1... | collective-permute-start | bytes 1572872 | tf_op jit(solution)/shard_map/ppermute | solution.py:256
  27.1 15.1 %collective-permute-start.3 = (bf16[128,3584]{1,0:T(8,128)(2,1)S(1)}, bf16[128,3584]{1,0:T(8,128)(2,1)S(1)}, u32[]{:S(2)}, u32[]{:S(2)}) collective-permute-start(bf16[128,3584]{1,0:T(8,128)(2,1)S(1)} %get-tuple-element.61.refs_2_), channel_id=1, source_target_pairs={{0,4},{4,0},{8,12},{12,8},{1,5},{5,1},{9,13},{13,9},{2,6},{6,2},{1... | collective-permute-start | bytes 2752520 | tf_op jit(solution)/shard_map/ppermute | solution.py:259
  27.5 13.6 %collective-permute-start.6 = (bf16[32,3584]{1,0:T(8,128)(2,1)S(1)}, bf16[32,3584]{1,0:T(8,128)(2,1)S(1)}, u32[]{:S(2)}, u32[]{:S(2)}) collective-permute-start(bf16[32,3584]{1,0:T(8,128)(2,1)S(1)} %get-tuple-element.65.refs_3_), channel_id=1, source_target_pairs={{0,8},{4,12},{8,0},{12,4},{1,9},{5,13},{9,1},{13,5},{2,10},{6,14},... | collective-permute-start | bytes 688136 | tf_op jit(solution)/shard_map/ppermute | solution.py:259
  41.0 10.1 %collective-permute-start.8 = (bf16[128,3584]{1,0:T(8,128)(2,1)S(1)}, bf16[128,3584]{1,0:T(8,128)(2,1)S(1)}, u32[]{:S(2)}, u32[]{:S(2)}) collective-permute-start(bf16[128,3584]{1,0:T(8,128)(2,1)S(1)} %get-tuple-element.66.refs_4_), channel_id=1, source_target_pairs={{0,4},{4,0},{8,12},{12,8},{1,5},{5,1},{9,13},{13,9},{2,6},{6,2},{1... | collective-permute-start | bytes 2752520 | tf_op jit(solution)/shard_map/ppermute | solution.py:259
  41.5 25.8 %collective-permute-start.17 = (bf16[32,3584]{1,0:T(8,128)(2,1)S(1)}, bf16[32,3584]{1,0:T(8,128)(2,1)S(1)}, u32[]{:S(2)}, u32[]{:S(2)}) collective-permute-start(bf16[32,3584]{1,0:T(8,128)(2,1)S(1)} %activate.5.refs_2_.refs_0_), channel_id=1, source_target_pairs={{0,8},{4,12},{8,0},{12,4},{1,9},{5,13},{9,1},{13,5},{2,10},{6,14},... | collective-permute-start | bytes 688136 | tf_op jit(solution)/shard_map/ppermute | solution.py:259
  42.1 38.5 %collective-permute-start.16 = (bf16[32,3584]{1,0:T(8,128)(2,1)S(1)}, bf16[32,3584]{1,0:T(8,128)(2,1)S(1)}, u32[]{:S(2)}, u32[]{:S(2)}) collective-permute-start(bf16[32,3584]{1,0:T(8,128)(2,1)S(1)} %activate.5.refs_2_.refs_0_), channel_id=1, source_target_pairs={{0,4},{4,0},{8,12},{12,8},{1,5},{5,1},{9,13},{13,9},{2,6},{6,2},{1... | collective-permute-start | bytes 688136 | tf_op jit(solution)/shard_map/ppermute | solution.py:259
  42.2 26.6 %collective-permute-start.12 = (bf16[128,2048]{1,0:T(8,128)(2,1)S(1)}, bf16[128,2048]{1,0:T(8,128)(2,1)S(1)}, u32[]{:S(2)}, u32[]{:S(2)}) collective-permute-start(bf16[128,2048]{1,0:T(8,128)(2,1)S(1)} %collective-permute-done.1.refs_4_.refs_1_.refs_0_), channel_id=1, source_target_pairs={{0,1},{1,2},{2,3},{3,0},{4,5},{5,6},{6,7},{7,4},{8,9},{9,10},{10,1... | collective-permute-start | bytes 1572872 | tf_op jit(solution)/shard_map/ppermute | solution.py:256
  42.7 16.6 %collective-permute-start.9 = (bf16[64,3584]{1,0:T(8,128)(2,1)S(1)}, bf16[64,3584]{1,0:T(8,128)(2,1)S(1)}, u32[]{:S(2)}, u32[]{:S(2)}) collective-permute-start(bf16[64,3584]{1,0:T(8,128)(2,1)S(1)} %get-tuple-element.67.refs_3_), channel_id=1, source_target_pairs={{0,8},{4,12},{8,0},{12,4},{1,9},{5,13},{9,1},{13,5},{2,10},{6,14},... | collective-permute-start | bytes 1376264 | tf_op jit(solution)/shard_map/ppermute | solution.py:259
  51.1 15.6 %collective-permute-start.7 = (bf16[128,3584]{1,0:T(8,128)(2,1)S(1)}, bf16[128,3584]{1,0:T(8,128)(2,1)S(1)}, u32[]{:S(2)}, u32[]{:S(2)}) collective-permute-start(bf16[128,3584]{1,0:T(8,128)(2,1)S(1)} %get-tuple-element.69.refs_2_), channel_id=1, source_target_pairs={{0,4},{4,0},{8,12},{12,8},{1,5},{5,1},{9,13},{13,9},{2,6},{6,2},{1... | collective-permute-start | bytes 2752520 | tf_op jit(solution)/shard_map/ppermute | solution.py:259
  59.3 13.1 %collective-permute-start.13 = (bf16[64,3584]{1,0:T(8,128)(2,1)S(1)}, bf16[64,3584]{1,0:T(8,128)(2,1)S(1)}, u32[]{:S(2)}, u32[]{:S(2)}) collective-permute-start(bf16[64,3584]{1,0:T(8,128)(2,1)S(1)} %get-tuple-element.71.refs_3_), channel_id=1, source_target_pairs={{0,8},{4,12},{8,0},{12,4},{1,9},{5,13},{9,1},{13,5},{2,10},{6,14},... | collective-permute-start | bytes 1376264 | tf_op jit(solution)/shard_map/ppermute | solution.py:259
  66.7 12.6 %collective-permute-start.11 = (bf16[128,3584]{1,0:T(8,128)(2,1)S(1)}, bf16[128,3584]{1,0:T(8,128)(2,1)S(1)}, u32[]{:S(2)}, u32[]{:S(2)}) collective-permute-start(bf16[128,3584]{1,0:T(8,128)(2,1)S(1)} %get-tuple-element.72.refs_2_), channel_id=1, source_target_pairs={{0,4},{4,0},{8,12},{12,8},{1,5},{5,1},{9,13},{13,9},{2,6},{6,2},{1... | collective-permute-start | bytes 2752520 | tf_op jit(solution)/shard_map/ppermute | solution.py:259
  67.3 15.4 %collective-permute-start.10 = (bf16[64,3584]{1,0:T(8,128)(2,1)S(1)}, bf16[64,3584]{1,0:T(8,128)(2,1)S(1)}, u32[]{:S(2)}, u32[]{:S(2)}) collective-permute-start(bf16[64,3584]{1,0:T(8,128)(2,1)S(1)} %get-tuple-element.74.refs_3_), channel_id=1, source_target_pairs={{0,8},{4,12},{8,0},{12,4},{1,9},{5,13},{9,1},{13,5},{2,10},{6,14},... | collective-permute-start | bytes 1376264 | tf_op jit(solution)/shard_map/ppermute | solution.py:259
  68.8 13.8 %collective-permute-start.18 = (bf16[32,3584]{1,0:T(8,128)(2,1)S(1)}, bf16[32,3584]{1,0:T(8,128)(2,1)S(1)}, u32[]{:S(2)}, u32[]{:S(2)}) collective-permute-start(bf16[32,3584]{1,0:T(8,128)(2,1)S(1)} %collective-permute-done.17.refs_5_.refs_2_), channel_id=1, source_target_pairs={{0,4},{4,0},{8,12},{12,8},{1,5},{5,1},{9,13},{13,9},{2,6},{6,2},{1... | collective-permute-start | bytes 688136 | tf_op jit(solution)/shard_map/ppermute | solution.py:259
  79.2 10.8 %collective-permute-start.15 = (bf16[128,3584]{1,0:T(8,128)(2,1)S(1)}, bf16[128,3584]{1,0:T(8,128)(2,1)S(1)}, u32[]{:S(2)}, u32[]{:S(2)}) collective-permute-start(bf16[128,3584]{1,0:T(8,128)(2,1)S(1)} %get-tuple-element.76.refs_2_), channel_id=1, source_target_pairs={{0,4},{4,0},{8,12},{12,8},{1,5},{5,1},{9,13},{13,9},{2,6},{6,2},{1... | collective-permute-start | bytes 2752520 | tf_op jit(solution)/shard_map/ppermute | solution.py:259
  79.8 16.9 %collective-permute-start.14 = (bf16[64,3584]{1,0:T(8,128)(2,1)S(1)}, bf16[64,3584]{1,0:T(8,128)(2,1)S(1)}, u32[]{:S(2)}, u32[]{:S(2)}) collective-permute-start(bf16[64,3584]{1,0:T(8,128)(2,1)S(1)} %get-tuple-element.78.refs_4_), channel_id=1, source_target_pairs={{0,8},{4,12},{8,0},{12,4},{1,9},{5,13},{9,1},{13,5},{2,10},{6,14},... | collective-permute-start | bytes 1376264 | tf_op jit(solution)/shard_map/ppermute | solution.py:259
  80.5 22.5 %collective-permute-start.22 = (bf16[64,3584]{1,0:T(8,128)(2,1)S(1)}, bf16[64,3584]{1,0:T(8,128)(2,1)S(1)}, u32[]{:S(2)}, u32[]{:S(2)}) collective-permute-start(bf16[64,3584]{1,0:T(8,128)(2,1)S(1)} %activate.6.refs_3_.refs_0_), channel_id=1, source_target_pairs={{0,8},{4,12},{8,0},{12,4},{1,9},{5,13},{9,1},{13,5},{2,10},{6,14},... | collective-permute-start | bytes 1376264 | tf_op jit(solution)/shard_map/ppermute | solution.py:259
  82.6 26.5 %collective-permute-start.21 = (bf16[64,3584]{1,0:T(8,128)(2,1)S(1)}, bf16[64,3584]{1,0:T(8,128)(2,1)S(1)}, u32[]{:S(2)}, u32[]{:S(2)}) collective-permute-start(bf16[64,3584]{1,0:T(8,128)(2,1)S(1)} %activate.6.refs_3_.refs_0_), channel_id=1, source_target_pairs={{0,4},{4,0},{8,12},{12,8},{1,5},{5,1},{9,13},{13,9},{2,6},{6,2},{1... | collective-permute-start | bytes 1376264 | tf_op jit(solution)/shard_map/ppermute | solution.py:259
  89.5 9.9 %collective-permute-start.23 = (bf16[128,3584]{1,0:T(8,128)(2,1)S(1)}, bf16[128,3584]{1,0:T(8,128)(2,1)S(1)}, u32[]{:S(2)}, u32[]{:S(2)}) collective-permute-start(bf16[128,3584]{1,0:T(8,128)(2,1)S(1)} %get-tuple-element.83.refs_2_), channel_id=1, source_target_pairs={{0,4},{4,0},{8,12},{12,8},{1,5},{5,1},{9,13},{13,9},{2,6},{6,2},{1... | collective-permute-start | bytes 2752520 | tf_op jit(solution)/shard_map/ppermute | solution.py:259
  90.5 32.7 %collective-permute-start.26 = (bf16[64,3584]{1,0:T(8,128)(2,1)S(1)}, bf16[64,3584]{1,0:T(8,128)(2,1)S(1)}, u32[]{:S(2)}, u32[]{:S(2)}) collective-permute-start(bf16[64,3584]{1,0:T(8,128)(2,1)S(1)} %get-tuple-element.84.refs_2_), channel_id=1, source_target_pairs={{0,8},{4,12},{8,0},{12,4},{1,9},{5,13},{9,1},{13,5},{2,10},{6,14},... | collective-permute-start | bytes 1376264 | tf_op jit(solution)/shard_map/ppermute | solution.py:259
  97.4 25.3 %collective-permute-start.20 = (bf16[64,3584]{1,0:T(8,128)(2,1)S(1)}, bf16[64,3584]{1,0:T(8,128)(2,1)S(1)}, u32[]{:S(2)}, u32[]{:S(2)}) collective-permute-start(bf16[64,3584]{1,0:T(8,128)(2,1)S(1)} %activate.7.refs_2_.refs_0_), channel_id=1, source_target_pairs={{0,8},{4,12},{8,0},{12,4},{1,9},{5,13},{9,1},{13,5},{2,10},{6,14},... | collective-permute-start | bytes 1376264 | tf_op jit(solution)/shard_map/ppermute | solution.py:259
  99.4 33.7 %collective-permute-start.19 = (bf16[64,3584]{1,0:T(8,128)(2,1)S(1)}, bf16[64,3584]{1,0:T(8,128)(2,1)S(1)}, u32[]{:S(2)}, u32[]{:S(2)}) collective-permute-start(bf16[64,3584]{1,0:T(8,128)(2,1)S(1)} %activate.7.refs_2_.refs_0_), channel_id=1, source_target_pairs={{0,4},{4,0},{8,12},{12,8},{1,5},{5,1},{9,13},{13,9},{2,6},{6,2},{1... | collective-permute-start | bytes 1376264 | tf_op jit(solution)/shard_map/ppermute | solution.py:259
  103.0 6.2 %collective-permute-start.24 = (bf16[64,3584]{1,0:T(8,128)(2,1)S(1)}, bf16[64,3584]{1,0:T(8,128)(2,1)S(1)}, u32[]{:S(2)}, u32[]{:S(2)}) collective-permute-start(bf16[64,3584]{1,0:T(8,128)(2,1)S(1)} %collective-permute-done.22.refs_2_), channel_id=1, source_target_pairs={{0,4},{4,0},{8,12},{12,8},{1,5},{5,1},{9,13},{13,9},{2,6},{6,2},{1... | collective-permute-start | bytes 1376264 | tf_op jit(solution)/shard_map/ppermute | solution.py:259
  109.1 23.0 %collective-permute-start.27 = (bf16[64,3584]{1,0:T(8,128)(2,1)S(1)}, bf16[64,3584]{1,0:T(8,128)(2,1)S(1)}, u32[]{:S(2)}, u32[]{:S(2)}) collective-permute-start(bf16[64,3584]{1,0:T(8,128)(2,1)S(1)} %get-tuple-element.87.refs_2_), channel_id=1, source_target_pairs={{0,8},{4,12},{8,0},{12,4},{1,9},{5,13},{9,1},{13,5},{2,10},{6,14},... | collective-permute-start | bytes 1376264 | tf_op jit(solution)/shard_map/ppermute | solution.py:259
  122.7 10.4 %collective-permute-start.25 = (bf16[64,3584]{1,0:T(8,128)(2,1)S(1)}, bf16[64,3584]{1,0:T(8,128)(2,1)S(1)}, u32[]{:S(2)}, u32[]{:S(2)}) collective-permute-start(bf16[64,3584]{1,0:T(8,128)(2,1)S(1)} %collective-permute-done.20.refs_2_), channel_id=1, source_target_pairs={{0,4},{4,0},{8,12},{12,8},{1,5},{5,1},{9,13},{13,9},{2,6},{6,2},{1... | collective-permute-start | bytes 1376264 | tf_op jit(solution)/shard_map/ppermute | solution.py:259
  122.7 17.4 %collective-permute-start.32 = (bf16[64,3584]{1,0:T(8,128)(2,1)S(1)}, bf16[64,3584]{1,0:T(8,128)(2,1)S(1)}, u32[]{:S(2)}, u32[]{:S(2)}) collective-permute-start(bf16[64,3584]{1,0:T(8,128)(2,1)S(1)} %get-tuple-element.85.refs_4_), channel_id=1, source_target_pairs={{0,4},{4,0},{8,12},{12,8},{1,5},{5,1},{9,13},{13,9},{2,6},{6,2},{1... | collective-permute-start | bytes 1376264 | tf_op jit(solution)/shard_map/ppermute | solution.py:259
  123.2 19.0 %collective-permute-start.31 = (bf16[64,3584]{1,0:T(8,128)(2,1)S(1)}, bf16[64,3584]{1,0:T(8,128)(2,1)S(1)}, u32[]{:S(2)}, u32[]{:S(2)}) collective-permute-start(bf16[64,3584]{1,0:T(8,128)(2,1)S(1)} %get-tuple-element.89.refs_5_), channel_id=1, source_target_pairs={{0,4},{4,0},{8,12},{12,8},{1,5},{5,1},{9,13},{13,9},{2,6},{6,2},{1... | collective-permute-start | bytes 1376264 | tf_op jit(solution)/shard_map/ppermute | solution.py:259
  132.7 13.5 %collective-permute-start.30 = (bf16[64,3584]{1,0:T(8,128)(2,1)S(1)}, bf16[64,3584]{1,0:T(8,128)(2,1)S(1)}, u32[]{:S(2)}, u32[]{:S(2)}) collective-permute-start(bf16[64,3584]{1,0:T(8,128)(2,1)S(1)} %activate.8.refs_6_.refs_0_), channel_id=1, source_target_pairs={{0,8},{4,12},{8,0},{12,4},{1,9},{5,13},{9,1},{13,5},{2,10},{6,14},... | collective-permute-start | bytes 1376264 | tf_op jit(solution)/shard_map/ppermute | solution.py:259
  133.1 22.6 %collective-permute-start.29 = (bf16[64,3584]{1,0:T(8,128)(2,1)S(1)}, bf16[64,3584]{1,0:T(8,128)(2,1)S(1)}, u32[]{:S(2)}, u32[]{:S(2)}) collective-permute-start(bf16[64,3584]{1,0:T(8,128)(2,1)S(1)} %activate.8.refs_6_.refs_0_), channel_id=1, source_target_pairs={{0,4},{4,0},{8,12},{12,8},{1,5},{5,1},{9,13},{13,9},{2,6},{6,2},{1... | collective-permute-start | bytes 1376264 | tf_op jit(solution)/shard_map/ppermute | solution.py:259
  140.0 22.6 %collective-permute-start.28 = (bf16[128,2048]{1,0:T(8,128)(2,1)S(1)}, bf16[128,2048]{1,0:T(8,128)(2,1)S(1)}, u32[]{:S(2)}, u32[]{:S(2)}) collective-permute-start(bf16[128,2048]{1,0:T(8,128)(2,1)S(1)} %get-tuple-element.95.refs_2_), channel_id=1, source_target_pairs={{0,1},{1,2},{2,3},{3,0},{4,5},{5,6},{6,7},{7,4},{8,9},{9,10},{10,1... | collective-permute-start | bytes 1572872 | tf_op jit(solution)/shard_map/ppermute | solution.py:256
  140.4 14.4 %collective-permute-start.34 = (bf16[32,3584]{1,0:T(8,128)(2,1)S(1)}, bf16[32,3584]{1,0:T(8,128)(2,1)S(1)}, u32[]{:S(2)}, u32[]{:S(2)}) collective-permute-start(bf16[32,3584]{1,0:T(8,128)(2,1)S(1)} %get-tuple-element.98.refs_2_), channel_id=1, source_target_pairs={{0,8},{4,12},{8,0},{12,4},{1,9},{5,13},{9,1},{13,5},{2,10},{6,14},... | collective-permute-start | bytes 688136 | tf_op jit(solution)/shard_map/ppermute | solution.py:259
  142.5 12.3 %collective-permute-start.35 = (bf16[32,3584]{1,0:T(8,128)(2,1)S(1)}, bf16[32,3584]{1,0:T(8,128)(2,1)S(1)}, u32[]{:S(2)}, u32[]{:S(2)}) collective-permute-start(bf16[32,3584]{1,0:T(8,128)(2,1)S(1)} %get-tuple-element.99.refs_6_), channel_id=1, source_target_pairs={{0,8},{4,12},{8,0},{12,4},{1,9},{5,13},{9,1},{13,5},{2,10},{6,14},... | collective-permute-start | bytes 688136 | tf_op jit(solution)/shard_map/ppermute | solution.py:259
  146.2 9.5 %collective-permute-start.33 = (bf16[64,3584]{1,0:T(8,128)(2,1)S(1)}, bf16[64,3584]{1,0:T(8,128)(2,1)S(1)}, u32[]{:S(2)}, u32[]{:S(2)}) collective-permute-start(bf16[64,3584]{1,0:T(8,128)(2,1)S(1)} %collective-permute-done.30.refs_2_), channel_id=1, source_target_pairs={{0,4},{4,0},{8,12},{12,8},{1,5},{5,1},{9,13},{13,9},{2,6},{6,2},{1... | collective-permute-start | bytes 1376264 | tf_op jit(solution)/shard_map/ppermute | solution.py:259
  155.1 7.8 %collective-permute-start.38 = (bf16[32,3584]{1,0:T(8,128)(2,1)S(1)}, bf16[32,3584]{1,0:T(8,128)(2,1)S(1)}, u32[]{:S(2)}, u32[]{:S(2)}) collective-permute-start(bf16[32,3584]{1,0:T(8,128)(2,1)S(1)} %activate.9.refs_6_.refs_0_), channel_id=1, source_target_pairs={{0,8},{4,12},{8,0},{12,4},{1,9},{5,13},{9,1},{13,5},{2,10},{6,14},... | collective-permute-start | bytes 688136 | tf_op jit(solution)/shard_map/ppermute | solution.py:259
  155.7 8.7 %collective-permute-start.37 = (bf16[32,3584]{1,0:T(8,128)(2,1)S(1)}, bf16[32,3584]{1,0:T(8,128)(2,1)S(1)}, u32[]{:S(2)}, u32[]{:S(2)}) collective-permute-start(bf16[32,3584]{1,0:T(8,128)(2,1)S(1)} %activate.9.refs_6_.refs_0_), channel_id=1, source_target_pairs={{0,4},{4,0},{8,12},{12,8},{1,5},{5,1},{9,13},{13,9},{2,6},{6,2},{1... | collective-permute-start | bytes 688136 | tf_op jit(solution)/shard_map/ppermute | solution.py:259
  162.9 1.7 collective-permute-start.39
  163.5 15.7 %collective-permute-start.36 = (bf16[128,2048]{1,0:T(8,128)(2,1)S(1)}, bf16[128,2048]{1,0:T(8,128)(2,1)S(1)}, u32[]{:S(2)}, u32[]{:S(2)}) collective-permute-start(bf16[128,2048]{1,0:T(8,128)(2,1)S(1)} %add.3.refs_6_), channel_id=1, source_target_pairs={{0,1},{1,2},{2,3},{3,0},{4,5},{5,6},{6,7},{7,4},{8,9},{9,10},{10,1... | collective-permute-start | bytes 1572872 | tf_op jit(solution)/shard_map/ppermute | solution.py:256
  164.6 29.8 %copy-start.2 = (bf16[128,2048]{1,0:T(8,128)(2,1)S(1)}, bf16[128,2048]{1,0:T(8,128)(2,1)}, u32[]{:S(2)}) copy-start(bf16[128,2048]{1,0:T(8,128)(2,1)} %refs_0_.9) | copy-start | bytes 1572868
  179.5 14.9 %collective-permute-start.40 = (bf16[128,2048]{1,0:T(8,128)(2,1)S(1)}, bf16[128,2048]{1,0:T(8,128)(2,1)S(1)}, u32[]{:S(2)}, u32[]{:S(2)}) collective-permute-start(bf16[128,2048]{1,0:T(8,128)(2,1)S(1)} %add.4.refs_3_), channel_id=1, source_target_pairs={{0,1},{1,2},{2,3},{3,0},{4,5},{5,6},{6,7},{7,4},{8,9},{9,10},{10,1... | collective-permute-start | bytes 1572872 | tf_op jit(solution)/shard_map/ppermute | solution.py:256

commit v2 on v1

--- a/solution.py
+++ b/solution.py
@@ -30,11 +30,12 @@
     return order
 
 
-def first_dot(shards, weight, columns, bits, fixed, after):
+def first_dot(shards, weight, columns, bits, parts, fixed, after):
     rows, depth = shards[0].shape
     at, width = columns
     n, g = 1 << bits, len(shards)
     r, m = rows // n, g * rows
+    share = m // 2 // parts
     step = block_of(width, 512)
     steps = width // step
     slots = min(4, steps)
@@ -42,7 +43,8 @@
 
     def kernel(*refs):
         x, w = refs[:g], refs[g]
-        keep, send, held, buf, x_sem, w_sem = refs[-6:]
+        keep, sends = refs[-5 - parts], refs[-4 - parts : -4]
+        held, buf, x_sem, w_sem = refs[-4:]
         c = pl.program_id(0)
 
         def load(block):
@@ -72,19 +74,19 @@
         load(c).wait()
         part = jnp.dot(held[...], buf[c % slots], preferred_element_type=F32).astype(BF16)
         keep[...] = part[: m // 2]
-        send[...] = part[m // 2 :]
+        for i, send in enumerate(sends):
+            send[...] = part[m // 2 + i * share : m // 2 + (i + 1) * share]
 
         @pl.when(c + slots < steps)
         def _():
             load(c + slots).start()
 
-    out = jax.ShapeDtypeStruct((m // 2, width), BF16)
     return pl.pallas_call(
         kernel,
         grid=(steps,),
         in_specs=[HBM if i in fixed else ANY for i in range(g)] + [HBM] + [ANY] * len(after),
-        out_specs=[pl.BlockSpec((m // 2, step), lambda c: (0, c))] * 2,
-        out_shape=[out, out],
+        out_specs=[pl.BlockSpec((h, step), lambda c: (0, c)) for h in [m // 2] + [share] * parts],
+        out_shape=[jax.ShapeDtypeStruct((h, width), BF16) for h in [m // 2] + [share] * parts],
         scratch_shapes=[
             pltpu.VMEM((m, depth), BF16),
             pltpu.VMEM((slots, depth, step), BF16),
@@ -100,10 +102,12 @@
 def fold(keep, got, after):
     m, width = keep.shape
     step = block_of(width, 1792)
+    k = len(got)
 
     def kernel(*refs):
         stay, send = refs[-2:]
-        total = (refs[0][...].astype(F32) + refs[1][...].astype(F32)).astype(BF16)
+        other = jnp.concatenate([ref[...] for ref in refs[1 : 1 + k]], axis=0)
+        total = (refs[0][...].astype(F32) + other.astype(F32)).astype(BF16)
         stay[...] = total[: m // 2]
         send[...] = total[m // 2 :]
 
@@ -111,13 +115,13 @@
     return pl.pallas_call(
         kernel,
         grid=(width // step,),
-        in_specs=[pl.BlockSpec((m, step), lambda c: (0, c))] * 2 + [ANY] * len(after),
+        in_specs=[pl.BlockSpec((a.shape[0], step), lambda c: (0, c)) for a in (keep, *got)] + [ANY] * len(after),
         out_specs=[pl.BlockSpec((m // 2, step), lambda c: (0, c))] * 2,
         out_shape=[out, out],
         compiler_params=params(40),
-        cost_estimate=cost(m * width, 6 * m * width),
+        cost_estimate=cost(1, 1),
         name="fold",
-    )(keep, got, *after)
+    )(keep, *got, *after)
 
 
 def activate(gate, up, after):
@@ -136,7 +140,7 @@
         out_specs=pl.BlockSpec((m, step), lambda c: (0, c)),
         out_shape=jax.ShapeDtypeStruct((m, width), BF16),
         compiler_params=params(40),
-        cost_estimate=cost(8 * m * width, 10 * m * width, m * width),
+        cost_estimate=cost(1, 1),
         name="activate",
     )(*gate, *up, *after)
 
@@ -230,7 +234,7 @@
         out_specs=pl.BlockSpec((m, step), lambda c: (0, c)),
         out_shape=jax.ShapeDtypeStruct((m, width), BF16),
         compiler_params=params(40),
-        cost_estimate=cost(m * width * len(values), 2 * m * width * (len(values) + 1)),
+        cost_estimate=cost(1, 1),
         name="add",
     )(*values, *after)
 
@@ -269,19 +273,20 @@
 
         def dot(k, w):
             rows, columns = rects[k]
-            keep, send = first_dot(
-                [held[i] for i in rows], weights[w], columns, bits, [j for j, i in enumerate(rows) if i == 0], last
+            parts = 2 * len(rows)
+            keep, *sends = first_dot(
+                [held[i] for i in rows], weights[w], columns, bits, parts, [j for j, i in enumerate(rows) if i == 0], last
             )
-            last[:] = [send]
-            dotted[k, w] = keep, swap(send, 0)
+            last[:] = sends[:1]
+            dotted[k, w] = keep, [swap(send, 0) for send in sends]
 
         def sum_core(k, w):
             keep, got = dotted[k, w]
             for bit in range(1, bits):
                 keep, send = fold(keep, got, last)
                 last[:] = [send]
-                got = swap(send, bit)
-            folded[k, w] = keep, got
+                got = [swap(send, bit)]
+            folded[k, w] = keep, got[0]
 
         def act(k):
             own = activate(folded[k, 0], folded[k, 1], last)
@@ -328,14 +333,14 @@
 
         if n_tensor == 4:
             plan = [
-                (dot, 0, 0), (dot, 0, 1), (sum_core, 0, 0), (dot, 1, 0), (sum_core, 0, 1), (need, 2),
-                (dot, 1, 1), (act, 0), (sum_core, 1, 0), (dot, 2, 0), (sum_core, 1, 1), (need_partial, 1, 0),
-                (dot, 2, 1), (sum_core, 2, 0), (forward, 0), (need_partial, 1, 1), (dot, 3, 0),
-                (sum_core, 2, 1), (act, 1), (need_hidden, 0), (need_partial, 2, 0), (dot, 3, 1),
-                (sum_core, 3, 0), (dot, 4, 0), (act, 2), (sum_core, 3, 1), (forward, 1), (dot, 4, 1),
-                (down, 1), (forward, 2), (act, 3), (down, 2), (pass_on, 1), (sum_core, 4, 0), (sum_core, 4, 1),
-                (forward, 3), (down, 0), (act, 4), (down, 3), (pass_on, 2), (forward, 4), (down, 4),
-                (pass_on, 3),
+                (dot, 0, 0), (dot, 0, 1), (sum_core, 0, 0), (dot, 1, 0), (sum_core, 0, 1), (sum_core, 1, 0),
+                (need, 2), (dot, 1, 1), (act, 0), (sum_core, 1, 1), (need_partial, 1, 0), (dot, 2, 0),
+                (sum_core, 2, 0), (need_partial, 1, 1), (dot, 2, 1), (act, 1), (need_partial, 2, 0),
+                (dot, 3, 0), (sum_core, 2, 1), (forward, 1), (dot, 3, 1), (sum_core, 3, 0), (forward, 0),
+                (need_partial, 2, 1), (dot, 4, 0), (act, 2), (sum_core, 3, 1), (need_hidden, 0),
+                (need_partial, 3, 0), (dot, 4, 1), (forward, 2), (down, 1), (act, 3), (down, 2), (pass_on, 1),
+                (sum_core, 4, 0), (sum_core, 4, 1), (forward, 3), (down, 0), (down, 3), (pass_on, 2), (act, 4),
+                (forward, 4), (down, 4), (pass_on, 3),
             ]
         else:
             plan = []

time: 196 us -> 203 us (1.036)
  starting transfers between devices: 22.5 us -> 35 us
  waiting for transfers between devices: 65.1 us -> 59.5 us
    ppermute x35 -> x57, starting transfers between devices: 16.9 us -> 28.6 us  [swap(): lax.ppermute(value, 'pipe', [(i, i ^ 1 << bit) for i in range(n_pipe)])]
    ppermute x35 -> x57, waiting for transfers between devices: 35.8 us -> 30.2 us  [swap(): lax.ppermute(value, 'pipe', [(i, i ^ 1 << bit) for i in range(n_pipe)])]
  transfers between devices with their start and end apart: 41 -> 63, of which waited for: 11 -> 19; matrix products, arithmetic and copies ran while one was open for 0% -> 0% of each run, Pallas kernels for 54% -> 52%
where the time goes in v2:
time: 203 us
  Pallas kernels  107 us (53%)
  waiting for transfers between devices  59.5 us (29%)
  starting transfers between devices  35 us (17%)
    pallas_call x10, Pallas kernels, first_dot(): pl.pallas_call(kernel, grid=(steps,), in_specs=[HBM if i in fixed else AN...  66 us
    pallas_call x5, Pallas kernels, last_dot(): pl.pallas_call(kernel, grid=(steps,), in_specs=[ANY] * n + [HBM] + [pl.Bl...  32.9 us
    ppermute x57, waiting for transfers between devices, swap(): lax.ppermute(value, 'pipe', [(i, i ^ 1 << bit) for i in range(n_pipe)])  30.2 us
    ppermute x6, waiting for transfers between devices, hop(): return lax.ppermute(value, 'tensor', ring)  29.4 us
    ppermute x57, starting transfers between devices, swap(): lax.ppermute(value, 'pipe', [(i, i ^ 1 << bit) for i in range(n_pipe)])  28.6 us
    ppermute x6, starting transfers between devices, hop(): return lax.ppermute(value, 'tensor', ring)  6.35 us
  transfers between devices with their start and end apart: 63, of which 19 were waited for; matrix products, arithmetic and copies ran while one was open for 0% of the time, Pallas kernels for 52%

profile of v2, /device:TPU:0, one launch (start us, length us, event | category | flops | bytes accessed | tf_op | source)
XLA Modules:
  0.0 203.1 jit_solution(7641674618068503036)
XLA Ops:
  0.0 3.0 %collective-permute-start = (bf16[128,2048]{1,0:T(8,128)(2,1)}, bf16[128,2048]{1,0:T(8,128)(2,1)S(1)}, u32[]{:S(2)}, u32[]{:S(2)}) collective-permute-start(bf16[128,2048]{1,0:T(8,128)(2,1)} %refs_0_.9), channel_id=1, source_target_pairs={{0,1},{1,2},{2,3},{3,0},{4,5},{5,6},{6,7},{7,4},{8,9},{9,10},{10,1... | collective-permute-start | bytes 1572872 | tf_op jit(solution)/shard_map/ppermute | solution.py:260
  3.0 1.1 copy-done
  4.1 6.1 %first_dot.10 = (bf16[64,3584]{1,0:T(8,128)(2,1)S(1)}, bf16[32,3584]{1,0:T(8,128)(2,1)S(1)}, bf16[32,3584]{1,0:T(8,128)(2,1)S(1)}) custom-call(bf16[128,2048]{1,0:T(8,128)(2,1)S(1)} %copy-done, bf16[2048,7168]{1,0:T(8,128)(2,1)} %refs_1_.6), custom_call_target="tpu_custom_call" | custom-call | flops 18790481920 | bytes 146800640 | tf_op jit(solution)/shard_map/first_dot/pallas_call | solution.py:84
  10.3 0.5 collective-permute-start.3
  10.8 6.1 %first_dot.11 = (bf16[64,3584]{1,0:T(8,128)(2,1)S(1)}, bf16[32,3584]{1,0:T(8,128)(2,1)S(1)}, bf16[32,3584]{1,0:T(8,128)(2,1)S(1)}) custom-call(bf16[128,2048]{1,0:T(8,128)(2,1)S(1)} %copy-done, bf16[2048,7168]{1,0:T(8,128)(2,1)} %refs_1_.7, bf16[32,3584]{1,0:T(8,128)(2,1)S(1)} %get-tuple-element.79.refs_2_), custom_call_target="tpu_custom_call" | custom-call | flops 18790481920 | bytes 146800640 | tf_op jit(solution)/shard_map/first_dot/pallas_call | solution.py:84
  17.7 1.6 collective-permute-start.1
  19.3 6.9 %first_dot.12 = (bf16[128,3584]{1,0:T(8,128)(2,1)S(1)}, bf16[32,3584]{1,0:T(8,128)(2,1)S(1)}, bf16[32,3584]{1,0:T(8,128)(2,1)S(1)}, bf16[32,3584]{1,0:T(8,128)(2,1)S(1)}, bf16[32,3584]{1,0:T(8,128)(2,1)S(1)}) custom-call(bf16[128,2048]{1,0:T(8,128)(2,1)S(1)} %copy-done.1, bf16[128,2048]{1,0:T(8,128)(2,1)S(1)} %collective-permute-done.refs_1_.refs_0_, ...), custom_call_target="tpu_custom_call" | custom-call | flops 37580963840 | bytes 146800640 | tf_op jit(solution)/shard_map/first_dot/pallas_call | solution.py:84
  26.4 0.5 collective-permute-start.5
  27.8 1.5 collective-permute-start.14
  29.3 0.5 collective-permute-start.15
  29.9 0.5 fold.12
  30.4 1.6 collective-permute-start.16
  31.9 1.6 collective-permute-done.1.refs_4_.refs_1_.refs_0_
  33.5 6.9 %first_dot.13 = (bf16[128,3584]{1,0:T(8,128)(2,1)S(1)}, bf16[32,3584]{1,0:T(8,128)(2,1)S(1)}, bf16[32,3584]{1,0:T(8,128)(2,1)S(1)}, bf16[32,3584]{1,0:T(8,128)(2,1)S(1)}, bf16[32,3584]{1,0:T(8,128)(2,1)S(1)}) custom-call(bf16[128,2048]{1,0:T(8,128)(2,1)S(1)} %copy-done.1, bf16[128,2048]{1,0:T(8,128)(2,1)S(1)} %collective-permute-done.refs_1_.refs_0_, ...), custom_call_target="tpu_custom_call" | custom-call | flops 37580963840 | bytes 146800640 | tf_op jit(solution)/shard_map/first_dot/pallas_call | solution.py:84
  40.6 0.5 collective-permute-start.11
  43.0 0.5 fold.13
  43.5 1.6 collective-permute-start.22
  45.0 6.0 %collective-permute-done.16.refs_4_.refs_1_ = bf16[64,3584]{1,0:T(8,128)(2,1)S(1)} collective-permute-done((bf16[64,3584]{1,0:T(8,128)(2,1)S(1)}, bf16[64,3584]{1,0:T(8,128)(2,1)S(1)}, u32[]{:S(2)}, u32[]{:S(2)}) %collective-permute-start.16) | collective-permute-done | bytes 458784 | tf_op jit(solution)/shard_map/ppermute | solution.py:263
  51.0 6.9 %first_dot.14 = (bf16[128,3584]{1,0:T(8,128)(2,1)S(1)}, bf16[32,3584]{1,0:T(8,128)(2,1)S(1)}, bf16[32,3584]{1,0:T(8,128)(2,1)S(1)}, bf16[32,3584]{1,0:T(8,128)(2,1)S(1)}, bf16[32,3584]{1,0:T(8,128)(2,1)S(1)}) custom-call(bf16[128,2048]{1,0:T(8,128)(2,1)S(1)} %collective-permute-done.refs_1_.refs_0_, ...), custom_call_target="tpu_custom_call" | custom-call | flops 37580963840 | bytes 146800640 | tf_op jit(solution)/shard_map/first_dot/pallas_call | solution.py:84
  58.1 0.5 collective-permute-start.18
  59.1 0.5 collective-permute-done.17.refs_1_
  59.5 1.6 collective-permute-start.27
  61.1 0.5 fold.14
  61.6 1.6 collective-permute-start.21
  63.2 6.9 %first_dot.15 = (bf16[128,3584]{1,0:T(8,128)(2,1)S(1)}, bf16[32,3584]{1,0:T(8,128)(2,1)S(1)}, bf16[32,3584]{1,0:T(8,128)(2,1)S(1)}, bf16[32,3584]{1,0:T(8,128)(2,1)S(1)}, bf16[32,3584]{1,0:T(8,128)(2,1)S(1)}) custom-call(bf16[128,2048]{1,0:T(8,128)(2,1)S(1)} %collective-permute-done.refs_1_.refs_0_, ...), custom_call_target="tpu_custom_call" | custom-call | flops 37580963840 | bytes 146800640 | tf_op jit(solution)/shard_map/first_dot/pallas_call | solution.py:84
  70.2 0.5 collective-permute-start.24
  70.8 0.6 activate.6.refs_3_.refs_0_
  71.4 3.9 %collective-permute-done.27.refs_1_.refs_0_ = bf16[128,2048]{1,0:T(8,128)(2,1)S(1)} collective-permute-done((bf16[128,2048]{1,0:T(8,128)(2,1)S(1)}, bf16[128,2048]{1,0:T(8,128)(2,1)S(1)}, u32[]{:S(2)}, u32[]{:S(2)}) %collective-permute-start.27) | collective-permute-done | bytes 524320 | tf_op jit(solution)/shard_map/ppermute | solution.py:260
  75.3 1.5 collective-permute-start.45
  76.8 6.9 %first_dot.16 = (bf16[128,3584]{1,0:T(8,128)(2,1)S(1)}, bf16[32,3584]{1,0:T(8,128)(2,1)S(1)}, bf16[32,3584]{1,0:T(8,128)(2,1)S(1)}, bf16[32,3584]{1,0:T(8,128)(2,1)S(1)}, bf16[32,3584]{1,0:T(8,128)(2,1)S(1)}) custom-call(bf16[128,2048]{1,0:T(8,128)(2,1)S(1)} %collective-permute-done.1.refs_4_.refs_1_.refs_0_, ...), custom_call_target="tpu_custom_call" | custom-call | flops 37580963840 | bytes 146800640 | tf_op jit(solution)/shard_map/first_dot/pallas_call | solution.py:84
  84.1 0.5 collective-permute-start.40
  84.6 0.5 collective-permute-start.31
  85.1 0.5 fold.15
  85.6 3.0 %collective-permute-done.45.refs_2_ = bf16[64,3584]{1,0:T(8,128)(2,1)S(1)} collective-permute-done((bf16[64,3584]{1,0:T(8,128)(2,1)S(1)}, bf16[64,3584]{1,0:T(8,128)(2,1)S(1)}, u32[]{:S(2)}, u32[]{:S(2)}) %collective-permute-start.45) | collective-permute-done | bytes 458784 | tf_op jit(solution)/shard_map/ppermute | solution.py:263
  88.6 1.5 collective-permute-start.28
  90.1 6.9 %first_dot.17 = (bf16[128,3584]{1,0:T(8,128)(2,1)S(1)}, bf16[32,3584]{1,0:T(8,128)(2,1)S(1)}, bf16[32,3584]{1,0:T(8,128)(2,1)S(1)}, bf16[32,3584]{1,0:T(8,128)(2,1)S(1)}, bf16[32,3584]{1,0:T(8,128)(2,1)S(1)}) custom-call(bf16[128,2048]{1,0:T(8,128)(2,1)S(1)} %collective-permute-done.1.refs_4_.refs_1_.refs_0_, ...), custom_call_target="tpu_custom_call" | custom-call | flops 37580963840 | bytes 146800640 | tf_op jit(solution)/shard_map/first_dot/pallas_call | solution.py:84
  99.0 0.5 collective-permute-start.42
  99.5 3.9 %collective-permute-done.28.refs_3_ = bf16[64,3584]{1,0:T(8,128)(2,1)S(1)} collective-permute-done((bf16[64,3584]{1,0:T(8,128)(2,1)S(1)}, bf16[64,3584]{1,0:T(8,128)(2,1)S(1)}, u32[]{:S(2)}, u32[]{:S(2)}) %collective-permute-start.28) | collective-permute-done | bytes 458784 | tf_op jit(solution)/shard_map/ppermute | solution.py:263
  103.4 6.1 %first_dot.18 = (bf16[64,3584]{1,0:T(8,128)(2,1)S(1)}, bf16[32,3584]{1,0:T(8,128)(2,1)S(1)}, bf16[32,3584]{1,0:T(8,128)(2,1)S(1)}) custom-call(bf16[128,2048]{1,0:T(8,128)(2,1)S(1)} %collective-permute-done.27.refs_1_.refs_0_, bf16[2048,7168]{1,0:T(8,128)(2,1)} %refs_1_.6, bf16[64,3584]{1,0:T(8,128)(2,1)S(1)} %get-tuple-element.122.refs_2_, ...), custom_call_target="tpu_custom_call" | custom-call | flops 18790481920 | bytes 146800640 | tf_op jit(solution)/shard_map/first_dot/pallas_call | solution.py:84
  109.5 0.6 activate.7.refs_5_.refs_0_
  110.1 0.6 collective-permute-start.44
  111.3 1.6 collective-permute-start.34
  113.0 1.3 collective-permute-start.47
  114.3 6.1 %first_dot.19 = (bf16[64,3584]{1,0:T(8,128)(2,1)S(1)}, bf16[32,3584]{1,0:T(8,128)(2,1)S(1)}, bf16[32,3584]{1,0:T(8,128)(2,1)S(1)}) custom-call(bf16[128,2048]{1,0:T(8,128)(2,1)S(1)} %collective-permute-done.27.refs_1_.refs_0_, bf16[2048,7168]{1,0:T(8,128)(2,1)} %refs_1_.7, bf16[64,3584]{1,0:T(8,128)(2,1)S(1)} %get-tuple-element.128.refs_2_, ...), custom_call_target="tpu_custom_call" | custom-call | flops 18790481920 | bytes 146800640 | tf_op jit(solution)/shard_map/first_dot/pallas_call | solution.py:84
  120.4 4.2 %collective-permute-done.34.refs_2_ = bf16[64,3584]{1,0:T(8,128)(2,1)S(1)} collective-permute-done((bf16[64,3584]{1,0:T(8,128)(2,1)S(1)}, bf16[64,3584]{1,0:T(8,128)(2,1)S(1)}, u32[]{:S(2)}, u32[]{:S(2)}) %collective-permute-start.34) | collective-permute-done | bytes 458784 | tf_op jit(solution)/shard_map/ppermute | solution.py:263
  124.7 0.5 collective-permute-start.54
  125.2 6.9 %last_dot.5 = (f32[128,2048]{1,0:T(8,128)S(1)}, f32[128,2048]{1,0:T(8,128)S(1)}) custom-call(bf16[64,3584]{1,0:T(8,128)(2,1)S(1)} %activate.6.refs_3_.refs_0_, bf16[64,3584]{1,0:T(8,128)(2,1)S(1)} %collective-permute-done.44.refs_1_, bf16[64,3584]{1,0:T(8,128)(2,1)S(1)} %collective-permute-done.45.refs_2_, ...), custom_call_target="tpu_custom_call" | custom-call | flops 37580963840 | bytes 146800640 | tf_op jit(solution)/shard_map/last_dot/pallas_call | solution.py:201
  132.1 1.9 collective-permute-done.47.refs_3_
  134.0 0.6 activate.8.refs_6_.refs_0_
  134.7 0.6 collective-permute-start.52
  135.2 1.5 collective-permute-start.50
  136.7 6.9 %last_dot.6 = (bf16[128,2048]{1,0:T(8,128)(2,1)S(1)}, f32[128,2048]{1,0:T(8,128)S(1)}) custom-call(bf16[64,3584]{1,0:T(8,128)(2,1)S(1)} %activate.7.refs_5_.refs_0_, bf16[64,3584]{1,0:T(8,128)(2,1)S(1)} %collective-permute-done.33.refs_1_, bf16[64,3584]{1,0:T(8,128)(2,1)S(1)} %collective-permute-done.34.refs_2_, ...), custom_call_target="tpu_custom_call" | custom-call | flops 37580963840 | bytes 146800640 | tf_op jit(solution)/shard_map/last_dot/pallas_call | solution.py:201
  144.1 0.6 collective-permute-start.57
  145.0 1.6 collective-permute-start.58
  146.5 1.7 collective-permute-done.50.refs_2_
  148.2 6.1 %last_dot.7.refs_6_.refs_2_ = bf16[128,2048]{1,0:T(8,128)(2,1)S(1)} custom-call(bf16[32,3584]{1,0:T(8,128)(2,1)S(1)} %activate.5.refs_5_.refs_0_, bf16[32,3584]{1,0:T(8,128)(2,1)S(1)} %collective-permute-done.39.refs_3_.refs_1_, bf16[32,3584]{1,0:T(8,128)(2,1)S(1)} %collective-permute-done.40.refs_4_.refs_2_, ...), custom_call_target="tpu_custom_call" | custom-call | flops 18790481920 | bytes 146800640 | tf_op jit(solution)/shard_map/last_dot/pallas_call | solution.py:201
  154.3 6.9 %last_dot.8 = (bf16[128,2048]{1,0:T(8,128)(2,1)S(1)}, f32[128,2048]{1,0:T(8,128)S(1)}) custom-call(bf16[64,3584]{1,0:T(8,128)(2,1)S(1)} %activate.8.refs_6_.refs_0_, bf16[64,3584]{1,0:T(8,128)(2,1)S(1)} %collective-permute-done.49.refs_1_, bf16[64,3584]{1,0:T(8,128)(2,1)S(1)} %collective-permute-done.50.refs_2_, ...), custom_call_target="tpu_custom_call" | custom-call | flops 37580963840 | bytes 146800640 | tf_op jit(solution)/shard_map/last_dot/pallas_call | solution.py:201
  162.0 1.9 collective-permute-start.60
  164.1 6.0 %collective-permute-done.60.refs_2_ = bf16[32,3584]{1,0:T(8,128)(2,1)S(1)} collective-permute-done((bf16[32,3584]{1,0:T(8,128)(2,1)S(1)}, bf16[32,3584]{1,0:T(8,128)(2,1)S(1)}, u32[]{:S(2)}, u32[]{:S(2)}) %collective-permute-start.60) | collective-permute-done | bytes 229408 | tf_op jit(solution)/shard_map/ppermute | solution.py:263
  170.2 1.5 collective-permute-done.61.refs_3_
  171.7 6.1 %last_dot.9.refs_1_.refs_2_ = bf16[128,2048]{1,0:T(8,128)(2,1)S(1)} custom-call(bf16[32,3584]{1,0:T(8,128)(2,1)S(1)} %activate.9.refs_0_.refs_6_, bf16[32,3584]{1,0:T(8,128)(2,1)S(1)} %collective-permute-done.59.refs_1_, bf16[32,3584]{1,0:T(8,128)(2,1)S(1)} %collective-permute-done.60.refs_2_, bf16[32,3584]{1,0:T(8,128)(2,1)S(1)} %collective-permute-done.61.refs_3_, ...), custom_call_target="tpu_custom_call" | custom-call | flops 18790481920 | bytes 146800640 | tf_op jit(solution)/shard_map/last_dot/pallas_call | solution.py:201
  177.8 8.5 %collective-permute-done.56.refs_0_ = bf16[128,2048]{1,0:T(8,128)(2,1)S(1)} collective-permute-done((bf16[128,2048]{1,0:T(8,128)(2,1)S(1)}, bf16[128,2048]{1,0:T(8,128)(2,1)S(1)}, u32[]{:S(2)}, u32[]{:S(2)}) %collective-permute-start.56) | collective-permute-done | bytes 524320 | tf_op jit(solution)/shard_map/ppermute | solution.py:260
  186.7 15.3 %collective-permute-done.62.refs_1_ = bf16[128,2048]{1,0:T(8,128)(2,1)S(1)} collective-permute-done((bf16[128,2048]{1,0:T(8,128)(2,1)S(1)}, bf16[128,2048]{1,0:T(8,128)(2,1)S(1)}, u32[]{:S(2)}, u32[]{:S(2)}) %collective-permute-start.62) | collective-permute-done | bytes 524320 | tf_op jit(solution)/shard_map/ppermute | solution.py:260
  202.0 1.0 add.5
  (101 shorter events, 9.7 us)
Async XLA Ops:
  0.0 17.7 %collective-permute-start = (bf16[128,2048]{1,0:T(8,128)(2,1)}, bf16[128,2048]{1,0:T(8,128)(2,1)S(1)}, u32[]{:S(2)}, u32[]{:S(2)}) collective-permute-start(bf16[128,2048]{1,0:T(8,128)(2,1)} %refs_0_.9), channel_id=1, source_target_pairs={{0,1},{1,2},{2,3},{3,0},{4,5},{5,6},{6,7},{7,4},{8,9},{9,10},{10,1... | collective-permute-start | bytes 1572872 | tf_op jit(solution)/shard_map/ppermute | solution.py:260
  10.2 7.2 %collective-permute-start.2 = (bf16[32,3584]{1,0:T(8,128)(2,1)S(1)}, bf16[32,3584]{1,0:T(8,128)(2,1)S(1)}, u32[]{:S(2)}, u32[]{:S(2)}) collective-permute-start(bf16[32,3584]{1,0:T(8,128)(2,1)S(1)} %get-tuple-element.79.refs_2_), channel_id=1, source_target_pairs={{0,4},{4,0},{8,12},{12,8},{1,5},{5,1},{9,13},{13,9},{2,6},{6,2},{1... | collective-permute-start | bytes 688136 | tf_op jit(solution)/shard_map/ppermute | solution.py:263
  10.3 7.1 %collective-permute-start.3 = (bf16[32,3584]{1,0:T(8,128)(2,1)S(1)}, bf16[32,3584]{1,0:T(8,128)(2,1)S(1)}, u32[]{:S(2)}, u32[]{:S(2)}) collective-permute-start(bf16[32,3584]{1,0:T(8,128)(2,1)S(1)} %get-tuple-element.80), channel_id=1, source_target_pairs={{0,4},{4,0},{8,12},{12,8},{1,5},{5,1},{9,13},{13,9},{2,6},{6,2},{1... | collective-permute-start | bytes 688136 | tf_op jit(solution)/shard_map/ppermute | solution.py:263
  16.8 10.0 %collective-permute-start.8 = (bf16[32,3584]{1,0:T(8,128)(2,1)S(1)}, bf16[32,3584]{1,0:T(8,128)(2,1)S(1)}, u32[]{:S(2)}, u32[]{:S(2)}) collective-permute-start(bf16[32,3584]{1,0:T(8,128)(2,1)S(1)} %get-tuple-element.81.refs_3_), channel_id=1, source_target_pairs={{0,4},{4,0},{8,12},{12,8},{1,5},{5,1},{9,13},{13,9},{2,6},{6,2},{1... | collective-permute-start | bytes 688136 | tf_op jit(solution)/shard_map/ppermute | solution.py:263
  17.0 9.9 %collective-permute-start.9 = (bf16[32,3584]{1,0:T(8,128)(2,1)S(1)}, bf16[32,3584]{1,0:T(8,128)(2,1)S(1)}, u32[]{:S(2)}, u32[]{:S(2)}) collective-permute-start(bf16[32,3584]{1,0:T(8,128)(2,1)S(1)} %get-tuple-element.89), channel_id=1, source_target_pairs={{0,4},{4,0},{8,12},{12,8},{1,5},{5,1},{9,13},{13,9},{2,6},{6,2},{1... | collective-permute-start | bytes 688136 | tf_op jit(solution)/shard_map/ppermute | solution.py:263
  17.7 15.8 %collective-permute-start.1 = (bf16[128,2048]{1,0:T(8,128)(2,1)S(1)}, bf16[128,2048]{1,0:T(8,128)(2,1)S(1)}, u32[]{:S(2)}, u32[]{:S(2)}) collective-permute-start(bf16[128,2048]{1,0:T(8,128)(2,1)S(1)} %collective-permute-done.refs_1_.refs_0_), channel_id=1, source_target_pairs={{0,1},{1,2},{2,3},{3,0},{4,5},{5,6},{6,7},{7,4},{8,9},{9,10},{10,1... | collective-permute-start | bytes 1572872 | tf_op jit(solution)/shard_map/ppermute | solution.py:260
  26.3 1.6 collective-permute-start.4
  26.4 3.0 %collective-permute-start.5 = (bf16[32,3584]{1,0:T(8,128)(2,1)S(1)}, bf16[32,3584]{1,0:T(8,128)(2,1)S(1)}, u32[]{:S(2)}, u32[]{:S(2)}) collective-permute-start(bf16[32,3584]{1,0:T(8,128)(2,1)S(1)} %get-tuple-element.85), channel_id=1, source_target_pairs={{0,4},{4,0},{8,12},{12,8},{1,5},{5,1},{9,13},{13,9},{2,6},{6,2},{1... | collective-permute-start | bytes 688136 | tf_op jit(solution)/shard_map/ppermute | solution.py:263
  26.9 3.0 %collective-permute-start.6 = (bf16[32,3584]{1,0:T(8,128)(2,1)S(1)}, bf16[32,3584]{1,0:T(8,128)(2,1)S(1)}, u32[]{:S(2)}, u32[]{:S(2)}) collective-permute-start(bf16[32,3584]{1,0:T(8,128)(2,1)S(1)} %get-tuple-element.86), channel_id=1, source_target_pairs={{0,4},{4,0},{8,12},{12,8},{1,5},{5,1},{9,13},{13,9},{2,6},{6,2},{1... | collective-permute-start | bytes 688136 | tf_op jit(solution)/shard_map/ppermute | solution.py:263
  26.9 2.9 %collective-permute-start.7 = (bf16[32,3584]{1,0:T(8,128)(2,1)S(1)}, bf16[32,3584]{1,0:T(8,128)(2,1)S(1)}, u32[]{:S(2)}, u32[]{:S(2)}) collective-permute-start(bf16[32,3584]{1,0:T(8,128)(2,1)S(1)} %get-tuple-element.87), channel_id=1, source_target_pairs={{0,4},{4,0},{8,12},{12,8},{1,5},{5,1},{9,13},{13,9},{2,6},{6,2},{1... | collective-permute-start | bytes 688136 | tf_op jit(solution)/shard_map/ppermute | solution.py:263
  27.8 13.2 %collective-permute-start.14 = (bf16[32,3584]{1,0:T(8,128)(2,1)S(1)}, bf16[32,3584]{1,0:T(8,128)(2,1)S(1)}, u32[]{:S(2)}, u32[]{:S(2)}) collective-permute-start(bf16[32,3584]{1,0:T(8,128)(2,1)S(1)} %get-tuple-element.82.refs_3_), channel_id=1, source_target_pairs={{0,8},{4,12},{8,0},{12,4},{1,9},{5,13},{9,1},{13,5},{2,10},{6,14},... | collective-permute-start | bytes 688136 | tf_op jit(solution)/shard_map/ppermute | solution.py:263
  29.3 11.9 %collective-permute-start.15 = (bf16[32,3584]{1,0:T(8,128)(2,1)S(1)}, bf16[32,3584]{1,0:T(8,128)(2,1)S(1)}, u32[]{:S(2)}, u32[]{:S(2)}) collective-permute-start(bf16[32,3584]{1,0:T(8,128)(2,1)S(1)} %get-tuple-element.90.refs_5_), channel_id=1, source_target_pairs={{0,8},{4,12},{8,0},{12,4},{1,9},{5,13},{9,1},{13,5},{2,10},{6,14},... | collective-permute-start | bytes 688136 | tf_op jit(solution)/shard_map/ppermute | solution.py:263
  30.4 20.7 %collective-permute-start.16 = (bf16[64,3584]{1,0:T(8,128)(2,1)S(1)}, bf16[64,3584]{1,0:T(8,128)(2,1)S(1)}, u32[]{:S(2)}, u32[]{:S(2)}) collective-permute-start(bf16[64,3584]{1,0:T(8,128)(2,1)S(1)} %get-tuple-element.91.refs_3_), channel_id=1, source_target_pairs={{0,8},{4,12},{8,0},{12,4},{1,9},{5,13},{9,1},{13,5},{2,10},{6,14},... | collective-permute-start | bytes 1376264 | tf_op jit(solution)/shard_map/ppermute | solution.py:263
  40.5 1.6 collective-permute-start.10
  40.6 1.8 collective-permute-start.11
  41.1 1.6 collective-permute-start.12
  41.2 1.8 collective-permute-start.13
  43.5 19.7 %collective-permute-start.22 = (bf16[64,3584]{1,0:T(8,128)(2,1)S(1)}, bf16[64,3584]{1,0:T(8,128)(2,1)S(1)}, u32[]{:S(2)}, u32[]{:S(2)}) collective-permute-start(bf16[64,3584]{1,0:T(8,128)(2,1)S(1)} %get-tuple-element.99.refs_3_), channel_id=1, source_target_pairs={{0,8},{4,12},{8,0},{12,4},{1,9},{5,13},{9,1},{13,5},{2,10},{6,14},... | collective-permute-start | bytes 1376264 | tf_op jit(solution)/shard_map/ppermute | solution.py:263
  58.0 1.6 collective-permute-start.17
  58.1 3.1 %collective-permute-start.18 = (bf16[32,3584]{1,0:T(8,128)(2,1)S(1)}, bf16[32,3584]{1,0:T(8,128)(2,1)S(1)}, u32[]{:S(2)}, u32[]{:S(2)}) collective-permute-start(bf16[32,3584]{1,0:T(8,128)(2,1)S(1)} %get-tuple-element.102), channel_id=1, source_target_pairs={{0,4},{4,0},{8,12},{12,8},{1,5},{5,1},{9,13},{13,9},{2,6},{6,2},{1... | collective-permute-start | bytes 688136 | tf_op jit(solution)/shard_map/ppermute | solution.py:263
  58.6 2.6 %collective-permute-start.19 = (bf16[32,3584]{1,0:T(8,128)(2,1)S(1)}, bf16[32,3584]{1,0:T(8,128)(2,1)S(1)}, u32[]{:S(2)}, u32[]{:S(2)}) collective-permute-start(bf16[32,3584]{1,0:T(8,128)(2,1)S(1)} %get-tuple-element.103), channel_id=1, source_target_pairs={{0,4},{4,0},{8,12},{12,8},{1,5},{5,1},{9,13},{13,9},{2,6},{6,2},{1... | collective-permute-start | bytes 688136 | tf_op jit(solution)/shard_map/ppermute | solution.py:263
  58.6 2.5 %collective-permute-start.20 = (bf16[32,3584]{1,0:T(8,128)(2,1)S(1)}, bf16[32,3584]{1,0:T(8,128)(2,1)S(1)}, u32[]{:S(2)}, u32[]{:S(2)}) collective-permute-start(bf16[32,3584]{1,0:T(8,128)(2,1)S(1)} %get-tuple-element.104), channel_id=1, source_target_pairs={{0,4},{4,0},{8,12},{12,8},{1,5},{5,1},{9,13},{13,9},{2,6},{6,2},{1... | collective-permute-start | bytes 688136 | tf_op jit(solution)/shard_map/ppermute | solution.py:263
  59.5 15.8 %collective-permute-start.27 = (bf16[128,2048]{1,0:T(8,128)(2,1)S(1)}, bf16[128,2048]{1,0:T(8,128)(2,1)S(1)}, u32[]{:S(2)}, u32[]{:S(2)}) collective-permute-start(bf16[128,2048]{1,0:T(8,128)(2,1)S(1)} %collective-permute-done.1.refs_4_.refs_1_.refs_0_), channel_id=1, source_target_pairs={{0,1},{1,2},{2,3},{3,0},{4,5},{5,6},{6,7},{7,4},{8,9},{9,10},{10,1... | collective-permute-start | bytes 1572872 | tf_op jit(solution)/shard_map/ppermute | solution.py:260
  61.6 13.7 %collective-permute-start.21 = (bf16[64,3584]{1,0:T(8,128)(2,1)S(1)}, bf16[64,3584]{1,0:T(8,128)(2,1)S(1)}, u32[]{:S(2)}, u32[]{:S(2)}) collective-permute-start(bf16[64,3584]{1,0:T(8,128)(2,1)S(1)} %get-tuple-element.106.refs_3_), channel_id=1, source_target_pairs={{0,8},{4,12},{8,0},{12,4},{1,9},{5,13},{9,1},{13,5},{2,10},{6,14},... | collective-permute-start | bytes 1376264 | tf_op jit(solution)/shard_map/ppermute | solution.py:263
  70.1 13.6 %collective-permute-start.23 = (bf16[32,3584]{1,0:T(8,128)(2,1)S(1)}, bf16[32,3584]{1,0:T(8,128)(2,1)S(1)}, u32[]{:S(2)}, u32[]{:S(2)}) collective-permute-start(bf16[32,3584]{1,0:T(8,128)(2,1)S(1)} %get-tuple-element.108.refs_4_), channel_id=1, source_target_pairs={{0,4},{4,0},{8,12},{12,8},{1,5},{5,1},{9,13},{13,9},{2,6},{6,2},{1... | collective-permute-start | bytes 688136 | tf_op jit(solution)/shard_map/ppermute | solution.py:263
  70.2 13.9 %collective-permute-start.24 = (bf16[32,3584]{1,0:T(8,128)(2,1)S(1)}, bf16[32,3584]{1,0:T(8,128)(2,1)S(1)}, u32[]{:S(2)}, u32[]{:S(2)}) collective-permute-start(bf16[32,3584]{1,0:T(8,128)(2,1)S(1)} %get-tuple-element.109), channel_id=1, source_target_pairs={{0,4},{4,0},{8,12},{12,8},{1,5},{5,1},{9,13},{13,9},{2,6},{6,2},{1... | collective-permute-start | bytes 688136 | tf_op jit(solution)/shard_map/ppermute | solution.py:263
  70.7 13.9 %collective-permute-start.25 = (bf16[32,3584]{1,0:T(8,128)(2,1)S(1)}, bf16[32,3584]{1,0:T(8,128)(2,1)S(1)}, u32[]{:S(2)}, u32[]{:S(2)}) collective-permute-start(bf16[32,3584]{1,0:T(8,128)(2,1)S(1)} %get-tuple-element.110), channel_id=1, source_target_pairs={{0,4},{4,0},{8,12},{12,8},{1,5},{5,1},{9,13},{13,9},{2,6},{6,2},{1... | collective-permute-start | bytes 688136 | tf_op jit(solution)/shard_map/ppermute | solution.py:263
  75.3 9.3 %collective-permute-start.26 = (bf16[32,3584]{1,0:T(8,128)(2,1)S(1)}, bf16[32,3584]{1,0:T(8,128)(2,1)S(1)}, u32[]{:S(2)}, u32[]{:S(2)}) collective-permute-start(bf16[32,3584]{1,0:T(8,128)(2,1)S(1)} %get-tuple-element.111), channel_id=1, source_target_pairs={{0,4},{4,0},{8,12},{12,8},{1,5},{5,1},{9,13},{13,9},{2,6},{6,2},{1... | collective-permute-start | bytes 688136 | tf_op jit(solution)/shard_map/ppermute | solution.py:263
  75.3 13.3 %collective-permute-start.45 = (bf16[64,3584]{1,0:T(8,128)(2,1)S(1)}, bf16[64,3584]{1,0:T(8,128)(2,1)S(1)}, u32[]{:S(2)}, u32[]{:S(2)}) collective-permute-start(bf16[64,3584]{1,0:T(8,128)(2,1)S(1)} %activate.6.refs_3_.refs_0_), channel_id=1, source_target_pairs={{0,8},{4,12},{8,0},{12,4},{1,9},{5,13},{9,1},{13,5},{2,10},{6,14},... | collective-permute-start | bytes 1376264 | tf_op jit(solution)/shard_map/ppermute | solution.py:263
  83.8 4.9 %collective-permute-start.29 = (bf16[32,3584]{1,0:T(8,128)(2,1)S(1)}, bf16[32,3584]{1,0:T(8,128)(2,1)S(1)}, u32[]{:S(2)}, u32[]{:S(2)}) collective-permute-start(bf16[32,3584]{1,0:T(8,128)(2,1)S(1)} %get-tuple-element.114.refs_5_), channel_id=1, source_target_pairs={{0,4},{4,0},{8,12},{12,8},{1,5},{5,1},{9,13},{13,9},{2,6},{6,2},{1... | collective-permute-start | bytes 688136 | tf_op jit(solution)/shard_map/ppermute | solution.py:263
  84.1 14.3 %collective-permute-start.40 = (bf16[32,3584]{1,0:T(8,128)(2,1)S(1)}, bf16[32,3584]{1,0:T(8,128)(2,1)S(1)}, u32[]{:S(2)}, u32[]{:S(2)}) collective-permute-start(bf16[32,3584]{1,0:T(8,128)(2,1)S(1)} %activate.5.refs_5_.refs_0_), channel_id=1, source_target_pairs={{0,8},{4,12},{8,0},{12,4},{1,9},{5,13},{9,1},{13,5},{2,10},{6,14},... | collective-permute-start | bytes 688136 | tf_op jit(solution)/shard_map/ppermute | solution.py:263
  84.6 12.5 %collective-permute-start.30 = (bf16[32,3584]{1,0:T(8,128)(2,1)S(1)}, bf16[32,3584]{1,0:T(8,128)(2,1)S(1)}, u32[]{:S(2)}, u32[]{:S(2)}) collective-permute-start(bf16[32,3584]{1,0:T(8,128)(2,1)S(1)} %get-tuple-element.118), channel_id=1, source_target_pairs={{0,4},{4,0},{8,12},{12,8},{1,5},{5,1},{9,13},{13,9},{2,6},{6,2},{1... | collective-permute-start | bytes 688136 | tf_op jit(solution)/shard_map/ppermute | solution.py:263
  84.6 12.8 %collective-permute-start.31 = (bf16[32,3584]{1,0:T(8,128)(2,1)S(1)}, bf16[32,3584]{1,0:T(8,128)(2,1)S(1)}, u32[]{:S(2)}, u32[]{:S(2)}) collective-permute-start(bf16[32,3584]{1,0:T(8,128)(2,1)S(1)} %get-tuple-element.119), channel_id=1, source_target_pairs={{0,4},{4,0},{8,12},{12,8},{1,5},{5,1},{9,13},{13,9},{2,6},{6,2},{1... | collective-permute-start | bytes 688136 | tf_op jit(solution)/shard_map/ppermute | solution.py:263
  88.6 9.0 %collective-permute-start.32 = (bf16[32,3584]{1,0:T(8,128)(2,1)S(1)}, bf16[32,3584]{1,0:T(8,128)(2,1)S(1)}, u32[]{:S(2)}, u32[]{:S(2)}) collective-permute-start(bf16[32,3584]{1,0:T(8,128)(2,1)S(1)} %get-tuple-element.120), channel_id=1, source_target_pairs={{0,4},{4,0},{8,12},{12,8},{1,5},{5,1},{9,13},{13,9},{2,6},{6,2},{1... | collective-permute-start | bytes 688136 | tf_op jit(solution)/shard_map/ppermute | solution.py:263
  88.6 14.7 %collective-permute-start.28 = (bf16[64,3584]{1,0:T(8,128)(2,1)S(1)}, bf16[64,3584]{1,0:T(8,128)(2,1)S(1)}, u32[]{:S(2)}, u32[]{:S(2)}) collective-permute-start(bf16[64,3584]{1,0:T(8,128)(2,1)S(1)} %get-tuple-element.116.refs_3_), channel_id=1, source_target_pairs={{0,8},{4,12},{8,0},{12,4},{1,9},{5,13},{9,1},{13,5},{2,10},{6,14},... | collective-permute-start | bytes 1376264 | tf_op jit(solution)/shard_map/ppermute | solution.py:263
  97.1 1.6 collective-permute-start.35
  97.4 1.6 collective-permute-start.36
  97.7 13.6 %collective-permute-start.39 = (bf16[32,3584]{1,0:T(8,128)(2,1)S(1)}, bf16[32,3584]{1,0:T(8,128)(2,1)S(1)}, u32[]{:S(2)}, u32[]{:S(2)}) collective-permute-start(bf16[32,3584]{1,0:T(8,128)(2,1)S(1)} %activate.5.refs_5_.refs_0_), channel_id=1, source_target_pairs={{0,4},{4,0},{8,12},{12,8},{1,5},{5,1},{9,13},{13,9},{2,6},{6,2},{1... | collective-permute-start | bytes 688136 | tf_op jit(solution)/shard_map/ppermute | solution.py:263
  98.4 11.7 %collective-permute-start.37 = (bf16[32,3584]{1,0:T(8,128)(2,1)S(1)}, bf16[32,3584]{1,0:T(8,128)(2,1)S(1)}, u32[]{:S(2)}, u32[]{:S(2)}) collective-permute-start(bf16[32,3584]{1,0:T(8,128)(2,1)S(1)} %get-tuple-element.126), channel_id=1, source_target_pairs={{0,4},{4,0},{8,12},{12,8},{1,5},{5,1},{9,13},{13,9},{2,6},{6,2},{1... | collective-permute-start | bytes 688136 | tf_op jit(solution)/shard_map/ppermute | solution.py:263
  98.7 12.0 %collective-permute-start.38 = (bf16[32,3584]{1,0:T(8,128)(2,1)S(1)}, bf16[32,3584]{1,0:T(8,128)(2,1)S(1)}, u32[]{:S(2)}, u32[]{:S(2)}) collective-permute-start(bf16[32,3584]{1,0:T(8,128)(2,1)S(1)} %get-tuple-element.127), channel_id=1, source_target_pairs={{0,4},{4,0},{8,12},{12,8},{1,5},{5,1},{9,13},{13,9},{2,6},{6,2},{1... | collective-permute-start | bytes 688136 | tf_op jit(solution)/shard_map/ppermute | solution.py:263
  99.0 14.0 %collective-permute-start.42 = (bf16[64,3584]{1,0:T(8,128)(2,1)S(1)}, bf16[64,3584]{1,0:T(8,128)(2,1)S(1)}, u32[]{:S(2)}, u32[]{:S(2)}) collective-permute-start(bf16[64,3584]{1,0:T(8,128)(2,1)S(1)} %get-tuple-element.122.refs_2_), channel_id=1, source_target_pairs={{0,8},{4,12},{8,0},{12,4},{1,9},{5,13},{9,1},{13,5},{2,10},{6,14},... | collective-permute-start | bytes 1376264 | tf_op jit(solution)/shard_map/ppermute | solution.py:263
  103.4 9.4 %collective-permute-start.41 = (bf16[32,3584]{1,0:T(8,128)(2,1)S(1)}, bf16[32,3584]{1,0:T(8,128)(2,1)S(1)}, u32[]{:S(2)}, u32[]{:S(2)}) collective-permute-start(bf16[32,3584]{1,0:T(8,128)(2,1)S(1)} %collective-permute-done.40.refs_4_.refs_2_), channel_id=1, source_target_pairs={{0,4},{4,0},{8,12},{12,8},{1,5},{5,1},{9,13},{13,9},{2,6},{6,2},{1... | collective-permute-start | bytes 688136 | tf_op jit(solution)/shard_map/ppermute | solution.py:263
  110.1 14.5 %collective-permute-start.44 = (bf16[64,3584]{1,0:T(8,128)(2,1)S(1)}, bf16[64,3584]{1,0:T(8,128)(2,1)S(1)}, u32[]{:S(2)}, u32[]{:S(2)}) collective-permute-start(bf16[64,3584]{1,0:T(8,128)(2,1)S(1)} %activate.6.refs_3_.refs_0_), channel_id=1, source_target_pairs={{0,4},{4,0},{8,12},{12,8},{1,5},{5,1},{9,13},{13,9},{2,6},{6,2},{1... | collective-permute-start | bytes 1376264 | tf_op jit(solution)/shard_map/ppermute | solution.py:263
  110.7 14.5 %collective-permute-start.46 = (bf16[64,3584]{1,0:T(8,128)(2,1)S(1)}, bf16[64,3584]{1,0:T(8,128)(2,1)S(1)}, u32[]{:S(2)}, u32[]{:S(2)}) collective-permute-start(bf16[64,3584]{1,0:T(8,128)(2,1)S(1)} %collective-permute-done.45.refs_2_), channel_id=1, source_target_pairs={{0,4},{4,0},{8,12},{12,8},{1,5},{5,1},{9,13},{13,9},{2,6},{6,2},{1... | collective-permute-start | bytes 1376264 | tf_op jit(solution)/shard_map/ppermute | solution.py:263
  111.3 13.4 %collective-permute-start.34 = (bf16[64,3584]{1,0:T(8,128)(2,1)S(1)}, bf16[64,3584]{1,0:T(8,128)(2,1)S(1)}, u32[]{:S(2)}, u32[]{:S(2)}) collective-permute-start(bf16[64,3584]{1,0:T(8,128)(2,1)S(1)} %activate.7.refs_5_.refs_0_), channel_id=1, source_target_pairs={{0,8},{4,12},{8,0},{12,4},{1,9},{5,13},{9,1},{13,5},{2,10},{6,14},... | collective-permute-start | bytes 1376264 | tf_op jit(solution)/shard_map/ppermute | solution.py:263
  112.8 21.8 %collective-permute-start.33 = (bf16[64,3584]{1,0:T(8,128)(2,1)S(1)}, bf16[64,3584]{1,0:T(8,128)(2,1)S(1)}, u32[]{:S(2)}, u32[]{:S(2)}) collective-permute-start(bf16[64,3584]{1,0:T(8,128)(2,1)S(1)} %activate.7.refs_5_.refs_0_), channel_id=1, source_target_pairs={{0,4},{4,0},{8,12},{12,8},{1,5},{5,1},{9,13},{13,9},{2,6},{6,2},{1... | collective-permute-start | bytes 1376264 | tf_op jit(solution)/shard_map/ppermute | solution.py:263
  113.0 21.0 %collective-permute-start.47 = (bf16[64,3584]{1,0:T(8,128)(2,1)S(1)}, bf16[64,3584]{1,0:T(8,128)(2,1)S(1)}, u32[]{:S(2)}, u32[]{:S(2)}) collective-permute-start(bf16[64,3584]{1,0:T(8,128)(2,1)S(1)} %get-tuple-element.128.refs_2_), channel_id=1, source_target_pairs={{0,8},{4,12},{8,0},{12,4},{1,9},{5,13},{9,1},{13,5},{2,10},{6,14},... | collective-permute-start | bytes 1376264 | tf_op jit(solution)/shard_map/ppermute | solution.py:263
  124.6 19.0 %collective-permute-start.53 = (bf16[32,3584]{1,0:T(8,128)(2,1)S(1)}, bf16[32,3584]{1,0:T(8,128)(2,1)S(1)}, u32[]{:S(2)}, u32[]{:S(2)}) collective-permute-start(bf16[32,3584]{1,0:T(8,128)(2,1)S(1)} %get-tuple-element.123.refs_4_), channel_id=1, source_target_pairs={{0,4},{4,0},{8,12},{12,8},{1,5},{5,1},{9,13},{13,9},{2,6},{6,2},{1... | collective-permute-start | bytes 688136 | tf_op jit(solution)/shard_map/ppermute | solution.py:263
  124.7 19.1 %collective-permute-start.54 = (bf16[32,3584]{1,0:T(8,128)(2,1)S(1)}, bf16[32,3584]{1,0:T(8,128)(2,1)S(1)}, u32[]{:S(2)}, u32[]{:S(2)}) collective-permute-start(bf16[32,3584]{1,0:T(8,128)(2,1)S(1)} %get-tuple-element.141), channel_id=1, source_target_pairs={{0,4},{4,0},{8,12},{12,8},{1,5},{5,1},{9,13},{13,9},{2,6},{6,2},{1... | collective-permute-start | bytes 688136 | tf_op jit(solution)/shard_map/ppermute | solution.py:263
  125.2 10.1 %collective-permute-start.43 = (bf16[64,3584]{1,0:T(8,128)(2,1)S(1)}, bf16[64,3584]{1,0:T(8,128)(2,1)S(1)}, u32[]{:S(2)}, u32[]{:S(2)}) collective-permute-start(bf16[64,3584]{1,0:T(8,128)(2,1)S(1)} %collective-permute-done.34.refs_2_), channel_id=1, source_target_pairs={{0,4},{4,0},{8,12},{12,8},{1,5},{5,1},{9,13},{13,9},{2,6},{6,2},{1... | collective-permute-start | bytes 1376264 | tf_op jit(solution)/shard_map/ppermute | solution.py:263
  134.0 10.1 %collective-permute-start.51 = (bf16[32,3584]{1,0:T(8,128)(2,1)S(1)}, bf16[32,3584]{1,0:T(8,128)(2,1)S(1)}, u32[]{:S(2)}, u32[]{:S(2)}) collective-permute-start(bf16[32,3584]{1,0:T(8,128)(2,1)S(1)} %get-tuple-element.130.refs_5_), channel_id=1, source_target_pairs={{0,4},{4,0},{8,12},{12,8},{1,5},{5,1},{9,13},{13,9},{2,6},{6,2},{1... | collective-permute-start | bytes 688136 | tf_op jit(solution)/shard_map/ppermute | solution.py:263
  134.7 10.1 %collective-permute-start.52 = (bf16[32,3584]{1,0:T(8,128)(2,1)S(1)}, bf16[32,3584]{1,0:T(8,128)(2,1)S(1)}, u32[]{:S(2)}, u32[]{:S(2)}) collective-permute-start(bf16[32,3584]{1,0:T(8,128)(2,1)S(1)} %get-tuple-element.139), channel_id=1, source_target_pairs={{0,4},{4,0},{8,12},{12,8},{1,5},{5,1},{9,13},{13,9},{2,6},{6,2},{1... | collective-permute-start | bytes 688136 | tf_op jit(solution)/shard_map/ppermute | solution.py:263
  135.2 13.0 %collective-permute-start.50 = (bf16[64,3584]{1,0:T(8,128)(2,1)S(1)}, bf16[64,3584]{1,0:T(8,128)(2,1)S(1)}, u32[]{:S(2)}, u32[]{:S(2)}) collective-permute-start(bf16[64,3584]{1,0:T(8,128)(2,1)S(1)} %activate.8.refs_6_.refs_0_), channel_id=1, source_target_pairs={{0,8},{4,12},{8,0},{12,4},{1,9},{5,13},{9,1},{13,5},{2,10},{6,14},... | collective-permute-start | bytes 1376264 | tf_op jit(solution)/shard_map/ppermute | solution.py:263
  143.7 10.7 %collective-permute-start.49 = (bf16[64,3584]{1,0:T(8,128)(2,1)S(1)}, bf16[64,3584]{1,0:T(8,128)(2,1)S(1)}, u32[]{:S(2)}, u32[]{:S(2)}) collective-permute-start(bf16[64,3584]{1,0:T(8,128)(2,1)S(1)} %activate.8.refs_6_.refs_0_), channel_id=1, source_target_pairs={{0,4},{4,0},{8,12},{12,8},{1,5},{5,1},{9,13},{13,9},{2,6},{6,2},{1... | collective-permute-start | bytes 1376264 | tf_op jit(solution)/shard_map/ppermute | solution.py:263
  143.7 17.5 %collective-permute-start.48 = (bf16[128,2048]{1,0:T(8,128)(2,1)S(1)}, bf16[128,2048]{1,0:T(8,128)(2,1)S(1)}, u32[]{:S(2)}, u32[]{:S(2)}) collective-permute-start(bf16[128,2048]{1,0:T(8,128)(2,1)S(1)} %get-tuple-element.137.refs_3_), channel_id=1, source_target_pairs={{0,1},{1,2},{2,3},{3,0},{4,5},{5,6},{6,7},{7,4},{8,9},{9,10},{10,1... | collective-permute-start | bytes 1572872 | tf_op jit(solution)/shard_map/ppermute | solution.py:260
  144.1 17.5 %collective-permute-start.57 = (bf16[32,3584]{1,0:T(8,128)(2,1)S(1)}, bf16[32,3584]{1,0:T(8,128)(2,1)S(1)}, u32[]{:S(2)}, u32[]{:S(2)}) collective-permute-start(bf16[32,3584]{1,0:T(8,128)(2,1)S(1)} %get-tuple-element.142.refs_3_), channel_id=1, source_target_pairs={{0,8},{4,12},{8,0},{12,4},{1,9},{5,13},{9,1},{13,5},{2,10},{6,14},... | collective-permute-start | bytes 688136 | tf_op jit(solution)/shard_map/ppermute | solution.py:263
  145.0 16.6 %collective-permute-start.58 = (bf16[32,3584]{1,0:T(8,128)(2,1)S(1)}, bf16[32,3584]{1,0:T(8,128)(2,1)S(1)}, u32[]{:S(2)}, u32[]{:S(2)}) collective-permute-start(bf16[32,3584]{1,0:T(8,128)(2,1)S(1)} %get-tuple-element.143.refs_6_), channel_id=1, source_target_pairs={{0,8},{4,12},{8,0},{12,4},{1,9},{5,13},{9,1},{13,5},{2,10},{6,14},... | collective-permute-start | bytes 688136 | tf_op jit(solution)/shard_map/ppermute | solution.py:263
  148.2 6.1 %collective-permute-start.55 = (bf16[64,3584]{1,0:T(8,128)(2,1)S(1)}, bf16[64,3584]{1,0:T(8,128)(2,1)S(1)}, u32[]{:S(2)}, u32[]{:S(2)}) collective-permute-start(bf16[64,3584]{1,0:T(8,128)(2,1)S(1)} %collective-permute-done.50.refs_2_), channel_id=1, source_target_pairs={{0,4},{4,0},{8,12},{12,8},{1,5},{5,1},{9,13},{13,9},{2,6},{6,2},{1... | collective-permute-start | bytes 1376264 | tf_op jit(solution)/shard_map/ppermute | solution.py:263
  162.0 8.2 %collective-permute-start.60 = (bf16[32,3584]{1,0:T(8,128)(2,1)S(1)}, bf16[32,3584]{1,0:T(8,128)(2,1)S(1)}, u32[]{:S(2)}, u32[]{:S(2)}) collective-permute-start(bf16[32,3584]{1,0:T(8,128)(2,1)S(1)} %activate.9.refs_0_.refs_6_), channel_id=1, source_target_pairs={{0,8},{4,12},{8,0},{12,4},{1,9},{5,13},{9,1},{13,5},{2,10},{6,14},... | collective-permute-start | bytes 688136 | tf_op jit(solution)/shard_map/ppermute | solution.py:263
  163.9 6.3 %collective-permute-start.59 = (bf16[32,3584]{1,0:T(8,128)(2,1)S(1)}, bf16[32,3584]{1,0:T(8,128)(2,1)S(1)}, u32[]{:S(2)}, u32[]{:S(2)}) collective-permute-start(bf16[32,3584]{1,0:T(8,128)(2,1)S(1)} %activate.9.refs_0_.refs_6_), channel_id=1, source_target_pairs={{0,4},{4,0},{8,12},{12,8},{1,5},{5,1},{9,13},{13,9},{2,6},{6,2},{1... | collective-permute-start | bytes 688136 | tf_op jit(solution)/shard_map/ppermute | solution.py:263
  170.2 1.5 collective-permute-start.61
  170.2 16.1 %collective-permute-start.56 = (bf16[128,2048]{1,0:T(8,128)(2,1)S(1)}, bf16[128,2048]{1,0:T(8,128)(2,1)S(1)}, u32[]{:S(2)}, u32[]{:S(2)}) collective-permute-start(bf16[128,2048]{1,0:T(8,128)(2,1)S(1)} %add.3.refs_4_), channel_id=1, source_target_pairs={{0,1},{1,2},{2,3},{3,0},{4,5},{5,6},{6,7},{7,4},{8,9},{9,10},{10,1... | collective-permute-start | bytes 1572872 | tf_op jit(solution)/shard_map/ppermute | solution.py:260
  171.7 30.3 %copy-start.2 = (bf16[128,2048]{1,0:T(8,128)(2,1)S(1)}, bf16[128,2048]{1,0:T(8,128)(2,1)}, u32[]{:S(2)}) copy-start(bf16[128,2048]{1,0:T(8,128)(2,1)} %refs_0_.9) | copy-start | bytes 1572868
  186.6 15.4 %collective-permute-start.62 = (bf16[128,2048]{1,0:T(8,128)(2,1)S(1)}, bf16[128,2048]{1,0:T(8,128)(2,1)S(1)}, u32[]{:S(2)}, u32[]{:S(2)}) collective-permute-start(bf16[128,2048]{1,0:T(8,128)(2,1)S(1)} %add.4.refs_3_), channel_id=1, source_target_pairs={{0,1},{1,2},{2,3},{3,0},{4,5},{5,6},{6,7},{7,4},{8,9},{9,10},{10,1... | collective-permute-start | bytes 1572872 | tf_op jit(solution)/shard_map/ppermute | solution.py:260
  (2 other events, 10.2 us)

commit v3 on v2

--- a/solution.py
+++ b/solution.py
@@ -30,31 +30,33 @@
     return order
 
 
-def first_dot(shards, weight, columns, bits, parts, fixed, after):
+def first_dots(shards, weights, columns, bits, parts, fixed, after):
     rows, depth = shards[0].shape
     at, width = columns
-    n, g = 1 << bits, len(shards)
+    n, g, k = 1 << bits, len(shards), len(weights)
     r, m = rows // n, g * rows
     share = m // 2 // parts
     step = block_of(width, 512)
     steps = width // step
-    slots = min(4, steps)
+    slots = min(3, steps)
     order = cut_order(bits)
 
     def kernel(*refs):
-        x, w = refs[:g], refs[g]
+        x, w = refs[:g], refs[g : g + k]
         keep, sends = refs[-5 - parts], refs[-4 - parts : -4]
         held, buf, x_sem, w_sem = refs[-4:]
         c = pl.program_id(0)
 
-        def load(block):
+        def load(i, block):
             start = pl.multiple_of(at + block * step, 128)
-            return pltpu.make_async_copy(w.at[:, pl.ds(start, step)], buf.at[block % slots], w_sem.at[block % slots])
+            slot = block % slots
+            return pltpu.make_async_copy(w[i].at[:, pl.ds(start, step)], buf.at[i, slot], w_sem.at[i, slot])
 
         @pl.when(c == 0)
         def _():
             for block in range(slots):
-                load(block).start()
+                for i in range(k):
+                    load(i, block).start()
             me = lax.axis_index("pipe")
             copies = []
             for spot, j in enumerate(order):
@@ -71,52 +73,56 @@
             for copy in copies:
                 copy.wait()
 
-        load(c).wait()
-        part = jnp.dot(held[...], buf[c % slots], preferred_element_type=F32).astype(BF16)
-        keep[...] = part[: m // 2]
-        for i, send in enumerate(sends):
-            send[...] = part[m // 2 + i * share : m // 2 + (i + 1) * share]
+        for i in range(k):
+            load(i, c).wait()
+            part = jnp.dot(held[...], buf[i, c % slots], preferred_element_type=F32).astype(BF16)
+            keep[i] = part[: m // 2]
+            for q, send in enumerate(sends):
+                send[i] = part[m // 2 + q * share : m // 2 + (q + 1) * share]
 
         @pl.when(c + slots < steps)
         def _():
-            load(c + slots).start()
-
+            for i in range(k):
+                load(i, c + slots).start()
+
+    heights = [m // 2] + [share] * parts
     return pl.pallas_call(
         kernel,
         grid=(steps,),
-        in_specs=[HBM if i in fixed else ANY for i in range(g)] + [HBM] + [ANY] * len(after),
-        out_specs=[pl.BlockSpec((h, step), lambda c: (0, c)) for h in [m // 2] + [share] * parts],
-        out_shape=[jax.ShapeDtypeStruct((h, width), BF16) for h in [m // 2] + [share] * parts],
+        in_specs=[HBM if i in fixed else ANY for i in range(g)] + [HBM] * k + [ANY] * len(after),
+        out_specs=[pl.BlockSpec((k, h, step), lambda c: (0, 0, c)) for h in heights],
+        out_shape=[jax.ShapeDtypeStruct((k, h, width), BF16) for h in heights],
         scratch_shapes=[
             pltpu.VMEM((m, depth), BF16),
-            pltpu.VMEM((slots, depth, step), BF16),
+            pltpu.VMEM((k, slots, depth, step), BF16),
             pltpu.SemaphoreType.DMA((n * g,)),
-            pltpu.SemaphoreType.DMA((slots,)),
+            pltpu.SemaphoreType.DMA((k, slots)),
         ],
         compiler_params=params(40),
-        cost_estimate=cost(2 * m * depth * width, 2 * depth * width),
-        name="first_dot",
-    )(*shards, weight, *after)
+        cost_estimate=cost(2 * k * m * depth * width, 2 * k * depth * width),
+        name="first_dots",
+    )(*shards, *weights, *after)
 
 
 def fold(keep, got, after):
-    m, width = keep.shape
-    step = block_of(width, 1792)
-    k = len(got)
+    k, m, width = keep.shape
+    step = block_of(width, 896)
+    count = len(got)
 
     def kernel(*refs):
         stay, send = refs[-2:]
-        other = jnp.concatenate([ref[...] for ref in refs[1 : 1 + k]], axis=0)
-        total = (refs[0][...].astype(F32) + other.astype(F32)).astype(BF16)
-        stay[...] = total[: m // 2]
-        send[...] = total[m // 2 :]
-
-    out = jax.ShapeDtypeStruct((m // 2, width), BF16)
+        for i in range(k):
+            other = jnp.concatenate([ref[i] for ref in refs[1 : 1 + count]], axis=0)
+            total = (refs[0][i].astype(F32) + other.astype(F32)).astype(BF16)
+            stay[i] = total[: m // 2]
+            send[i] = total[m // 2 :]
+
+    out = jax.ShapeDtypeStruct((k, m // 2, width), BF16)
     return pl.pallas_call(
         kernel,
         grid=(width // step,),
-        in_specs=[pl.BlockSpec((a.shape[0], step), lambda c: (0, c)) for a in (keep, *got)] + [ANY] * len(after),
-        out_specs=[pl.BlockSpec((m // 2, step), lambda c: (0, c))] * 2,
+        in_specs=[pl.BlockSpec((k, a.shape[1], step), lambda c: (0, 0, c)) for a in (keep, *got)] + [ANY] * len(after),
+        out_specs=[pl.BlockSpec((k, m // 2, step), lambda c: (0, 0, c))] * 2,
         out_shape=[out, out],
         compiler_params=params(40),
         cost_estimate=cost(1, 1),
@@ -124,25 +130,26 @@
     )(keep, *got, *after)
 
 
-def activate(gate, up, after):
-    m, width = gate[0].shape
+def activate(kept, got, after):
+    _, m, width = kept.shape
     step = block_of(width, 1792)
 
     def kernel(*refs):
-        g = refs[0][...].astype(F32) + refs[1][...].astype(F32)
-        u = refs[2][...].astype(F32) + refs[3][...].astype(F32)
-        refs[-1][...] = (g / (1.0 + jnp.exp(-g)) * u).astype(BF16)
+        a, b, out = refs[0], refs[1], refs[-1]
+        g = a[0].astype(F32) + b[0].astype(F32)
+        u = a[1].astype(F32) + b[1].astype(F32)
+        out[...] = (g / (1.0 + jnp.exp(-g)) * u).astype(BF16)
 
     return pl.pallas_call(
         kernel,
         grid=(width // step,),
-        in_specs=[pl.BlockSpec((m, step), lambda c: (0, c))] * 4 + [ANY] * len(after),
+        in_specs=[pl.BlockSpec((2, m, step), lambda c: (0, 0, c))] * 2 + [ANY] * len(after),
         out_specs=pl.BlockSpec((m, step), lambda c: (0, c)),
         out_shape=jax.ShapeDtypeStruct((m, width), BF16),
         compiler_params=params(40),
         cost_estimate=cost(1, 1),
         name="activate",
-    )(*gate, *up, *after)
+    )(kept, got, *after)
 
 
 def last_dot(pieces, weight, at, carries, finals, after):
@@ -212,7 +219,7 @@
             pltpu.SemaphoreType.DMA((slots,)),
         ],
         compiler_params=params(40),
-        cost_estimate=cost(2 * m * depth * width, 2 * depth * width),
+        cost_estimate=cost(1, 1),
         name="last_dot",
     )(*pieces, weight, *given, *after)
 
@@ -268,28 +275,33 @@
             held.append(hop(held[-1]))
         rects = rectangles(n_tensor, gate_weight.shape[1])
         left = {i: sum(i in s for s, _ in rects) for i in range(n_tensor)}
-        weights = (gate_weight, up_weight)
         last, dotted, folded, hidden, sums = [], {}, {}, {}, {}
 
-        def dot(k, w):
+        def dot(k):
             rows, columns = rects[k]
-            parts = 2 * len(rows)
-            keep, *sends = first_dot(
-                [held[i] for i in rows], weights[w], columns, bits, parts, [j for j, i in enumerate(rows) if i == 0], last
+            parts = 4 * len(rows)
+            keep, *sends = first_dots(
+                [held[i] for i in rows],
+                (gate_weight, up_weight),
+                columns,
+                bits,
+                parts,
+                [j for j, i in enumerate(rows) if i == 0],
+                last,
             )
             last[:] = sends[:1]
-            dotted[k, w] = keep, [swap(send, 0) for send in sends]
-
-        def sum_core(k, w):
-            keep, got = dotted[k, w]
+            dotted[k] = keep, [swap(send, 0) for send in sends]
+
+        def sum_core(k):
+            keep, got = dotted[k]
             for bit in range(1, bits):
                 keep, send = fold(keep, got, last)
                 last[:] = [send]
                 got = [swap(send, bit)]
-            folded[k, w] = keep, got[0]
+            folded[k] = keep, got[0]
 
         def act(k):
-            own = activate(folded[k, 0], folded[k, 1], last)
+            own = activate(*folded[k], last)
             last[:] = [own]
             pieces = {0: own}
             for bit in reversed(range(1, bits)):
@@ -304,8 +316,11 @@
                 piece, _ = lax.optimization_barrier((pieces[j], last[0]))
                 pieces[j + 1] = swap(piece, 0)
 
-        def need_partial(k, w):
-            last.append(folded[k, w][1])
+        def need_partial(k):
+            last.append(folded[k][1])
+
+        def need_gathered(k):
+            last.extend(hidden[k][j] for j in range(2, n_pipe, 2))
 
         def need_hidden(k):
             last.extend(hidden[k][j] for j in range(1, n_pipe))
@@ -333,19 +348,16 @@
 
         if n_tensor == 4:
             plan = [
-                (dot, 0, 0), (dot, 0, 1), (sum_core, 0, 0), (dot, 1, 0), (sum_core, 0, 1), (sum_core, 1, 0),
-                (need, 2), (dot, 1, 1), (act, 0), (sum_core, 1, 1), (need_partial, 1, 0), (dot, 2, 0),
-                (sum_core, 2, 0), (need_partial, 1, 1), (dot, 2, 1), (act, 1), (need_partial, 2, 0),
-                (dot, 3, 0), (sum_core, 2, 1), (forward, 1), (dot, 3, 1), (sum_core, 3, 0), (forward, 0),
-                (need_partial, 2, 1), (dot, 4, 0), (act, 2), (sum_core, 3, 1), (need_hidden, 0),
-                (need_partial, 3, 0), (dot, 4, 1), (forward, 2), (down, 1), (act, 3), (down, 2), (pass_on, 1),
-                (sum_core, 4, 0), (sum_core, 4, 1), (forward, 3), (down, 0), (down, 3), (pass_on, 2), (act, 4),
-                (forward, 4), (down, 4), (pass_on, 3),
+                (dot, 0), (sum_core, 0), (dot, 1), (act, 0), (sum_core, 1), (dot, 2), (sum_core, 2),
+                (need_partial, 1), (act, 1), (need_gathered, 0), (dot, 3), (sum_core, 3), (need_partial, 2),
+                (forward, 0), (forward, 1), (dot, 4), (act, 2), (act, 3), (sum_core, 4), (down, 1),
+                (forward, 2), (down, 2), (pass_on, 1), (forward, 3), (down, 0), (act, 4), (down, 3),
+                (pass_on, 2), (forward, 4), (down, 4), (pass_on, 3),
             ]
         else:
             plan = []
             for k in range(len(rects)):
-                plan += [(dot, k, 0), (dot, k, 1), (sum_core, k, 0), (sum_core, k, 1), (act, k), (forward, k), (down, k)]
+                plan += [(dot, k), (sum_core, k), (act, k), (forward, k), (down, k)]
             plan += [(pass_on, i) for i in range(1, n_tensor)]
         for task, *which in plan:
             task(*which)

time: 203 us -> 188 us (0.926)
  Pallas kernels: 107 us -> 99 us
  starting transfers between devices: 35 us -> 29 us
    ppermute x6, waiting for transfers between devices: 29.4 us -> 16.9 us  [hop(): return lax.ppermute(value, 'tensor', ring)]
    ppermute x57 -> x52, waiting for transfers between devices: 30.2 us -> 42 us  [swap(): lax.ppermute(value, 'pipe', [(i, i ^ 1 << bit) for i in range(n_pipe)])]
    ppermute x57 -> x52, starting transfers between devices: 28.6 us -> 20.4 us  [swap(): lax.ppermute(value, 'pipe', [(i, i ^ 1 << bit) for i in range(n_pipe)])]
    pallas_call x25 -> x15, Pallas kernels: 72.4 us -> 64.5 us  [the longest x5 57.8 us: first_dots(): pl.pallas_call(kernel, grid=(steps,), in_specs=[HBM if i in fixed else AN...]
    ppermute x6, starting transfers between devices: 6.35 us -> 8.62 us  [hop(): return lax.ppermute(value, 'tensor', ring)]
  transfers between devices with their start and end apart: 63 -> 58, of which waited for: 19 -> 32; matrix products, arithmetic and copies ran while one was open for 0% -> 0% of each run, Pallas kernels for 52% -> 52%
where the time goes in v3:
time: 188 us
  Pallas kernels  99 us (53%)
  waiting for transfers between devices  58.8 us (31%)
  starting transfers between devices  29 us (15%)
    pallas_call x5, Pallas kernels, first_dots(): pl.pallas_call(kernel, grid=(steps,), in_specs=[HBM if i in fixed else AN...  57.8 us
    ppermute x52, waiting for transfers between devices, swap(): lax.ppermute(value, 'pipe', [(i, i ^ 1 << bit) for i in range(n_pipe)])  42 us
    pallas_call x5, Pallas kernels, last_dot(): pl.pallas_call(kernel, grid=(steps,), in_specs=[ANY] * n + [HBM] + [pl.Bl...  32.9 us
    ppermute x52, starting transfers between devices, swap(): lax.ppermute(value, 'pipe', [(i, i ^ 1 << bit) for i in range(n_pipe)])  20.4 us
    ppermute x6, waiting for transfers between devices, hop(): return lax.ppermute(value, 'tensor', ring)  16.9 us
    ppermute x6, starting transfers between devices, hop(): return lax.ppermute(value, 'tensor', ring)  8.62 us
    pallas_call x5, Pallas kernels, fold(): pl.pallas_call(kernel, grid=(width // step,), in_specs=[pl.BlockSpec((k,...  4.16 us
  transfers between devices with their start and end apart: 58, of which 32 were waited for; matrix products, arithmetic and copies ran while one was open for 0% of the time, Pallas kernels for 52%

profile of v3, /device:TPU:0, one launch (start us, length us, event | category | flops | bytes accessed | tf_op | source)
XLA Modules:
  0.0 188.3 jit_solution(7140215559954151767)
XLA Ops:
  0.0 3.0 %collective-permute-start = (bf16[128,2048]{1,0:T(8,128)(2,1)}, bf16[128,2048]{1,0:T(8,128)(2,1)S(1)}, u32[]{:S(2)}, u32[]{:S(2)}) collective-permute-start(bf16[128,2048]{1,0:T(8,128)(2,1)} %refs_0_.5), channel_id=1, source_target_pairs={{0,1},{1,2},{2,3},{3,0},{4,5},{5,6},{6,7},{7,4},{8,9},{9,10},{10,1... | collective-permute-start | bytes 1572872 | tf_op jit(solution)/shard_map/ppermute | solution.py:267
  3.0 1.1 copy-done
  4.1 10.5 %first_dots.5 = (bf16[2,64,3584]{2,1,0:T(8,128)(2,1)S(1)}, bf16[2,16,3584]{2,1,0:T(8,128)(2,1)S(1)}, bf16[2,16,3584]{2,1,0:T(8,128)(2,1)S(1)}, bf16[2,16,3584]{2,1,0:T(8,128)(2,1)S(1)}, bf16[2,16,3584]{2,1,0:T(8,128)(2,1)S(1)}) custom-call(bf16[128,2048]{1,0:T(8,128)(2,1)S(1)} %copy-done, bf16[2048,7168]{1,0:T(8,128)(2,1)} %refs_1_.3, bf16[2048,7168]{1,0:T(8,128)(2,1)} %refs_2_.9), custom_call_target="tpu_custom_call" | custom-call | flops 37580963840 | bytes 293601280 | tf_op jit(solution)/shard_map/first_dots/pallas_call | solution.py:89
  14.7 0.5 collective-permute-start.3
  15.3 0.4 collective-permute-start.5
  15.7 0.5 collective-permute-done.2.refs_1_
  17.2 0.6 fold.5
  17.7 1.6 collective-permute-start.14
  19.3 1.6 collective-permute-start.1
  20.9 12.3 %first_dots.6 = (bf16[2,128,3584]{2,1,0:T(8,128)(2,1)S(1)}, bf16[2,16,3584]{2,1,0:T(8,128)(2,1)S(1)}, bf16[2,16,3584]{2,1,0:T(8,128)(2,1)S(1)}, bf16[2,16,3584]{...) custom-call(bf16[128,2048]{1,0:T(8,128)(2,1)S(1)} %copy-done.1, ...), custom_call_target="tpu_custom_call" | custom-call | flops 75161927680 | bytes 293601280 | tf_op jit(solution)/shard_map/first_dots/pallas_call | solution.py:89
  33.2 0.5 collective-permute-start.7
  33.8 0.4 collective-permute-start.9
  34.2 0.5 collective-permute-done.6.refs_1_
  35.9 0.3 activate.5.refs_9_.refs_0_
  37.2 1.0 fold.6
  38.2 0.6 collective-permute-start.25
  38.8 12.3 %first_dots.7 = (bf16[2,128,3584]{2,1,0:T(8,128)(2,1)S(1)}, bf16[2,16,3584]{2,1,0:T(8,128)(2,1)S(1)}, bf16[2,16,3584]{2,1,0:T(8,128)(2,1)S(1)}, bf16[2,16,3584]{...) custom-call(bf16[128,2048]{1,0:T(8,128)(2,1)S(1)} %collective-permut, ...), custom_call_target="tpu_custom_call" | custom-call | flops 75161927680 | bytes 293601280 | tf_op jit(solution)/shard_map/first_dots/pallas_call | solution.py:89
  51.2 0.5 collective-permute-start.16
  51.7 1.6 collective-permute-start.24
  54.0 0.8 collective-permute-done.18.refs_4_
  55.5 1.5 collective-permute-start.26
  57.0 1.0 fold.7
  58.0 1.2 collective-permute-start.23
  59.2 2.2 %collective-permute-done.25.refs_1_.refs_3_ = bf16[2,64,3584]{2,1,0:T(8,128)(2,1)S(1)} collective-permute-done((bf16[2,64,3584]{2,1,0:T(8,128)(2,1)S(1)}, bf16[2,64,3584]{2,1,0:T(8,128)(2,1)S(1)}, u32[]{:S(2)}, u32[]{:S(2)}) %collective-permute-start.25) | collective-permute-done | bytes 917536 | tf_op jit(solution)/shard_map/ppermute | solution.py:270
  61.5 0.6 activate.6.refs_4_.refs_0_
  62.1 4.3 %collective-permute-done.26.refs_5_.refs_2_ = bf16[32,3584]{1,0:T(8,128)(2,1)S(1)} collective-permute-done((bf16[32,3584]{1,0:T(8,128)(2,1)S(1)}, bf16[32,3584]{1,0:T(8,128)(2,1)S(1)}, u32[]{:S(2)}, u32[]{:S(2)}) %collective-permute-start.26) | collective-permute-done | bytes 229408 | tf_op jit(solution)/shard_map/ppermute | solution.py:270
  66.4 1.5 collective-permute-done.24.refs_1_.refs_0_
  67.8 12.3 %first_dots.8 = (bf16[2,128,3584]{2,1,0:T(8,128)(2,1)S(1)}, bf16[2,16,3584]{2,1,0:T(8,128)(2,1)S(1)}, bf16[2,16,3584]{2,1,0:T(8,128)(2,1)S(1)}, bf16[2,16,3584]{...) custom-call(bf16[128,2048]{1,0:T(8,128)(2,1)S(1)} %collective-permut, ...), custom_call_target="tpu_custom_call" | custom-call | flops 75161927680 | bytes 293601280 | tf_op jit(solution)/shard_map/first_dots/pallas_call | solution.py:89
  80.2 0.5 collective-permute-start.28
  80.8 0.4 collective-permute-start.30
  81.2 0.5 collective-permute-done.27.refs_1_
  83.2 1.5 collective-permute-start.38
  84.7 1.0 fold.8
  85.7 1.0 collective-permute-start.44
  86.7 10.5 %first_dots.9 = (bf16[2,64,3584]{2,1,0:T(8,128)(2,1)S(1)}, bf16[2,16,3584]{2,1,0:T(8,128)(2,1)S(1)}, bf16[2,16,3584]{2,1,0:T(8,128)(2,1)S(1)}, bf16[2,16,3584]{2,1,0:T(8,128)(2,1)S(1)}, bf16[2,16,3584]{2,1,0:T(8,128)(2,1)S(1)}) custom-call(bf16[128,2048]{1,0:T(8,128)(2,1)S(1)} %collective-permute-done.24.refs_1_.refs_0_, bf16[2048,7168]{1,0:T(8,128)(2,1)} %refs_1_.3, ...), custom_call_target="tpu_custom_call" | custom-call | flops 37580963840 | bytes 293601280 | tf_op jit(solution)/shard_map/first_dots/pallas_call | solution.py:89
  97.3 0.5 collective-permute-start.41
  97.8 0.4 collective-permute-start.39
  98.3 0.6 activate.7.refs_2_.refs_0_
  98.9 1.1 collective-permute-start.36
  100.0 16.1 %collective-permute-done.44.refs_1_ = bf16[2,64,3584]{2,1,0:T(8,128)(2,1)S(1)} collective-permute-done((bf16[2,64,3584]{2,1,0:T(8,128)(2,1)S(1)}, bf16[2,64,3584]{2,1,0:T(8,128)(2,1)S(1)}, u32[]{:S(2)}, u32[]{:S(2)}) %collective-permute-start.44) | collective-permute-done | bytes 917536 | tf_op jit(solution)/shard_map/ppermute | solution.py:270
  116.2 0.6 activate.8.refs_5_.refs_0_
  116.8 0.6 collective-permute-start.35
  117.7 0.6 fold.9
  118.2 6.9 %last_dot.5 = (f32[128,2048]{1,0:T(8,128)S(1)}, f32[128,2048]{1,0:T(8,128)S(1)}) custom-call(bf16[64,3584]{1,0:T(8,128)(2,1)S(1)} %activate.6.refs_4_.refs_0_, bf16[64,3584]{1,0:T(8,128)(2,1)S(1)} %collective-permute-done.37.refs_1_, bf16[64,3584]{1,0:T(8,128)(2,1)S(1)} %collective-permute-done.38.refs_2_, ...), custom_call_target="tpu_custom_call" | custom-call | flops 10 | bytes 10 | tf_op jit(solution)/shard_map/last_dot/pallas_call | solution.py:208
  125.4 1.5 collective-permute-start.48
  127.0 6.9 %last_dot.6 = (bf16[128,2048]{1,0:T(8,128)(2,1)S(1)}, f32[128,2048]{1,0:T(8,128)S(1)}) custom-call(bf16[64,3584]{1,0:T(8,128)(2,1)S(1)} %activate.7.refs_2_.refs_0_, bf16[64,3584]{1,0:T(8,128)(2,1)S(1)} %collective-permute-done.35.refs_1_, bf16[64,3584]{1,0:T(8,128)(2,1)S(1)} %collective-permute-done.36.refs_2_, ...), custom_call_target="tpu_custom_call" | custom-call | flops 10 | bytes 10 | tf_op jit(solution)/shard_map/last_dot/pallas_call | solution.py:208
  134.0 1.0 collective-permute-start.46
  135.0 0.5 collective-permute-start.47
  135.5 0.6 collective-permute-start.50
  136.1 2.1 %collective-permute-done.48.refs_2_ = bf16[64,3584]{1,0:T(8,128)(2,1)S(1)} collective-permute-done((bf16[64,3584]{1,0:T(8,128)(2,1)S(1)}, bf16[64,3584]{1,0:T(8,128)(2,1)S(1)}, u32[]{:S(2)}, u32[]{:S(2)}) %collective-permute-start.48) | collective-permute-done | bytes 458784 | tf_op jit(solution)/shard_map/ppermute | solution.py:270
  138.2 0.5 collective-permute-start.52
  138.7 1.6 collective-permute-done.52.refs_3_
  140.3 6.1 %last_dot.7.refs_2_ = bf16[128,2048]{1,0:T(8,128)(2,1)S(1)} custom-call(bf16[32,3584]{1,0:T(8,128)(2,1)S(1)} %activate.5.refs_9_.refs_0_, bf16[32,3584]{1,0:T(8,128)(2,1)S(1)} %collective-permute-done.51.refs_1_, bf16[32,3584]{1,0:T(8,128)(2,1)S(1)} %collective-permute-done.26.refs_5_.refs_2_, bf16[32,3584]{1,0:T(8,128)(2,1)S(1)} %collective-permute-done.52.refs_3_, ...), custom_call_target="tpu_custom_call" | custom-call | flops 10 | bytes 10 | tf_op jit(solution)/shard_map/last_dot/pallas_call | solution.py:208
  146.4 1.6 collective-permute-done.50.refs_1_
  148.0 0.4 activate.9.refs_6_.refs_0_
  148.4 7.0 %last_dot.8 = (bf16[128,2048]{1,0:T(8,128)(2,1)S(1)}, f32[128,2048]{1,0:T(8,128)S(1)}) custom-call(bf16[64,3584]{1,0:T(8,128)(2,1)S(1)} %activate.8.refs_5_.refs_0_, bf16[64,3584]{1,0:T(8,128)(2,1)S(1)} %collective-permute-done.47.refs_1_, bf16[64,3584]{1,0:T(8,128)(2,1)S(1)} %collective-permute-done.48.refs_2_, ...), custom_call_target="tpu_custom_call" | custom-call | flops 10 | bytes 10 | tf_op jit(solution)/shard_map/last_dot/pallas_call | solution.py:208
  155.7 1.0 collective-permute-start.53
  156.7 0.6 collective-permute-start.55
  157.3 6.3 %collective-permute-done.55.refs_2_ = bf16[32,3584]{1,0:T(8,128)(2,1)S(1)} collective-permute-done((bf16[32,3584]{1,0:T(8,128)(2,1)S(1)}, bf16[32,3584]{1,0:T(8,128)(2,1)S(1)}, u32[]{:S(2)}, u32[]{:S(2)}) %collective-permute-start.55) | collective-permute-done | bytes 229408 | tf_op jit(solution)/shard_map/ppermute | solution.py:270
  163.6 1.5 collective-permute-done.56.refs_3_
  165.1 6.1 %last_dot.9.refs_1_.refs_2_ = bf16[128,2048]{1,0:T(8,128)(2,1)S(1)} custom-call(bf16[32,3584]{1,0:T(8,128)(2,1)S(1)} %activate.9.refs_6_.refs_0_, bf16[32,3584]{1,0:T(8,128)(2,1)S(1)} %collective-permute-done.54.refs_1_, bf16[32,3584]{1,0:T(8,128)(2,1)S(1)} %collective-permute-done.55.refs_2_, bf16[32,3584]{1,0:T(8,128)(2,1)S(1)} %collective-permute-done.56.refs_3_, ...), custom_call_target="tpu_custom_call" | custom-call | flops 10 | bytes 10 | tf_op jit(solution)/shard_map/last_dot/pallas_call | solution.py:208
  171.5 0.4 collective-permute-start.57
  171.9 15.4 %collective-permute-done.57.refs_1_ = bf16[128,2048]{1,0:T(8,128)(2,1)S(1)} collective-permute-done((bf16[128,2048]{1,0:T(8,128)(2,1)S(1)}, bf16[128,2048]{1,0:T(8,128)(2,1)S(1)}, u32[]{:S(2)}, u32[]{:S(2)}) %collective-permute-start.57) | collective-permute-done | bytes 524320 | tf_op jit(solution)/shard_map/ppermute | solution.py:267
  187.3 1.0 add.5
  (81 shorter events, 8.0 us)
Async XLA Ops:
  0.0 19.3 %collective-permute-start = (bf16[128,2048]{1,0:T(8,128)(2,1)}, bf16[128,2048]{1,0:T(8,128)(2,1)S(1)}, u32[]{:S(2)}, u32[]{:S(2)}) collective-permute-start(bf16[128,2048]{1,0:T(8,128)(2,1)} %refs_0_.5), channel_id=1, source_target_pairs={{0,1},{1,2},{2,3},{3,0},{4,5},{5,6},{6,7},{7,4},{8,9},{9,10},{10,1... | collective-permute-start | bytes 1572872 | tf_op jit(solution)/shard_map/ppermute | solution.py:267
  3.0 1.1 copy-start
  4.1 16.8 %copy-start.1 = (bf16[128,2048]{1,0:T(8,128)(2,1)S(1)}, bf16[128,2048]{1,0:T(8,128)(2,1)}, u32[]{:S(2)}) copy-start(bf16[128,2048]{1,0:T(8,128)(2,1)} %refs_0_.5) | copy-start | bytes 1572868
  14.6 1.6 collective-permute-start.2
  14.7 1.8 collective-permute-start.3
  15.2 1.6 collective-permute-start.4
  15.3 1.9 collective-permute-start.5
  17.7 16.1 %collective-permute-start.14 = (bf16[2,32,3584]{2,1,0:T(8,128)(2,1)S(1)}, bf16[2,32,3584]{2,1,0:T(8,128)(2,1)S(1)}, u32[]{:S(2)}, u32[]{:S(2)}) collective-permute-start(bf16[2,32,3584]{2,1,0:T(8,128)(2,1)S(1)} %get-tuple-element.68.refs_4_), channel_id=1, source_target_pairs={{0,8},{4,12},{8,0},{12,4},{1,9},{5,13},{9,1},{13,5},{2,10},{6,14},... | collective-permute-start | bytes 1376264 | tf_op jit(solution)/shard_map/ppermute | solution.py:270
  19.3 19.5 %collective-permute-start.1 = (bf16[128,2048]{1,0:T(8,128)(2,1)S(1)}, bf16[128,2048]{1,0:T(8,128)(2,1)S(1)}, u32[]{:S(2)}, u32[]{:S(2)}) collective-permute-start(bf16[128,2048]{1,0:T(8,128)(2,1)S(1)} %collective-permute-done.refs_1_.refs_0_), channel_id=1, source_target_pairs={{0,1},{1,2},{2,3},{3,0},{4,5},{5,6},{6,7},{7,4},{8,9},{9,10},{10,1... | collective-permute-start | bytes 1572872 | tf_op jit(solution)/shard_map/ppermute | solution.py:267
  33.1 1.6 collective-permute-start.6
  33.2 1.8 collective-permute-start.7
  33.7 1.6 collective-permute-start.8
  33.8 1.9 collective-permute-start.9
  34.7 1.5 collective-permute-start.10
  35.0 1.5 collective-permute-start.11
  35.4 1.5 collective-permute-start.12
  35.7 1.5 collective-permute-start.13
  38.2 23.3 %collective-permute-start.25 = (bf16[2,64,3584]{2,1,0:T(8,128)(2,1)S(1)}, bf16[2,64,3584]{2,1,0:T(8,128)(2,1)S(1)}, u32[]{:S(2)}, u32[]{:S(2)}) collective-permute-start(bf16[2,64,3584]{2,1,0:T(8,128)(2,1)S(1)} %get-tuple-element.79.refs_4_), channel_id=1, source_target_pairs={{0,8},{4,12},{8,0},{12,4},{1,9},{5,13},{9,1},{13,5},{2,10},{6,14},... | collective-permute-start | bytes 2752520 | tf_op jit(solution)/shard_map/ppermute | solution.py:270
  51.1 2.2 %collective-permute-start.15 = (bf16[2,16,3584]{2,1,0:T(8,128)(2,1)S(1)}, bf16[2,16,3584]{2,1,0:T(8,128)(2,1)S(1)}, u32[]{:S(2)}, u32[]{:S(2)}) collective-permute-start(bf16[2,16,3584]{2,1,0:T(8,128)(2,1)S(1)} %get-tuple-element.81.refs_9_), channel_id=1, source_target_pairs={{0,4},{4,0},{8,12},{12,8},{1,5},{5,1},{9,13},{13,9},{2,6},{6,2},{1... | collective-permute-start | bytes 688136 | tf_op jit(solution)/shard_map/ppermute | solution.py:270
  51.2 2.3 %collective-permute-start.16 = (bf16[2,16,3584]{2,1,0:T(8,128)(2,1)S(1)}, bf16[2,16,3584]{2,1,0:T(8,128)(2,1)S(1)}, u32[]{:S(2)}, u32[]{:S(2)}) collective-permute-start(bf16[2,16,3584]{2,1,0:T(8,128)(2,1)S(1)} %get-tuple-element.82), channel_id=1, source_target_pairs={{0,4},{4,0},{8,12},{12,8},{1,5},{5,1},{9,13},{13,9},{2,6},{6,2},{1... | collective-permute-start | bytes 688136 | tf_op jit(solution)/shard_map/ppermute | solution.py:270
  51.7 2.2 %collective-permute-start.17 = (bf16[2,16,3584]{2,1,0:T(8,128)(2,1)S(1)}, bf16[2,16,3584]{2,1,0:T(8,128)(2,1)S(1)}, u32[]{:S(2)}, u32[]{:S(2)}) collective-permute-start(bf16[2,16,3584]{2,1,0:T(8,128)(2,1)S(1)} %get-tuple-element.83), channel_id=1, source_target_pairs={{0,4},{4,0},{8,12},{12,8},{1,5},{5,1},{9,13},{13,9},{2,6},{6,2},{1... | collective-permute-start | bytes 688136 | tf_op jit(solution)/shard_map/ppermute | solution.py:270
  51.7 16.1 %collective-permute-start.24 = (bf16[128,2048]{1,0:T(8,128)(2,1)S(1)}, bf16[128,2048]{1,0:T(8,128)(2,1)S(1)}, u32[]{:S(2)}, u32[]{:S(2)}) collective-permute-start(bf16[128,2048]{1,0:T(8,128)(2,1)S(1)} %collective-permute-done.1.refs_1_.refs_0_), channel_id=1, source_target_pairs={{0,1},{1,2},{2,3},{3,0},{4,5},{5,6},{6,7},{7,4},{8,9},{9,10},{10,1... | collective-permute-start | bytes 1572872 | tf_op jit(solution)/shard_map/ppermute | solution.py:267
  53.3 1.5 collective-permute-start.18
  53.5 1.6 collective-permute-start.19
  53.8 1.6 collective-permute-start.20
  54.8 2.2 %collective-permute-start.21 = (bf16[2,16,3584]{2,1,0:T(8,128)(2,1)S(1)}, bf16[2,16,3584]{2,1,0:T(8,128)(2,1)S(1)}, u32[]{:S(2)}, u32[]{:S(2)}) collective-permute-start(bf16[2,16,3584]{2,1,0:T(8,128)(2,1)S(1)} %get-tuple-element.87), channel_id=1, source_target_pairs={{0,4},{4,0},{8,12},{12,8},{1,5},{5,1},{9,13},{13,9},{2,6},{6,2},{1... | collective-permute-start | bytes 688136 | tf_op jit(solution)/shard_map/ppermute | solution.py:270
  55.1 1.8 collective-permute-start.22
  55.5 10.9 %collective-permute-start.26 = (bf16[32,3584]{1,0:T(8,128)(2,1)S(1)}, bf16[32,3584]{1,0:T(8,128)(2,1)S(1)}, u32[]{:S(2)}, u32[]{:S(2)}) collective-permute-start(bf16[32,3584]{1,0:T(8,128)(2,1)S(1)} %activate.5.refs_9_.refs_0_), channel_id=1, source_target_pairs={{0,8},{4,12},{8,0},{12,4},{1,9},{5,13},{9,1},{13,5},{2,10},{6,14},... | collective-permute-start | bytes 688136 | tf_op jit(solution)/shard_map/ppermute | solution.py:270
  58.0 28.7 %collective-permute-start.23 = (bf16[2,64,3584]{2,1,0:T(8,128)(2,1)S(1)}, bf16[2,64,3584]{2,1,0:T(8,128)(2,1)S(1)}, u32[]{:S(2)}, u32[]{:S(2)}) collective-permute-start(bf16[2,64,3584]{2,1,0:T(8,128)(2,1)S(1)} %get-tuple-element.90.refs_2_), channel_id=1, source_target_pairs={{0,8},{4,12},{8,0},{12,4},{1,9},{5,13},{9,1},{13,5},{2,10},{6,14},... | collective-permute-start | bytes 2752520 | tf_op jit(solution)/shard_map/ppermute | solution.py:270
  80.1 1.6 collective-permute-start.27
  80.2 1.8 collective-permute-start.28
  80.7 1.6 collective-permute-start.29
  80.8 1.9 collective-permute-start.30
  81.7 1.5 collective-permute-start.31
  82.0 2.7 %collective-permute-start.32 = (bf16[2,16,3584]{2,1,0:T(8,128)(2,1)S(1)}, bf16[2,16,3584]{2,1,0:T(8,128)(2,1)S(1)}, u32[]{:S(2)}, u32[]{:S(2)}) collective-permute-start(bf16[2,16,3584]{2,1,0:T(8,128)(2,1)S(1)} %get-tuple-element.98), channel_id=1, source_target_pairs={{0,4},{4,0},{8,12},{12,8},{1,5},{5,1},{9,13},{13,9},{2,6},{6,2},{1... | collective-permute-start | bytes 688136 | tf_op jit(solution)/shard_map/ppermute | solution.py:270
  82.3 2.3 %collective-permute-start.33 = (bf16[2,16,3584]{2,1,0:T(8,128)(2,1)S(1)}, bf16[2,16,3584]{2,1,0:T(8,128)(2,1)S(1)}, u32[]{:S(2)}, u32[]{:S(2)}) collective-permute-start(bf16[2,16,3584]{2,1,0:T(8,128)(2,1)S(1)} %get-tuple-element.99), channel_id=1, source_target_pairs={{0,4},{4,0},{8,12},{12,8},{1,5},{5,1},{9,13},{13,9},{2,6},{6,2},{1... | collective-permute-start | bytes 688136 | tf_op jit(solution)/shard_map/ppermute | solution.py:270
  82.6 2.0 %collective-permute-start.34 = (bf16[2,16,3584]{2,1,0:T(8,128)(2,1)S(1)}, bf16[2,16,3584]{2,1,0:T(8,128)(2,1)S(1)}, u32[]{:S(2)}, u32[]{:S(2)}) collective-permute-start(bf16[2,16,3584]{2,1,0:T(8,128)(2,1)S(1)} %get-tuple-element.100), channel_id=1, source_target_pairs={{0,4},{4,0},{8,12},{12,8},{1,5},{5,1},{9,13},{13,9},{2,6},{6,2},{1... | collective-permute-start | bytes 688136 | tf_op jit(solution)/shard_map/ppermute | solution.py:270
  83.2 14.7 %collective-permute-start.38 = (bf16[64,3584]{1,0:T(8,128)(2,1)S(1)}, bf16[64,3584]{1,0:T(8,128)(2,1)S(1)}, u32[]{:S(2)}, u32[]{:S(2)}) collective-permute-start(bf16[64,3584]{1,0:T(8,128)(2,1)S(1)} %activate.6.refs_4_.refs_0_), channel_id=1, source_target_pairs={{0,8},{4,12},{8,0},{12,4},{1,9},{5,13},{9,1},{13,5},{2,10},{6,14},... | collective-permute-start | bytes 1376264 | tf_op jit(solution)/shard_map/ppermute | solution.py:270
  85.7 30.5 %collective-permute-start.44 = (bf16[2,64,3584]{2,1,0:T(8,128)(2,1)S(1)}, bf16[2,64,3584]{2,1,0:T(8,128)(2,1)S(1)}, u32[]{:S(2)}, u32[]{:S(2)}) collective-permute-start(bf16[2,64,3584]{2,1,0:T(8,128)(2,1)S(1)} %get-tuple-element.101.refs_3_), channel_id=1, source_target_pairs={{0,8},{4,12},{8,0},{12,4},{1,9},{5,13},{9,1},{13,5},{2,10},{6,14},... | collective-permute-start | bytes 2752520 | tf_op jit(solution)/shard_map/ppermute | solution.py:270
  97.2 1.7 collective-permute-start.40
  97.3 2.8 %collective-permute-start.41 = (bf16[2,16,3584]{2,1,0:T(8,128)(2,1)S(1)}, bf16[2,16,3584]{2,1,0:T(8,128)(2,1)S(1)}, u32[]{:S(2)}, u32[]{:S(2)}) collective-permute-start(bf16[2,16,3584]{2,1,0:T(8,128)(2,1)S(1)} %get-tuple-element.105), channel_id=1, source_target_pairs={{0,4},{4,0},{8,12},{12,8},{1,5},{5,1},{9,13},{13,9},{2,6},{6,2},{1... | collective-permute-start | bytes 688136 | tf_op jit(solution)/shard_map/ppermute | solution.py:270
  97.8 20.5 %collective-permute-start.37 = (bf16[64,3584]{1,0:T(8,128)(2,1)S(1)}, bf16[64,3584]{1,0:T(8,128)(2,1)S(1)}, u32[]{:S(2)}, u32[]{:S(2)}) collective-permute-start(bf16[64,3584]{1,0:T(8,128)(2,1)S(1)} %activate.6.refs_4_.refs_0_), channel_id=1, source_target_pairs={{0,4},{4,0},{8,12},{12,8},{1,5},{5,1},{9,13},{13,9},{2,6},{6,2},{1... | collective-permute-start | bytes 1376264 | tf_op jit(solution)/shard_map/ppermute | solution.py:270
  97.8 20.4 %collective-permute-start.39 = (bf16[64,3584]{1,0:T(8,128)(2,1)S(1)}, bf16[64,3584]{1,0:T(8,128)(2,1)S(1)}, u32[]{:S(2)}, u32[]{:S(2)}) collective-permute-start(bf16[64,3584]{1,0:T(8,128)(2,1)S(1)} %collective-permute-done.38.refs_2_), channel_id=1, source_target_pairs={{0,4},{4,0},{8,12},{12,8},{1,5},{5,1},{9,13},{13,9},{2,6},{6,2},{1... | collective-permute-start | bytes 1376264 | tf_op jit(solution)/shard_map/ppermute | solution.py:270
  98.9 26.3 %collective-permute-start.36 = (bf16[64,3584]{1,0:T(8,128)(2,1)S(1)}, bf16[64,3584]{1,0:T(8,128)(2,1)S(1)}, u32[]{:S(2)}, u32[]{:S(2)}) collective-permute-start(bf16[64,3584]{1,0:T(8,128)(2,1)S(1)} %activate.7.refs_2_.refs_0_), channel_id=1, source_target_pairs={{0,8},{4,12},{8,0},{12,4},{1,9},{5,13},{9,1},{13,5},{2,10},{6,14},... | collective-permute-start | bytes 1376264 | tf_op jit(solution)/shard_map/ppermute | solution.py:270
  100.0 16.8 %collective-permute-start.42 = (bf16[2,16,3584]{2,1,0:T(8,128)(2,1)S(1)}, bf16[2,16,3584]{2,1,0:T(8,128)(2,1)S(1)}, u32[]{:S(2)}, u32[]{:S(2)}) collective-permute-start(bf16[2,16,3584]{2,1,0:T(8,128)(2,1)S(1)} %get-tuple-element.106), channel_id=1, source_target_pairs={{0,4},{4,0},{8,12},{12,8},{1,5},{5,1},{9,13},{13,9},{2,6},{6,2},{1... | collective-permute-start | bytes 688136 | tf_op jit(solution)/shard_map/ppermute | solution.py:270
  116.2 1.5 collective-permute-start.43
  116.8 10.1 %collective-permute-start.35 = (bf16[64,3584]{1,0:T(8,128)(2,1)S(1)}, bf16[64,3584]{1,0:T(8,128)(2,1)S(1)}, u32[]{:S(2)}, u32[]{:S(2)}) collective-permute-start(bf16[64,3584]{1,0:T(8,128)(2,1)S(1)} %activate.7.refs_2_.refs_0_), channel_id=1, source_target_pairs={{0,4},{4,0},{8,12},{12,8},{1,5},{5,1},{9,13},{13,9},{2,6},{6,2},{1... | collective-permute-start | bytes 1376264 | tf_op jit(solution)/shard_map/ppermute | solution.py:270
  125.2 1.8 collective-permute-start.45
  125.4 12.8 %collective-permute-start.48 = (bf16[64,3584]{1,0:T(8,128)(2,1)S(1)}, bf16[64,3584]{1,0:T(8,128)(2,1)S(1)}, u32[]{:S(2)}, u32[]{:S(2)}) collective-permute-start(bf16[64,3584]{1,0:T(8,128)(2,1)S(1)} %activate.8.refs_5_.refs_0_), channel_id=1, source_target_pairs={{0,8},{4,12},{8,0},{12,4},{1,9},{5,13},{9,1},{13,5},{2,10},{6,14},... | collective-permute-start | bytes 1376264 | tf_op jit(solution)/shard_map/ppermute | solution.py:270
  134.0 21.4 %collective-permute-start.46 = (bf16[128,2048]{1,0:T(8,128)(2,1)S(1)}, bf16[128,2048]{1,0:T(8,128)(2,1)S(1)}, u32[]{:S(2)}, u32[]{:S(2)}) collective-permute-start(bf16[128,2048]{1,0:T(8,128)(2,1)S(1)} %get-tuple-element.113.refs_6_), channel_id=1, source_target_pairs={{0,1},{1,2},{2,3},{3,0},{4,5},{5,6},{6,7},{7,4},{8,9},{9,10},{10,1... | collective-permute-start | bytes 1572872 | tf_op jit(solution)/shard_map/ppermute | solution.py:267
  135.0 3.2 %collective-permute-start.51 = (bf16[32,3584]{1,0:T(8,128)(2,1)S(1)}, bf16[32,3584]{1,0:T(8,128)(2,1)S(1)}, u32[]{:S(2)}, u32[]{:S(2)}) collective-permute-start(bf16[32,3584]{1,0:T(8,128)(2,1)S(1)} %activate.5.refs_9_.refs_0_), channel_id=1, source_target_pairs={{0,4},{4,0},{8,12},{12,8},{1,5},{5,1},{9,13},{13,9},{2,6},{6,2},{1... | collective-permute-start | bytes 688136 | tf_op jit(solution)/shard_map/ppermute | solution.py:270
  135.0 13.4 %collective-permute-start.47 = (bf16[64,3584]{1,0:T(8,128)(2,1)S(1)}, bf16[64,3584]{1,0:T(8,128)(2,1)S(1)}, u32[]{:S(2)}, u32[]{:S(2)}) collective-permute-start(bf16[64,3584]{1,0:T(8,128)(2,1)S(1)} %activate.8.refs_5_.refs_0_), channel_id=1, source_target_pairs={{0,4},{4,0},{8,12},{12,8},{1,5},{5,1},{9,13},{13,9},{2,6},{6,2},{1... | collective-permute-start | bytes 1376264 | tf_op jit(solution)/shard_map/ppermute | solution.py:270
  135.5 12.5 %collective-permute-start.50 = (bf16[2,32,3584]{2,1,0:T(8,128)(2,1)S(1)}, bf16[2,32,3584]{2,1,0:T(8,128)(2,1)S(1)}, u32[]{:S(2)}, u32[]{:S(2)}) collective-permute-start(bf16[2,32,3584]{2,1,0:T(8,128)(2,1)S(1)} %get-tuple-element.109.refs_5_), channel_id=1, source_target_pairs={{0,8},{4,12},{8,0},{12,4},{1,9},{5,13},{9,1},{13,5},{2,10},{6,14},... | collective-permute-start | bytes 1376264 | tf_op jit(solution)/shard_map/ppermute | solution.py:270
  138.2 10.2 %collective-permute-start.49 = (bf16[64,3584]{1,0:T(8,128)(2,1)S(1)}, bf16[64,3584]{1,0:T(8,128)(2,1)S(1)}, u32[]{:S(2)}, u32[]{:S(2)}) collective-permute-start(bf16[64,3584]{1,0:T(8,128)(2,1)S(1)} %collective-permute-done.48.refs_2_), channel_id=1, source_target_pairs={{0,4},{4,0},{8,12},{12,8},{1,5},{5,1},{9,13},{13,9},{2,6},{6,2},{1... | collective-permute-start | bytes 1376264 | tf_op jit(solution)/shard_map/ppermute | solution.py:270
  138.2 2.1 %collective-permute-start.52 = (bf16[32,3584]{1,0:T(8,128)(2,1)S(1)}, bf16[32,3584]{1,0:T(8,128)(2,1)S(1)}, u32[]{:S(2)}, u32[]{:S(2)}) collective-permute-start(bf16[32,3584]{1,0:T(8,128)(2,1)S(1)} %collective-permute-done.26.refs_5_.refs_2_), channel_id=1, source_target_pairs={{0,4},{4,0},{8,12},{12,8},{1,5},{5,1},{9,13},{13,9},{2,6},{6,2},{1... | collective-permute-start | bytes 688136 | tf_op jit(solution)/shard_map/ppermute | solution.py:270
  148.4 38.9 %copy-start.2 = (bf16[128,2048]{1,0:T(8,128)(2,1)S(1)}, bf16[128,2048]{1,0:T(8,128)(2,1)}, u32[]{:S(2)}) copy-start(bf16[128,2048]{1,0:T(8,128)(2,1)} %refs_0_.5) | copy-start | bytes 1572868
  155.7 15.5 %collective-permute-start.53 = (bf16[128,2048]{1,0:T(8,128)(2,1)S(1)}, bf16[128,2048]{1,0:T(8,128)(2,1)S(1)}, u32[]{:S(2)}, u32[]{:S(2)}) collective-permute-start(bf16[128,2048]{1,0:T(8,128)(2,1)S(1)} %add.3.refs_6_), channel_id=1, source_target_pairs={{0,1},{1,2},{2,3},{3,0},{4,5},{5,6},{6,7},{7,4},{8,9},{9,10},{10,1... | collective-permute-start | bytes 1572872 | tf_op jit(solution)/shard_map/ppermute | solution.py:267
  156.7 6.9 %collective-permute-start.55 = (bf16[32,3584]{1,0:T(8,128)(2,1)S(1)}, bf16[32,3584]{1,0:T(8,128)(2,1)S(1)}, u32[]{:S(2)}, u32[]{:S(2)}) collective-permute-start(bf16[32,3584]{1,0:T(8,128)(2,1)S(1)} %activate.9.refs_6_.refs_0_), channel_id=1, source_target_pairs={{0,8},{4,12},{8,0},{12,4},{1,9},{5,13},{9,1},{13,5},{2,10},{6,14},... | collective-permute-start | bytes 688136 | tf_op jit(solution)/shard_map/ppermute | solution.py:270
  157.3 6.3 %collective-permute-start.54 = (bf16[32,3584]{1,0:T(8,128)(2,1)S(1)}, bf16[32,3584]{1,0:T(8,128)(2,1)S(1)}, u32[]{:S(2)}, u32[]{:S(2)}) collective-permute-start(bf16[32,3584]{1,0:T(8,128)(2,1)S(1)} %activate.9.refs_6_.refs_0_), channel_id=1, source_target_pairs={{0,4},{4,0},{8,12},{12,8},{1,5},{5,1},{9,13},{13,9},{2,6},{6,2},{1... | collective-permute-start | bytes 688136 | tf_op jit(solution)/shard_map/ppermute | solution.py:270
  163.6 1.5 collective-permute-start.56
  171.5 15.8 %collective-permute-start.57 = (bf16[128,2048]{1,0:T(8,128)(2,1)S(1)}, bf16[128,2048]{1,0:T(8,128)(2,1)S(1)}, u32[]{:S(2)}, u32[]{:S(2)}) collective-permute-start(bf16[128,2048]{1,0:T(8,128)(2,1)S(1)} %add.4.refs_3_), channel_id=1, source_target_pairs={{0,1},{1,2},{2,3},{3,0},{4,5},{5,6},{6,7},{7,4},{8,9},{9,10},{10,1... | collective-permute-start | bytes 1572872 | tf_op jit(solution)/shard_map/ppermute | solution.py:267

commit v4 on v3

--- a/solution.py
+++ b/solution.py
@@ -152,7 +152,7 @@
     )(kept, got, *after)
 
 
-def last_dot(pieces, weight, at, carries, finals, after):
+def last_dot(pieces, weight, at, carries, finals, weigh, after):
     n, g = len(pieces), len(carries)
     m1, depth = pieces[0].shape
     width = weight.shape[1]
@@ -219,9 +219,24 @@
             pltpu.SemaphoreType.DMA((slots,)),
         ],
         compiler_params=params(40),
-        cost_estimate=cost(1, 1),
+        cost_estimate=cost(weigh * 2 * m * depth * width, weigh * 2 * depth * width),
         name="last_dot",
     )(*pieces, weight, *given, *after)
+
+
+def join(after):
+    def kernel(*refs):
+        refs[-1][...] = jnp.zeros_like(refs[-1])
+
+    return pl.pallas_call(
+        kernel,
+        in_specs=[ANY] * len(after),
+        out_specs=pl.BlockSpec(memory_space=pltpu.VMEM),
+        out_shape=jax.ShapeDtypeStruct((8, 128), F32),
+        compiler_params=pltpu.CompilerParams(vmem_limit_bytes=40 * MIB),
+        cost_estimate=cost(1, 1),
+        name="join",
+    )(*after)
 
 
 def add(values, after):
@@ -279,7 +294,7 @@
 
         def dot(k):
             rows, columns = rects[k]
-            parts = 4 * len(rows)
+            parts = 1 if k == len(rects) - 1 else 4 * len(rows)
             keep, *sends = first_dots(
                 [held[i] for i in rows],
                 (gate_weight, up_weight),
@@ -325,12 +340,12 @@
         def need_hidden(k):
             last.extend(hidden[k][j] for j in range(1, n_pipe))
 
-        def down(k):
+        def down(k, weigh=1):
             rows, columns = rects[k]
             for i in rows:
                 left[i] -= 1
             out = last_dot(
-                [hidden[k][j] for j in range(n_pipe)], down_weight, columns[0], [sums.get(i) for i in rows], [not left[i] for i in rows], last
+                [hidden[k][j] for j in range(n_pipe)], down_weight, columns[0], [sums.get(i) for i in rows], [not left[i] for i in rows], weigh, last
             )
             last[:] = out[:1]
             sums.update(zip(rows, out))
@@ -339,6 +354,12 @@
 
         def need(i):
             last.append(held[i])
+
+        def fill(k):
+            down(k, 0)
+
+        def wait():
+            last[:] = [join(last)]
 
         def pass_on(i):
             value = sums[i] if i == 1 else add([total[i - 1], sums[i]], last)
@@ -346,13 +367,17 @@
                 last[:] = [value]
             total[i] = hop(value)
 
+        def need_total(i):
+            last.append(total[i])
+
         if n_tensor == 4:
             plan = [
-                (dot, 0), (sum_core, 0), (dot, 1), (act, 0), (sum_core, 1), (dot, 2), (sum_core, 2),
-                (need_partial, 1), (act, 1), (need_gathered, 0), (dot, 3), (sum_core, 3), (need_partial, 2),
-                (forward, 0), (forward, 1), (dot, 4), (act, 2), (act, 3), (sum_core, 4), (down, 1),
-                (forward, 2), (down, 2), (pass_on, 1), (forward, 3), (down, 0), (act, 4), (down, 3),
-                (pass_on, 2), (forward, 4), (down, 4), (pass_on, 3),
+                (dot, 0), (sum_core, 0), (dot, 1), (act, 0), (sum_core, 1), (dot, 2), (need, 3),
+                (need_gathered, 0), (wait,), (forward, 0), (sum_core, 2), (need_partial, 1), (need_hidden, 0),
+                (dot, 3), (act, 1), (sum_core, 3), (need_partial, 2), (dot, 4), (act, 2), (forward, 1),
+                (fill, 1), (act, 3), (sum_core, 4), (forward, 2), (down, 2), (pass_on, 1), (fill, 0),
+                (forward, 3), (act, 4), (need_total, 1), (down, 3), (pass_on, 2), (forward, 4), (down, 4),
+                (pass_on, 3),
             ]
         else:
             plan = []

time: 188 us -> 187 us (level)
  starting transfers between devices: 29 us -> 25.6 us
  waiting for transfers between devices: 58.8 us -> 61.4 us
    ppermute x6, waiting for transfers between devices: 16.9 us -> 23.9 us  [hop(): return lax.ppermute(value, 'tensor', ring)]
    ppermute x52 -> x49, waiting for transfers between devices: 42 us -> 37.6 us  [swap(): lax.ppermute(value, 'pipe', [(i, i ^ 1 << bit) for i in range(n_pipe)])]
    ppermute x52 -> x49, starting transfers between devices: 20.4 us -> 16.7 us  [swap(): lax.ppermute(value, 'pipe', [(i, i ^ 1 << bit) for i in range(n_pipe)])]
  transfers between devices with their start and end apart: 58 -> 55, of which waited for: 32 -> 33; matrix products, arithmetic and copies ran while one was open for 0% -> 0% of each run, Pallas kernels for 52% -> 52%
where the time goes in v4:
time: 187 us
  Pallas kernels  98.9 us (53%)
  waiting for transfers between devices  61.4 us (33%)
  starting transfers between devices  25.6 us (14%)
    pallas_call x5, Pallas kernels, first_dots(): pl.pallas_call(kernel, grid=(steps,), in_specs=[HBM if i in fixed else AN...  57.7 us
    ppermute x49, waiting for transfers between devices, swap(): lax.ppermute(value, 'pipe', [(i, i ^ 1 << bit) for i in range(n_pipe)])  37.6 us
    pallas_call x5, Pallas kernels, last_dot(): pl.pallas_call(kernel, grid=(steps,), in_specs=[ANY] * n + [HBM] + [pl.Bl...  32.9 us
    ppermute x6, waiting for transfers between devices, hop(): return lax.ppermute(value, 'tensor', ring)  23.9 us
    ppermute x49, starting transfers between devices, swap(): lax.ppermute(value, 'pipe', [(i, i ^ 1 << bit) for i in range(n_pipe)])  16.7 us
    ppermute x6, starting transfers between devices, hop(): return lax.ppermute(value, 'tensor', ring)  8.87 us
    pallas_call x5, Pallas kernels, fold(): pl.pallas_call(kernel, grid=(width // step,), in_specs=[pl.BlockSpec((k,...  4.14 us
  transfers between devices with their start and end apart: 55, of which 33 were waited for; matrix products, arithmetic and copies ran while one was open for 0% of the time, Pallas kernels for 52%

profile of v4, /device:TPU:0, one launch (start us, length us, event | category | flops | bytes accessed | tf_op | source)
XLA Modules:
  0.0 187.3 jit_solution(2122484389457108675)
XLA Ops:
  0.0 3.0 %collective-permute-start = (bf16[128,2048]{1,0:T(8,128)(2,1)}, bf16[128,2048]{1,0:T(8,128)(2,1)S(1)}, u32[]{:S(2)}, u32[]{:S(2)}) collective-permute-start(bf16[128,2048]{1,0:T(8,128)(2,1)} %refs_0_.5), channel_id=1, source_target_pairs={{0,1},{1,2},{2,3},{3,0},{4,5},{5,6},{6,7},{7,4},{8,9},{9,10},{10,1... | collective-permute-start | bytes 1572872 | tf_op jit(solution)/shard_map/ppermute | solution.py:282
  3.0 1.1 copy-done.2
  4.1 10.5 %first_dots.5 = (bf16[2,64,3584]{2,1,0:T(8,128)(2,1)S(1)}, bf16[2,16,3584]{2,1,0:T(8,128)(2,1)S(1)}, bf16[2,16,3584]{2,1,0:T(8,128)(2,1)S(1)}, bf16[2,16,3584]{2,1,0:T(8,128)(2,1)S(1)}, bf16[2,16,3584]{2,1,0:T(8,128)(2,1)S(1)}) custom-call(bf16[128,2048]{1,0:T(8,128)(2,1)S(1)} %copy-done.2, bf16[2048,7168]{1,0:T(8,128)(2,1)} %refs_1_.3, ...), custom_call_target="tpu_custom_call" | custom-call | flops 37580963840 | bytes 293601280 | tf_op jit(solution)/shard_map/first_dots/pallas_call | solution.py:89
  14.7 0.5 collective-permute-start.3
  15.3 0.4 collective-permute-start.5
  15.7 0.5 collective-permute-done.2.refs_1_
  16.2 0.3 collective-permute-done.3.refs_2_
  16.5 0.3 collective-permute-done.4.refs_3_
  16.8 0.3 collective-permute-done.5.refs_4_
  17.2 0.6 fold.5
  17.7 1.6 collective-permute-start.14
  19.3 1.6 collective-permute-start.1
  20.9 12.3 %first_dots.6 = (bf16[2,128,3584]{2,1,0:T(8,128)(2,1)S(1)}, bf16[2,16,3584]{2,1,0:T(8,128)(2,1)S(1)}, bf16[2,16,3584]{2,1,0:T(8,128)(2,1)S(1)}, bf16[2,16,3584]{...) custom-call(bf16[128,2048]{1,0:T(8,128)(2,1)S(1)} %copy-done.3, ...), custom_call_target="tpu_custom_call" | custom-call | flops 75161927680 | bytes 293601280 | tf_op jit(solution)/shard_map/first_dots/pallas_call | solution.py:89
  33.2 0.5 collective-permute-start.10
  33.8 0.4 collective-permute-start.12
  34.2 0.5 collective-permute-done.6.refs_1_
  35.9 0.3 activate.5.refs_9_.refs_0_
  36.3 0.6 collective-permute-start.24
  37.2 1.0 fold.6
  38.2 1.3 collective-permute-start.26
  39.5 1.6 collective-permute-start.23
  41.0 12.3 %first_dots.7 = (bf16[2,128,3584]{2,1,0:T(8,128)(2,1)S(1)}, bf16[2,16,3584]{2,1,0:T(8,128)(2,1)S(1)}, bf16[2,16,3584]{2,1,0:T(8,128)(2,1)S(1)}, bf16[2,16,3584]{...) custom-call(bf16[128,2048]{1,0:T(8,128)(2,1)S(1)} %collective-permut, ...), custom_call_target="tpu_custom_call" | custom-call | flops 75161927680 | bytes 293601280 | tf_op jit(solution)/shard_map/first_dots/pallas_call | solution.py:89
  53.4 0.5 collective-permute-start.16
  54.0 0.9 collective-permute-done.15.refs_1_
  55.9 0.5 collective-permute-done.18.refs_4_
  57.4 0.5 collective-permute-done.22.refs_8_
  57.9 1.0 fold.7
  58.9 0.9 collective-permute-start.25
  59.8 4.6 %collective-permute-done.26.refs_5_.refs_1_ = bf16[2,64,3584]{2,1,0:T(8,128)(2,1)S(1)} collective-permute-done((bf16[2,64,3584]{2,1,0:T(8,128)(2,1)S(1)}, bf16[2,64,3584]{2,1,0:T(8,128)(2,1)S(1)}, u32[]{:S(2)}, u32[]{:S(2)}) %collective-permute-start.26) | collective-permute-done | bytes 917536 | tf_op jit(solution)/shard_map/ppermute | solution.py:285
  64.4 12.2 %first_dots.8 = (bf16[2,128,3584]{2,1,0:T(8,128)(2,1)S(1)}, bf16[2,16,3584]{2,1,0:T(8,128)(2,1)S(1)}, bf16[2,16,3584]{2,1,0:T(8,128)(2,1)S(1)}, bf16[2,16,3584]{...) custom-call(bf16[128,2048]{1,0:T(8,128)(2,1)S(1)} %collective-permut, ...), custom_call_target="tpu_custom_call" | custom-call | flops 75161927680 | bytes 293601280 | tf_op jit(solution)/shard_map/first_dots/pallas_call | solution.py:89
  76.7 0.5 collective-permute-start.30
  77.2 0.4 collective-permute-start.32
  77.7 0.5 collective-permute-done.29.refs_1_
  79.3 0.6 activate.6.refs_9_.refs_0_
  79.9 0.6 collective-permute-start.42
  80.6 1.0 fold.8
  81.6 1.5 collective-permute-start.40
  83.1 0.8 collective-permute-done.25.refs_4_.refs_1_
  84.0 10.4 %first_dots.9 = (bf16[2,64,3584]{2,1,0:T(8,128)(2,1)S(1)}, bf16[2,64,3584]{2,1,0:T(8,128)(2,1)S(1)}) custom-call(bf16[128,2048]{1,0:T(8,128)(2,1)S(1)} %collective-permute-done.23.refs_1_.refs_0_, bf16[2048,7168]{1,0:T(8,128)(2,1)} %refs_1_.3, bf16[2048,7168]{1,0:T(8,128)(2,1)} %refs_2_.9, bf16[2,64,3584]{2,1,0:T(8,128)(2,1)S(1)} %get-tuple-element.99.refs_3_, ...), custom_call_target="tpu_custom_call" | custom-call | flops 37580963840 | bytes 293601280 | tf_op jit(solution)/shard_map/first_dots/pallas_call | solution.py:89
  94.5 0.5 collective-permute-start.41
  95.0 0.6 activate.7.refs_5_.refs_0_
  95.8 0.5 collective-permute-start.38
  96.3 1.3 collective-permute-done.41.refs_1_
  97.7 0.5 collective-permute-done.43.refs_3_
  98.3 6.9 %last_dot.5 = (f32[128,2048]{1,0:T(8,128)S(1)}, f32[128,2048]{1,0:T(8,128)S(1)}) custom-call(bf16[64,3584]{1,0:T(8,128)(2,1)S(1)} %activate.6.refs_9_.refs_0_, bf16[64,3584]{1,0:T(8,128)(2,1)S(1)} %collective-permute-done.41.refs_1_, bf16[64,3584]{1,0:T(8,128)(2,1)S(1)} %collective-permute-done.42.refs_2_, ...), custom_call_target="tpu_custom_call" | custom-call | tf_op jit(solution)/shard_map/last_dot/pallas_call | solution.py:208
  105.2 8.3 %collective-permute-done.40.refs_1_ = bf16[2,64,3584]{2,1,0:T(8,128)(2,1)S(1)} collective-permute-done((bf16[2,64,3584]{2,1,0:T(8,128)(2,1)S(1)}, bf16[2,64,3584]{2,1,0:T(8,128)(2,1)S(1)}, u32[]{:S(2)}, u32[]{:S(2)}) %collective-permute-start.40) | collective-permute-done | bytes 917536 | tf_op jit(solution)/shard_map/ppermute | solution.py:285
  113.5 0.6 activate.8.refs_2_.refs_0_
  114.1 0.5 fold.9
  114.6 8.2 %collective-permute-done.38.refs_2_ = bf16[64,3584]{1,0:T(8,128)(2,1)S(1)} collective-permute-done((bf16[64,3584]{1,0:T(8,128)(2,1)S(1)}, bf16[64,3584]{1,0:T(8,128)(2,1)S(1)}, u32[]{:S(2)}, u32[]{:S(2)}) %collective-permute-start.38) | collective-permute-done | bytes 458784 | tf_op jit(solution)/shard_map/ppermute | solution.py:285
  122.8 0.5 collective-permute-start.47
  123.3 1.3 collective-permute-done.44.refs_3_
  124.6 7.0 %last_dot.6 = (bf16[128,2048]{1,0:T(8,128)(2,1)S(1)}, f32[128,2048]{1,0:T(8,128)S(1)}) custom-call(bf16[64,3584]{1,0:T(8,128)(2,1)S(1)} %activate.7.refs_5_.refs_0_, bf16[64,3584]{1,0:T(8,128)(2,1)S(1)} %collective-permute-done.37.refs_1_, bf16[64,3584]{1,0:T(8,128)(2,1)S(1)} %collective-permute-done.38.refs_2_, ...), custom_call_target="tpu_custom_call" | custom-call | flops 37580963840 | bytes 146800640 | tf_op jit(solution)/shard_map/last_dot/pallas_call | solution.py:208
  131.6 1.6 collective-permute-start.45
  133.2 0.5 collective-permute-start.49
  133.7 6.1 %last_dot.7.refs_2_ = bf16[128,2048]{1,0:T(8,128)(2,1)S(1)} custom-call(bf16[32,3584]{1,0:T(8,128)(2,1)S(1)} %copy-done.1, bf16[32,3584]{1,0:T(8,128)(2,1)S(1)} %collective-permute-done.27.refs_6_.refs_1_, bf16[32,3584]{1,0:T(8,128)(2,1)S(1)} %collective-permute-done.24.refs_2_.refs_7_, bf16[32,3584]{1,0:T(8,128)(2,1)S(1)} %collective-permute-done.28.refs_8_.refs_3_, ...), custom_call_target="tpu_custom_call" | custom-call | tf_op jit(solution)/shard_map/last_dot/pallas_call | solution.py:208
  140.1 6.0 %collective-permute-done.49.refs_1_ = bf16[2,32,3584]{2,1,0:T(8,128)(2,1)S(1)} collective-permute-done((bf16[2,32,3584]{2,1,0:T(8,128)(2,1)S(1)}, bf16[2,32,3584]{2,1,0:T(8,128)(2,1)S(1)}, u32[]{:S(2)}, u32[]{:S(2)}) %collective-permute-start.49) | collective-permute-done | bytes 458784 | tf_op jit(solution)/shard_map/ppermute | solution.py:285
  146.1 0.4 activate.9.refs_6_.refs_0_
  146.5 0.6 collective-permute-start.52
  147.4 6.9 %last_dot.8 = (bf16[128,2048]{1,0:T(8,128)(2,1)S(1)}, f32[128,2048]{1,0:T(8,128)S(1)}) custom-call(bf16[64,3584]{1,0:T(8,128)(2,1)S(1)} %activate.8.refs_2_.refs_0_, bf16[64,3584]{1,0:T(8,128)(2,1)S(1)} %collective-permute-done.46.refs_1_, bf16[64,3584]{1,0:T(8,128)(2,1)S(1)} %collective-permute-done.47.refs_2_, ...), custom_call_target="tpu_custom_call" | custom-call | flops 37580963840 | bytes 146800640 | tf_op jit(solution)/shard_map/last_dot/pallas_call | solution.py:208
  154.9 1.0 collective-permute-start.50
  156.2 6.1 %last_dot.9.refs_1_.refs_2_ = bf16[128,2048]{1,0:T(8,128)(2,1)S(1)} custom-call(bf16[32,3584]{1,0:T(8,128)(2,1)S(1)} %activate.9.refs_6_.refs_0_, bf16[32,3584]{1,0:T(8,128)(2,1)S(1)} %collective-permute-done.51.refs_1_, bf16[32,3584]{1,0:T(8,128)(2,1)S(1)} %collective-permute-done.52.refs_2_, bf16[32,3584]{1,0:T(8,128)(2,1)S(1)} %collective-permute-done.53.refs_3_, ...), custom_call_target="tpu_custom_call" | custom-call | flops 18790481920 | bytes 146800640 | tf_op jit(solution)/shard_map/last_dot/pallas_call | solution.py:208
  162.3 8.5 %collective-permute-done.50.refs_0_ = bf16[128,2048]{1,0:T(8,128)(2,1)S(1)} collective-permute-done((bf16[128,2048]{1,0:T(8,128)(2,1)S(1)}, bf16[128,2048]{1,0:T(8,128)(2,1)S(1)}, u32[]{:S(2)}, u32[]{:S(2)}) %collective-permute-start.50) | collective-permute-done | bytes 524320 | tf_op jit(solution)/shard_map/ppermute | solution.py:282
  171.2 15.1 %collective-permute-done.54.refs_1_ = bf16[128,2048]{1,0:T(8,128)(2,1)S(1)} collective-permute-done((bf16[128,2048]{1,0:T(8,128)(2,1)S(1)}, bf16[128,2048]{1,0:T(8,128)(2,1)S(1)}, u32[]{:S(2)}, u32[]{:S(2)}) %collective-permute-start.54) | collective-permute-done | bytes 524320 | tf_op jit(solution)/shard_map/ppermute | solution.py:282
  186.2 1.0 add.5
  (80 shorter events, 7.5 us)
Async XLA Ops:
  0.0 19.3 %collective-permute-start = (bf16[128,2048]{1,0:T(8,128)(2,1)}, bf16[128,2048]{1,0:T(8,128)(2,1)S(1)}, u32[]{:S(2)}, u32[]{:S(2)}) collective-permute-start(bf16[128,2048]{1,0:T(8,128)(2,1)} %refs_0_.5), channel_id=1, source_target_pairs={{0,1},{1,2},{2,3},{3,0},{4,5},{5,6},{6,7},{7,4},{8,9},{9,10},{10,1... | collective-permute-start | bytes 1572872 | tf_op jit(solution)/shard_map/ppermute | solution.py:282
  3.0 1.1 copy-start.2
  4.1 16.8 %copy-start.3 = (bf16[128,2048]{1,0:T(8,128)(2,1)S(1)}, bf16[128,2048]{1,0:T(8,128)(2,1)}, u32[]{:S(2)}) copy-start(bf16[128,2048]{1,0:T(8,128)(2,1)} %refs_0_.5) | copy-start | bytes 1572868
  14.6 1.6 collective-permute-start.2
  14.7 1.8 collective-permute-start.3
  15.2 1.6 collective-permute-start.4
  15.3 1.9 %collective-permute-start.5 = (bf16[2,16,3584]{2,1,0:T(8,128)(2,1)S(1)}, bf16[2,16,3584]{2,1,0:T(8,128)(2,1)S(1)}, u32[]{:S(2)}, u32[]{:S(2)}) collective-permute-start(bf16[2,16,3584]{2,1,0:T(8,128)(2,1)S(1)} %get-tuple-element.64), channel_id=1, source_target_pairs={{0,4},{4,0},{8,12},{12,8},{1,5},{5,1},{9,13},{13,9},{2,6},{6,2},{1... | collective-permute-start | bytes 688136 | tf_op jit(solution)/shard_map/ppermute | solution.py:285
  17.7 16.1 %collective-permute-start.14 = (bf16[2,32,3584]{2,1,0:T(8,128)(2,1)S(1)}, bf16[2,32,3584]{2,1,0:T(8,128)(2,1)S(1)}, u32[]{:S(2)}, u32[]{:S(2)}) collective-permute-start(bf16[2,32,3584]{2,1,0:T(8,128)(2,1)S(1)} %get-tuple-element.65.refs_4_), channel_id=1, source_target_pairs={{0,8},{4,12},{8,0},{12,4},{1,9},{5,13},{9,1},{13,5},{2,10},{6,14},... | collective-permute-start | bytes 1376264 | tf_op jit(solution)/shard_map/ppermute | solution.py:285
  19.3 20.2 %collective-permute-start.1 = (bf16[128,2048]{1,0:T(8,128)(2,1)S(1)}, bf16[128,2048]{1,0:T(8,128)(2,1)S(1)}, u32[]{:S(2)}, u32[]{:S(2)}) collective-permute-start(bf16[128,2048]{1,0:T(8,128)(2,1)S(1)} %collective-permute-done.refs_1_.refs_0_), channel_id=1, source_target_pairs={{0,1},{1,2},{2,3},{3,0},{4,5},{5,6},{6,7},{7,4},{8,9},{9,10},{10,1... | collective-permute-start | bytes 1572872 | tf_op jit(solution)/shard_map/ppermute | solution.py:282
  33.1 1.6 collective-permute-start.6
  33.2 1.8 collective-permute-start.10
  33.7 1.6 collective-permute-start.11
  33.8 1.9 %collective-permute-start.12 = (bf16[2,16,3584]{2,1,0:T(8,128)(2,1)S(1)}, bf16[2,16,3584]{2,1,0:T(8,128)(2,1)S(1)}, u32[]{:S(2)}, u32[]{:S(2)}) collective-permute-start(bf16[2,16,3584]{2,1,0:T(8,128)(2,1)S(1)} %get-tuple-element.73), channel_id=1, source_target_pairs={{0,4},{4,0},{8,12},{12,8},{1,5},{5,1},{9,13},{13,9},{2,6},{6,2},{1... | collective-permute-start | bytes 688136 | tf_op jit(solution)/shard_map/ppermute | solution.py:285
  34.7 1.5 collective-permute-start.13
  35.0 1.8 collective-permute-start.7
  35.4 1.5 collective-permute-start.8
  35.7 1.5 collective-permute-start.9
  36.2 20.5 %copy-start = (bf16[32,3584]{1,0:T(8,128)(2,1)}, bf16[32,3584]{1,0:T(8,128)(2,1)S(1)}, u32[]{:S(2)}) copy-start(bf16[32,3584]{1,0:T(8,128)(2,1)S(1)} %activate.5.refs_9_.refs_0_) | copy-start | bytes 688132
  36.3 17.7 %collective-permute-start.24 = (bf16[32,3584]{1,0:T(8,128)(2,1)S(1)}, bf16[32,3584]{1,0:T(8,128)(2,1)S(1)}, u32[]{:S(2)}, u32[]{:S(2)}) collective-permute-start(bf16[32,3584]{1,0:T(8,128)(2,1)S(1)} %activate.5.refs_9_.refs_0_), channel_id=1, source_target_pairs={{0,8},{4,12},{8,0},{12,4},{1,9},{5,13},{9,1},{13,5},{2,10},{6,14},... | collective-permute-start | bytes 688136 | tf_op jit(solution)/shard_map/ppermute | solution.py:285
  38.2 26.2 %collective-permute-start.26 = (bf16[2,64,3584]{2,1,0:T(8,128)(2,1)S(1)}, bf16[2,64,3584]{2,1,0:T(8,128)(2,1)S(1)}, u32[]{:S(2)}, u32[]{:S(2)}) collective-permute-start(bf16[2,64,3584]{2,1,0:T(8,128)(2,1)S(1)} %get-tuple-element.76.refs_4_), channel_id=1, source_target_pairs={{0,8},{4,12},{8,0},{12,4},{1,9},{5,13},{9,1},{13,5},{2,10},{6,14},... | collective-permute-start | bytes 2752520 | tf_op jit(solution)/shard_map/ppermute | solution.py:285
  39.5 15.9 %collective-permute-start.23 = (bf16[128,2048]{1,0:T(8,128)(2,1)S(1)}, bf16[128,2048]{1,0:T(8,128)(2,1)S(1)}, u32[]{:S(2)}, u32[]{:S(2)}) collective-permute-start(bf16[128,2048]{1,0:T(8,128)(2,1)S(1)} %collective-permute-done.1.refs_1_.refs_0_), channel_id=1, source_target_pairs={{0,1},{1,2},{2,3},{3,0},{4,5},{5,6},{6,7},{7,4},{8,9},{9,10},{10,1... | collective-permute-start | bytes 1572872 | tf_op jit(solution)/shard_map/ppermute | solution.py:282
  53.3 1.6 collective-permute-start.15
  53.4 1.8 collective-permute-start.16
  53.9 1.8 collective-permute-start.17
  54.9 1.5 collective-permute-start.18
  55.2 1.5 collective-permute-start.19
  55.4 1.6 collective-permute-start.20
  55.7 1.6 collective-permute-start.21
  56.4 1.5 collective-permute-start.22
  56.7 3.1 %collective-permute-start.27 = (bf16[32,3584]{1,0:T(8,128)(2,1)S(1)}, bf16[32,3584]{1,0:T(8,128)(2,1)S(1)}, u32[]{:S(2)}, u32[]{:S(2)}) collective-permute-start(bf16[32,3584]{1,0:T(8,128)(2,1)S(1)} %activate.5.refs_9_.refs_0_), channel_id=1, source_target_pairs={{0,4},{4,0},{8,12},{12,8},{1,5},{5,1},{9,13},{13,9},{2,6},{6,2},{1... | collective-permute-start | bytes 688136 | tf_op jit(solution)/shard_map/ppermute | solution.py:285
  57.0 7.4 %collective-permute-start.28 = (bf16[32,3584]{1,0:T(8,128)(2,1)S(1)}, bf16[32,3584]{1,0:T(8,128)(2,1)S(1)}, u32[]{:S(2)}, u32[]{:S(2)}) collective-permute-start(bf16[32,3584]{1,0:T(8,128)(2,1)S(1)} %collective-permute-done.24.refs_2_.refs_7_), channel_id=1, source_target_pairs={{0,4},{4,0},{8,12},{12,8},{1,5},{5,1},{9,13},{13,9},{2,6},{6,2},{1... | collective-permute-start | bytes 688136 | tf_op jit(solution)/shard_map/ppermute | solution.py:285
  58.9 25.1 %collective-permute-start.25 = (bf16[2,64,3584]{2,1,0:T(8,128)(2,1)S(1)}, bf16[2,64,3584]{2,1,0:T(8,128)(2,1)S(1)}, u32[]{:S(2)}, u32[]{:S(2)}) collective-permute-start(bf16[2,64,3584]{2,1,0:T(8,128)(2,1)S(1)} %get-tuple-element.87.refs_4_), channel_id=1, source_target_pairs={{0,8},{4,12},{8,0},{12,4},{1,9},{5,13},{9,1},{13,5},{2,10},{6,14},... | collective-permute-start | bytes 2752520 | tf_op jit(solution)/shard_map/ppermute | solution.py:285
  76.6 1.6 collective-permute-start.29
  76.7 1.8 collective-permute-start.30
  77.2 1.6 collective-permute-start.31
  77.2 1.9 %collective-permute-start.32 = (bf16[2,16,3584]{2,1,0:T(8,128)(2,1)S(1)}, bf16[2,16,3584]{2,1,0:T(8,128)(2,1)S(1)}, u32[]{:S(2)}, u32[]{:S(2)}) collective-permute-start(bf16[2,16,3584]{2,1,0:T(8,128)(2,1)S(1)} %get-tuple-element.93), channel_id=1, source_target_pairs={{0,4},{4,0},{8,12},{12,8},{1,5},{5,1},{9,13},{13,9},{2,6},{6,2},{1... | collective-permute-start | bytes 688136 | tf_op jit(solution)/shard_map/ppermute | solution.py:285
  78.1 1.8 collective-permute-start.33
  78.5 2.1 %collective-permute-start.34 = (bf16[2,16,3584]{2,1,0:T(8,128)(2,1)S(1)}, bf16[2,16,3584]{2,1,0:T(8,128)(2,1)S(1)}, u32[]{:S(2)}, u32[]{:S(2)}) collective-permute-start(bf16[2,16,3584]{2,1,0:T(8,128)(2,1)S(1)} %get-tuple-element.95), channel_id=1, source_target_pairs={{0,4},{4,0},{8,12},{12,8},{1,5},{5,1},{9,13},{13,9},{2,6},{6,2},{1... | collective-permute-start | bytes 688136 | tf_op jit(solution)/shard_map/ppermute | solution.py:285
  78.8 1.7 collective-permute-start.35
  79.1 1.5 collective-permute-start.36
  79.9 15.7 %collective-permute-start.42 = (bf16[64,3584]{1,0:T(8,128)(2,1)S(1)}, bf16[64,3584]{1,0:T(8,128)(2,1)S(1)}, u32[]{:S(2)}, u32[]{:S(2)}) collective-permute-start(bf16[64,3584]{1,0:T(8,128)(2,1)S(1)} %activate.6.refs_9_.refs_0_), channel_id=1, source_target_pairs={{0,8},{4,12},{8,0},{12,4},{1,9},{5,13},{9,1},{13,5},{2,10},{6,14},... | collective-permute-start | bytes 1376264 | tf_op jit(solution)/shard_map/ppermute | solution.py:285
  81.6 31.8 %collective-permute-start.40 = (bf16[2,64,3584]{2,1,0:T(8,128)(2,1)S(1)}, bf16[2,64,3584]{2,1,0:T(8,128)(2,1)S(1)}, u32[]{:S(2)}, u32[]{:S(2)}) collective-permute-start(bf16[2,64,3584]{2,1,0:T(8,128)(2,1)S(1)} %get-tuple-element.99.refs_3_), channel_id=1, source_target_pairs={{0,8},{4,12},{8,0},{12,4},{1,9},{5,13},{9,1},{13,5},{2,10},{6,14},... | collective-permute-start | bytes 2752520 | tf_op jit(solution)/shard_map/ppermute | solution.py:285
  94.4 19.7 %collective-permute-start.39 = (bf16[2,64,3584]{2,1,0:T(8,128)(2,1)S(1)}, bf16[2,64,3584]{2,1,0:T(8,128)(2,1)S(1)}, u32[]{:S(2)}, u32[]{:S(2)}) collective-permute-start(bf16[2,64,3584]{2,1,0:T(8,128)(2,1)S(1)} %get-tuple-element.100.refs_2_), channel_id=1, source_target_pairs={{0,4},{4,0},{8,12},{12,8},{1,5},{5,1},{9,13},{13,9},{2,6},{6,2},{1... | collective-permute-start | bytes 2752520 | tf_op jit(solution)/shard_map/ppermute | solution.py:285
  94.5 3.1 %collective-permute-start.41 = (bf16[64,3584]{1,0:T(8,128)(2,1)S(1)}, bf16[64,3584]{1,0:T(8,128)(2,1)S(1)}, u32[]{:S(2)}, u32[]{:S(2)}) collective-permute-start(bf16[64,3584]{1,0:T(8,128)(2,1)S(1)} %activate.6.refs_9_.refs_0_), channel_id=1, source_target_pairs={{0,4},{4,0},{8,12},{12,8},{1,5},{5,1},{9,13},{13,9},{2,6},{6,2},{1... | collective-permute-start | bytes 1376264 | tf_op jit(solution)/shard_map/ppermute | solution.py:285
  95.6 2.6 %collective-permute-start.43 = (bf16[64,3584]{1,0:T(8,128)(2,1)S(1)}, bf16[64,3584]{1,0:T(8,128)(2,1)S(1)}, u32[]{:S(2)}, u32[]{:S(2)}) collective-permute-start(bf16[64,3584]{1,0:T(8,128)(2,1)S(1)} %collective-permute-done.42.refs_2_), channel_id=1, source_target_pairs={{0,4},{4,0},{8,12},{12,8},{1,5},{5,1},{9,13},{13,9},{2,6},{6,2},{1... | collective-permute-start | bytes 1376264 | tf_op jit(solution)/shard_map/ppermute | solution.py:285
  95.8 27.0 %collective-permute-start.38 = (bf16[64,3584]{1,0:T(8,128)(2,1)S(1)}, bf16[64,3584]{1,0:T(8,128)(2,1)S(1)}, u32[]{:S(2)}, u32[]{:S(2)}) collective-permute-start(bf16[64,3584]{1,0:T(8,128)(2,1)S(1)} %activate.7.refs_5_.refs_0_), channel_id=1, source_target_pairs={{0,8},{4,12},{8,0},{12,4},{1,9},{5,13},{9,1},{13,5},{2,10},{6,14},... | collective-permute-start | bytes 1376264 | tf_op jit(solution)/shard_map/ppermute | solution.py:285
  97.6 25.7 %collective-permute-start.37 = (bf16[64,3584]{1,0:T(8,128)(2,1)S(1)}, bf16[64,3584]{1,0:T(8,128)(2,1)S(1)}, u32[]{:S(2)}, u32[]{:S(2)}) collective-permute-start(bf16[64,3584]{1,0:T(8,128)(2,1)S(1)} %activate.7.refs_5_.refs_0_), channel_id=1, source_target_pairs={{0,4},{4,0},{8,12},{12,8},{1,5},{5,1},{9,13},{13,9},{2,6},{6,2},{1... | collective-permute-start | bytes 1376264 | tf_op jit(solution)/shard_map/ppermute | solution.py:285
  122.8 1.8 collective-permute-start.44
  122.8 17.0 %collective-permute-start.47 = (bf16[64,3584]{1,0:T(8,128)(2,1)S(1)}, bf16[64,3584]{1,0:T(8,128)(2,1)S(1)}, u32[]{:S(2)}, u32[]{:S(2)}) collective-permute-start(bf16[64,3584]{1,0:T(8,128)(2,1)S(1)} %activate.8.refs_2_.refs_0_), channel_id=1, source_target_pairs={{0,8},{4,12},{8,0},{12,4},{1,9},{5,13},{9,1},{13,5},{2,10},{6,14},... | collective-permute-start | bytes 1376264 | tf_op jit(solution)/shard_map/ppermute | solution.py:285
  124.6 9.1 %copy-start.1 = (bf16[32,3584]{1,0:T(8,128)(2,1)S(1)}, bf16[32,3584]{1,0:T(8,128)(2,1)}, u32[]{:S(2)}) copy-start(bf16[32,3584]{1,0:T(8,128)(2,1)} %copy-done) | copy-start | bytes 688132
  131.6 15.8 %collective-permute-start.45 = (bf16[128,2048]{1,0:T(8,128)(2,1)S(1)}, bf16[128,2048]{1,0:T(8,128)(2,1)S(1)}, u32[]{:S(2)}, u32[]{:S(2)}) collective-permute-start(bf16[128,2048]{1,0:T(8,128)(2,1)S(1)} %get-tuple-element.108.refs_6_), channel_id=1, source_target_pairs={{0,1},{1,2},{2,3},{3,0},{4,5},{5,6},{6,7},{7,4},{8,9},{9,10},{10,1... | collective-permute-start | bytes 1572872 | tf_op jit(solution)/shard_map/ppermute | solution.py:282
  133.2 13.9 %collective-permute-start.46 = (bf16[64,3584]{1,0:T(8,128)(2,1)S(1)}, bf16[64,3584]{1,0:T(8,128)(2,1)S(1)}, u32[]{:S(2)}, u32[]{:S(2)}) collective-permute-start(bf16[64,3584]{1,0:T(8,128)(2,1)S(1)} %activate.8.refs_2_.refs_0_), channel_id=1, source_target_pairs={{0,4},{4,0},{8,12},{12,8},{1,5},{5,1},{9,13},{13,9},{2,6},{6,2},{1... | collective-permute-start | bytes 1376264 | tf_op jit(solution)/shard_map/ppermute | solution.py:285
  133.2 12.9 %collective-permute-start.49 = (bf16[2,32,3584]{2,1,0:T(8,128)(2,1)S(1)}, bf16[2,32,3584]{2,1,0:T(8,128)(2,1)S(1)}, u32[]{:S(2)}, u32[]{:S(2)}) collective-permute-start(bf16[2,32,3584]{2,1,0:T(8,128)(2,1)S(1)} %get-tuple-element.105.refs_6_), channel_id=1, source_target_pairs={{0,8},{4,12},{8,0},{12,4},{1,9},{5,13},{9,1},{13,5},{2,10},{6,14},... | collective-permute-start | bytes 1376264 | tf_op jit(solution)/shard_map/ppermute | solution.py:285
  139.8 7.3 %collective-permute-start.48 = (bf16[64,3584]{1,0:T(8,128)(2,1)S(1)}, bf16[64,3584]{1,0:T(8,128)(2,1)S(1)}, u32[]{:S(2)}, u32[]{:S(2)}) collective-permute-start(bf16[64,3584]{1,0:T(8,128)(2,1)S(1)} %collective-permute-done.47.refs_2_), channel_id=1, source_target_pairs={{0,4},{4,0},{8,12},{12,8},{1,5},{5,1},{9,13},{13,9},{2,6},{6,2},{1... | collective-permute-start | bytes 1376264 | tf_op jit(solution)/shard_map/ppermute | solution.py:285
  146.5 8.1 %collective-permute-start.52 = (bf16[32,3584]{1,0:T(8,128)(2,1)S(1)}, bf16[32,3584]{1,0:T(8,128)(2,1)S(1)}, u32[]{:S(2)}, u32[]{:S(2)}) collective-permute-start(bf16[32,3584]{1,0:T(8,128)(2,1)S(1)} %activate.9.refs_6_.refs_0_), channel_id=1, source_target_pairs={{0,8},{4,12},{8,0},{12,4},{1,9},{5,13},{9,1},{13,5},{2,10},{6,14},... | collective-permute-start | bytes 688136 | tf_op jit(solution)/shard_map/ppermute | solution.py:285
  147.1 8.8 %collective-permute-start.51 = (bf16[32,3584]{1,0:T(8,128)(2,1)S(1)}, bf16[32,3584]{1,0:T(8,128)(2,1)S(1)}, u32[]{:S(2)}, u32[]{:S(2)}) collective-permute-start(bf16[32,3584]{1,0:T(8,128)(2,1)S(1)} %activate.9.refs_6_.refs_0_), channel_id=1, source_target_pairs={{0,4},{4,0},{8,12},{12,8},{1,5},{5,1},{9,13},{13,9},{2,6},{6,2},{1... | collective-permute-start | bytes 688136 | tf_op jit(solution)/shard_map/ppermute | solution.py:285
  154.6 1.6 collective-permute-start.53
  154.9 15.9 %collective-permute-start.50 = (bf16[128,2048]{1,0:T(8,128)(2,1)S(1)}, bf16[128,2048]{1,0:T(8,128)(2,1)S(1)}, u32[]{:S(2)}, u32[]{:S(2)}) collective-permute-start(bf16[128,2048]{1,0:T(8,128)(2,1)S(1)} %add.3.refs_6_), channel_id=1, source_target_pairs={{0,1},{1,2},{2,3},{3,0},{4,5},{5,6},{6,7},{7,4},{8,9},{9,10},{10,1... | collective-permute-start | bytes 1572872 | tf_op jit(solution)/shard_map/ppermute | solution.py:282
  156.2 30.1 %copy-start.4 = (bf16[128,2048]{1,0:T(8,128)(2,1)S(1)}, bf16[128,2048]{1,0:T(8,128)(2,1)}, u32[]{:S(2)}) copy-start(bf16[128,2048]{1,0:T(8,128)(2,1)} %refs_0_.5) | copy-start | bytes 1572868
  171.1 15.1 %collective-permute-start.54 = (bf16[128,2048]{1,0:T(8,128)(2,1)S(1)}, bf16[128,2048]{1,0:T(8,128)(2,1)S(1)}, u32[]{:S(2)}, u32[]{:S(2)}) collective-permute-start(bf16[128,2048]{1,0:T(8,128)(2,1)S(1)} %add.4.refs_3_), channel_id=1, source_target_pairs={{0,1},{1,2},{2,3},{3,0},{4,5},{5,6},{6,7},{7,4},{8,9},{9,10},{10,1... | collective-permute-start | bytes 1572872 | tf_op jit(solution)/shard_map/ppermute | solution.py:282

commit v5 on v4

--- a/solution.py
+++ b/solution.py
@@ -130,22 +130,24 @@
     )(keep, *got, *after)
 
 
-def activate(kept, got, after):
+def activate(kept, got, parts, after):
     _, m, width = kept.shape
     step = block_of(width, 1792)
 
     def kernel(*refs):
-        a, b, out = refs[0], refs[1], refs[-1]
+        a, b = refs[:2]
         g = a[0].astype(F32) + b[0].astype(F32)
         u = a[1].astype(F32) + b[1].astype(F32)
-        out[...] = (g / (1.0 + jnp.exp(-g)) * u).astype(BF16)
+        value = (g / (1.0 + jnp.exp(-g)) * u).astype(BF16)
+        for i, out in enumerate(refs[-parts:]):
+            out[...] = value[i * m // parts : (i + 1) * m // parts]
 
     return pl.pallas_call(
         kernel,
         grid=(width // step,),
         in_specs=[pl.BlockSpec((2, m, step), lambda c: (0, 0, c))] * 2 + [ANY] * len(after),
-        out_specs=pl.BlockSpec((m, step), lambda c: (0, c)),
-        out_shape=jax.ShapeDtypeStruct((m, width), BF16),
+        out_specs=[pl.BlockSpec((m // parts, step), lambda c: (0, c))] * parts,
+        out_shape=[jax.ShapeDtypeStruct((m // parts, width), BF16)] * parts,
         compiler_params=params(40),
         cost_estimate=cost(1, 1),
         name="activate",
@@ -154,7 +156,9 @@
 
 def last_dot(pieces, weight, at, carries, finals, weigh, after):
     n, g = len(pieces), len(carries)
-    m1, depth = pieces[0].shape
+    count = len(pieces[0])
+    share, depth = pieces[0][0].shape
+    m1 = count * share
     width = weight.shape[1]
     r, m = m1 // g, n * m1
     step = block_of(depth, 512)
@@ -163,7 +167,7 @@
     given = [c for c in carries if c is not None]
 
     def kernel(*refs):
-        h, w = refs[:n], refs[n]
+        h, w = refs[: n * count], refs[n * count]
         outs = refs[-5 - g : -5]
         total, rows, buf, h_sem, w_sem = refs[-5:]
         c = pl.program_id(0)
@@ -176,7 +180,10 @@
         def _():
             for block in range(slots):
                 load(block).start()
-            copies = [pltpu.make_async_copy(h[j], rows.at[j], h_sem.at[j]) for j in range(n)]
+            copies = [
+                pltpu.make_async_copy(h[i], rows.at[i // count, pl.ds(i % count * share, share)], h_sem.at[i])
+                for i in range(n * count)
+            ]
             for copy in copies:
                 copy.start()
             total[...] = jnp.zeros_like(total)
@@ -196,7 +203,7 @@
             me = lax.axis_index("pipe")
             for j in range(n):
                 here = pl.ds(pl.multiple_of((me ^ j) * r, r), r)
-                carry_at = n + 1
+                carry_at = n * count + 1
                 for i in range(g):
                     spot = (j * g + i) * r
                     value = total[spot : spot + r, :]
@@ -208,20 +215,20 @@
     return pl.pallas_call(
         kernel,
         grid=(steps,),
-        in_specs=[ANY] * n + [HBM] + [pl.BlockSpec((n * r, width), lambda c: (0, 0))] * len(given) + [ANY] * len(after),
+        in_specs=[ANY] * (n * count) + [HBM] + [pl.BlockSpec((n * r, width), lambda c: (0, 0))] * len(given) + [ANY] * len(after),
         out_specs=[pl.BlockSpec((n * r, width), lambda c: (0, 0))] * g,
         out_shape=[jax.ShapeDtypeStruct((n * r, width), BF16 if final else F32) for final in finals],
         scratch_shapes=[
             pltpu.VMEM((m, width), F32),
             pltpu.VMEM((n, m1, depth), BF16),
             pltpu.VMEM((slots, step, width), BF16),
-            pltpu.SemaphoreType.DMA((n,)),
+            pltpu.SemaphoreType.DMA((n * count,)),
             pltpu.SemaphoreType.DMA((slots,)),
         ],
         compiler_params=params(40),
         cost_estimate=cost(weigh * 2 * m * depth * width, weigh * 2 * depth * width),
         name="last_dot",
-    )(*pieces, weight, *given, *after)
+    )(*(piece for some in pieces for piece in some), weight, *given, *after)
 
 
 def join(after):
@@ -315,30 +322,29 @@
                 got = [swap(send, bit)]
             folded[k] = keep, got[0]
 
-        def act(k):
-            own = activate(*folded[k], last)
-            last[:] = [own]
+        def act(k, parts=1):
+            own = activate(*folded[k], parts, last)
+            last[:] = own[:1]
             pieces = {0: own}
             for bit in reversed(range(1, bits)):
                 for j in list(pieces):
-                    pieces[j | 1 << bit] = swap(pieces[j], bit)
-            pieces[1] = swap(own, 0)
+                    pieces[j | 1 << bit] = [swap(piece, bit) for piece in pieces[j]]
+            pieces[1] = [swap(piece, 0) for piece in own]
             hidden[k] = pieces
 
         def forward(k):
             pieces = hidden[k]
             for j in range(2, n_pipe, 2):
-                piece, _ = lax.optimization_barrier((pieces[j], last[0]))
-                pieces[j + 1] = swap(piece, 0)
+                pieces[j + 1] = [swap(lax.optimization_barrier((piece, last[0]))[0], 0) for piece in pieces[j]]
 
         def need_partial(k):
             last.append(folded[k][1])
 
         def need_gathered(k):
-            last.extend(hidden[k][j] for j in range(2, n_pipe, 2))
+            last.extend(piece for j in range(2, n_pipe, 2) for piece in hidden[k][j])
 
         def need_hidden(k):
-            last.extend(hidden[k][j] for j in range(1, n_pipe))
+            last.extend(piece for j in range(1, n_pipe) for piece in hidden[k][j])
 
         def down(k, weigh=1):
             rows, columns = rects[k]
@@ -374,9 +380,9 @@
             plan = [
                 (dot, 0), (sum_core, 0), (dot, 1), (act, 0), (sum_core, 1), (dot, 2), (need, 3),
                 (need_gathered, 0), (wait,), (forward, 0), (sum_core, 2), (need_partial, 1), (need_hidden, 0),
-                (dot, 3), (act, 1), (sum_core, 3), (need_partial, 2), (dot, 4), (act, 2), (forward, 1),
-                (fill, 1), (act, 3), (sum_core, 4), (forward, 2), (down, 2), (pass_on, 1), (fill, 0),
-                (forward, 3), (act, 4), (need_total, 1), (down, 3), (pass_on, 2), (forward, 4), (down, 4),
+                (dot, 3), (act, 1, 2), (sum_core, 3), (need_partial, 2), (act, 2), (dot, 4), (forward, 1),
+                (fill, 1), (act, 3), (forward, 2), (down, 2), (pass_on, 1), (fill, 0), (forward, 3),
+                (sum_core, 4), (need_total, 1), (down, 3), (pass_on, 2), (act, 4), (forward, 4), (down, 4),
                 (pass_on, 3),
             ]
         else:

time: 187 us -> 195 us (1.043)
  waiting for transfers between devices: 61.4 us -> 66.8 us
    ppermute x6, waiting for transfers between devices: 23.9 us -> 29.9 us  [hop(): return lax.ppermute(value, 'tensor', ring)]
    ppermute x49 -> x52, starting transfers between devices: 16.7 us -> 18.8 us  [swap(): lax.ppermute(value, 'pipe', [(i, i ^ 1 << bit) for i in range(n_pipe)])]
    ppermute x49 -> x52, waiting for transfers between devices: 37.6 us -> 36.8 us  [swap(): lax.ppermute(value, 'pipe', [(i, i ^ 1 << bit) for i in range(n_pipe)])]
  transfers between devices with their start and end apart: 55 -> 58, of which waited for: 33 -> 34; matrix products, arithmetic and copies ran while one was open for 0% -> 0% of each run, Pallas kernels for 52% -> 50%
where the time goes in v5:
time: 195 us
  Pallas kernels  99.8 us (51%)
  waiting for transfers between devices  66.8 us (34%)
  starting transfers between devices  26.7 us (14%)
    pallas_call x5, Pallas kernels, first_dots(): pl.pallas_call(kernel, grid=(steps,), in_specs=[HBM if i in fixed else AN...  57.7 us
    ppermute x52, waiting for transfers between devices, swap(): lax.ppermute(value, 'pipe', [(i, i ^ 1 << bit) for i in range(n_pipe)])  36.8 us
    pallas_call x5, Pallas kernels, last_dot(): pl.pallas_call(kernel, grid=(steps,), in_specs=[ANY] * (n * count) + [HBM...  33.9 us
    ppermute x6, waiting for transfers between devices, hop(): return lax.ppermute(value, 'tensor', ring)  29.9 us
    ppermute x52, starting transfers between devices, swap(): lax.ppermute(value, 'pipe', [(i, i ^ 1 << bit) for i in range(n_pipe)])  18.8 us
    ppermute x6, starting transfers between devices, hop(): return lax.ppermute(value, 'tensor', ring)  7.87 us
    pallas_call x5, Pallas kernels, fold(): pl.pallas_call(kernel, grid=(width // step,), in_specs=[pl.BlockSpec((k,...  4.12 us
  transfers between devices with their start and end apart: 58, of which 34 were waited for; matrix products, arithmetic and copies ran while one was open for 0% of the time, Pallas kernels for 50%

profile of v5, /device:TPU:0, one launch (start us, length us, event | category | flops | bytes accessed | tf_op | source)
XLA Modules:
  0.0 194.8 jit_solution(10665397317219195295)
XLA Ops:
  0.0 3.0 %collective-permute-start = (bf16[128,2048]{1,0:T(8,128)(2,1)}, bf16[128,2048]{1,0:T(8,128)(2,1)S(1)}, u32[]{:S(2)}, u32[]{:S(2)}) collective-permute-start(bf16[128,2048]{1,0:T(8,128)(2,1)} %refs_0_.5), channel_id=1, source_target_pairs={{0,1},{1,2},{2,3},{3,0},{4,5},{5,6},{6,7},{7,4},{8,9},{9,10},{10,1... | collective-permute-start | bytes 1572872 | tf_op jit(solution)/shard_map/ppermute | solution.py:289
  3.0 1.1 copy-done.2
  4.1 10.5 %first_dots.5 = (bf16[2,64,3584]{2,1,0:T(8,128)(2,1)S(1)}, bf16[2,16,3584]{2,1,0:T(8,128)(2,1)S(1)}, bf16[2,16,3584]{2,1,0:T(8,128)(2,1)S(1)}, bf16[2,16,3584]{2,1,0:T(8,128)(2,1)S(1)}, bf16[2,16,3584]{2,1,0:T(8,128)(2,1)S(1)}) custom-call(bf16[128,2048]{1,0:T(8,128)(2,1)S(1)} %copy-done.2, bf16[2048,7168]{1,0:T(8,128)(2,1)} %refs_1_.3, ...), custom_call_target="tpu_custom_call" | custom-call | flops 37580963840 | bytes 293601280 | tf_op jit(solution)/shard_map/first_dots/pallas_call | solution.py:89
  14.7 0.5 collective-permute-start.3
  15.3 0.4 collective-permute-start.5
  15.7 0.5 collective-permute-done.2.refs_1_
  16.8 0.3 collective-permute-done.5.refs_4_
  17.2 0.6 fold.5
  17.7 1.6 collective-permute-start.14
  19.3 1.6 collective-permute-start.1
  20.9 12.3 %first_dots.6 = (bf16[2,128,3584]{2,1,0:T(8,128)(2,1)S(1)}, bf16[2,16,3584]{2,1,0:T(8,128)(2,1)S(1)}, bf16[2,16,3584]{2,1,0:T(8,128)(2,1)S(1)}, bf16[2,16,3584]{...) custom-call(bf16[128,2048]{1,0:T(8,128)(2,1)S(1)} %copy-done.3, ...), custom_call_target="tpu_custom_call" | custom-call | flops 75161927680 | bytes 293601280 | tf_op jit(solution)/shard_map/first_dots/pallas_call | solution.py:89
  33.2 0.5 collective-permute-start.10
  33.8 0.4 collective-permute-start.12
  34.2 0.5 collective-permute-done.6.refs_1_
  35.9 0.3 activate.5.refs_9_.refs_0_
  36.3 0.6 collective-permute-start.24
  37.2 1.0 fold.6
  38.2 1.3 collective-permute-start.26
  39.5 1.6 collective-permute-start.23
  41.0 12.3 %first_dots.7 = (bf16[2,128,3584]{2,1,0:T(8,128)(2,1)S(1)}, bf16[2,16,3584]{2,1,0:T(8,128)(2,1)S(1)}, bf16[2,16,3584]{2,1,0:T(8,128)(2,1)S(1)}, bf16[2,16,3584]{...) custom-call(bf16[128,2048]{1,0:T(8,128)(2,1)S(1)} %collective-permut, ...), custom_call_target="tpu_custom_call" | custom-call | flops 75161927680 | bytes 293601280 | tf_op jit(solution)/shard_map/first_dots/pallas_call | solution.py:89
  53.4 0.5 collective-permute-start.16
  54.0 0.9 collective-permute-done.15.refs_1_
  55.9 0.5 collective-permute-done.18.refs_4_
  57.4 0.5 collective-permute-done.22.refs_8_
  57.9 1.0 fold.7
  58.9 0.9 collective-permute-start.25
  59.8 4.6 %collective-permute-done.26.refs_5_.refs_1_ = bf16[2,64,3584]{2,1,0:T(8,128)(2,1)S(1)} collective-permute-done((bf16[2,64,3584]{2,1,0:T(8,128)(2,1)S(1)}, bf16[2,64,3584]{2,1,0:T(8,128)(2,1)S(1)}, u32[]{:S(2)}, u32[]{:S(2)}) %collective-permute-start.26) | collective-permute-done | bytes 917536 | tf_op jit(solution)/shard_map/ppermute | solution.py:292
  64.4 12.2 %first_dots.8 = (bf16[2,128,3584]{2,1,0:T(8,128)(2,1)S(1)}, bf16[2,16,3584]{2,1,0:T(8,128)(2,1)S(1)}, bf16[2,16,3584]{2,1,0:T(8,128)(2,1)S(1)}, bf16[2,16,3584]{...) custom-call(bf16[128,2048]{1,0:T(8,128)(2,1)S(1)} %collective-permut, ...), custom_call_target="tpu_custom_call" | custom-call | flops 75161927680 | bytes 293601280 | tf_op jit(solution)/shard_map/first_dots/pallas_call | solution.py:89
  76.7 0.5 collective-permute-start.30
  77.2 0.4 collective-permute-start.32
  77.7 0.5 collective-permute-done.29.refs_1_
  79.3 0.6 activate.6
  79.9 0.6 collective-permute-start.42
  80.6 1.5 collective-permute-start.43
  82.1 1.0 fold.8
  83.1 0.6 collective-permute-start.39
  84.0 0.6 activate.7.refs_3_.refs_0_
  84.6 1.3 collective-permute-start.38
  85.9 10.4 %first_dots.9 = (bf16[2,64,3584]{2,1,0:T(8,128)(2,1)S(1)}, bf16[2,64,3584]{2,1,0:T(8,128)(2,1)S(1)}) custom-call(bf16[128,2048]{1,0:T(8,128)(2,1)S(1)} %collective-permute-done.23.refs_1_.refs_0_, bf16[2048,7168]{1,0:T(8,128)(2,1)} %refs_1_.3, bf16[2048,7168]{1,0:T(8,128)(2,1)} %refs_2_.9, bf16[64,3584]{1,0:T(8,128)(2,1)S(1)} %activate.7.refs_3_.refs_0_), custom_call_target="tpu_custom_call" | custom-call | flops 37580963840 | bytes 293601280 | tf_op jit(solution)/shard_map/first_dots/pallas_call | solution.py:89
  96.5 0.5 collective-permute-start.45
  97.0 0.9 collective-permute-done.41.refs_3_
  98.6 7.8 %last_dot.5 = (f32[128,2048]{1,0:T(8,128)S(1)}, f32[128,2048]{1,0:T(8,128)S(1)}) custom-call(bf16[32,3584]{1,0:T(8,128)(2,1)S(1)} %get-tuple-element.102.refs_9_.refs_0_, bf16[32,3584]{1,0:T(8,128)(2,1)S(1)} %get-tuple-element.105.refs_1_, bf16[32,3584]{1,0:T(8,128)(2,1)S(1)} %collective-permute-done.40.refs_2_, ...), custom_call_target="tpu_custom_call" | custom-call | tf_op jit(solution)/shard_map/last_dot/pallas_call | solution.py:215
  106.4 7.0 %collective-permute-done.39.refs_1_ = bf16[2,64,3584]{2,1,0:T(8,128)(2,1)S(1)} collective-permute-done((bf16[2,64,3584]{2,1,0:T(8,128)(2,1)S(1)}, bf16[2,64,3584]{2,1,0:T(8,128)(2,1)S(1)}, u32[]{:S(2)}, u32[]{:S(2)}) %collective-permute-start.39) | collective-permute-done | bytes 917536 | tf_op jit(solution)/shard_map/ppermute | solution.py:292
  113.5 0.6 activate.8.refs_6_.refs_0_
  114.1 8.7 %collective-permute-done.38.refs_2_ = bf16[64,3584]{1,0:T(8,128)(2,1)S(1)} collective-permute-done((bf16[64,3584]{1,0:T(8,128)(2,1)S(1)}, bf16[64,3584]{1,0:T(8,128)(2,1)S(1)}, u32[]{:S(2)}, u32[]{:S(2)}) %collective-permute-start.38) | collective-permute-done | bytes 458784 | tf_op jit(solution)/shard_map/ppermute | solution.py:292
  122.8 0.5 collective-permute-start.51
  123.3 0.5 collective-permute-start.49
  123.8 0.8 collective-permute-done.46.refs_3_
  124.6 7.0 %last_dot.6 = (bf16[128,2048]{1,0:T(8,128)(2,1)S(1)}, f32[128,2048]{1,0:T(8,128)S(1)}) custom-call(bf16[64,3584]{1,0:T(8,128)(2,1)S(1)} %activate.7.refs_3_.refs_0_, bf16[64,3584]{1,0:T(8,128)(2,1)S(1)} %collective-permute-done.37.refs_1_, bf16[64,3584]{1,0:T(8,128)(2,1)S(1)} %collective-permute-done.38.refs_2_, ...), custom_call_target="tpu_custom_call" | custom-call | flops 37580963840 | bytes 146800640 | tf_op jit(solution)/shard_map/last_dot/pallas_call | solution.py:215
  131.6 1.6 collective-permute-start.47
  133.2 6.1 %last_dot.7.refs_2_ = bf16[128,2048]{1,0:T(8,128)(2,1)S(1)} custom-call(bf16[32,3584]{1,0:T(8,128)(2,1)S(1)} %copy-done.1, bf16[32,3584]{1,0:T(8,128)(2,1)S(1)} %collective-permute-done.27.refs_6_.refs_1_, bf16[32,3584]{1,0:T(8,128)(2,1)S(1)} %collective-permute-done.24.refs_2_.refs_7_, bf16[32,3584]{1,0:T(8,128)(2,1)S(1)} %collective-permute-done.28.refs_8_.refs_3_, ...), custom_call_target="tpu_custom_call" | custom-call | tf_op jit(solution)/shard_map/last_dot/pallas_call | solution.py:215
  139.3 0.6 collective-permute-start.50
  139.9 0.5 fold.9
  140.4 0.8 collective-permute-start.53
  141.3 6.1 %collective-permute-done.47.refs_7_.refs_0_ = bf16[128,2048]{1,0:T(8,128)(2,1)S(1)} collective-permute-done((bf16[128,2048]{1,0:T(8,128)(2,1)S(1)}, bf16[128,2048]{1,0:T(8,128)(2,1)S(1)}, u32[]{:S(2)}, u32[]{:S(2)}) %collective-permute-start.47) | collective-permute-done | bytes 524320 | tf_op jit(solution)/shard_map/ppermute | solution.py:289
  147.4 6.9 %last_dot.8 = (bf16[128,2048]{1,0:T(8,128)(2,1)S(1)}, f32[128,2048]{1,0:T(8,128)S(1)}) custom-call(bf16[64,3584]{1,0:T(8,128)(2,1)S(1)} %activate.8.refs_6_.refs_0_, bf16[64,3584]{1,0:T(8,128)(2,1)S(1)} %collective-permute-done.48.refs_1_, bf16[64,3584]{1,0:T(8,128)(2,1)S(1)} %collective-permute-done.49.refs_2_, ...), custom_call_target="tpu_custom_call" | custom-call | flops 37580963840 | bytes 146800640 | tf_op jit(solution)/shard_map/last_dot/pallas_call | solution.py:215
  154.6 0.4 activate.9.refs_0_.refs_6_
  155.0 0.6 collective-permute-start.55
  155.6 6.3 %collective-permute-done.55.refs_2_ = bf16[32,3584]{1,0:T(8,128)(2,1)S(1)} collective-permute-done((bf16[32,3584]{1,0:T(8,128)(2,1)S(1)}, bf16[32,3584]{1,0:T(8,128)(2,1)S(1)}, u32[]{:S(2)}, u32[]{:S(2)}) %collective-permute-start.55) | collective-permute-done | bytes 229408 | tf_op jit(solution)/shard_map/ppermute | solution.py:292
  161.9 1.5 collective-permute-done.56.refs_3_
  163.4 6.1 %last_dot.9.refs_1_.refs_2_ = bf16[128,2048]{1,0:T(8,128)(2,1)S(1)} custom-call(bf16[32,3584]{1,0:T(8,128)(2,1)S(1)} %activate.9.refs_0_.refs_6_, bf16[32,3584]{1,0:T(8,128)(2,1)S(1)} %collective-permute-done.54.refs_1_, bf16[32,3584]{1,0:T(8,128)(2,1)S(1)} %collective-permute-done.55.refs_2_, bf16[32,3584]{1,0:T(8,128)(2,1)S(1)} %collective-permute-done.56.refs_3_, ...), custom_call_target="tpu_custom_call" | custom-call | flops 18790481920 | bytes 146800640 | tf_op jit(solution)/shard_map/last_dot/pallas_call | solution.py:215
  169.5 8.5 %collective-permute-done.52.refs_0_ = bf16[128,2048]{1,0:T(8,128)(2,1)S(1)} collective-permute-done((bf16[128,2048]{1,0:T(8,128)(2,1)S(1)}, bf16[128,2048]{1,0:T(8,128)(2,1)S(1)}, u32[]{:S(2)}, u32[]{:S(2)}) %collective-permute-start.52) | collective-permute-done | bytes 524320 | tf_op jit(solution)/shard_map/ppermute | solution.py:289
  178.4 15.3 %collective-permute-done.57.refs_1_ = bf16[128,2048]{1,0:T(8,128)(2,1)S(1)} collective-permute-done((bf16[128,2048]{1,0:T(8,128)(2,1)S(1)}, bf16[128,2048]{1,0:T(8,128)(2,1)S(1)}, u32[]{:S(2)}, u32[]{:S(2)}) %collective-permute-start.57) | collective-permute-done | bytes 524320 | tf_op jit(solution)/shard_map/ppermute | solution.py:289
  193.7 1.0 add.5
  (86 shorter events, 7.8 us)
Async XLA Ops:
  0.0 19.3 %collective-permute-start = (bf16[128,2048]{1,0:T(8,128)(2,1)}, bf16[128,2048]{1,0:T(8,128)(2,1)S(1)}, u32[]{:S(2)}, u32[]{:S(2)}) collective-permute-start(bf16[128,2048]{1,0:T(8,128)(2,1)} %refs_0_.5), channel_id=1, source_target_pairs={{0,1},{1,2},{2,3},{3,0},{4,5},{5,6},{6,7},{7,4},{8,9},{9,10},{10,1... | collective-permute-start | bytes 1572872 | tf_op jit(solution)/shard_map/ppermute | solution.py:289
  3.0 1.1 copy-start.2
  4.1 16.8 %copy-start.3 = (bf16[128,2048]{1,0:T(8,128)(2,1)S(1)}, bf16[128,2048]{1,0:T(8,128)(2,1)}, u32[]{:S(2)}) copy-start(bf16[128,2048]{1,0:T(8,128)(2,1)} %refs_0_.5) | copy-start | bytes 1572868
  14.6 1.6 collective-permute-start.2
  14.7 1.8 collective-permute-start.3
  15.2 1.6 collective-permute-start.4
  15.3 1.9 collective-permute-start.5
  17.7 16.1 %collective-permute-start.14 = (bf16[2,32,3584]{2,1,0:T(8,128)(2,1)S(1)}, bf16[2,32,3584]{2,1,0:T(8,128)(2,1)S(1)}, u32[]{:S(2)}, u32[]{:S(2)}) collective-permute-start(bf16[2,32,3584]{2,1,0:T(8,128)(2,1)S(1)} %get-tuple-element.68.refs_4_), channel_id=1, source_target_pairs={{0,8},{4,12},{8,0},{12,4},{1,9},{5,13},{9,1},{13,5},{2,10},{6,14},... | collective-permute-start | bytes 1376264 | tf_op jit(solution)/shard_map/ppermute | solution.py:292
  19.3 20.2 %collective-permute-start.1 = (bf16[128,2048]{1,0:T(8,128)(2,1)S(1)}, bf16[128,2048]{1,0:T(8,128)(2,1)S(1)}, u32[]{:S(2)}, u32[]{:S(2)}) collective-permute-start(bf16[128,2048]{1,0:T(8,128)(2,1)S(1)} %collective-permute-done.refs_1_.refs_0_), channel_id=1, source_target_pairs={{0,1},{1,2},{2,3},{3,0},{4,5},{5,6},{6,7},{7,4},{8,9},{9,10},{10,1... | collective-permute-start | bytes 1572872 | tf_op jit(solution)/shard_map/ppermute | solution.py:289
  33.1 1.6 collective-permute-start.6
  33.2 1.8 collective-permute-start.10
  33.7 1.6 collective-permute-start.11
  33.8 1.9 collective-permute-start.12
  34.7 1.5 collective-permute-start.13
  35.0 1.8 collective-permute-start.7
  35.4 1.5 collective-permute-start.8
  35.7 1.5 collective-permute-start.9
  36.2 20.5 %copy-start = (bf16[32,3584]{1,0:T(8,128)(2,1)}, bf16[32,3584]{1,0:T(8,128)(2,1)S(1)}, u32[]{:S(2)}) copy-start(bf16[32,3584]{1,0:T(8,128)(2,1)S(1)} %activate.5.refs_9_.refs_0_) | copy-start | bytes 688132
  36.3 17.7 %collective-permute-start.24 = (bf16[32,3584]{1,0:T(8,128)(2,1)S(1)}, bf16[32,3584]{1,0:T(8,128)(2,1)S(1)}, u32[]{:S(2)}, u32[]{:S(2)}) collective-permute-start(bf16[32,3584]{1,0:T(8,128)(2,1)S(1)} %activate.5.refs_9_.refs_0_), channel_id=1, source_target_pairs={{0,8},{4,12},{8,0},{12,4},{1,9},{5,13},{9,1},{13,5},{2,10},{6,14},... | collective-permute-start | bytes 688136 | tf_op jit(solution)/shard_map/ppermute | solution.py:292
  38.2 26.2 %collective-permute-start.26 = (bf16[2,64,3584]{2,1,0:T(8,128)(2,1)S(1)}, bf16[2,64,3584]{2,1,0:T(8,128)(2,1)S(1)}, u32[]{:S(2)}, u32[]{:S(2)}) collective-permute-start(bf16[2,64,3584]{2,1,0:T(8,128)(2,1)S(1)} %get-tuple-element.79.refs_4_), channel_id=1, source_target_pairs={{0,8},{4,12},{8,0},{12,4},{1,9},{5,13},{9,1},{13,5},{2,10},{6,14},... | collective-permute-start | bytes 2752520 | tf_op jit(solution)/shard_map/ppermute | solution.py:292
  39.5 15.9 %collective-permute-start.23 = (bf16[128,2048]{1,0:T(8,128)(2,1)S(1)}, bf16[128,2048]{1,0:T(8,128)(2,1)S(1)}, u32[]{:S(2)}, u32[]{:S(2)}) collective-permute-start(bf16[128,2048]{1,0:T(8,128)(2,1)S(1)} %collective-permute-done.1.refs_1_.refs_0_), channel_id=1, source_target_pairs={{0,1},{1,2},{2,3},{3,0},{4,5},{5,6},{6,7},{7,4},{8,9},{9,10},{10,1... | collective-permute-start | bytes 1572872 | tf_op jit(solution)/shard_map/ppermute | solution.py:289
  53.3 1.6 collective-permute-start.15
  53.4 1.8 collective-permute-start.16
  53.9 1.8 collective-permute-start.17
  54.9 1.5 collective-permute-start.18
  55.2 1.5 collective-permute-start.19
  55.4 1.6 collective-permute-start.20
  55.7 1.6 collective-permute-start.21
  56.4 1.5 collective-permute-start.22
  56.7 3.1 %collective-permute-start.27 = (bf16[32,3584]{1,0:T(8,128)(2,1)S(1)}, bf16[32,3584]{1,0:T(8,128)(2,1)S(1)}, u32[]{:S(2)}, u32[]{:S(2)}) collective-permute-start(bf16[32,3584]{1,0:T(8,128)(2,1)S(1)} %activate.5.refs_9_.refs_0_), channel_id=1, source_target_pairs={{0,4},{4,0},{8,12},{12,8},{1,5},{5,1},{9,13},{13,9},{2,6},{6,2},{1... | collective-permute-start | bytes 688136 | tf_op jit(solution)/shard_map/ppermute | solution.py:292
  57.0 7.4 %collective-permute-start.28 = (bf16[32,3584]{1,0:T(8,128)(2,1)S(1)}, bf16[32,3584]{1,0:T(8,128)(2,1)S(1)}, u32[]{:S(2)}, u32[]{:S(2)}) collective-permute-start(bf16[32,3584]{1,0:T(8,128)(2,1)S(1)} %collective-permute-done.24.refs_2_.refs_7_), channel_id=1, source_target_pairs={{0,4},{4,0},{8,12},{12,8},{1,5},{5,1},{9,13},{13,9},{2,6},{6,2},{1... | collective-permute-start | bytes 688136 | tf_op jit(solution)/shard_map/ppermute | solution.py:292
  58.9 25.1 %collective-permute-start.25 = (bf16[2,64,3584]{2,1,0:T(8,128)(2,1)S(1)}, bf16[2,64,3584]{2,1,0:T(8,128)(2,1)S(1)}, u32[]{:S(2)}, u32[]{:S(2)}) collective-permute-start(bf16[2,64,3584]{2,1,0:T(8,128)(2,1)S(1)} %get-tuple-element.90.refs_4_), channel_id=1, source_target_pairs={{0,8},{4,12},{8,0},{12,4},{1,9},{5,13},{9,1},{13,5},{2,10},{6,14},... | collective-permute-start | bytes 2752520 | tf_op jit(solution)/shard_map/ppermute | solution.py:292
  76.6 1.6 collective-permute-start.29
  76.7 1.8 collective-permute-start.30
  77.2 1.6 collective-permute-start.31
  77.2 1.9 collective-permute-start.32
  78.1 1.8 collective-permute-start.33
  78.5 2.1 %collective-permute-start.34 = (bf16[2,16,3584]{2,1,0:T(8,128)(2,1)S(1)}, bf16[2,16,3584]{2,1,0:T(8,128)(2,1)S(1)}, u32[]{:S(2)}, u32[]{:S(2)}) collective-permute-start(bf16[2,16,3584]{2,1,0:T(8,128)(2,1)S(1)} %get-tuple-element.98), channel_id=1, source_target_pairs={{0,4},{4,0},{8,12},{12,8},{1,5},{5,1},{9,13},{13,9},{2,6},{6,2},{1... | collective-permute-start | bytes 688136 | tf_op jit(solution)/shard_map/ppermute | solution.py:292
  78.8 1.8 collective-permute-start.35
  79.1 3.0 %collective-permute-start.36 = (bf16[2,16,3584]{2,1,0:T(8,128)(2,1)S(1)}, bf16[2,16,3584]{2,1,0:T(8,128)(2,1)S(1)}, u32[]{:S(2)}, u32[]{:S(2)}) collective-permute-start(bf16[2,16,3584]{2,1,0:T(8,128)(2,1)S(1)} %get-tuple-element.100), channel_id=1, source_target_pairs={{0,4},{4,0},{8,12},{12,8},{1,5},{5,1},{9,13},{13,9},{2,6},{6,2},{1... | collective-permute-start | bytes 688136 | tf_op jit(solution)/shard_map/ppermute | solution.py:292
  79.9 16.5 %collective-permute-start.42 = (bf16[32,3584]{1,0:T(8,128)(2,1)S(1)}, bf16[32,3584]{1,0:T(8,128)(2,1)S(1)}, u32[]{:S(2)}, u32[]{:S(2)}) collective-permute-start(bf16[32,3584]{1,0:T(8,128)(2,1)S(1)} %get-tuple-element.102.refs_9_.refs_0_), channel_id=1, source_target_pairs={{0,8},{4,12},{8,0},{12,4},{1,9},{5,13},{9,1},{13,5},{2,10},{6,14},... | collective-permute-start | bytes 688136 | tf_op jit(solution)/shard_map/ppermute | solution.py:292
  80.5 16.4 %collective-permute-start.40 = (bf16[32,3584]{1,0:T(8,128)(2,1)S(1)}, bf16[32,3584]{1,0:T(8,128)(2,1)S(1)}, u32[]{:S(2)}, u32[]{:S(2)}) collective-permute-start(bf16[32,3584]{1,0:T(8,128)(2,1)S(1)} %get-tuple-element.102.refs_9_.refs_0_), channel_id=1, source_target_pairs={{0,4},{4,0},{8,12},{12,8},{1,5},{5,1},{9,13},{13,9},{2,6},{6,2},{1... | collective-permute-start | bytes 688136 | tf_op jit(solution)/shard_map/ppermute | solution.py:292
  80.6 15.8 %collective-permute-start.43 = (bf16[32,3584]{1,0:T(8,128)(2,1)S(1)}, bf16[32,3584]{1,0:T(8,128)(2,1)S(1)}, u32[]{:S(2)}, u32[]{:S(2)}) collective-permute-start(bf16[32,3584]{1,0:T(8,128)(2,1)S(1)} %get-tuple-element.105.refs_1_), channel_id=1, source_target_pairs={{0,8},{4,12},{8,0},{12,4},{1,9},{5,13},{9,1},{13,5},{2,10},{6,14},... | collective-permute-start | bytes 688136 | tf_op jit(solution)/shard_map/ppermute | solution.py:292
  83.1 30.3 %collective-permute-start.39 = (bf16[2,64,3584]{2,1,0:T(8,128)(2,1)S(1)}, bf16[2,64,3584]{2,1,0:T(8,128)(2,1)S(1)}, u32[]{:S(2)}, u32[]{:S(2)}) collective-permute-start(bf16[2,64,3584]{2,1,0:T(8,128)(2,1)S(1)} %get-tuple-element.103.refs_2_), channel_id=1, source_target_pairs={{0,8},{4,12},{8,0},{12,4},{1,9},{5,13},{9,1},{13,5},{2,10},{6,14},... | collective-permute-start | bytes 2752520 | tf_op jit(solution)/shard_map/ppermute | solution.py:292
  84.6 38.2 %collective-permute-start.38 = (bf16[64,3584]{1,0:T(8,128)(2,1)S(1)}, bf16[64,3584]{1,0:T(8,128)(2,1)S(1)}, u32[]{:S(2)}, u32[]{:S(2)}) collective-permute-start(bf16[64,3584]{1,0:T(8,128)(2,1)S(1)} %activate.7.refs_3_.refs_0_), channel_id=1, source_target_pairs={{0,8},{4,12},{8,0},{12,4},{1,9},{5,13},{9,1},{13,5},{2,10},{6,14},... | collective-permute-start | bytes 1376264 | tf_op jit(solution)/shard_map/ppermute | solution.py:292
  96.4 1.6 collective-permute-start.41
  96.5 1.8 collective-permute-start.45
  96.9 1.6 collective-permute-start.44
  97.9 25.9 %collective-permute-start.37 = (bf16[64,3584]{1,0:T(8,128)(2,1)S(1)}, bf16[64,3584]{1,0:T(8,128)(2,1)S(1)}, u32[]{:S(2)}, u32[]{:S(2)}) collective-permute-start(bf16[64,3584]{1,0:T(8,128)(2,1)S(1)} %activate.7.refs_3_.refs_0_), channel_id=1, source_target_pairs={{0,4},{4,0},{8,12},{12,8},{1,5},{5,1},{9,13},{13,9},{2,6},{6,2},{1... | collective-permute-start | bytes 1376264 | tf_op jit(solution)/shard_map/ppermute | solution.py:292
  122.8 1.8 collective-permute-start.46
  122.8 17.1 %collective-permute-start.51 = (bf16[2,64,3584]{2,1,0:T(8,128)(2,1)S(1)}, bf16[2,64,3584]{2,1,0:T(8,128)(2,1)S(1)}, u32[]{:S(2)}, u32[]{:S(2)}) collective-permute-start(bf16[2,64,3584]{2,1,0:T(8,128)(2,1)S(1)} %get-tuple-element.106.refs_9_), channel_id=1, source_target_pairs={{0,4},{4,0},{8,12},{12,8},{1,5},{5,1},{9,13},{13,9},{2,6},{6,2},{1... | collective-permute-start | bytes 2752520 | tf_op jit(solution)/shard_map/ppermute | solution.py:292
  123.3 16.0 %collective-permute-start.49 = (bf16[64,3584]{1,0:T(8,128)(2,1)S(1)}, bf16[64,3584]{1,0:T(8,128)(2,1)S(1)}, u32[]{:S(2)}, u32[]{:S(2)}) collective-permute-start(bf16[64,3584]{1,0:T(8,128)(2,1)S(1)} %activate.8.refs_6_.refs_0_), channel_id=1, source_target_pairs={{0,8},{4,12},{8,0},{12,4},{1,9},{5,13},{9,1},{13,5},{2,10},{6,14},... | collective-permute-start | bytes 1376264 | tf_op jit(solution)/shard_map/ppermute | solution.py:292
  124.6 8.6 %copy-start.1 = (bf16[32,3584]{1,0:T(8,128)(2,1)S(1)}, bf16[32,3584]{1,0:T(8,128)(2,1)}, u32[]{:S(2)}) copy-start(bf16[32,3584]{1,0:T(8,128)(2,1)} %copy-done) | copy-start | bytes 688132
  131.6 15.8 %collective-permute-start.47 = (bf16[128,2048]{1,0:T(8,128)(2,1)S(1)}, bf16[128,2048]{1,0:T(8,128)(2,1)S(1)}, u32[]{:S(2)}, u32[]{:S(2)}) collective-permute-start(bf16[128,2048]{1,0:T(8,128)(2,1)S(1)} %get-tuple-element.112.refs_6_), channel_id=1, source_target_pairs={{0,1},{1,2},{2,3},{3,0},{4,5},{5,6},{6,7},{7,4},{8,9},{9,10},{10,1... | collective-permute-start | bytes 1572872 | tf_op jit(solution)/shard_map/ppermute | solution.py:289
  133.2 8.0 %collective-permute-start.48 = (bf16[64,3584]{1,0:T(8,128)(2,1)S(1)}, bf16[64,3584]{1,0:T(8,128)(2,1)S(1)}, u32[]{:S(2)}, u32[]{:S(2)}) collective-permute-start(bf16[64,3584]{1,0:T(8,128)(2,1)S(1)} %activate.8.refs_6_.refs_0_), channel_id=1, source_target_pairs={{0,4},{4,0},{8,12},{12,8},{1,5},{5,1},{9,13},{13,9},{2,6},{6,2},{1... | collective-permute-start | bytes 1376264 | tf_op jit(solution)/shard_map/ppermute | solution.py:292
  139.3 2.0 %collective-permute-start.50 = (bf16[64,3584]{1,0:T(8,128)(2,1)S(1)}, bf16[64,3584]{1,0:T(8,128)(2,1)S(1)}, u32[]{:S(2)}, u32[]{:S(2)}) collective-permute-start(bf16[64,3584]{1,0:T(8,128)(2,1)S(1)} %collective-permute-done.49.refs_2_), channel_id=1, source_target_pairs={{0,4},{4,0},{8,12},{12,8},{1,5},{5,1},{9,13},{13,9},{2,6},{6,2},{1... | collective-permute-start | bytes 1376264 | tf_op jit(solution)/shard_map/ppermute | solution.py:292
  140.4 14.2 %collective-permute-start.53 = (bf16[2,32,3584]{2,1,0:T(8,128)(2,1)S(1)}, bf16[2,32,3584]{2,1,0:T(8,128)(2,1)S(1)}, u32[]{:S(2)}, u32[]{:S(2)}) collective-permute-start(bf16[2,32,3584]{2,1,0:T(8,128)(2,1)S(1)} %get-tuple-element.116.refs_6_), channel_id=1, source_target_pairs={{0,8},{4,12},{8,0},{12,4},{1,9},{5,13},{9,1},{13,5},{2,10},{6,14},... | collective-permute-start | bytes 1376264 | tf_op jit(solution)/shard_map/ppermute | solution.py:292
  155.0 6.9 %collective-permute-start.55 = (bf16[32,3584]{1,0:T(8,128)(2,1)S(1)}, bf16[32,3584]{1,0:T(8,128)(2,1)S(1)}, u32[]{:S(2)}, u32[]{:S(2)}) collective-permute-start(bf16[32,3584]{1,0:T(8,128)(2,1)S(1)} %activate.9.refs_0_.refs_6_), channel_id=1, source_target_pairs={{0,8},{4,12},{8,0},{12,4},{1,9},{5,13},{9,1},{13,5},{2,10},{6,14},... | collective-permute-start | bytes 688136 | tf_op jit(solution)/shard_map/ppermute | solution.py:292
  155.6 6.3 %collective-permute-start.54 = (bf16[32,3584]{1,0:T(8,128)(2,1)S(1)}, bf16[32,3584]{1,0:T(8,128)(2,1)S(1)}, u32[]{:S(2)}, u32[]{:S(2)}) collective-permute-start(bf16[32,3584]{1,0:T(8,128)(2,1)S(1)} %activate.9.refs_0_.refs_6_), channel_id=1, source_target_pairs={{0,4},{4,0},{8,12},{12,8},{1,5},{5,1},{9,13},{13,9},{2,6},{6,2},{1... | collective-permute-start | bytes 688136 | tf_op jit(solution)/shard_map/ppermute | solution.py:292
  161.9 1.5 collective-permute-start.56
  161.9 16.1 %collective-permute-start.52 = (bf16[128,2048]{1,0:T(8,128)(2,1)S(1)}, bf16[128,2048]{1,0:T(8,128)(2,1)S(1)}, u32[]{:S(2)}, u32[]{:S(2)}) collective-permute-start(bf16[128,2048]{1,0:T(8,128)(2,1)S(1)} %add.3.refs_2_), channel_id=1, source_target_pairs={{0,1},{1,2},{2,3},{3,0},{4,5},{5,6},{6,7},{7,4},{8,9},{9,10},{10,1... | collective-permute-start | bytes 1572872 | tf_op jit(solution)/shard_map/ppermute | solution.py:289
  163.4 30.3 %copy-start.4 = (bf16[128,2048]{1,0:T(8,128)(2,1)S(1)}, bf16[128,2048]{1,0:T(8,128)(2,1)}, u32[]{:S(2)}) copy-start(bf16[128,2048]{1,0:T(8,128)(2,1)} %refs_0_.5) | copy-start | bytes 1572868
  178.3 15.4 %collective-permute-start.57 = (bf16[128,2048]{1,0:T(8,128)(2,1)S(1)}, bf16[128,2048]{1,0:T(8,128)(2,1)S(1)}, u32[]{:S(2)}, u32[]{:S(2)}) collective-permute-start(bf16[128,2048]{1,0:T(8,128)(2,1)S(1)} %add.4.refs_3_), channel_id=1, source_target_pairs={{0,1},{1,2},{2,3},{3,0},{4,5},{5,6},{6,7},{7,4},{8,9},{9,10},{10,1... | collective-permute-start | bytes 1572872 | tf_op jit(solution)/shard_map/ppermute | solution.py:289

commit v6 on v5

--- a/solution.py
+++ b/solution.py
@@ -130,28 +130,38 @@
     )(keep, *got, *after)
 
 
-def activate(kept, got, parts, after):
-    _, m, width = kept.shape
-    step = block_of(width, 1792)
-
-    def kernel(*refs):
-        a, b = refs[:2]
-        g = a[0].astype(F32) + b[0].astype(F32)
-        u = a[1].astype(F32) + b[1].astype(F32)
-        value = (g / (1.0 + jnp.exp(-g)) * u).astype(BF16)
-        for i, out in enumerate(refs[-parts:]):
-            out[...] = value[i * m // parts : (i + 1) * m // parts]
-
-    return pl.pallas_call(
-        kernel,
-        grid=(width // step,),
-        in_specs=[pl.BlockSpec((2, m, step), lambda c: (0, 0, c))] * 2 + [ANY] * len(after),
-        out_specs=[pl.BlockSpec((m // parts, step), lambda c: (0, c))] * parts,
-        out_shape=[jax.ShapeDtypeStruct((m // parts, width), BF16)] * parts,
+def activate(pairs, after):
+    m = pairs[0][0].shape[1]
+    widths = [kept.shape[2] for kept, _ in pairs]
+    step = min(block_of(width, 1792 if len(pairs) == 1 else 512) for width in widths)
+    ends = [sum(widths[: i + 1]) // step for i in range(len(widths))]
+    starts = [0] + ends[:-1]
+
+    def kernel(*refs):
+        out = refs[-1]
+        c = pl.program_id(0)
+        for i in range(len(pairs)):
+
+            @pl.when((c >= starts[i]) & (c < ends[i]))
+            def _():
+                a, b = refs[2 * i], refs[2 * i + 1]
+                g = a[0].astype(F32) + b[0].astype(F32)
+                u = a[1].astype(F32) + b[1].astype(F32)
+                out[...] = (g / (1.0 + jnp.exp(-g)) * u).astype(BF16)
+
+    def spec(i):
+        return pl.BlockSpec((2, m, step), lambda c: (0, 0, jnp.clip(c - starts[i], 0, ends[i] - starts[i] - 1)))
+
+    return pl.pallas_call(
+        kernel,
+        grid=(ends[-1],),
+        in_specs=[spec(i) for i in range(len(pairs)) for _ in range(2)] + [ANY] * len(after),
+        out_specs=pl.BlockSpec((m, step), lambda c: (0, c)),
+        out_shape=jax.ShapeDtypeStruct((m, sum(widths)), BF16),
         compiler_params=params(40),
         cost_estimate=cost(1, 1),
         name="activate",
-    )(kept, got, *after)
+    )(*(a for pair in pairs for a in pair), *after)
 
 
 def last_dot(pieces, weight, at, carries, finals, weigh, after):
@@ -276,7 +286,9 @@
         mid = list(range(1, n - 1))
         rows = [[0]] + [mid[i : i + 2] for i in range(0, len(mid), 2)] + [[n - 1]]
         return [(s, c) for s in rows for c in (low, high)]
-    return [([0], low), ([0, 1], high), ([1, 2], low), ([2, 3], high), ([3], low)]
+    half = (high[1] // block + 1) // 2 * block
+    first, second = (cut, half), (cut + half, high[1] - half)
+    return [([0], low), ([0, 1], first), ([0, 1], second), ([1, 2], low), ([2, 3], high), ([3], low)]
 
 
 def solution(mesh):
@@ -296,12 +308,12 @@
         for _ in range(n_tensor - 1):
             held.append(hop(held[-1]))
         rects = rectangles(n_tensor, gate_weight.shape[1])
-        left = {i: sum(i in s for s, _ in rects) for i in range(n_tensor)}
+        left = {i: sum(i in s for s, _ in rects) - (n_tensor == 4 and i < 2) for i in range(n_tensor)}
         last, dotted, folded, hidden, sums = [], {}, {}, {}, {}
 
         def dot(k):
             rows, columns = rects[k]
-            parts = 1 if k == len(rects) - 1 else 4 * len(rows)
+            parts = 1
             keep, *sends = first_dots(
                 [held[i] for i in rows],
                 (gate_weight, up_weight),
@@ -322,9 +334,11 @@
                 got = [swap(send, bit)]
             folded[k] = keep, got[0]
 
-        def act(k, parts=1):
-            own = activate(*folded[k], parts, last)
-            last[:] = own[:1]
+        total = {}
+
+        def act(k, *more):
+            own = [activate([folded[i] for i in (k, *more)], last)]
+            last[:] = own
             pieces = {0: own}
             for bit in reversed(range(1, bits)):
                 for j in list(pieces):
@@ -332,10 +346,11 @@
             pieces[1] = [swap(piece, 0) for piece in own]
             hidden[k] = pieces
 
-        def forward(k):
+        def forward(k, i=None):
             pieces = hidden[k]
+            first = [last[0]] if i is None else [last[0], total[i]]
             for j in range(2, n_pipe, 2):
-                pieces[j + 1] = [swap(lax.optimization_barrier((piece, last[0]))[0], 0) for piece in pieces[j]]
+                pieces[j + 1] = [swap(lax.optimization_barrier((piece, *first))[0], 0) for piece in pieces[j]]
 
         def need_partial(k):
             last.append(folded[k][1])
@@ -356,8 +371,6 @@
             last[:] = out[:1]
             sums.update(zip(rows, out))
 
-        total = {}
-
         def need(i):
             last.append(held[i])
 
@@ -378,12 +391,11 @@
 
         if n_tensor == 4:
             plan = [
-                (dot, 0), (sum_core, 0), (dot, 1), (act, 0), (sum_core, 1), (dot, 2), (need, 3),
-                (need_gathered, 0), (wait,), (forward, 0), (sum_core, 2), (need_partial, 1), (need_hidden, 0),
-                (dot, 3), (act, 1, 2), (sum_core, 3), (need_partial, 2), (act, 2), (dot, 4), (forward, 1),
-                (fill, 1), (act, 3), (forward, 2), (down, 2), (pass_on, 1), (fill, 0), (forward, 3),
-                (sum_core, 4), (need_total, 1), (down, 3), (pass_on, 2), (act, 4), (forward, 4), (down, 4),
-                (pass_on, 3),
+                (dot, 0), (dot, 1), (sum_core, 0), (need, 2), (dot, 2), (sum_core, 1), (dot, 3), (act, 0),
+                (sum_core, 2), (need_partial, 1), (dot, 4), (sum_core, 3), (act, 1, 2), (dot, 5), (forward, 0),
+                (fill, 0), (act, 3), (sum_core, 4), (forward, 1), (fill, 1), (forward, 3), (down, 3),
+                (pass_on, 1), (act, 4), (sum_core, 5), (forward, 4, 1), (down, 4), (pass_on, 2), (act, 5),
+                (forward, 5), (need_total, 2), (down, 5), (pass_on, 3),
             ]
         else:
             plan = []

time: 195 us -> 197 us (1.010)
  waiting for transfers between devices: 66.8 us -> 78.7 us
  starting transfers between devices: 26.7 us -> 17.2 us
    ppermute x52 -> x27, waiting for transfers between devices: 36.8 us -> 52.8 us  [swap(): lax.ppermute(value, 'pipe', [(i, i ^ 1 << bit) for i in range(n_pipe)])]
    ppermute x52 -> x27, starting transfers between devices: 18.8 us -> 13.3 us  [swap(): lax.ppermute(value, 'pipe', [(i, i ^ 1 << bit) for i in range(n_pipe)])]
    ppermute x6, starting transfers between devices: 7.87 us -> 3.86 us  [hop(): return lax.ppermute(value, 'tensor', ring)]
    ppermute x6, waiting for transfers between devices: 29.9 us -> 26 us  [hop(): return lax.ppermute(value, 'tensor', ring)]
    pallas_call x5 -> x6, Pallas kernels: 57.7 us -> 58.3 us  [first_dots(): pl.pallas_call(kernel, grid=(steps,), in_specs=[HBM if i in fixed else AN...]
    pallas_call x5 -> x6, Pallas kernels: 4.12 us -> 3.94 us  [fold(): pl.pallas_call(kernel, grid=(width // step,), in_specs=[pl.BlockSpec((k,...]
  transfers between devices with their start and end apart: 58 -> 33, of which waited for: 34 -> 16; matrix products, arithmetic and copies ran while one was open for 0% -> 0% of each run, Pallas kernels for 50% -> 47%
where the time goes in v6:
time: 197 us
  Pallas kernels  99.8 us (51%)
  waiting for transfers between devices  78.7 us (40%)
  starting transfers between devices  17.2 us (9%)
    pallas_call x6, Pallas kernels, first_dots(): pl.pallas_call(kernel, grid=(steps,), in_specs=[HBM if i in fixed else AN...  58.3 us
    ppermute x27, waiting for transfers between devices, swap(): lax.ppermute(value, 'pipe', [(i, i ^ 1 << bit) for i in range(n_pipe)])  52.8 us
    pallas_call x5, Pallas kernels, last_dot(): pl.pallas_call(kernel, grid=(steps,), in_specs=[ANY] * (n * count) + [HBM...  32.9 us
    ppermute x6, waiting for transfers between devices, hop(): return lax.ppermute(value, 'tensor', ring)  26 us
    ppermute x27, starting transfers between devices, swap(): lax.ppermute(value, 'pipe', [(i, i ^ 1 << bit) for i in range(n_pipe)])  13.3 us
    pallas_call x6, Pallas kernels, fold(): pl.pallas_call(kernel, grid=(width // step,), in_specs=[pl.BlockSpec((k,...  3.94 us
  transfers between devices with their start and end apart: 33, of which 16 were waited for; matrix products, arithmetic and copies ran while one was open for 0% of the time, Pallas kernels for 47%

profile of v6, /device:TPU:0, one launch (start us, length us, event | category | flops | bytes accessed | tf_op | source)
XLA Modules:
  0.0 197.1 jit_solution(16842762723557086966)
XLA Ops:
  0.0 3.0 %collective-permute-start = (bf16[128,2048]{1,0:T(8,128)(2,1)}, bf16[128,2048]{1,0:T(8,128)(2,1)S(1)}, u32[]{:S(2)}, u32[]{:S(2)}) collective-permute-start(bf16[128,2048]{1,0:T(8,128)(2,1)} %refs_0_.7), channel_id=1, source_target_pairs={{0,1},{1,2},{2,3},{3,0},{4,5},{5,6},{6,7},{7,4},{8,9},{9,10},{10,1... | collective-permute-start | bytes 1572872 | tf_op jit(solution)/shard_map/ppermute | solution.py:301
  3.0 1.1 copy-done
  4.1 10.4 %first_dots.6 = (bf16[2,64,3584]{2,1,0:T(8,128)(2,1)S(1)}, bf16[2,64,3584]{2,1,0:T(8,128)(2,1)S(1)}) custom-call(bf16[128,2048]{1,0:T(8,128)(2,1)S(1)} %copy-done, bf16[2048,7168]{1,0:T(8,128)(2,1)} %refs_1_.3, bf16[2048,7168]{1,0:T(8,128)(2,1)} %refs_2_.11), custom_call_target="tpu_custom_call" | custom-call | flops 37580963840 | bytes 293601280 | tf_op jit(solution)/shard_map/first_dots/pallas_call | solution.py:89
  14.5 0.1 collective-permute-start.3
  14.6 2.6 %collective-permute-done.refs_1_.refs_0_ = bf16[128,2048]{1,0:T(8,128)(2,1)S(1)} collective-permute-done((bf16[128,2048]{1,0:T(8,128)(2,1)}, bf16[128,2048]{1,0:T(8,128)(2,1)S(1)}, u32[]{:S(2)}, u32[]{:S(2)}) %collective-permute-start) | collective-permute-done | bytes 524320 | tf_op jit(solution)/shard_map/ppermute | solution.py:301
  17.2 7.5 %first_dots.7 = (bf16[2,128,2048]{2,1,0:T(8,128)(2,1)S(1)}, bf16[2,128,2048]{2,1,0:T(8,128)(2,1)S(1)}) custom-call(bf16[128,2048]{1,0:T(8,128)(2,1)S(1)} %copy-done, bf16[128,2048]{1,0:T(8,128)(2,1)S(1)} %collective-permute-done.refs_1_.refs_0_, bf16[2048,7168]{1,0:T(8,128)(2,1)} %refs_1_.3, bf16[2048,7168]{1,0:T(8,128)(2,1)} %refs_2_.11, ...), custom_call_target="tpu_custom_call" | custom-call | flops 42949672960 | bytes 167772160 | tf_op jit(solution)/shard_map/first_dots/pallas_call | solution.py:89
  24.8 0.5 fold.6
  25.4 1.6 collective-permute-start.7
  26.9 5.2 %collective-permute-done.1.refs_5_.refs_1_.refs_0_ = bf16[128,2048]{1,0:T(8,128)(2,1)S(1)} collective-permute-done((bf16[128,2048]{1,0:T(8,128)(2,1)S(1)}, bf16[128,2048]{1,0:T(8,128)(2,1)S(1)}, u32[]{:S(2)}, u32[]{:S(2)}) %collective-permute-start.1) | collective-permute-done | bytes 524320 | tf_op jit(solution)/shard_map/ppermute | solution.py:301
  32.1 6.1 %first_dots.8 = (bf16[2,128,1536]{2,1,0:T(8,128)(2,1)S(1)}, bf16[2,128,1536]{2,1,0:T(8,128)(2,1)S(1)}) custom-call(bf16[128,2048]{1,0:T(8,128)(2,1)S(1)} %copy-done, bf16[128,2048]{1,0:T(8,128)(2,1)S(1)} %collective-permute-done.refs_1_.refs_0_, bf16[2048,7168]{1,0:T(8,128)(2,1)} %refs_1_.3, bf16[2048,7168]{1,0:T(8,128)(2,1)} %refs_2_.11, ...), custom_call_target="tpu_custom_call" | custom-call | flops 32212254720 | bytes 125829120 | tf_op jit(solution)/shard_map/first_dots/pallas_call | solution.py:89
  38.2 0.1 collective-permute-start.6
  38.3 0.5 fold.7
  38.9 1.3 collective-permute-start.8
  40.2 11.9 %first_dots.9 = (bf16[2,128,3584]{2,1,0:T(8,128)(2,1)S(1)}, bf16[2,128,3584]{2,1,0:T(8,128)(2,1)S(1)}) custom-call(bf16[128,2048]{1,0:T(8,128)(2,1)S(1)} %collective-permute-done.refs_1_.refs_0_, bf16[128,2048]{1,0:T(8,128)(2,1)S(1)} %collective-permute-done.1.refs_5_.refs_1_.refs_0_, bf16[2048,7168]{1,0:T(8,128)(2,1)} %refs_1_.3, ...), custom_call_target="tpu_custom_call" | custom-call | flops 75161927680 | bytes 293601280 | tf_op jit(solution)/shard_map/first_dots/pallas_call | solution.py:89
  52.1 0.2 collective-permute-start.4
  52.3 0.4 activate.5.refs_2_.refs_0_
  52.7 0.4 collective-permute-start.10
  53.2 0.8 collective-permute-start.11
  53.9 0.4 fold.8
  54.4 1.3 collective-permute-start.12
  55.7 11.9 %first_dots.10 = (bf16[2,128,3584]{2,1,0:T(8,128)(2,1)S(1)}, bf16[2,128,3584]{2,1,0:T(8,128)(2,1)S(1)}) custom-call(bf16[128,2048]{1,0:T(8,128)(2,1)S(1)} %collective-permute-done.1.refs_5_.refs_1_.refs_0_, bf16[128,2048]{1,0:T(8,128)(2,1)S(1)} %collective-permute-done.5.refs_1_.refs_0_, bf16[2048,7168]{1,0:T(8,128)(2,1)} %refs_1_.3, ...), custom_call_target="tpu_custom_call" | custom-call | flops 75161927680 | bytes 293601280 | tf_op jit(solution)/shard_map/first_dots/pallas_call | solution.py:89
  67.6 0.1 collective-permute-start.18
  67.7 1.0 fold.9
  68.7 0.8 collective-permute-start.9
  69.5 1.0 activate.6.refs_3_.refs_0_
  70.5 1.3 collective-permute-start.17
  71.8 10.4 %first_dots.11 = (bf16[2,64,3584]{2,1,0:T(8,128)(2,1)S(1)}, bf16[2,64,3584]{2,1,0:T(8,128)(2,1)S(1)}) custom-call(bf16[128,2048]{1,0:T(8,128)(2,1)S(1)} %collective-permute-done.5.refs_1_.refs_0_, bf16[2048,7168]{1,0:T(8,128)(2,1)} %refs_1_.3, bf16[2048,7168]{1,0:T(8,128)(2,1)} %refs_2_.11, bf16[64,3584]{1,0:T(8,128)(2,1)S(1)} %activate.6.refs_3_.refs_0_), custom_call_target="tpu_custom_call" | custom-call | flops 37580963840 | bytes 293601280 | tf_op jit(solution)/shard_map/first_dots/pallas_call | solution.py:89
  82.3 0.5 collective-permute-start.16
  82.8 1.0 collective-permute-done.13.refs_3_
  83.8 6.1 %last_dot.5.refs_2_.refs_5_ = f32[128,2048]{1,0:T(8,128)S(1)} custom-call(bf16[32,3584]{1,0:T(8,128)(2,1)S(1)} %activate.5.refs_2_.refs_0_, bf16[32,3584]{1,0:T(8,128)(2,1)S(1)} %collective-permute-done.10.refs_1_, bf16[32,3584]{1,0:T(8,128)(2,1)S(1)} %collective-permute-done.11.refs_2_, bf16[32,3584]{1,0:T(8,128)(2,1)S(1)} %collective-permute-done.13.refs_3_, ...), custom_call_target="tpu_custom_call" | custom-call | tf_op jit(solution)/shard_map/last_dot/pallas_call | solution.py:225
  89.8 2.0 %collective-permute-done.9.refs_1_ = bf16[2,64,3584]{2,1,0:T(8,128)(2,1)S(1)} collective-permute-done((bf16[2,64,3584]{2,1,0:T(8,128)(2,1)S(1)}, bf16[2,64,3584]{2,1,0:T(8,128)(2,1)S(1)}, u32[]{:S(2)}, u32[]{:S(2)}) %collective-permute-start.9) | collective-permute-done | bytes 917536 | tf_op jit(solution)/shard_map/ppermute | solution.py:304
  91.9 0.7 activate.7.refs_2_.refs_0_
  92.5 1.0 fold.10
  93.5 7.8 %collective-permute-done.17.refs_2_ = bf16[64,3584]{1,0:T(8,128)(2,1)S(1)} collective-permute-done((bf16[64,3584]{1,0:T(8,128)(2,1)S(1)}, bf16[64,3584]{1,0:T(8,128)(2,1)S(1)}, u32[]{:S(2)}, u32[]{:S(2)}) %collective-permute-start.17) | collective-permute-done | bytes 458784 | tf_op jit(solution)/shard_map/ppermute | solution.py:304
  101.3 0.8 collective-permute-start.15
  102.1 0.2 collective-permute-start.14
  102.3 0.8 collective-permute-done.19.refs_3_
  103.1 6.9 %last_dot.6 = (bf16[128,2048]{1,0:T(8,128)(2,1)S(1)}, f32[128,2048]{1,0:T(8,128)S(1)}) custom-call(bf16[64,3584]{1,0:T(8,128)(2,1)S(1)} %activate.6.refs_3_.refs_0_, bf16[64,3584]{1,0:T(8,128)(2,1)S(1)} %collective-permute-done.16.refs_1_, bf16[64,3584]{1,0:T(8,128)(2,1)S(1)} %collective-permute-done.17.refs_2_, ...), custom_call_target="tpu_custom_call" | custom-call | tf_op jit(solution)/shard_map/last_dot/pallas_call | solution.py:225
  110.0 4.2 %collective-permute-done.15.refs_2_ = bf16[64,3584]{1,0:T(8,128)(2,1)S(1)} collective-permute-done((bf16[64,3584]{1,0:T(8,128)(2,1)S(1)}, bf16[64,3584]{1,0:T(8,128)(2,1)S(1)}, u32[]{:S(2)}, u32[]{:S(2)}) %collective-permute-start.15) | collective-permute-done | bytes 458784 | tf_op jit(solution)/shard_map/ppermute | solution.py:304
  114.2 0.5 collective-permute-start.25
  114.7 0.8 collective-permute-start.22
  115.5 0.5 collective-permute-done.20.refs_3_
  116.0 6.9 %last_dot.7 = (bf16[128,2048]{1,0:T(8,128)(2,1)S(1)}, f32[128,2048]{1,0:T(8,128)S(1)}) custom-call(bf16[64,3584]{1,0:T(8,128)(2,1)S(1)} %activate.7.refs_2_.refs_0_, bf16[64,3584]{1,0:T(8,128)(2,1)S(1)} %collective-permute-done.14.refs_1_, bf16[64,3584]{1,0:T(8,128)(2,1)S(1)} %collective-permute-done.15.refs_2_, ...), custom_call_target="tpu_custom_call" | custom-call | flops 37580963840 | bytes 146800640 | tf_op jit(solution)/shard_map/last_dot/pallas_call | solution.py:225
  123.0 0.4 collective-permute-start.21
  123.4 13.6 %collective-permute-done.22.refs_1_ = bf16[2,64,3584]{2,1,0:T(8,128)(2,1)S(1)} collective-permute-done((bf16[2,64,3584]{2,1,0:T(8,128)(2,1)S(1)}, bf16[2,64,3584]{2,1,0:T(8,128)(2,1)S(1)}, u32[]{:S(2)}, u32[]{:S(2)}) %collective-permute-start.22) | collective-permute-done | bytes 917536 | tf_op jit(solution)/shard_map/ppermute | solution.py:304
  137.0 0.7 activate.8.refs_2_.refs_0_
  137.6 0.8 collective-permute-start.24
  138.5 0.5 fold.11
  139.0 10.3 %collective-permute-done.24.refs_2_ = bf16[64,3584]{1,0:T(8,128)(2,1)S(1)} collective-permute-done((bf16[64,3584]{1,0:T(8,128)(2,1)S(1)}, bf16[64,3584]{1,0:T(8,128)(2,1)S(1)}, u32[]{:S(2)}, u32[]{:S(2)}) %collective-permute-start.24) | collective-permute-done | bytes 458784 | tf_op jit(solution)/shard_map/ppermute | solution.py:304
  149.3 0.8 collective-permute-start.28
  150.1 1.0 collective-permute-done.26.refs_3_
  151.1 6.9 %last_dot.8 = (bf16[128,2048]{1,0:T(8,128)(2,1)S(1)}, f32[128,2048]{1,0:T(8,128)S(1)}) custom-call(bf16[64,3584]{1,0:T(8,128)(2,1)S(1)} %activate.8.refs_2_.refs_0_, bf16[64,3584]{1,0:T(8,128)(2,1)S(1)} %collective-permute-done.23.refs_1_, bf16[64,3584]{1,0:T(8,128)(2,1)S(1)} %collective-permute-done.24.refs_2_, ...), custom_call_target="tpu_custom_call" | custom-call | flops 37580963840 | bytes 146800640 | tf_op jit(solution)/shard_map/last_dot/pallas_call | solution.py:225
  158.0 0.3 add.3.refs_2_
  158.3 0.3 collective-permute-start.27
  158.6 3.6 %collective-permute-done.28.refs_1_ = bf16[2,32,3584]{2,1,0:T(8,128)(2,1)S(1)} collective-permute-done((bf16[2,32,3584]{2,1,0:T(8,128)(2,1)S(1)}, bf16[2,32,3584]{2,1,0:T(8,128)(2,1)S(1)}, u32[]{:S(2)}, u32[]{:S(2)}) %collective-permute-start.28) | collective-permute-done | bytes 458784 | tf_op jit(solution)/shard_map/ppermute | solution.py:304
  162.2 0.4 activate.9.refs_0_.refs_6_
  162.6 0.8 collective-permute-start.30
  163.5 6.5 %collective-permute-done.30.refs_2_ = bf16[32,3584]{1,0:T(8,128)(2,1)S(1)} collective-permute-done((bf16[32,3584]{1,0:T(8,128)(2,1)S(1)}, bf16[32,3584]{1,0:T(8,128)(2,1)S(1)}, u32[]{:S(2)}, u32[]{:S(2)}) %collective-permute-start.30) | collective-permute-done | bytes 229408 | tf_op jit(solution)/shard_map/ppermute | solution.py:304
  169.9 1.5 collective-permute-done.31.refs_3_
  171.4 3.0 %collective-permute-done.27.refs_7_.refs_0_ = bf16[128,2048]{1,0:T(8,128)(2,1)S(1)} collective-permute-done((bf16[128,2048]{1,0:T(8,128)(2,1)S(1)}, bf16[128,2048]{1,0:T(8,128)(2,1)S(1)}, u32[]{:S(2)}, u32[]{:S(2)}) %collective-permute-start.27) | collective-permute-done | bytes 524320 | tf_op jit(solution)/shard_map/ppermute | solution.py:301
  174.4 6.1 %last_dot.9.refs_1_.refs_2_ = bf16[128,2048]{1,0:T(8,128)(2,1)S(1)} custom-call(bf16[32,3584]{1,0:T(8,128)(2,1)S(1)} %activate.9.refs_0_.refs_6_, bf16[32,3584]{1,0:T(8,128)(2,1)S(1)} %collective-permute-done.29.refs_1_, bf16[32,3584]{1,0:T(8,128)(2,1)S(1)} %collective-permute-done.30.refs_2_, bf16[32,3584]{1,0:T(8,128)(2,1)S(1)} %collective-permute-done.31.refs_3_, ...), custom_call_target="tpu_custom_call" | custom-call | flops 18790481920 | bytes 146800640 | tf_op jit(solution)/shard_map/last_dot/pallas_call | solution.py:225
  180.5 0.3 add.4.refs_3_
  180.8 15.2 %collective-permute-done.32.refs_1_ = bf16[128,2048]{1,0:T(8,128)(2,1)S(1)} collective-permute-done((bf16[128,2048]{1,0:T(8,128)(2,1)S(1)}, bf16[128,2048]{1,0:T(8,128)(2,1)S(1)}, u32[]{:S(2)}, u32[]{:S(2)}) %collective-permute-start.32) | collective-permute-done | bytes 524320 | tf_op jit(solution)/shard_map/ppermute | solution.py:301
  196.1 1.0 add.5
  (31 shorter events, 0.4 us)
Async XLA Ops:
  0.0 17.2 %collective-permute-start = (bf16[128,2048]{1,0:T(8,128)(2,1)}, bf16[128,2048]{1,0:T(8,128)(2,1)S(1)}, u32[]{:S(2)}, u32[]{:S(2)}) collective-permute-start(bf16[128,2048]{1,0:T(8,128)(2,1)} %refs_0_.7), channel_id=1, source_target_pairs={{0,1},{1,2},{2,3},{3,0},{4,5},{5,6},{6,7},{7,4},{8,9},{9,10},{10,1... | collective-permute-start | bytes 1572872 | tf_op jit(solution)/shard_map/ppermute | solution.py:301
  3.0 1.1 copy-start
  14.5 10.3 %collective-permute-start.3 = (bf16[2,64,3584]{2,1,0:T(8,128)(2,1)S(1)}, bf16[2,64,3584]{2,1,0:T(8,128)(2,1)S(1)}, u32[]{:S(2)}, u32[]{:S(2)}) collective-permute-start(bf16[2,64,3584]{2,1,0:T(8,128)(2,1)S(1)} %get-tuple-element.40.refs_4_), channel_id=1, source_target_pairs={{0,4},{4,0},{8,12},{12,8},{1,5},{5,1},{9,13},{13,9},{2,6},{6,2},{1... | collective-permute-start | bytes 2752520 | tf_op jit(solution)/shard_map/ppermute | solution.py:304
  17.2 14.9 %collective-permute-start.1 = (bf16[128,2048]{1,0:T(8,128)(2,1)S(1)}, bf16[128,2048]{1,0:T(8,128)(2,1)S(1)}, u32[]{:S(2)}, u32[]{:S(2)}) collective-permute-start(bf16[128,2048]{1,0:T(8,128)(2,1)S(1)} %collective-permute-done.refs_1_.refs_0_), channel_id=1, source_target_pairs={{0,1},{1,2},{2,3},{3,0},{4,5},{5,6},{6,7},{7,4},{8,9},{9,10},{10,1... | collective-permute-start | bytes 1572872 | tf_op jit(solution)/shard_map/ppermute | solution.py:301
  24.7 13.6 %collective-permute-start.2 = (bf16[2,128,2048]{2,1,0:T(8,128)(2,1)S(1)}, bf16[2,128,2048]{2,1,0:T(8,128)(2,1)S(1)}, u32[]{:S(2)}, u32[]{:S(2)}) collective-permute-start(bf16[2,128,2048]{2,1,0:T(8,128)(2,1)S(1)} %get-tuple-element.42.refs_2_), channel_id=1, source_target_pairs={{0,4},{4,0},{8,12},{12,8},{1,5},{5,1},{9,13},{13,9},{2,6},{6,2},{1... | collective-permute-start | bytes 3145736 | tf_op jit(solution)/shard_map/ppermute | solution.py:304
  25.4 27.0 %collective-permute-start.7 = (bf16[2,32,3584]{2,1,0:T(8,128)(2,1)S(1)}, bf16[2,32,3584]{2,1,0:T(8,128)(2,1)S(1)}, u32[]{:S(2)}, u32[]{:S(2)}) collective-permute-start(bf16[2,32,3584]{2,1,0:T(8,128)(2,1)S(1)} %get-tuple-element.44.refs_4_), channel_id=1, source_target_pairs={{0,8},{4,12},{8,0},{12,4},{1,9},{5,13},{9,1},{13,5},{2,10},{6,14},... | collective-permute-start | bytes 1376264 | tf_op jit(solution)/shard_map/ppermute | solution.py:304
  38.2 15.0 %collective-permute-start.6 = (bf16[2,128,1536]{2,1,0:T(8,128)(2,1)S(1)}, bf16[2,128,1536]{2,1,0:T(8,128)(2,1)S(1)}, u32[]{:S(2)}, u32[]{:S(2)}) collective-permute-start(bf16[2,128,1536]{2,1,0:T(8,128)(2,1)S(1)} %get-tuple-element.45.refs_2_), channel_id=1, source_target_pairs={{0,4},{4,0},{8,12},{12,8},{1,5},{5,1},{9,13},{13,9},{2,6},{6,2},{1... | collective-permute-start | bytes 2359304 | tf_op jit(solution)/shard_map/ppermute | solution.py:304
  38.3 16.1 %collective-permute-start.5 = (bf16[128,2048]{1,0:T(8,128)(2,1)S(1)}, bf16[128,2048]{1,0:T(8,128)(2,1)S(1)}, u32[]{:S(2)}, u32[]{:S(2)}) collective-permute-start(bf16[128,2048]{1,0:T(8,128)(2,1)S(1)} %collective-permute-done.1.refs_5_.refs_1_.refs_0_), channel_id=1, source_target_pairs={{0,1},{1,2},{2,3},{3,0},{4,5},{5,6},{6,7},{7,4},{8,9},{9,10},{10,1... | collective-permute-start | bytes 1572872 | tf_op jit(solution)/shard_map/ppermute | solution.py:301
  38.9 16.8 %collective-permute-start.8 = (bf16[2,64,2048]{2,1,0:T(8,128)(2,1)S(1)}, bf16[2,64,2048]{2,1,0:T(8,128)(2,1)S(1)}, u32[]{:S(2)}, u32[]{:S(2)}) collective-permute-start(bf16[2,64,2048]{2,1,0:T(8,128)(2,1)S(1)} %get-tuple-element.46.refs_4_), channel_id=1, source_target_pairs={{0,8},{4,12},{8,0},{12,4},{1,9},{5,13},{9,1},{13,5},{2,10},{6,14},... | collective-permute-start | bytes 1572872 | tf_op jit(solution)/shard_map/ppermute | solution.py:304
  52.1 15.5 %collective-permute-start.4 = (bf16[2,128,3584]{2,1,0:T(8,128)(2,1)S(1)}, bf16[2,128,3584]{2,1,0:T(8,128)(2,1)S(1)}, u32[]{:S(2)}, u32[]{:S(2)}) collective-permute-start(bf16[2,128,3584]{2,1,0:T(8,128)(2,1)S(1)} %get-tuple-element.48.refs_2_), channel_id=1, source_target_pairs={{0,4},{4,0},{8,12},{12,8},{1,5},{5,1},{9,13},{13,9},{2,6},{6,2},{1... | collective-permute-start | bytes 5505032 | tf_op jit(solution)/shard_map/ppermute | solution.py:304
  52.7 29.6 %collective-permute-start.10 = (bf16[32,3584]{1,0:T(8,128)(2,1)S(1)}, bf16[32,3584]{1,0:T(8,128)(2,1)S(1)}, u32[]{:S(2)}, u32[]{:S(2)}) collective-permute-start(bf16[32,3584]{1,0:T(8,128)(2,1)S(1)} %activate.5.refs_2_.refs_0_), channel_id=1, source_target_pairs={{0,4},{4,0},{8,12},{12,8},{1,5},{5,1},{9,13},{13,9},{2,6},{6,2},{1... | collective-permute-start | bytes 688136 | tf_op jit(solution)/shard_map/ppermute | solution.py:304
  53.2 29.1 %collective-permute-start.11 = (bf16[32,3584]{1,0:T(8,128)(2,1)S(1)}, bf16[32,3584]{1,0:T(8,128)(2,1)S(1)}, u32[]{:S(2)}, u32[]{:S(2)}) collective-permute-start(bf16[32,3584]{1,0:T(8,128)(2,1)S(1)} %activate.5.refs_2_.refs_0_), channel_id=1, source_target_pairs={{0,8},{4,12},{8,0},{12,4},{1,9},{5,13},{9,1},{13,5},{2,10},{6,14},... | collective-permute-start | bytes 688136 | tf_op jit(solution)/shard_map/ppermute | solution.py:304
  54.4 15.1 %collective-permute-start.12 = (bf16[2,64,1536]{2,1,0:T(8,128)(2,1)S(1)}, bf16[2,64,1536]{2,1,0:T(8,128)(2,1)S(1)}, u32[]{:S(2)}, u32[]{:S(2)}) collective-permute-start(bf16[2,64,1536]{2,1,0:T(8,128)(2,1)S(1)} %get-tuple-element.51.refs_4_), channel_id=1, source_target_pairs={{0,8},{4,12},{8,0},{12,4},{1,9},{5,13},{9,1},{13,5},{2,10},{6,14},... | collective-permute-start | bytes 1179656 | tf_op jit(solution)/shard_map/ppermute | solution.py:304
  67.6 24.9 %collective-permute-start.18 = (bf16[2,128,3584]{2,1,0:T(8,128)(2,1)S(1)}, bf16[2,128,3584]{2,1,0:T(8,128)(2,1)S(1)}, u32[]{:S(2)}, u32[]{:S(2)}) collective-permute-start(bf16[2,128,3584]{2,1,0:T(8,128)(2,1)S(1)} %get-tuple-element.52.refs_2_), channel_id=1, source_target_pairs={{0,4},{4,0},{8,12},{12,8},{1,5},{5,1},{9,13},{13,9},{2,6},{6,2},{1... | collective-permute-start | bytes 5505032 | tf_op jit(solution)/shard_map/ppermute | solution.py:304
  68.7 23.2 %collective-permute-start.9 = (bf16[2,64,3584]{2,1,0:T(8,128)(2,1)S(1)}, bf16[2,64,3584]{2,1,0:T(8,128)(2,1)S(1)}, u32[]{:S(2)}, u32[]{:S(2)}) collective-permute-start(bf16[2,64,3584]{2,1,0:T(8,128)(2,1)S(1)} %get-tuple-element.54.refs_4_), channel_id=1, source_target_pairs={{0,8},{4,12},{8,0},{12,4},{1,9},{5,13},{9,1},{13,5},{2,10},{6,14},... | collective-permute-start | bytes 2752520 | tf_op jit(solution)/shard_map/ppermute | solution.py:304
  70.5 30.8 %collective-permute-start.17 = (bf16[64,3584]{1,0:T(8,128)(2,1)S(1)}, bf16[64,3584]{1,0:T(8,128)(2,1)S(1)}, u32[]{:S(2)}, u32[]{:S(2)}) collective-permute-start(bf16[64,3584]{1,0:T(8,128)(2,1)S(1)} %activate.6.refs_3_.refs_0_), channel_id=1, source_target_pairs={{0,8},{4,12},{8,0},{12,4},{1,9},{5,13},{9,1},{13,5},{2,10},{6,14},... | collective-permute-start | bytes 1376264 | tf_op jit(solution)/shard_map/ppermute | solution.py:304
  82.2 1.6 collective-permute-start.13
  82.3 20.0 %collective-permute-start.16 = (bf16[64,3584]{1,0:T(8,128)(2,1)S(1)}, bf16[64,3584]{1,0:T(8,128)(2,1)S(1)}, u32[]{:S(2)}, u32[]{:S(2)}) collective-permute-start(bf16[64,3584]{1,0:T(8,128)(2,1)S(1)} %activate.6.refs_3_.refs_0_), channel_id=1, source_target_pairs={{0,4},{4,0},{8,12},{12,8},{1,5},{5,1},{9,13},{13,9},{2,6},{6,2},{1... | collective-permute-start | bytes 1376264 | tf_op jit(solution)/shard_map/ppermute | solution.py:304
  101.3 1.8 collective-permute-start.19
  101.3 12.9 %collective-permute-start.15 = (bf16[64,3584]{1,0:T(8,128)(2,1)S(1)}, bf16[64,3584]{1,0:T(8,128)(2,1)S(1)}, u32[]{:S(2)}, u32[]{:S(2)}) collective-permute-start(bf16[64,3584]{1,0:T(8,128)(2,1)S(1)} %activate.7.refs_2_.refs_0_), channel_id=1, source_target_pairs={{0,8},{4,12},{8,0},{12,4},{1,9},{5,13},{9,1},{13,5},{2,10},{6,14},... | collective-permute-start | bytes 1376264 | tf_op jit(solution)/shard_map/ppermute | solution.py:304
  102.1 13.4 %collective-permute-start.14 = (bf16[64,3584]{1,0:T(8,128)(2,1)S(1)}, bf16[64,3584]{1,0:T(8,128)(2,1)S(1)}, u32[]{:S(2)}, u32[]{:S(2)}) collective-permute-start(bf16[64,3584]{1,0:T(8,128)(2,1)S(1)} %activate.7.refs_2_.refs_0_), channel_id=1, source_target_pairs={{0,4},{4,0},{8,12},{12,8},{1,5},{5,1},{9,13},{13,9},{2,6},{6,2},{1... | collective-permute-start | bytes 1376264 | tf_op jit(solution)/shard_map/ppermute | solution.py:304
  114.2 1.8 collective-permute-start.20
  114.2 24.3 %collective-permute-start.25 = (bf16[2,64,3584]{2,1,0:T(8,128)(2,1)S(1)}, bf16[2,64,3584]{2,1,0:T(8,128)(2,1)S(1)}, u32[]{:S(2)}, u32[]{:S(2)}) collective-permute-start(bf16[2,64,3584]{2,1,0:T(8,128)(2,1)S(1)} %get-tuple-element.57.refs_5_), channel_id=1, source_target_pairs={{0,4},{4,0},{8,12},{12,8},{1,5},{5,1},{9,13},{13,9},{2,6},{6,2},{1... | collective-permute-start | bytes 2752520 | tf_op jit(solution)/shard_map/ppermute | solution.py:304
  114.7 22.3 %collective-permute-start.22 = (bf16[2,64,3584]{2,1,0:T(8,128)(2,1)S(1)}, bf16[2,64,3584]{2,1,0:T(8,128)(2,1)S(1)}, u32[]{:S(2)}, u32[]{:S(2)}) collective-permute-start(bf16[2,64,3584]{2,1,0:T(8,128)(2,1)S(1)} %get-tuple-element.60.refs_6_), channel_id=1, source_target_pairs={{0,8},{4,12},{8,0},{12,4},{1,9},{5,13},{9,1},{13,5},{2,10},{6,14},... | collective-permute-start | bytes 2752520 | tf_op jit(solution)/shard_map/ppermute | solution.py:304
  123.0 26.3 %collective-permute-start.21 = (bf16[128,2048]{1,0:T(8,128)(2,1)S(1)}, bf16[128,2048]{1,0:T(8,128)(2,1)S(1)}, u32[]{:S(2)}, u32[]{:S(2)}) collective-permute-start(bf16[128,2048]{1,0:T(8,128)(2,1)S(1)} %get-tuple-element.65.refs_2_), channel_id=1, source_target_pairs={{0,1},{1,2},{2,3},{3,0},{4,5},{5,6},{6,7},{7,4},{8,9},{9,10},{10,1... | collective-permute-start | bytes 1572872 | tf_op jit(solution)/shard_map/ppermute | solution.py:301
  137.6 11.6 %collective-permute-start.24 = (bf16[64,3584]{1,0:T(8,128)(2,1)S(1)}, bf16[64,3584]{1,0:T(8,128)(2,1)S(1)}, u32[]{:S(2)}, u32[]{:S(2)}) collective-permute-start(bf16[64,3584]{1,0:T(8,128)(2,1)S(1)} %activate.8.refs_2_.refs_0_), channel_id=1, source_target_pairs={{0,8},{4,12},{8,0},{12,4},{1,9},{5,13},{9,1},{13,5},{2,10},{6,14},... | collective-permute-start | bytes 1376264 | tf_op jit(solution)/shard_map/ppermute | solution.py:304
  138.5 11.6 %collective-permute-start.23 = (bf16[64,3584]{1,0:T(8,128)(2,1)S(1)}, bf16[64,3584]{1,0:T(8,128)(2,1)S(1)}, u32[]{:S(2)}, u32[]{:S(2)}) collective-permute-start(bf16[64,3584]{1,0:T(8,128)(2,1)S(1)} %activate.8.refs_2_.refs_0_), channel_id=1, source_target_pairs={{0,4},{4,0},{8,12},{12,8},{1,5},{5,1},{9,13},{13,9},{2,6},{6,2},{1... | collective-permute-start | bytes 1376264 | tf_op jit(solution)/shard_map/ppermute | solution.py:304
  149.3 1.8 collective-permute-start.26
  149.3 12.9 %collective-permute-start.28 = (bf16[2,32,3584]{2,1,0:T(8,128)(2,1)S(1)}, bf16[2,32,3584]{2,1,0:T(8,128)(2,1)S(1)}, u32[]{:S(2)}, u32[]{:S(2)}) collective-permute-start(bf16[2,32,3584]{2,1,0:T(8,128)(2,1)S(1)} %get-tuple-element.68.refs_6_), channel_id=1, source_target_pairs={{0,8},{4,12},{8,0},{12,4},{1,9},{5,13},{9,1},{13,5},{2,10},{6,14},... | collective-permute-start | bytes 1376264 | tf_op jit(solution)/shard_map/ppermute | solution.py:304
  158.3 16.1 %collective-permute-start.27 = (bf16[128,2048]{1,0:T(8,128)(2,1)S(1)}, bf16[128,2048]{1,0:T(8,128)(2,1)S(1)}, u32[]{:S(2)}, u32[]{:S(2)}) collective-permute-start(bf16[128,2048]{1,0:T(8,128)(2,1)S(1)} %add.3.refs_2_), channel_id=1, source_target_pairs={{0,1},{1,2},{2,3},{3,0},{4,5},{5,6},{6,7},{7,4},{8,9},{9,10},{10,1... | collective-permute-start | bytes 1572872 | tf_op jit(solution)/shard_map/ppermute | solution.py:301
  162.6 7.3 %collective-permute-start.30 = (bf16[32,3584]{1,0:T(8,128)(2,1)S(1)}, bf16[32,3584]{1,0:T(8,128)(2,1)S(1)}, u32[]{:S(2)}, u32[]{:S(2)}) collective-permute-start(bf16[32,3584]{1,0:T(8,128)(2,1)S(1)} %activate.9.refs_0_.refs_6_), channel_id=1, source_target_pairs={{0,8},{4,12},{8,0},{12,4},{1,9},{5,13},{9,1},{13,5},{2,10},{6,14},... | collective-permute-start | bytes 688136 | tf_op jit(solution)/shard_map/ppermute | solution.py:304
  163.5 6.5 %collective-permute-start.29 = (bf16[32,3584]{1,0:T(8,128)(2,1)S(1)}, bf16[32,3584]{1,0:T(8,128)(2,1)S(1)}, u32[]{:S(2)}, u32[]{:S(2)}) collective-permute-start(bf16[32,3584]{1,0:T(8,128)(2,1)S(1)} %activate.9.refs_0_.refs_6_), channel_id=1, source_target_pairs={{0,4},{4,0},{8,12},{12,8},{1,5},{5,1},{9,13},{13,9},{2,6},{6,2},{1... | collective-permute-start | bytes 688136 | tf_op jit(solution)/shard_map/ppermute | solution.py:304
  169.9 1.5 collective-permute-start.31
  180.5 15.6 %copy-start.1 = (bf16[128,2048]{1,0:T(8,128)(2,1)S(1)}, bf16[128,2048]{1,0:T(8,128)(2,1)}, u32[]{:S(2)}) copy-start(bf16[128,2048]{1,0:T(8,128)(2,1)} %refs_0_.7) | copy-start | bytes 1572868
  180.8 15.3 %collective-permute-start.32 = (bf16[128,2048]{1,0:T(8,128)(2,1)S(1)}, bf16[128,2048]{1,0:T(8,128)(2,1)S(1)}, u32[]{:S(2)}, u32[]{:S(2)}) collective-permute-start(bf16[128,2048]{1,0:T(8,128)(2,1)S(1)} %add.4.refs_3_), channel_id=1, source_target_pairs={{0,1},{1,2},{2,3},{3,0},{4,5},{5,6},{6,7},{7,4},{8,9},{9,10},{10,1... | collective-permute-start | bytes 1572872 | tf_op jit(solution)/shard_map/ppermute | solution.py:301

commit v7 on v5

--- a/solution.py
+++ b/solution.py
@@ -380,10 +380,9 @@
             plan = [
                 (dot, 0), (sum_core, 0), (dot, 1), (act, 0), (sum_core, 1), (dot, 2), (need, 3),
                 (need_gathered, 0), (wait,), (forward, 0), (sum_core, 2), (need_partial, 1), (need_hidden, 0),
-                (dot, 3), (act, 1, 2), (sum_core, 3), (need_partial, 2), (act, 2), (dot, 4), (forward, 1),
-                (fill, 1), (act, 3), (forward, 2), (down, 2), (pass_on, 1), (fill, 0), (forward, 3),
-                (sum_core, 4), (need_total, 1), (down, 3), (pass_on, 2), (act, 4), (forward, 4), (down, 4),
-                (pass_on, 3),
+                (dot, 3), (act, 1), (sum_core, 3), (need_partial, 2), (dot, 4), (act, 2, 2), (forward, 1),
+                (fill, 1), (act, 3), (sum_core, 4), (forward, 2), (fill, 2), (pass_on, 1), (forward, 3),
+                (down, 3), (pass_on, 2), (act, 4), (down, 0), (forward, 4), (fill, 4), (pass_on, 3),
             ]
         else:
             plan = []

time: 195 us -> 184 us (0.944)
  waiting for transfers between devices: 66.8 us -> 55.9 us
    ppermute x52, waiting for transfers between devices: 36.8 us -> 31.1 us  [swap(): lax.ppermute(value, 'pipe', [(i, i ^ 1 << bit) for i in range(n_pipe)])]
    ppermute x6, waiting for transfers between devices: 29.9 us -> 24.7 us  [hop(): return lax.ppermute(value, 'tensor', ring)]
  transfers between devices with their start and end apart: 58 -> 58, of which waited for: 34 -> 33; matrix products, arithmetic and copies ran while one was open for 0% -> 0% of each run, Pallas kernels for 50% -> 53%
where the time goes in v7:
time: 184 us
  Pallas kernels  99.8 us (54%)
  waiting for transfers between devices  55.9 us (30%)
  starting transfers between devices  27.1 us (15%)
    pallas_call x5, Pallas kernels, first_dots(): pl.pallas_call(kernel, grid=(steps,), in_specs=[HBM if i in fixed else AN...  57.7 us
    pallas_call x5, Pallas kernels, last_dot(): pl.pallas_call(kernel, grid=(steps,), in_specs=[ANY] * (n * count) + [HBM...  33.9 us
    ppermute x52, waiting for transfers between devices, swap(): lax.ppermute(value, 'pipe', [(i, i ^ 1 << bit) for i in range(n_pipe)])  31.1 us
    ppermute x6, waiting for transfers between devices, hop(): return lax.ppermute(value, 'tensor', ring)  24.7 us
    ppermute x52, starting transfers between devices, swap(): lax.ppermute(value, 'pipe', [(i, i ^ 1 << bit) for i in range(n_pipe)])  19.3 us
    ppermute x6, starting transfers between devices, hop(): return lax.ppermute(value, 'tensor', ring)  7.82 us
    pallas_call x5, Pallas kernels, fold(): pl.pallas_call(kernel, grid=(width // step,), in_specs=[pl.BlockSpec((k,...  4.12 us
  transfers between devices with their start and end apart: 58, of which 33 were waited for; matrix products, arithmetic and copies ran while one was open for 0% of the time, Pallas kernels for 53%

profile of v7, /device:TPU:0, one launch (start us, length us, event | category | flops | bytes accessed | tf_op | source)
XLA Modules:
  0.0 184.2 jit_solution(6556408856117593308)
XLA Ops:
  0.0 3.0 %collective-permute-start = (bf16[128,2048]{1,0:T(8,128)(2,1)}, bf16[128,2048]{1,0:T(8,128)(2,1)S(1)}, u32[]{:S(2)}, u32[]{:S(2)}) collective-permute-start(bf16[128,2048]{1,0:T(8,128)(2,1)} %refs_0_.5), channel_id=1, source_target_pairs={{0,1},{1,2},{2,3},{3,0},{4,5},{5,6},{6,7},{7,4},{8,9},{9,10},{10,1... | collective-permute-start | bytes 1572872 | tf_op jit(solution)/shard_map/ppermute | solution.py:289
  3.0 1.1 copy-done.2
  4.1 10.5 %first_dots.5 = (bf16[2,64,3584]{2,1,0:T(8,128)(2,1)S(1)}, bf16[2,16,3584]{2,1,0:T(8,128)(2,1)S(1)}, bf16[2,16,3584]{2,1,0:T(8,128)(2,1)S(1)}, bf16[2,16,3584]{2,1,0:T(8,128)(2,1)S(1)}, bf16[2,16,3584]{2,1,0:T(8,128)(2,1)S(1)}) custom-call(bf16[128,2048]{1,0:T(8,128)(2,1)S(1)} %copy-done.2, bf16[2048,7168]{1,0:T(8,128)(2,1)} %refs_1_.3, ...), custom_call_target="tpu_custom_call" | custom-call | flops 37580963840 | bytes 293601280 | tf_op jit(solution)/shard_map/first_dots/pallas_call | solution.py:89
  14.7 0.5 collective-permute-start.3
  15.3 0.4 collective-permute-start.5
  15.7 0.5 collective-permute-done.2.refs_1_
  17.2 0.6 fold.5
  17.7 1.6 collective-permute-start.14
  19.3 1.6 collective-permute-start.1
  20.9 12.3 %first_dots.6 = (bf16[2,128,3584]{2,1,0:T(8,128)(2,1)S(1)}, bf16[2,16,3584]{2,1,0:T(8,128)(2,1)S(1)}, bf16[2,16,3584]{2,1,0:T(8,128)(2,1)S(1)}, bf16[2,16,3584]{...) custom-call(bf16[128,2048]{1,0:T(8,128)(2,1)S(1)} %copy-done.3, ...), custom_call_target="tpu_custom_call" | custom-call | flops 75161927680 | bytes 293601280 | tf_op jit(solution)/shard_map/first_dots/pallas_call | solution.py:89
  33.2 0.5 collective-permute-start.10
  33.8 0.4 collective-permute-start.12
  34.2 0.5 collective-permute-done.6.refs_1_
  36.3 0.6 collective-permute-start.24
  37.2 1.0 fold.6
  38.2 1.3 collective-permute-start.26
  39.5 1.6 collective-permute-start.23
  41.0 12.3 %first_dots.7 = (bf16[2,128,3584]{2,1,0:T(8,128)(2,1)S(1)}, bf16[2,16,3584]{2,1,0:T(8,128)(2,1)S(1)}, bf16[2,16,3584]{2,1,0:T(8,128)(2,1)S(1)}, bf16[2,16,3584]{...) custom-call(bf16[128,2048]{1,0:T(8,128)(2,1)S(1)} %collective-permut, ...), custom_call_target="tpu_custom_call" | custom-call | flops 75161927680 | bytes 293601280 | tf_op jit(solution)/shard_map/first_dots/pallas_call | solution.py:89
  53.4 0.5 collective-permute-start.16
  54.0 0.9 collective-permute-done.15.refs_1_
  55.9 0.5 collective-permute-done.18.refs_4_
  57.4 0.5 collective-permute-done.22.refs_8_
  57.9 1.0 fold.7
  58.9 0.9 collective-permute-start.25
  59.8 4.6 %collective-permute-done.26.refs_5_.refs_1_ = bf16[2,64,3584]{2,1,0:T(8,128)(2,1)S(1)} collective-permute-done((bf16[2,64,3584]{2,1,0:T(8,128)(2,1)S(1)}, bf16[2,64,3584]{2,1,0:T(8,128)(2,1)S(1)}, u32[]{:S(2)}, u32[]{:S(2)}) %collective-permute-start.26) | collective-permute-done | bytes 917536 | tf_op jit(solution)/shard_map/ppermute | solution.py:292
  64.4 12.2 %first_dots.8 = (bf16[2,128,3584]{2,1,0:T(8,128)(2,1)S(1)}, bf16[2,16,3584]{2,1,0:T(8,128)(2,1)S(1)}, bf16[2,16,3584]{2,1,0:T(8,128)(2,1)S(1)}, bf16[2,16,3584]{...) custom-call(bf16[128,2048]{1,0:T(8,128)(2,1)S(1)} %collective-permut, ...), custom_call_target="tpu_custom_call" | custom-call | flops 75161927680 | bytes 293601280 | tf_op jit(solution)/shard_map/first_dots/pallas_call | solution.py:89
  76.7 0.5 collective-permute-start.30
  77.2 0.4 collective-permute-start.32
  77.7 0.5 collective-permute-done.29.refs_1_
  79.3 0.6 activate.6.refs_9_.refs_0_
  79.9 0.6 collective-permute-start.44
  80.6 1.0 fold.8
  81.6 1.5 collective-permute-start.42
  83.1 0.8 collective-permute-done.25.refs_4_.refs_1_
  84.0 10.4 %first_dots.9 = (bf16[2,64,3584]{2,1,0:T(8,128)(2,1)S(1)}, bf16[2,64,3584]{2,1,0:T(8,128)(2,1)S(1)}) custom-call(bf16[128,2048]{1,0:T(8,128)(2,1)S(1)} %collective-permute-done.23.refs_1_.refs_0_, bf16[2048,7168]{1,0:T(8,128)(2,1)} %refs_1_.3, bf16[2048,7168]{1,0:T(8,128)(2,1)} %refs_2_.9, bf16[2,64,3584]{2,1,0:T(8,128)(2,1)S(1)} %get-tuple-element.102.refs_3_, ...), custom_call_target="tpu_custom_call" | custom-call | flops 37580963840 | bytes 293601280 | tf_op jit(solution)/shard_map/first_dots/pallas_call | solution.py:89
  94.5 0.5 collective-permute-start.43
  95.0 0.6 activate.7
  95.8 0.5 collective-permute-start.40
  96.3 1.3 collective-permute-done.43.refs_1_
  97.6 0.5 collective-permute-start.39
  98.3 6.9 %last_dot.5 = (f32[128,2048]{1,0:T(8,128)S(1)}, f32[128,2048]{1,0:T(8,128)S(1)}) custom-call(bf16[64,3584]{1,0:T(8,128)(2,1)S(1)} %activate.6.refs_9_.refs_0_, bf16[64,3584]{1,0:T(8,128)(2,1)S(1)} %collective-permute-done.43.refs_1_, bf16[64,3584]{1,0:T(8,128)(2,1)S(1)} %collective-permute-done.44.refs_2_, ...), custom_call_target="tpu_custom_call" | custom-call | tf_op jit(solution)/shard_map/last_dot/pallas_call | solution.py:215
  105.2 8.3 %collective-permute-done.42.refs_1_ = bf16[2,64,3584]{2,1,0:T(8,128)(2,1)S(1)} collective-permute-done((bf16[2,64,3584]{2,1,0:T(8,128)(2,1)S(1)}, bf16[2,64,3584]{2,1,0:T(8,128)(2,1)S(1)}, u32[]{:S(2)}, u32[]{:S(2)}) %collective-permute-start.42) | collective-permute-done | bytes 917536 | tf_op jit(solution)/shard_map/ppermute | solution.py:292
  113.5 0.6 activate.8.refs_2_.refs_0_
  114.1 0.6 collective-permute-start.50
  114.7 0.5 collective-permute-start.38
  115.2 0.5 fold.9
  115.7 2.7 %collective-permute-done.40.refs_5_ = bf16[32,3584]{1,0:T(8,128)(2,1)S(1)} collective-permute-done((bf16[32,3584]{1,0:T(8,128)(2,1)S(1)}, bf16[32,3584]{1,0:T(8,128)(2,1)S(1)}, u32[]{:S(2)}, u32[]{:S(2)}) %collective-permute-start.40) | collective-permute-done | bytes 229408 | tf_op jit(solution)/shard_map/ppermute | solution.py:292
  118.4 4.9 %collective-permute-done.39.refs_4_ = bf16[32,3584]{1,0:T(8,128)(2,1)S(1)} collective-permute-done((bf16[32,3584]{1,0:T(8,128)(2,1)S(1)}, bf16[32,3584]{1,0:T(8,128)(2,1)S(1)}, u32[]{:S(2)}, u32[]{:S(2)}) %collective-permute-start.39) | collective-permute-done | bytes 229408 | tf_op jit(solution)/shard_map/ppermute | solution.py:292
  123.3 0.5 collective-permute-start.49
  123.8 1.0 collective-permute-done.46.refs_6_
  124.8 7.8 %last_dot.6 = (bf16[128,2048]{1,0:T(8,128)(2,1)S(1)}, f32[128,2048]{1,0:T(8,128)S(1)}) custom-call(bf16[32,3584]{1,0:T(8,128)(2,1)S(1)} %get-tuple-element.104.refs_5_.refs_0_, bf16[32,3584]{1,0:T(8,128)(2,1)S(1)} %get-tuple-element.105.refs_1_, bf16[32,3584]{1,0:T(8,128)(2,1)S(1)} %collective-permute-done.37.refs_2_, ...), custom_call_target="tpu_custom_call" | custom-call | tf_op jit(solution)/shard_map/last_dot/pallas_call | solution.py:215
  132.9 0.5 collective-permute-start.53
  133.4 1.6 collective-permute-start.48
  135.0 7.0 %last_dot.7 = (bf16[128,2048]{1,0:T(8,128)(2,1)S(1)}, f32[128,2048]{1,0:T(8,128)S(1)}) custom-call(bf16[64,3584]{1,0:T(8,128)(2,1)S(1)} %activate.8.refs_2_.refs_0_, bf16[64,3584]{1,0:T(8,128)(2,1)S(1)} %collective-permute-done.49.refs_1_, bf16[64,3584]{1,0:T(8,128)(2,1)S(1)} %collective-permute-done.50.refs_2_, ...), custom_call_target="tpu_custom_call" | custom-call | flops 37580963840 | bytes 146800640 | tf_op jit(solution)/shard_map/last_dot/pallas_call | solution.py:215
  142.0 7.1 %collective-permute-done.48.refs_0_ = bf16[128,2048]{1,0:T(8,128)(2,1)S(1)} collective-permute-done((bf16[128,2048]{1,0:T(8,128)(2,1)S(1)}, bf16[128,2048]{1,0:T(8,128)(2,1)S(1)}, u32[]{:S(2)}, u32[]{:S(2)}) %collective-permute-start.48) | collective-permute-done | bytes 524320 | tf_op jit(solution)/shard_map/ppermute | solution.py:289
  149.4 0.4 activate.9.refs_6_.refs_0_
  149.8 1.6 collective-permute-start.55
  151.3 6.1 %last_dot.8.refs_6_.refs_2_ = bf16[128,2048]{1,0:T(8,128)(2,1)S(1)} custom-call(bf16[32,3584]{1,0:T(8,128)(2,1)S(1)} %copy-done.1, bf16[32,3584]{1,0:T(8,128)(2,1)S(1)} %collective-permute-done.27.refs_6_.refs_1_, bf16[32,3584]{1,0:T(8,128)(2,1)S(1)} %collective-permute-done.24.refs_2_.refs_7_, bf16[32,3584]{1,0:T(8,128)(2,1)S(1)} %collective-permute-done.28.refs_8_.refs_3_, ...), custom_call_target="tpu_custom_call" | custom-call | flops 18790481920 | bytes 146800640 | tf_op jit(solution)/shard_map/last_dot/pallas_call | solution.py:215
  157.5 0.6 collective-permute-start.56
  158.0 1.1 collective-permute-done.56.refs_3_
  159.1 6.1 %last_dot.9.refs_1_.refs_2_ = bf16[128,2048]{1,0:T(8,128)(2,1)S(1)} custom-call(bf16[32,3584]{1,0:T(8,128)(2,1)S(1)} %activate.9.refs_6_.refs_0_, bf16[32,3584]{1,0:T(8,128)(2,1)S(1)} %collective-permute-done.54.refs_1_, bf16[32,3584]{1,0:T(8,128)(2,1)S(1)} %collective-permute-done.55.refs_2_, bf16[32,3584]{1,0:T(8,128)(2,1)S(1)} %collective-permute-done.56.refs_3_, ...), custom_call_target="tpu_custom_call" | custom-call | tf_op jit(solution)/shard_map/last_dot/pallas_call | solution.py:215
  165.2 2.3 %collective-permute-done.52.refs_0_ = bf16[128,2048]{1,0:T(8,128)(2,1)S(1)} collective-permute-done((bf16[128,2048]{1,0:T(8,128)(2,1)S(1)}, bf16[128,2048]{1,0:T(8,128)(2,1)S(1)}, u32[]{:S(2)}, u32[]{:S(2)}) %collective-permute-start.52) | collective-permute-done | bytes 524320 | tf_op jit(solution)/shard_map/ppermute | solution.py:289
  167.8 15.3 %collective-permute-done.57.refs_1_ = bf16[128,2048]{1,0:T(8,128)(2,1)S(1)} collective-permute-done((bf16[128,2048]{1,0:T(8,128)(2,1)S(1)}, bf16[128,2048]{1,0:T(8,128)(2,1)S(1)}, u32[]{:S(2)}, u32[]{:S(2)}) %collective-permute-start.57) | collective-permute-done | bytes 524320 | tf_op jit(solution)/shard_map/ppermute | solution.py:289
  183.2 1.0 add.5
  (86 shorter events, 7.9 us)
Async XLA Ops:
  0.0 19.3 %collective-permute-start = (bf16[128,2048]{1,0:T(8,128)(2,1)}, bf16[128,2048]{1,0:T(8,128)(2,1)S(1)}, u32[]{:S(2)}, u32[]{:S(2)}) collective-permute-start(bf16[128,2048]{1,0:T(8,128)(2,1)} %refs_0_.5), channel_id=1, source_target_pairs={{0,1},{1,2},{2,3},{3,0},{4,5},{5,6},{6,7},{7,4},{8,9},{9,10},{10,1... | collective-permute-start | bytes 1572872 | tf_op jit(solution)/shard_map/ppermute | solution.py:289
  3.0 1.1 copy-start.2
  4.1 16.8 %copy-start.3 = (bf16[128,2048]{1,0:T(8,128)(2,1)S(1)}, bf16[128,2048]{1,0:T(8,128)(2,1)}, u32[]{:S(2)}) copy-start(bf16[128,2048]{1,0:T(8,128)(2,1)} %refs_0_.5) | copy-start | bytes 1572868
  14.6 1.6 collective-permute-start.2
  14.7 1.8 collective-permute-start.3
  15.2 1.6 collective-permute-start.4
  15.3 1.9 %collective-permute-start.5 = (bf16[2,16,3584]{2,1,0:T(8,128)(2,1)S(1)}, bf16[2,16,3584]{2,1,0:T(8,128)(2,1)S(1)}, u32[]{:S(2)}, u32[]{:S(2)}) collective-permute-start(bf16[2,16,3584]{2,1,0:T(8,128)(2,1)S(1)} %get-tuple-element.67), channel_id=1, source_target_pairs={{0,4},{4,0},{8,12},{12,8},{1,5},{5,1},{9,13},{13,9},{2,6},{6,2},{1... | collective-permute-start | bytes 688136 | tf_op jit(solution)/shard_map/ppermute | solution.py:292
  17.7 16.1 %collective-permute-start.14 = (bf16[2,32,3584]{2,1,0:T(8,128)(2,1)S(1)}, bf16[2,32,3584]{2,1,0:T(8,128)(2,1)S(1)}, u32[]{:S(2)}, u32[]{:S(2)}) collective-permute-start(bf16[2,32,3584]{2,1,0:T(8,128)(2,1)S(1)} %get-tuple-element.68.refs_4_), channel_id=1, source_target_pairs={{0,8},{4,12},{8,0},{12,4},{1,9},{5,13},{9,1},{13,5},{2,10},{6,14},... | collective-permute-start | bytes 1376264 | tf_op jit(solution)/shard_map/ppermute | solution.py:292
  19.3 20.2 %collective-permute-start.1 = (bf16[128,2048]{1,0:T(8,128)(2,1)S(1)}, bf16[128,2048]{1,0:T(8,128)(2,1)S(1)}, u32[]{:S(2)}, u32[]{:S(2)}) collective-permute-start(bf16[128,2048]{1,0:T(8,128)(2,1)S(1)} %collective-permute-done.refs_1_.refs_0_), channel_id=1, source_target_pairs={{0,1},{1,2},{2,3},{3,0},{4,5},{5,6},{6,7},{7,4},{8,9},{9,10},{10,1... | collective-permute-start | bytes 1572872 | tf_op jit(solution)/shard_map/ppermute | solution.py:289
  33.1 1.6 collective-permute-start.6
  33.2 1.8 collective-permute-start.10
  33.7 1.6 collective-permute-start.11
  33.8 1.9 %collective-permute-start.12 = (bf16[2,16,3584]{2,1,0:T(8,128)(2,1)S(1)}, bf16[2,16,3584]{2,1,0:T(8,128)(2,1)S(1)}, u32[]{:S(2)}, u32[]{:S(2)}) collective-permute-start(bf16[2,16,3584]{2,1,0:T(8,128)(2,1)S(1)} %get-tuple-element.76), channel_id=1, source_target_pairs={{0,4},{4,0},{8,12},{12,8},{1,5},{5,1},{9,13},{13,9},{2,6},{6,2},{1... | collective-permute-start | bytes 688136 | tf_op jit(solution)/shard_map/ppermute | solution.py:292
  34.7 1.5 collective-permute-start.13
  35.0 1.8 collective-permute-start.7
  35.4 1.5 collective-permute-start.8
  35.7 1.5 collective-permute-start.9
  36.2 20.5 %copy-start = (bf16[32,3584]{1,0:T(8,128)(2,1)}, bf16[32,3584]{1,0:T(8,128)(2,1)S(1)}, u32[]{:S(2)}) copy-start(bf16[32,3584]{1,0:T(8,128)(2,1)S(1)} %activate.5.refs_9_.refs_0_) | copy-start | bytes 688132
  36.3 17.7 %collective-permute-start.24 = (bf16[32,3584]{1,0:T(8,128)(2,1)S(1)}, bf16[32,3584]{1,0:T(8,128)(2,1)S(1)}, u32[]{:S(2)}, u32[]{:S(2)}) collective-permute-start(bf16[32,3584]{1,0:T(8,128)(2,1)S(1)} %activate.5.refs_9_.refs_0_), channel_id=1, source_target_pairs={{0,8},{4,12},{8,0},{12,4},{1,9},{5,13},{9,1},{13,5},{2,10},{6,14},... | collective-permute-start | bytes 688136 | tf_op jit(solution)/shard_map/ppermute | solution.py:292
  38.2 26.2 %collective-permute-start.26 = (bf16[2,64,3584]{2,1,0:T(8,128)(2,1)S(1)}, bf16[2,64,3584]{2,1,0:T(8,128)(2,1)S(1)}, u32[]{:S(2)}, u32[]{:S(2)}) collective-permute-start(bf16[2,64,3584]{2,1,0:T(8,128)(2,1)S(1)} %get-tuple-element.79.refs_4_), channel_id=1, source_target_pairs={{0,8},{4,12},{8,0},{12,4},{1,9},{5,13},{9,1},{13,5},{2,10},{6,14},... | collective-permute-start | bytes 2752520 | tf_op jit(solution)/shard_map/ppermute | solution.py:292
  39.5 15.9 %collective-permute-start.23 = (bf16[128,2048]{1,0:T(8,128)(2,1)S(1)}, bf16[128,2048]{1,0:T(8,128)(2,1)S(1)}, u32[]{:S(2)}, u32[]{:S(2)}) collective-permute-start(bf16[128,2048]{1,0:T(8,128)(2,1)S(1)} %collective-permute-done.1.refs_1_.refs_0_), channel_id=1, source_target_pairs={{0,1},{1,2},{2,3},{3,0},{4,5},{5,6},{6,7},{7,4},{8,9},{9,10},{10,1... | collective-permute-start | bytes 1572872 | tf_op jit(solution)/shard_map/ppermute | solution.py:289
  53.3 1.6 collective-permute-start.15
  53.4 1.8 collective-permute-start.16
  53.9 1.8 collective-permute-start.17
  54.9 1.5 collective-permute-start.18
  55.2 1.5 collective-permute-start.19
  55.4 1.6 collective-permute-start.20
  55.7 1.6 collective-permute-start.21
  56.4 1.5 collective-permute-start.22
  56.7 3.1 %collective-permute-start.27 = (bf16[32,3584]{1,0:T(8,128)(2,1)S(1)}, bf16[32,3584]{1,0:T(8,128)(2,1)S(1)}, u32[]{:S(2)}, u32[]{:S(2)}) collective-permute-start(bf16[32,3584]{1,0:T(8,128)(2,1)S(1)} %activate.5.refs_9_.refs_0_), channel_id=1, source_target_pairs={{0,4},{4,0},{8,12},{12,8},{1,5},{5,1},{9,13},{13,9},{2,6},{6,2},{1... | collective-permute-start | bytes 688136 | tf_op jit(solution)/shard_map/ppermute | solution.py:292
  57.0 7.4 %collective-permute-start.28 = (bf16[32,3584]{1,0:T(8,128)(2,1)S(1)}, bf16[32,3584]{1,0:T(8,128)(2,1)S(1)}, u32[]{:S(2)}, u32[]{:S(2)}) collective-permute-start(bf16[32,3584]{1,0:T(8,128)(2,1)S(1)} %collective-permute-done.24.refs_2_.refs_7_), channel_id=1, source_target_pairs={{0,4},{4,0},{8,12},{12,8},{1,5},{5,1},{9,13},{13,9},{2,6},{6,2},{1... | collective-permute-start | bytes 688136 | tf_op jit(solution)/shard_map/ppermute | solution.py:292
  58.9 25.1 %collective-permute-start.25 = (bf16[2,64,3584]{2,1,0:T(8,128)(2,1)S(1)}, bf16[2,64,3584]{2,1,0:T(8,128)(2,1)S(1)}, u32[]{:S(2)}, u32[]{:S(2)}) collective-permute-start(bf16[2,64,3584]{2,1,0:T(8,128)(2,1)S(1)} %get-tuple-element.90.refs_4_), channel_id=1, source_target_pairs={{0,8},{4,12},{8,0},{12,4},{1,9},{5,13},{9,1},{13,5},{2,10},{6,14},... | collective-permute-start | bytes 2752520 | tf_op jit(solution)/shard_map/ppermute | solution.py:292
  76.6 1.6 collective-permute-start.29
  76.7 1.8 collective-permute-start.30
  77.2 1.6 collective-permute-start.31
  77.2 1.9 %collective-permute-start.32 = (bf16[2,16,3584]{2,1,0:T(8,128)(2,1)S(1)}, bf16[2,16,3584]{2,1,0:T(8,128)(2,1)S(1)}, u32[]{:S(2)}, u32[]{:S(2)}) collective-permute-start(bf16[2,16,3584]{2,1,0:T(8,128)(2,1)S(1)} %get-tuple-element.96), channel_id=1, source_target_pairs={{0,4},{4,0},{8,12},{12,8},{1,5},{5,1},{9,13},{13,9},{2,6},{6,2},{1... | collective-permute-start | bytes 688136 | tf_op jit(solution)/shard_map/ppermute | solution.py:292
  78.1 1.8 collective-permute-start.33
  78.5 2.1 %collective-permute-start.34 = (bf16[2,16,3584]{2,1,0:T(8,128)(2,1)S(1)}, bf16[2,16,3584]{2,1,0:T(8,128)(2,1)S(1)}, u32[]{:S(2)}, u32[]{:S(2)}) collective-permute-start(bf16[2,16,3584]{2,1,0:T(8,128)(2,1)S(1)} %get-tuple-element.98), channel_id=1, source_target_pairs={{0,4},{4,0},{8,12},{12,8},{1,5},{5,1},{9,13},{13,9},{2,6},{6,2},{1... | collective-permute-start | bytes 688136 | tf_op jit(solution)/shard_map/ppermute | solution.py:292
  78.8 1.7 collective-permute-start.35
  79.1 1.5 collective-permute-start.36
  79.9 15.7 %collective-permute-start.44 = (bf16[64,3584]{1,0:T(8,128)(2,1)S(1)}, bf16[64,3584]{1,0:T(8,128)(2,1)S(1)}, u32[]{:S(2)}, u32[]{:S(2)}) collective-permute-start(bf16[64,3584]{1,0:T(8,128)(2,1)S(1)} %activate.6.refs_9_.refs_0_), channel_id=1, source_target_pairs={{0,8},{4,12},{8,0},{12,4},{1,9},{5,13},{9,1},{13,5},{2,10},{6,14},... | collective-permute-start | bytes 1376264 | tf_op jit(solution)/shard_map/ppermute | solution.py:292
  81.6 31.8 %collective-permute-start.42 = (bf16[2,64,3584]{2,1,0:T(8,128)(2,1)S(1)}, bf16[2,64,3584]{2,1,0:T(8,128)(2,1)S(1)}, u32[]{:S(2)}, u32[]{:S(2)}) collective-permute-start(bf16[2,64,3584]{2,1,0:T(8,128)(2,1)S(1)} %get-tuple-element.102.refs_3_), channel_id=1, source_target_pairs={{0,8},{4,12},{8,0},{12,4},{1,9},{5,13},{9,1},{13,5},{2,10},{6,14},... | collective-permute-start | bytes 2752520 | tf_op jit(solution)/shard_map/ppermute | solution.py:292
  94.4 20.3 %collective-permute-start.41 = (bf16[2,64,3584]{2,1,0:T(8,128)(2,1)S(1)}, bf16[2,64,3584]{2,1,0:T(8,128)(2,1)S(1)}, u32[]{:S(2)}, u32[]{:S(2)}) collective-permute-start(bf16[2,64,3584]{2,1,0:T(8,128)(2,1)S(1)} %get-tuple-element.103.refs_2_), channel_id=1, source_target_pairs={{0,4},{4,0},{8,12},{12,8},{1,5},{5,1},{9,13},{13,9},{2,6},{6,2},{1... | collective-permute-start | bytes 2752520 | tf_op jit(solution)/shard_map/ppermute | solution.py:292
  94.5 3.1 %collective-permute-start.43 = (bf16[64,3584]{1,0:T(8,128)(2,1)S(1)}, bf16[64,3584]{1,0:T(8,128)(2,1)S(1)}, u32[]{:S(2)}, u32[]{:S(2)}) collective-permute-start(bf16[64,3584]{1,0:T(8,128)(2,1)S(1)} %activate.6.refs_9_.refs_0_), channel_id=1, source_target_pairs={{0,4},{4,0},{8,12},{12,8},{1,5},{5,1},{9,13},{13,9},{2,6},{6,2},{1... | collective-permute-start | bytes 1376264 | tf_op jit(solution)/shard_map/ppermute | solution.py:292
  95.6 2.6 %collective-permute-start.45 = (bf16[64,3584]{1,0:T(8,128)(2,1)S(1)}, bf16[64,3584]{1,0:T(8,128)(2,1)S(1)}, u32[]{:S(2)}, u32[]{:S(2)}) collective-permute-start(bf16[64,3584]{1,0:T(8,128)(2,1)S(1)} %collective-permute-done.44.refs_2_), channel_id=1, source_target_pairs={{0,4},{4,0},{8,12},{12,8},{1,5},{5,1},{9,13},{13,9},{2,6},{6,2},{1... | collective-permute-start | bytes 1376264 | tf_op jit(solution)/shard_map/ppermute | solution.py:292
  95.8 22.6 %collective-permute-start.40 = (bf16[32,3584]{1,0:T(8,128)(2,1)S(1)}, bf16[32,3584]{1,0:T(8,128)(2,1)S(1)}, u32[]{:S(2)}, u32[]{:S(2)}) collective-permute-start(bf16[32,3584]{1,0:T(8,128)(2,1)S(1)} %get-tuple-element.105.refs_1_), channel_id=1, source_target_pairs={{0,8},{4,12},{8,0},{12,4},{1,9},{5,13},{9,1},{13,5},{2,10},{6,14},... | collective-permute-start | bytes 688136 | tf_op jit(solution)/shard_map/ppermute | solution.py:292
  97.6 25.7 %collective-permute-start.39 = (bf16[32,3584]{1,0:T(8,128)(2,1)S(1)}, bf16[32,3584]{1,0:T(8,128)(2,1)S(1)}, u32[]{:S(2)}, u32[]{:S(2)}) collective-permute-start(bf16[32,3584]{1,0:T(8,128)(2,1)S(1)} %get-tuple-element.104.refs_5_.refs_0_), channel_id=1, source_target_pairs={{0,8},{4,12},{8,0},{12,4},{1,9},{5,13},{9,1},{13,5},{2,10},{6,14},... | collective-permute-start | bytes 688136 | tf_op jit(solution)/shard_map/ppermute | solution.py:292
  114.1 18.6 %collective-permute-start.50 = (bf16[64,3584]{1,0:T(8,128)(2,1)S(1)}, bf16[64,3584]{1,0:T(8,128)(2,1)S(1)}, u32[]{:S(2)}, u32[]{:S(2)}) collective-permute-start(bf16[64,3584]{1,0:T(8,128)(2,1)S(1)} %activate.8.refs_2_.refs_0_), channel_id=1, source_target_pairs={{0,8},{4,12},{8,0},{12,4},{1,9},{5,13},{9,1},{13,5},{2,10},{6,14},... | collective-permute-start | bytes 1376264 | tf_op jit(solution)/shard_map/ppermute | solution.py:292
  114.7 8.6 %collective-permute-start.37 = (bf16[32,3584]{1,0:T(8,128)(2,1)S(1)}, bf16[32,3584]{1,0:T(8,128)(2,1)S(1)}, u32[]{:S(2)}, u32[]{:S(2)}) collective-permute-start(bf16[32,3584]{1,0:T(8,128)(2,1)S(1)} %get-tuple-element.104.refs_5_.refs_0_), channel_id=1, source_target_pairs={{0,4},{4,0},{8,12},{12,8},{1,5},{5,1},{9,13},{13,9},{2,6},{6,2},{1... | collective-permute-start | bytes 688136 | tf_op jit(solution)/shard_map/ppermute | solution.py:292
  114.7 9.1 %collective-permute-start.38 = (bf16[32,3584]{1,0:T(8,128)(2,1)S(1)}, bf16[32,3584]{1,0:T(8,128)(2,1)S(1)}, u32[]{:S(2)}, u32[]{:S(2)}) collective-permute-start(bf16[32,3584]{1,0:T(8,128)(2,1)S(1)} %get-tuple-element.105.refs_1_), channel_id=1, source_target_pairs={{0,4},{4,0},{8,12},{12,8},{1,5},{5,1},{9,13},{13,9},{2,6},{6,2},{1... | collective-permute-start | bytes 688136 | tf_op jit(solution)/shard_map/ppermute | solution.py:292
  118.4 5.4 %collective-permute-start.47 = (bf16[32,3584]{1,0:T(8,128)(2,1)S(1)}, bf16[32,3584]{1,0:T(8,128)(2,1)S(1)}, u32[]{:S(2)}, u32[]{:S(2)}) collective-permute-start(bf16[32,3584]{1,0:T(8,128)(2,1)S(1)} %collective-permute-done.40.refs_5_), channel_id=1, source_target_pairs={{0,4},{4,0},{8,12},{12,8},{1,5},{5,1},{9,13},{13,9},{2,6},{6,2},{1... | collective-permute-start | bytes 688136 | tf_op jit(solution)/shard_map/ppermute | solution.py:292
  123.3 1.5 collective-permute-start.46
  123.3 11.7 %collective-permute-start.49 = (bf16[64,3584]{1,0:T(8,128)(2,1)S(1)}, bf16[64,3584]{1,0:T(8,128)(2,1)S(1)}, u32[]{:S(2)}, u32[]{:S(2)}) collective-permute-start(bf16[64,3584]{1,0:T(8,128)(2,1)S(1)} %activate.8.refs_2_.refs_0_), channel_id=1, source_target_pairs={{0,4},{4,0},{8,12},{12,8},{1,5},{5,1},{9,13},{13,9},{2,6},{6,2},{1... | collective-permute-start | bytes 1376264 | tf_op jit(solution)/shard_map/ppermute | solution.py:292
  132.7 2.3 %collective-permute-start.51 = (bf16[64,3584]{1,0:T(8,128)(2,1)S(1)}, bf16[64,3584]{1,0:T(8,128)(2,1)S(1)}, u32[]{:S(2)}, u32[]{:S(2)}) collective-permute-start(bf16[64,3584]{1,0:T(8,128)(2,1)S(1)} %collective-permute-done.50.refs_2_), channel_id=1, source_target_pairs={{0,4},{4,0},{8,12},{12,8},{1,5},{5,1},{9,13},{13,9},{2,6},{6,2},{1... | collective-permute-start | bytes 1376264 | tf_op jit(solution)/shard_map/ppermute | solution.py:292
  132.9 16.5 %collective-permute-start.53 = (bf16[2,32,3584]{2,1,0:T(8,128)(2,1)S(1)}, bf16[2,32,3584]{2,1,0:T(8,128)(2,1)S(1)}, u32[]{:S(2)}, u32[]{:S(2)}) collective-permute-start(bf16[2,32,3584]{2,1,0:T(8,128)(2,1)S(1)} %get-tuple-element.110.refs_10_), channel_id=1, source_target_pairs={{0,8},{4,12},{8,0},{12,4},{1,9},{5,13},{9,1},{13,5},{2,10},{6,14},... | collective-permute-start | bytes 1376264 | tf_op jit(solution)/shard_map/ppermute | solution.py:292
  133.4 15.7 %collective-permute-start.48 = (bf16[128,2048]{1,0:T(8,128)(2,1)S(1)}, bf16[128,2048]{1,0:T(8,128)(2,1)S(1)}, u32[]{:S(2)}, u32[]{:S(2)}) collective-permute-start(bf16[128,2048]{1,0:T(8,128)(2,1)S(1)} %get-tuple-element.114.refs_6_), channel_id=1, source_target_pairs={{0,1},{1,2},{2,3},{3,0},{4,5},{5,6},{6,7},{7,4},{8,9},{9,10},{10,1... | collective-permute-start | bytes 1572872 | tf_op jit(solution)/shard_map/ppermute | solution.py:289
  135.0 16.4 %copy-start.1 = (bf16[32,3584]{1,0:T(8,128)(2,1)S(1)}, bf16[32,3584]{1,0:T(8,128)(2,1)}, u32[]{:S(2)}) copy-start(bf16[32,3584]{1,0:T(8,128)(2,1)} %copy-done) | copy-start | bytes 688132
  149.8 7.7 %collective-permute-start.55 = (bf16[32,3584]{1,0:T(8,128)(2,1)S(1)}, bf16[32,3584]{1,0:T(8,128)(2,1)S(1)}, u32[]{:S(2)}, u32[]{:S(2)}) collective-permute-start(bf16[32,3584]{1,0:T(8,128)(2,1)S(1)} %activate.9.refs_6_.refs_0_), channel_id=1, source_target_pairs={{0,8},{4,12},{8,0},{12,4},{1,9},{5,13},{9,1},{13,5},{2,10},{6,14},... | collective-permute-start | bytes 688136 | tf_op jit(solution)/shard_map/ppermute | solution.py:292
  151.3 6.7 %collective-permute-start.54 = (bf16[32,3584]{1,0:T(8,128)(2,1)S(1)}, bf16[32,3584]{1,0:T(8,128)(2,1)S(1)}, u32[]{:S(2)}, u32[]{:S(2)}) collective-permute-start(bf16[32,3584]{1,0:T(8,128)(2,1)S(1)} %activate.9.refs_6_.refs_0_), channel_id=1, source_target_pairs={{0,4},{4,0},{8,12},{12,8},{1,5},{5,1},{9,13},{13,9},{2,6},{6,2},{1... | collective-permute-start | bytes 688136 | tf_op jit(solution)/shard_map/ppermute | solution.py:292
  151.3 16.1 %collective-permute-start.52 = (bf16[128,2048]{1,0:T(8,128)(2,1)S(1)}, bf16[128,2048]{1,0:T(8,128)(2,1)S(1)}, u32[]{:S(2)}, u32[]{:S(2)}) collective-permute-start(bf16[128,2048]{1,0:T(8,128)(2,1)S(1)} %add.3.refs_2_), channel_id=1, source_target_pairs={{0,1},{1,2},{2,3},{3,0},{4,5},{5,6},{6,7},{7,4},{8,9},{9,10},{10,1... | collective-permute-start | bytes 1572872 | tf_op jit(solution)/shard_map/ppermute | solution.py:289
  157.4 25.7 %copy-start.4 = (bf16[128,2048]{1,0:T(8,128)(2,1)S(1)}, bf16[128,2048]{1,0:T(8,128)(2,1)}, u32[]{:S(2)}) copy-start(bf16[128,2048]{1,0:T(8,128)(2,1)} %refs_0_.5) | copy-start | bytes 1572868
  157.5 1.7 collective-permute-start.56
  167.8 15.4 %collective-permute-start.57 = (bf16[128,2048]{1,0:T(8,128)(2,1)S(1)}, bf16[128,2048]{1,0:T(8,128)(2,1)S(1)}, u32[]{:S(2)}, u32[]{:S(2)}) collective-permute-start(bf16[128,2048]{1,0:T(8,128)(2,1)S(1)} %add.4.refs_3_), channel_id=1, source_target_pairs={{0,1},{1,2},{2,3},{3,0},{4,5},{5,6},{6,7},{7,4},{8,9},{9,10},{10,1... | collective-permute-start | bytes 1572872 | tf_op jit(solution)/shard_map/ppermute | solution.py:289

commit v8 on v7

--- a/solution.py
+++ b/solution.py
@@ -314,13 +314,20 @@
             last[:] = sends[:1]
             dotted[k] = keep, [swap(send, 0) for send in sends]
 
-        def sum_core(k):
+        def sum_core(k, held_back=0):
             keep, got = dotted[k]
             for bit in range(1, bits):
                 keep, send = fold(keep, got, last)
                 last[:] = [send]
+                if held_back and bit == bits - 1:
+                    folded[k] = keep, send
+                    return
                 got = [swap(send, bit)]
             folded[k] = keep, got[0]
+
+        def cross(k):
+            keep, send = folded[k]
+            folded[k] = keep, swap(lax.optimization_barrier((send, last[0]))[0], bits - 1)
 
         def act(k, parts=1):
             own = activate(*folded[k], parts, last)
@@ -332,10 +339,13 @@
             pieces[1] = [swap(piece, 0) for piece in own]
             hidden[k] = pieces
 
-        def forward(k):
+        total = {}
+
+        def forward(k, i=None):
             pieces = hidden[k]
+            first = [last[0]] if i is None else [last[0], total[i]]
             for j in range(2, n_pipe, 2):
-                pieces[j + 1] = [swap(lax.optimization_barrier((piece, last[0]))[0], 0) for piece in pieces[j]]
+                pieces[j + 1] = [swap(lax.optimization_barrier((piece, *first))[0], 0) for piece in pieces[j]]
 
         def need_partial(k):
             last.append(folded[k][1])
@@ -356,8 +366,6 @@
             last[:] = out[:1]
             sums.update(zip(rows, out))
 
-        total = {}
-
         def need(i):
             last.append(held[i])
 
@@ -380,9 +388,9 @@
             plan = [
                 (dot, 0), (sum_core, 0), (dot, 1), (act, 0), (sum_core, 1), (dot, 2), (need, 3),
                 (need_gathered, 0), (wait,), (forward, 0), (sum_core, 2), (need_partial, 1), (need_hidden, 0),
-                (dot, 3), (act, 1), (sum_core, 3), (need_partial, 2), (dot, 4), (act, 2, 2), (forward, 1),
-                (fill, 1), (act, 3), (sum_core, 4), (forward, 2), (fill, 2), (pass_on, 1), (forward, 3),
-                (down, 3), (pass_on, 2), (act, 4), (down, 0), (forward, 4), (fill, 4), (pass_on, 3),
+                (dot, 3), (act, 1, 2), (sum_core, 3, 1), (act, 2), (cross, 3), (dot, 4), (forward, 1),
+                (fill, 1), (forward, 2), (fill, 2), (pass_on, 1), (fill, 0), (act, 3), (sum_core, 4),
+                (forward, 3, 1), (fill, 3), (pass_on, 2), (act, 4), (forward, 4), (fill, 4), (pass_on, 3),
             ]
         else:
             plan = []

time: 184 us -> 182 us (0.989)
  waiting for transfers between devices: 55.9 us -> 53.9 us
    ppermute x6, waiting for transfers between devices: 24.7 us -> 15.4 us  [hop(): return lax.ppermute(value, 'tensor', ring)]
    ppermute x52, waiting for transfers between devices: 31.1 us -> 38.5 us  [swap(): lax.ppermute(value, 'pipe', [(i, i ^ 1 << bit) for i in range(n_pipe)])]
  transfers between devices with their start and end apart: 58 -> 58, of which waited for: 33 -> 32; matrix products, arithmetic and copies ran while one was open for 0% -> 0% of each run, Pallas kernels for 53% -> 54%
where the time goes in v8:
time: 182 us
  Pallas kernels  99.8 us (55%)
  waiting for transfers between devices  53.9 us (30%)
  starting transfers between devices  27 us (15%)
    pallas_call x5, Pallas kernels, first_dots(): pl.pallas_call(kernel, grid=(steps,), in_specs=[HBM if i in fixed else AN...  57.7 us
    ppermute x52, waiting for transfers between devices, swap(): lax.ppermute(value, 'pipe', [(i, i ^ 1 << bit) for i in range(n_pipe)])  38.5 us
    pallas_call x5, Pallas kernels, last_dot(): pl.pallas_call(kernel, grid=(steps,), in_specs=[ANY] * (n * count) + [HBM...  33.8 us
    ppermute x52, starting transfers between devices, swap(): lax.ppermute(value, 'pipe', [(i, i ^ 1 << bit) for i in range(n_pipe)])  18.3 us
    ppermute x6, waiting for transfers between devices, hop(): return lax.ppermute(value, 'tensor', ring)  15.4 us
    ppermute x6, starting transfers between devices, hop(): return lax.ppermute(value, 'tensor', ring)  8.71 us
    pallas_call x5, Pallas kernels, fold(): pl.pallas_call(kernel, grid=(width // step,), in_specs=[pl.BlockSpec((k,...  4.12 us
  transfers between devices with their start and end apart: 58, of which 32 were waited for; matrix products, arithmetic and copies ran while one was open for 0% of the time, Pallas kernels for 54%

profile of v8, /device:TPU:0, one launch (start us, length us, event | category | flops | bytes accessed | tf_op | source)
XLA Modules:
  0.0 182.0 jit_solution(11981332973741101208)
XLA Ops:
  0.0 3.0 %collective-permute-start = (bf16[128,2048]{1,0:T(8,128)(2,1)}, bf16[128,2048]{1,0:T(8,128)(2,1)S(1)}, u32[]{:S(2)}, u32[]{:S(2)}) collective-permute-start(bf16[128,2048]{1,0:T(8,128)(2,1)} %refs_0_.5), channel_id=1, source_target_pairs={{0,1},{1,2},{2,3},{3,0},{4,5},{5,6},{6,7},{7,4},{8,9},{9,10},{10,1... | collective-permute-start | bytes 1572872 | tf_op jit(solution)/shard_map/ppermute | solution.py:289
  3.0 1.1 copy-done
  4.1 10.5 %first_dots.5 = (bf16[2,64,3584]{2,1,0:T(8,128)(2,1)S(1)}, bf16[2,16,3584]{2,1,0:T(8,128)(2,1)S(1)}, bf16[2,16,3584]{2,1,0:T(8,128)(2,1)S(1)}, bf16[2,16,3584]{2,1,0:T(8,128)(2,1)S(1)}, bf16[2,16,3584]{2,1,0:T(8,128)(2,1)S(1)}) custom-call(bf16[128,2048]{1,0:T(8,128)(2,1)S(1)} %copy-done, bf16[2048,7168]{1,0:T(8,128)(2,1)} %refs_1_.3, bf16[2048,7168]{1,0:T(8,128)(2,1)} %refs_2_.9), custom_call_target="tpu_custom_call" | custom-call | flops 37580963840 | bytes 293601280 | tf_op jit(solution)/shard_map/first_dots/pallas_call | solution.py:89
  14.7 0.5 collective-permute-start.3
  15.3 0.4 collective-permute-start.5
  15.7 0.5 collective-permute-done.2.refs_1_
  16.8 0.3 collective-permute-done.5.refs_4_
  17.2 0.6 fold.5
  17.7 1.6 collective-permute-start.14
  19.3 1.6 collective-permute-start.1
  20.9 12.3 %first_dots.6 = (bf16[2,128,3584]{2,1,0:T(8,128)(2,1)S(1)}, bf16[2,16,3584]{2,1,0:T(8,128)(2,1)S(1)}, bf16[2,16,3584]{2,1,0:T(8,128)(2,1)S(1)}, bf16[2,16,3584]{...) custom-call(bf16[128,2048]{1,0:T(8,128)(2,1)S(1)} %copy-done.1, ...), custom_call_target="tpu_custom_call" | custom-call | flops 75161927680 | bytes 293601280 | tf_op jit(solution)/shard_map/first_dots/pallas_call | solution.py:89
  33.2 0.5 collective-permute-start.10
  33.8 0.4 collective-permute-start.12
  34.2 0.5 collective-permute-done.6.refs_1_
  35.9 0.3 activate.5.refs_9_.refs_0_
  36.2 0.6 collective-permute-start.24
  37.2 1.0 fold.6
  38.2 1.2 collective-permute-start.26
  39.5 1.6 collective-permute-start.23
  41.0 12.3 %first_dots.7 = (bf16[2,128,3584]{2,1,0:T(8,128)(2,1)S(1)}, bf16[2,16,3584]{2,1,0:T(8,128)(2,1)S(1)}, bf16[2,16,3584]{2,1,0:T(8,128)(2,1)S(1)}, bf16[2,16,3584]{...) custom-call(bf16[128,2048]{1,0:T(8,128)(2,1)S(1)} %collective-permut, ...), custom_call_target="tpu_custom_call" | custom-call | flops 75161927680 | bytes 293601280 | tf_op jit(solution)/shard_map/first_dots/pallas_call | solution.py:89
  53.4 0.5 collective-permute-start.16
  54.0 0.9 collective-permute-done.15.refs_1_
  55.9 0.5 collective-permute-done.18.refs_4_
  57.3 0.5 collective-permute-done.22.refs_8_
  57.9 1.0 fold.7
  58.9 0.9 collective-permute-start.25
  59.8 4.6 %collective-permute-done.26.refs_5_.refs_1_ = bf16[2,64,3584]{2,1,0:T(8,128)(2,1)S(1)} collective-permute-done((bf16[2,64,3584]{2,1,0:T(8,128)(2,1)S(1)}, bf16[2,64,3584]{2,1,0:T(8,128)(2,1)S(1)}, u32[]{:S(2)}, u32[]{:S(2)}) %collective-permute-start.26) | collective-permute-done | bytes 917536 | tf_op jit(solution)/shard_map/ppermute | solution.py:292
  64.4 12.2 %first_dots.8 = (bf16[2,128,3584]{2,1,0:T(8,128)(2,1)S(1)}, bf16[2,16,3584]{2,1,0:T(8,128)(2,1)S(1)}, bf16[2,16,3584]{2,1,0:T(8,128)(2,1)S(1)}, bf16[2,16,3584]{...) custom-call(bf16[128,2048]{1,0:T(8,128)(2,1)S(1)} %collective-permut, ...), custom_call_target="tpu_custom_call" | custom-call | flops 75161927680 | bytes 293601280 | tf_op jit(solution)/shard_map/first_dots/pallas_call | solution.py:89
  76.6 0.5 collective-permute-start.30
  77.2 0.4 collective-permute-start.32
  77.7 0.5 collective-permute-done.29.refs_1_
  79.3 0.6 activate.6
  79.9 0.6 collective-permute-start.41
  80.6 1.5 collective-permute-start.42
  82.1 1.0 fold.8
  83.1 0.8 collective-permute-done.25.refs_1_
  83.9 0.6 activate.7.refs_3_.refs_0_
  84.6 0.6 collective-permute-start.38
  85.2 1.5 collective-permute-start.47
  86.7 10.4 %first_dots.9 = (bf16[2,64,3584]{2,1,0:T(8,128)(2,1)S(1)}, bf16[2,64,3584]{2,1,0:T(8,128)(2,1)S(1)}) custom-call(bf16[128,2048]{1,0:T(8,128)(2,1)S(1)} %collective-permute-done.23.refs_1_.refs_0_, bf16[2048,7168]{1,0:T(8,128)(2,1)} %refs_1_.3, bf16[2048,7168]{1,0:T(8,128)(2,1)} %refs_2_.9, bf16[64,3584]{1,0:T(8,128)(2,1)S(1)} %activate.7.refs_3_.refs_0_), custom_call_target="tpu_custom_call" | custom-call | flops 37580963840 | bytes 293601280 | tf_op jit(solution)/shard_map/first_dots/pallas_call | solution.py:89
  97.2 0.5 collective-permute-start.44
  97.8 0.9 collective-permute-done.40.refs_3_
  99.3 7.8 %last_dot.5 = (f32[128,2048]{1,0:T(8,128)S(1)}, f32[128,2048]{1,0:T(8,128)S(1)}) custom-call(bf16[32,3584]{1,0:T(8,128)(2,1)S(1)} %get-tuple-element.103.refs_9_.refs_0_, bf16[32,3584]{1,0:T(8,128)(2,1)S(1)} %get-tuple-element.105.refs_1_, bf16[32,3584]{1,0:T(8,128)(2,1)S(1)} %collective-permute-done.39.refs_2_, ...), custom_call_target="tpu_custom_call" | custom-call | tf_op jit(solution)/shard_map/last_dot/pallas_call | solution.py:215
  107.7 1.3 collective-permute-done.45.refs_3_
  109.0 6.9 %last_dot.6 = (bf16[128,2048]{1,0:T(8,128)(2,1)S(1)}, f32[128,2048]{1,0:T(8,128)S(1)}) custom-call(bf16[64,3584]{1,0:T(8,128)(2,1)S(1)} %activate.7.refs_3_.refs_0_, bf16[64,3584]{1,0:T(8,128)(2,1)S(1)} %collective-permute-done.37.refs_1_, bf16[64,3584]{1,0:T(8,128)(2,1)S(1)} %collective-permute-done.38.refs_2_, ...), custom_call_target="tpu_custom_call" | custom-call | tf_op jit(solution)/shard_map/last_dot/pallas_call | solution.py:215
  116.0 1.6 collective-permute-start.46
  117.6 6.1 %last_dot.7.refs_2_ = bf16[128,2048]{1,0:T(8,128)(2,1)S(1)} custom-call(bf16[32,3584]{1,0:T(8,128)(2,1)S(1)} %activate.5.refs_9_.refs_0_, bf16[32,3584]{1,0:T(8,128)(2,1)S(1)} %collective-permute-done.27.refs_6_.refs_1_, bf16[32,3584]{1,0:T(8,128)(2,1)S(1)} %collective-permute-done.24.refs_2_.refs_7_, ...), custom_call_target="tpu_custom_call" | custom-call | tf_op jit(solution)/shard_map/last_dot/pallas_call | solution.py:215
  123.7 0.6 activate.8.refs_2_.refs_0_
  124.3 0.6 collective-permute-start.49
  124.9 0.5 fold.9
  125.4 11.3 %collective-permute-done.49.refs_2_ = bf16[64,3584]{1,0:T(8,128)(2,1)S(1)} collective-permute-done((bf16[64,3584]{1,0:T(8,128)(2,1)S(1)}, bf16[64,3584]{1,0:T(8,128)(2,1)S(1)}, u32[]{:S(2)}, u32[]{:S(2)}) %collective-permute-start.49) | collective-permute-done | bytes 458784 | tf_op jit(solution)/shard_map/ppermute | solution.py:292
  136.7 0.5 collective-permute-start.53
  137.2 1.3 collective-permute-done.51.refs_3_
  138.5 7.0 %last_dot.8 = (bf16[128,2048]{1,0:T(8,128)(2,1)S(1)}, f32[128,2048]{1,0:T(8,128)S(1)}) custom-call(bf16[64,3584]{1,0:T(8,128)(2,1)S(1)} %activate.8.refs_2_.refs_0_, bf16[64,3584]{1,0:T(8,128)(2,1)S(1)} %collective-permute-done.48.refs_1_, bf16[64,3584]{1,0:T(8,128)(2,1)S(1)} %collective-permute-done.49.refs_2_, ...), custom_call_target="tpu_custom_call" | custom-call | tf_op jit(solution)/shard_map/last_dot/pallas_call | solution.py:215
  145.8 0.4 collective-permute-start.52
  146.3 3.4 %collective-permute-done.53.refs_1_ = bf16[2,32,3584]{2,1,0:T(8,128)(2,1)S(1)} collective-permute-done((bf16[2,32,3584]{2,1,0:T(8,128)(2,1)S(1)}, bf16[2,32,3584]{2,1,0:T(8,128)(2,1)S(1)}, u32[]{:S(2)}, u32[]{:S(2)}) %collective-permute-start.53) | collective-permute-done | bytes 458784 | tf_op jit(solution)/shard_map/ppermute | solution.py:292
  149.6 0.4 activate.9.refs_0_.refs_6_
  150.0 0.6 collective-permute-start.55
  150.6 6.7 %collective-permute-done.55.refs_2_ = bf16[32,3584]{1,0:T(8,128)(2,1)S(1)} collective-permute-done((bf16[32,3584]{1,0:T(8,128)(2,1)S(1)}, bf16[32,3584]{1,0:T(8,128)(2,1)S(1)}, u32[]{:S(2)}, u32[]{:S(2)}) %collective-permute-start.55) | collective-permute-done | bytes 229408 | tf_op jit(solution)/shard_map/ppermute | solution.py:292
  157.3 1.5 collective-permute-done.56.refs_3_
  158.8 6.1 %last_dot.9.refs_1_.refs_2_ = bf16[128,2048]{1,0:T(8,128)(2,1)S(1)} custom-call(bf16[32,3584]{1,0:T(8,128)(2,1)S(1)} %activate.9.refs_0_.refs_6_, bf16[32,3584]{1,0:T(8,128)(2,1)S(1)} %collective-permute-done.54.refs_1_, bf16[32,3584]{1,0:T(8,128)(2,1)S(1)} %collective-permute-done.55.refs_2_, bf16[32,3584]{1,0:T(8,128)(2,1)S(1)} %collective-permute-done.56.refs_3_, ...), custom_call_target="tpu_custom_call" | custom-call | tf_op jit(solution)/shard_map/last_dot/pallas_call | solution.py:215
  165.2 0.5 collective-permute-start.57
  165.6 15.4 %collective-permute-done.57.refs_1_ = bf16[128,2048]{1,0:T(8,128)(2,1)S(1)} collective-permute-done((bf16[128,2048]{1,0:T(8,128)(2,1)S(1)}, bf16[128,2048]{1,0:T(8,128)(2,1)S(1)}, u32[]{:S(2)}, u32[]{:S(2)}) %collective-permute-start.57) | collective-permute-done | bytes 524320 | tf_op jit(solution)/shard_map/ppermute | solution.py:289
  181.0 1.0 add.5
  (82 shorter events, 8.0 us)
Async XLA Ops:
  0.0 19.3 %collective-permute-start = (bf16[128,2048]{1,0:T(8,128)(2,1)}, bf16[128,2048]{1,0:T(8,128)(2,1)S(1)}, u32[]{:S(2)}, u32[]{:S(2)}) collective-permute-start(bf16[128,2048]{1,0:T(8,128)(2,1)} %refs_0_.5), channel_id=1, source_target_pairs={{0,1},{1,2},{2,3},{3,0},{4,5},{5,6},{6,7},{7,4},{8,9},{9,10},{10,1... | collective-permute-start | bytes 1572872 | tf_op jit(solution)/shard_map/ppermute | solution.py:289
  3.0 1.1 copy-start
  4.1 16.8 %copy-start.1 = (bf16[128,2048]{1,0:T(8,128)(2,1)S(1)}, bf16[128,2048]{1,0:T(8,128)(2,1)}, u32[]{:S(2)}) copy-start(bf16[128,2048]{1,0:T(8,128)(2,1)} %refs_0_.5) | copy-start | bytes 1572868
  14.6 1.6 collective-permute-start.2
  14.7 1.8 collective-permute-start.3
  15.2 1.6 collective-permute-start.4
  15.3 1.9 %collective-permute-start.5 = (bf16[2,16,3584]{2,1,0:T(8,128)(2,1)S(1)}, bf16[2,16,3584]{2,1,0:T(8,128)(2,1)S(1)}, u32[]{:S(2)}, u32[]{:S(2)}) collective-permute-start(bf16[2,16,3584]{2,1,0:T(8,128)(2,1)S(1)} %get-tuple-element.68), channel_id=1, source_target_pairs={{0,4},{4,0},{8,12},{12,8},{1,5},{5,1},{9,13},{13,9},{2,6},{6,2},{1... | collective-permute-start | bytes 688136 | tf_op jit(solution)/shard_map/ppermute | solution.py:292
  17.7 16.1 %collective-permute-start.14 = (bf16[2,32,3584]{2,1,0:T(8,128)(2,1)S(1)}, bf16[2,32,3584]{2,1,0:T(8,128)(2,1)S(1)}, u32[]{:S(2)}, u32[]{:S(2)}) collective-permute-start(bf16[2,32,3584]{2,1,0:T(8,128)(2,1)S(1)} %get-tuple-element.69.refs_4_), channel_id=1, source_target_pairs={{0,8},{4,12},{8,0},{12,4},{1,9},{5,13},{9,1},{13,5},{2,10},{6,14},... | collective-permute-start | bytes 1376264 | tf_op jit(solution)/shard_map/ppermute | solution.py:292
  19.3 20.2 %collective-permute-start.1 = (bf16[128,2048]{1,0:T(8,128)(2,1)S(1)}, bf16[128,2048]{1,0:T(8,128)(2,1)S(1)}, u32[]{:S(2)}, u32[]{:S(2)}) collective-permute-start(bf16[128,2048]{1,0:T(8,128)(2,1)S(1)} %collective-permute-done.refs_1_.refs_0_), channel_id=1, source_target_pairs={{0,1},{1,2},{2,3},{3,0},{4,5},{5,6},{6,7},{7,4},{8,9},{9,10},{10,1... | collective-permute-start | bytes 1572872 | tf_op jit(solution)/shard_map/ppermute | solution.py:289
  33.1 1.6 collective-permute-start.6
  33.2 1.8 collective-permute-start.10
  33.7 1.6 collective-permute-start.11
  33.8 1.9 %collective-permute-start.12 = (bf16[2,16,3584]{2,1,0:T(8,128)(2,1)S(1)}, bf16[2,16,3584]{2,1,0:T(8,128)(2,1)S(1)}, u32[]{:S(2)}, u32[]{:S(2)}) collective-permute-start(bf16[2,16,3584]{2,1,0:T(8,128)(2,1)S(1)} %get-tuple-element.77), channel_id=1, source_target_pairs={{0,4},{4,0},{8,12},{12,8},{1,5},{5,1},{9,13},{13,9},{2,6},{6,2},{1... | collective-permute-start | bytes 688136 | tf_op jit(solution)/shard_map/ppermute | solution.py:292
  34.7 1.5 collective-permute-start.13
  35.0 1.8 collective-permute-start.7
  35.4 1.5 collective-permute-start.8
  35.7 1.5 collective-permute-start.9
  36.2 17.7 %collective-permute-start.24 = (bf16[32,3584]{1,0:T(8,128)(2,1)S(1)}, bf16[32,3584]{1,0:T(8,128)(2,1)S(1)}, u32[]{:S(2)}, u32[]{:S(2)}) collective-permute-start(bf16[32,3584]{1,0:T(8,128)(2,1)S(1)} %activate.5.refs_9_.refs_0_), channel_id=1, source_target_pairs={{0,8},{4,12},{8,0},{12,4},{1,9},{5,13},{9,1},{13,5},{2,10},{6,14},... | collective-permute-start | bytes 688136 | tf_op jit(solution)/shard_map/ppermute | solution.py:292
  38.2 26.2 %collective-permute-start.26 = (bf16[2,64,3584]{2,1,0:T(8,128)(2,1)S(1)}, bf16[2,64,3584]{2,1,0:T(8,128)(2,1)S(1)}, u32[]{:S(2)}, u32[]{:S(2)}) collective-permute-start(bf16[2,64,3584]{2,1,0:T(8,128)(2,1)S(1)} %get-tuple-element.80.refs_4_), channel_id=1, source_target_pairs={{0,8},{4,12},{8,0},{12,4},{1,9},{5,13},{9,1},{13,5},{2,10},{6,14},... | collective-permute-start | bytes 2752520 | tf_op jit(solution)/shard_map/ppermute | solution.py:292
  39.5 15.9 %collective-permute-start.23 = (bf16[128,2048]{1,0:T(8,128)(2,1)S(1)}, bf16[128,2048]{1,0:T(8,128)(2,1)S(1)}, u32[]{:S(2)}, u32[]{:S(2)}) collective-permute-start(bf16[128,2048]{1,0:T(8,128)(2,1)S(1)} %collective-permute-done.1.refs_1_.refs_0_), channel_id=1, source_target_pairs={{0,1},{1,2},{2,3},{3,0},{4,5},{5,6},{6,7},{7,4},{8,9},{9,10},{10,1... | collective-permute-start | bytes 1572872 | tf_op jit(solution)/shard_map/ppermute | solution.py:289
  53.3 1.6 collective-permute-start.15
  53.4 1.8 collective-permute-start.16
  53.9 1.8 %collective-permute-start.17 = (bf16[2,16,3584]{2,1,0:T(8,128)(2,1)S(1)}, bf16[2,16,3584]{2,1,0:T(8,128)(2,1)S(1)}, u32[]{:S(2)}, u32[]{:S(2)}) collective-permute-start(bf16[2,16,3584]{2,1,0:T(8,128)(2,1)S(1)} %get-tuple-element.84), channel_id=1, source_target_pairs={{0,4},{4,0},{8,12},{12,8},{1,5},{5,1},{9,13},{13,9},{2,6},{6,2},{1... | collective-permute-start | bytes 688136 | tf_op jit(solution)/shard_map/ppermute | solution.py:292
  54.9 1.5 collective-permute-start.18
  55.2 1.5 collective-permute-start.19
  55.4 1.6 collective-permute-start.20
  55.7 1.6 collective-permute-start.21
  56.4 1.5 collective-permute-start.22
  56.7 3.1 %collective-permute-start.27 = (bf16[32,3584]{1,0:T(8,128)(2,1)S(1)}, bf16[32,3584]{1,0:T(8,128)(2,1)S(1)}, u32[]{:S(2)}, u32[]{:S(2)}) collective-permute-start(bf16[32,3584]{1,0:T(8,128)(2,1)S(1)} %activate.5.refs_9_.refs_0_), channel_id=1, source_target_pairs={{0,4},{4,0},{8,12},{12,8},{1,5},{5,1},{9,13},{13,9},{2,6},{6,2},{1... | collective-permute-start | bytes 688136 | tf_op jit(solution)/shard_map/ppermute | solution.py:292
  57.0 7.4 %collective-permute-start.28 = (bf16[32,3584]{1,0:T(8,128)(2,1)S(1)}, bf16[32,3584]{1,0:T(8,128)(2,1)S(1)}, u32[]{:S(2)}, u32[]{:S(2)}) collective-permute-start(bf16[32,3584]{1,0:T(8,128)(2,1)S(1)} %collective-permute-done.24.refs_2_.refs_7_), channel_id=1, source_target_pairs={{0,4},{4,0},{8,12},{12,8},{1,5},{5,1},{9,13},{13,9},{2,6},{6,2},{1... | collective-permute-start | bytes 688136 | tf_op jit(solution)/shard_map/ppermute | solution.py:292
  58.9 25.1 %collective-permute-start.25 = (bf16[2,64,3584]{2,1,0:T(8,128)(2,1)S(1)}, bf16[2,64,3584]{2,1,0:T(8,128)(2,1)S(1)}, u32[]{:S(2)}, u32[]{:S(2)}) collective-permute-start(bf16[2,64,3584]{2,1,0:T(8,128)(2,1)S(1)} %get-tuple-element.91.refs_4_), channel_id=1, source_target_pairs={{0,8},{4,12},{8,0},{12,4},{1,9},{5,13},{9,1},{13,5},{2,10},{6,14},... | collective-permute-start | bytes 2752520 | tf_op jit(solution)/shard_map/ppermute | solution.py:292
  76.6 1.6 collective-permute-start.29
  76.6 1.8 collective-permute-start.30
  77.1 1.6 collective-permute-start.31
  77.2 1.9 %collective-permute-start.32 = (bf16[2,16,3584]{2,1,0:T(8,128)(2,1)S(1)}, bf16[2,16,3584]{2,1,0:T(8,128)(2,1)S(1)}, u32[]{:S(2)}, u32[]{:S(2)}) collective-permute-start(bf16[2,16,3584]{2,1,0:T(8,128)(2,1)S(1)} %get-tuple-element.97), channel_id=1, source_target_pairs={{0,4},{4,0},{8,12},{12,8},{1,5},{5,1},{9,13},{13,9},{2,6},{6,2},{1... | collective-permute-start | bytes 688136 | tf_op jit(solution)/shard_map/ppermute | solution.py:292
  78.1 1.8 collective-permute-start.33
  78.4 2.1 %collective-permute-start.34 = (bf16[2,16,3584]{2,1,0:T(8,128)(2,1)S(1)}, bf16[2,16,3584]{2,1,0:T(8,128)(2,1)S(1)}, u32[]{:S(2)}, u32[]{:S(2)}) collective-permute-start(bf16[2,16,3584]{2,1,0:T(8,128)(2,1)S(1)} %get-tuple-element.99), channel_id=1, source_target_pairs={{0,4},{4,0},{8,12},{12,8},{1,5},{5,1},{9,13},{13,9},{2,6},{6,2},{1... | collective-permute-start | bytes 688136 | tf_op jit(solution)/shard_map/ppermute | solution.py:292
  78.8 1.8 collective-permute-start.35
  79.1 3.0 %collective-permute-start.36 = (bf16[2,16,3584]{2,1,0:T(8,128)(2,1)S(1)}, bf16[2,16,3584]{2,1,0:T(8,128)(2,1)S(1)}, u32[]{:S(2)}, u32[]{:S(2)}) collective-permute-start(bf16[2,16,3584]{2,1,0:T(8,128)(2,1)S(1)} %get-tuple-element.101), channel_id=1, source_target_pairs={{0,4},{4,0},{8,12},{12,8},{1,5},{5,1},{9,13},{13,9},{2,6},{6,2},{1... | collective-permute-start | bytes 688136 | tf_op jit(solution)/shard_map/ppermute | solution.py:292
  79.9 17.3 %collective-permute-start.41 = (bf16[32,3584]{1,0:T(8,128)(2,1)S(1)}, bf16[32,3584]{1,0:T(8,128)(2,1)S(1)}, u32[]{:S(2)}, u32[]{:S(2)}) collective-permute-start(bf16[32,3584]{1,0:T(8,128)(2,1)S(1)} %get-tuple-element.103.refs_9_.refs_0_), channel_id=1, source_target_pairs={{0,8},{4,12},{8,0},{12,4},{1,9},{5,13},{9,1},{13,5},{2,10},{6,14},... | collective-permute-start | bytes 688136 | tf_op jit(solution)/shard_map/ppermute | solution.py:292
  80.5 17.2 %collective-permute-start.39 = (bf16[32,3584]{1,0:T(8,128)(2,1)S(1)}, bf16[32,3584]{1,0:T(8,128)(2,1)S(1)}, u32[]{:S(2)}, u32[]{:S(2)}) collective-permute-start(bf16[32,3584]{1,0:T(8,128)(2,1)S(1)} %get-tuple-element.103.refs_9_.refs_0_), channel_id=1, source_target_pairs={{0,4},{4,0},{8,12},{12,8},{1,5},{5,1},{9,13},{13,9},{2,6},{6,2},{1... | collective-permute-start | bytes 688136 | tf_op jit(solution)/shard_map/ppermute | solution.py:292
  80.6 16.5 %collective-permute-start.42 = (bf16[32,3584]{1,0:T(8,128)(2,1)S(1)}, bf16[32,3584]{1,0:T(8,128)(2,1)S(1)}, u32[]{:S(2)}, u32[]{:S(2)}) collective-permute-start(bf16[32,3584]{1,0:T(8,128)(2,1)S(1)} %get-tuple-element.105.refs_1_), channel_id=1, source_target_pairs={{0,8},{4,12},{8,0},{12,4},{1,9},{5,13},{9,1},{13,5},{2,10},{6,14},... | collective-permute-start | bytes 688136 | tf_op jit(solution)/shard_map/ppermute | solution.py:292
  84.6 22.6 %collective-permute-start.38 = (bf16[64,3584]{1,0:T(8,128)(2,1)S(1)}, bf16[64,3584]{1,0:T(8,128)(2,1)S(1)}, u32[]{:S(2)}, u32[]{:S(2)}) collective-permute-start(bf16[64,3584]{1,0:T(8,128)(2,1)S(1)} %activate.7.refs_3_.refs_0_), channel_id=1, source_target_pairs={{0,8},{4,12},{8,0},{12,4},{1,9},{5,13},{9,1},{13,5},{2,10},{6,14},... | collective-permute-start | bytes 1376264 | tf_op jit(solution)/shard_map/ppermute | solution.py:292
  85.2 38.5 %collective-permute-start.47 = (bf16[2,64,3584]{2,1,0:T(8,128)(2,1)S(1)}, bf16[2,64,3584]{2,1,0:T(8,128)(2,1)S(1)}, u32[]{:S(2)}, u32[]{:S(2)}) collective-permute-start(bf16[2,64,3584]{2,1,0:T(8,128)(2,1)S(1)} %get-tuple-element.114.refs_2_), channel_id=1, source_target_pairs={{0,8},{4,12},{8,0},{12,4},{1,9},{5,13},{9,1},{13,5},{2,10},{6,14},... | collective-permute-start | bytes 2752520 | tf_op jit(solution)/shard_map/ppermute | solution.py:292
  97.1 1.6 collective-permute-start.40
  97.2 1.8 collective-permute-start.44
  97.7 1.6 collective-permute-start.43
  98.7 9.1 %collective-permute-start.37 = (bf16[64,3584]{1,0:T(8,128)(2,1)S(1)}, bf16[64,3584]{1,0:T(8,128)(2,1)S(1)}, u32[]{:S(2)}, u32[]{:S(2)}) collective-permute-start(bf16[64,3584]{1,0:T(8,128)(2,1)S(1)} %activate.7.refs_3_.refs_0_), channel_id=1, source_target_pairs={{0,4},{4,0},{8,12},{12,8},{1,5},{5,1},{9,13},{13,9},{2,6},{6,2},{1... | collective-permute-start | bytes 1376264 | tf_op jit(solution)/shard_map/ppermute | solution.py:292
  107.2 1.9 %collective-permute-start.45 = (bf16[64,3584]{1,0:T(8,128)(2,1)S(1)}, bf16[64,3584]{1,0:T(8,128)(2,1)S(1)}, u32[]{:S(2)}, u32[]{:S(2)}) collective-permute-start(bf16[64,3584]{1,0:T(8,128)(2,1)S(1)} %collective-permute-done.38.refs_2_), channel_id=1, source_target_pairs={{0,4},{4,0},{8,12},{12,8},{1,5},{5,1},{9,13},{13,9},{2,6},{6,2},{1... | collective-permute-start | bytes 1376264 | tf_op jit(solution)/shard_map/ppermute | solution.py:292
  107.4 17.5 %collective-permute-start.50 = (bf16[2,64,3584]{2,1,0:T(8,128)(2,1)S(1)}, bf16[2,64,3584]{2,1,0:T(8,128)(2,1)S(1)}, u32[]{:S(2)}, u32[]{:S(2)}) collective-permute-start(bf16[2,64,3584]{2,1,0:T(8,128)(2,1)S(1)} %get-tuple-element.106.refs_9_), channel_id=1, source_target_pairs={{0,4},{4,0},{8,12},{12,8},{1,5},{5,1},{9,13},{13,9},{2,6},{6,2},{1... | collective-permute-start | bytes 2752520 | tf_op jit(solution)/shard_map/ppermute | solution.py:292
  116.0 20.7 %collective-permute-start.46 = (bf16[128,2048]{1,0:T(8,128)(2,1)S(1)}, bf16[128,2048]{1,0:T(8,128)(2,1)S(1)}, u32[]{:S(2)}, u32[]{:S(2)}) collective-permute-start(bf16[128,2048]{1,0:T(8,128)(2,1)S(1)} %get-tuple-element.112.refs_6_), channel_id=1, source_target_pairs={{0,1},{1,2},{2,3},{3,0},{4,5},{5,6},{6,7},{7,4},{8,9},{9,10},{10,1... | collective-permute-start | bytes 1572872 | tf_op jit(solution)/shard_map/ppermute | solution.py:289
  124.3 12.4 %collective-permute-start.49 = (bf16[64,3584]{1,0:T(8,128)(2,1)S(1)}, bf16[64,3584]{1,0:T(8,128)(2,1)S(1)}, u32[]{:S(2)}, u32[]{:S(2)}) collective-permute-start(bf16[64,3584]{1,0:T(8,128)(2,1)S(1)} %activate.8.refs_2_.refs_0_), channel_id=1, source_target_pairs={{0,8},{4,12},{8,0},{12,4},{1,9},{5,13},{9,1},{13,5},{2,10},{6,14},... | collective-permute-start | bytes 1376264 | tf_op jit(solution)/shard_map/ppermute | solution.py:292
  124.9 12.3 %collective-permute-start.48 = (bf16[64,3584]{1,0:T(8,128)(2,1)S(1)}, bf16[64,3584]{1,0:T(8,128)(2,1)S(1)}, u32[]{:S(2)}, u32[]{:S(2)}) collective-permute-start(bf16[64,3584]{1,0:T(8,128)(2,1)S(1)} %activate.8.refs_2_.refs_0_), channel_id=1, source_target_pairs={{0,4},{4,0},{8,12},{12,8},{1,5},{5,1},{9,13},{13,9},{2,6},{6,2},{1... | collective-permute-start | bytes 1376264 | tf_op jit(solution)/shard_map/ppermute | solution.py:292
  136.7 1.8 collective-permute-start.51
  136.7 12.9 %collective-permute-start.53 = (bf16[2,32,3584]{2,1,0:T(8,128)(2,1)S(1)}, bf16[2,32,3584]{2,1,0:T(8,128)(2,1)S(1)}, u32[]{:S(2)}, u32[]{:S(2)}) collective-permute-start(bf16[2,32,3584]{2,1,0:T(8,128)(2,1)S(1)} %get-tuple-element.116.refs_6_), channel_id=1, source_target_pairs={{0,8},{4,12},{8,0},{12,4},{1,9},{5,13},{9,1},{13,5},{2,10},{6,14},... | collective-permute-start | bytes 1376264 | tf_op jit(solution)/shard_map/ppermute | solution.py:292
  138.5 42.5 %copy-start.2 = (bf16[128,2048]{1,0:T(8,128)(2,1)S(1)}, bf16[128,2048]{1,0:T(8,128)(2,1)}, u32[]{:S(2)}) copy-start(bf16[128,2048]{1,0:T(8,128)(2,1)} %refs_0_.5) | copy-start | bytes 1572868
  145.8 19.1 %collective-permute-start.52 = (bf16[128,2048]{1,0:T(8,128)(2,1)S(1)}, bf16[128,2048]{1,0:T(8,128)(2,1)S(1)}, u32[]{:S(2)}, u32[]{:S(2)}) collective-permute-start(bf16[128,2048]{1,0:T(8,128)(2,1)S(1)} %add.3.refs_2_), channel_id=1, source_target_pairs={{0,1},{1,2},{2,3},{3,0},{4,5},{5,6},{6,7},{7,4},{8,9},{9,10},{10,1... | collective-permute-start | bytes 1572872 | tf_op jit(solution)/shard_map/ppermute | solution.py:289
  150.0 7.3 %collective-permute-start.55 = (bf16[32,3584]{1,0:T(8,128)(2,1)S(1)}, bf16[32,3584]{1,0:T(8,128)(2,1)S(1)}, u32[]{:S(2)}, u32[]{:S(2)}) collective-permute-start(bf16[32,3584]{1,0:T(8,128)(2,1)S(1)} %activate.9.refs_0_.refs_6_), channel_id=1, source_target_pairs={{0,8},{4,12},{8,0},{12,4},{1,9},{5,13},{9,1},{13,5},{2,10},{6,14},... | collective-permute-start | bytes 688136 | tf_op jit(solution)/shard_map/ppermute | solution.py:292
  150.6 6.7 %collective-permute-start.54 = (bf16[32,3584]{1,0:T(8,128)(2,1)S(1)}, bf16[32,3584]{1,0:T(8,128)(2,1)S(1)}, u32[]{:S(2)}, u32[]{:S(2)}) collective-permute-start(bf16[32,3584]{1,0:T(8,128)(2,1)S(1)} %activate.9.refs_0_.refs_6_), channel_id=1, source_target_pairs={{0,4},{4,0},{8,12},{12,8},{1,5},{5,1},{9,13},{13,9},{2,6},{6,2},{1... | collective-permute-start | bytes 688136 | tf_op jit(solution)/shard_map/ppermute | solution.py:292
  157.3 1.5 collective-permute-start.56
  165.2 15.8 %collective-permute-start.57 = (bf16[128,2048]{1,0:T(8,128)(2,1)S(1)}, bf16[128,2048]{1,0:T(8,128)(2,1)S(1)}, u32[]{:S(2)}, u32[]{:S(2)}) collective-permute-start(bf16[128,2048]{1,0:T(8,128)(2,1)S(1)} %add.4.refs_3_), channel_id=1, source_target_pairs={{0,1},{1,2},{2,3},{3,0},{4,5},{5,6},{6,7},{7,4},{8,9},{9,10},{10,1... | collective-permute-start | bytes 1572872 | tf_op jit(solution)/shard_map/ppermute | solution.py:289

commit v9 on v8

--- a/solution.py
+++ b/solution.py
@@ -389,8 +389,8 @@
                 (dot, 0), (sum_core, 0), (dot, 1), (act, 0), (sum_core, 1), (dot, 2), (need, 3),
                 (need_gathered, 0), (wait,), (forward, 0), (sum_core, 2), (need_partial, 1), (need_hidden, 0),
                 (dot, 3), (act, 1, 2), (sum_core, 3, 1), (act, 2), (cross, 3), (dot, 4), (forward, 1),
-                (fill, 1), (forward, 2), (fill, 2), (pass_on, 1), (fill, 0), (act, 3), (sum_core, 4),
-                (forward, 3, 1), (fill, 3), (pass_on, 2), (act, 4), (forward, 4), (fill, 4), (pass_on, 3),
+                (fill, 1), (forward, 2), (fill, 2), (pass_on, 1), (act, 3, 2), (sum_core, 4), (forward, 3),
+                (fill, 3), (pass_on, 2), (act, 4), (fill, 0), (forward, 4), (fill, 4), (pass_on, 3),
             ]
         else:
             plan = []

time: 182 us -> 181 us (level)
  waiting for transfers between devices: 53.9 us -> 49.7 us
  starting transfers between devices: 27 us -> 29.3 us
    ppermute x52 -> x55, waiting for transfers between devices: 38.5 us -> 34.2 us  [swap(): lax.ppermute(value, 'pipe', [(i, i ^ 1 << bit) for i in range(n_pipe)])]
    ppermute x52 -> x55, starting transfers between devices: 18.3 us -> 19.5 us  [swap(): lax.ppermute(value, 'pipe', [(i, i ^ 1 << bit) for i in range(n_pipe)])]
  transfers between devices with their start and end apart: 58 -> 61, of which waited for: 32 -> 34; matrix products, arithmetic and copies ran while one was open for 0% -> 0% of each run, Pallas kernels for 54% -> 55%
where the time goes in v9:
time: 181 us
  Pallas kernels  101 us (56%)
  waiting for transfers between devices  49.7 us (27%)
  starting transfers between devices  29.3 us (16%)
    pallas_call x5, Pallas kernels, first_dots(): pl.pallas_call(kernel, grid=(steps,), in_specs=[HBM if i in fixed else AN...  57.7 us
    pallas_call x5, Pallas kernels, last_dot(): pl.pallas_call(kernel, grid=(steps,), in_specs=[ANY] * (n * count) + [HBM...  34.7 us
    ppermute x55, waiting for transfers between devices, swap(): lax.ppermute(value, 'pipe', [(i, i ^ 1 << bit) for i in range(n_pipe)])  34.2 us
    ppermute x55, starting transfers between devices, swap(): lax.ppermute(value, 'pipe', [(i, i ^ 1 << bit) for i in range(n_pipe)])  19.5 us
    ppermute x6, waiting for transfers between devices, hop(): return lax.ppermute(value, 'tensor', ring)  15.5 us
    ppermute x6, starting transfers between devices, hop(): return lax.ppermute(value, 'tensor', ring)  9.81 us
    pallas_call x5, Pallas kernels, fold(): pl.pallas_call(kernel, grid=(width // step,), in_specs=[pl.BlockSpec((k,...  4.12 us
  transfers between devices with their start and end apart: 61, of which 34 were waited for; matrix products, arithmetic and copies ran while one was open for 0% of the time, Pallas kernels for 55%

profile of v9, /device:TPU:0, one launch (start us, length us, event | category | flops | bytes accessed | tf_op | source)
XLA Modules:
  0.0 181.1 jit_solution(14138428294679667925)
XLA Ops:
  0.0 3.0 %collective-permute-start = (bf16[128,2048]{1,0:T(8,128)(2,1)}, bf16[128,2048]{1,0:T(8,128)(2,1)S(1)}, u32[]{:S(2)}, u32[]{:S(2)}) collective-permute-start(bf16[128,2048]{1,0:T(8,128)(2,1)} %refs_0_.5), channel_id=1, source_target_pairs={{0,1},{1,2},{2,3},{3,0},{4,5},{5,6},{6,7},{7,4},{8,9},{9,10},{10,1... | collective-permute-start | bytes 1572872 | tf_op jit(solution)/shard_map/ppermute | solution.py:289
  3.0 1.1 copy-done
  4.1 10.5 %first_dots.5 = (bf16[2,64,3584]{2,1,0:T(8,128)(2,1)S(1)}, bf16[2,16,3584]{2,1,0:T(8,128)(2,1)S(1)}, bf16[2,16,3584]{2,1,0:T(8,128)(2,1)S(1)}, bf16[2,16,3584]{2,1,0:T(8,128)(2,1)S(1)}, bf16[2,16,3584]{2,1,0:T(8,128)(2,1)S(1)}) custom-call(bf16[128,2048]{1,0:T(8,128)(2,1)S(1)} %copy-done, bf16[2048,7168]{1,0:T(8,128)(2,1)} %refs_1_.3, bf16[2048,7168]{1,0:T(8,128)(2,1)} %refs_2_.9), custom_call_target="tpu_custom_call" | custom-call | flops 37580963840 | bytes 293601280 | tf_op jit(solution)/shard_map/first_dots/pallas_call | solution.py:89
  14.7 0.5 collective-permute-start.3
  15.3 0.4 collective-permute-start.5
  15.7 0.5 collective-permute-done.2.refs_1_
  17.2 0.6 fold.5
  17.7 1.6 collective-permute-start.14
  19.3 1.6 collective-permute-start.1
  20.9 12.3 %first_dots.6 = (bf16[2,128,3584]{2,1,0:T(8,128)(2,1)S(1)}, bf16[2,16,3584]{2,1,0:T(8,128)(2,1)S(1)}, bf16[2,16,3584]{2,1,0:T(8,128)(2,1)S(1)}, bf16[2,16,3584]{...) custom-call(bf16[128,2048]{1,0:T(8,128)(2,1)S(1)} %copy-done.1, ...), custom_call_target="tpu_custom_call" | custom-call | flops 75161927680 | bytes 293601280 | tf_op jit(solution)/shard_map/first_dots/pallas_call | solution.py:89
  33.2 0.5 collective-permute-start.10
  33.8 0.4 collective-permute-start.12
  34.2 0.5 collective-permute-done.6.refs_1_
  36.2 0.6 collective-permute-start.24
  37.2 1.0 fold.6
  38.2 1.2 collective-permute-start.26
  39.5 1.6 collective-permute-start.23
  41.0 12.3 %first_dots.7 = (bf16[2,128,3584]{2,1,0:T(8,128)(2,1)S(1)}, bf16[2,16,3584]{2,1,0:T(8,128)(2,1)S(1)}, bf16[2,16,3584]{2,1,0:T(8,128)(2,1)S(1)}, bf16[2,16,3584]{...) custom-call(bf16[128,2048]{1,0:T(8,128)(2,1)S(1)} %collective-permut, ...), custom_call_target="tpu_custom_call" | custom-call | flops 75161927680 | bytes 293601280 | tf_op jit(solution)/shard_map/first_dots/pallas_call | solution.py:89
  53.4 0.5 collective-permute-start.16
  54.0 0.9 collective-permute-done.15.refs_1_
  55.9 0.5 collective-permute-done.18.refs_4_
  57.3 0.5 collective-permute-done.22.refs_8_
  57.9 1.0 fold.7
  58.9 0.9 collective-permute-start.25
  59.8 4.6 %collective-permute-done.26.refs_5_.refs_1_ = bf16[2,64,3584]{2,1,0:T(8,128)(2,1)S(1)} collective-permute-done((bf16[2,64,3584]{2,1,0:T(8,128)(2,1)S(1)}, bf16[2,64,3584]{2,1,0:T(8,128)(2,1)S(1)}, u32[]{:S(2)}, u32[]{:S(2)}) %collective-permute-start.26) | collective-permute-done | bytes 917536 | tf_op jit(solution)/shard_map/ppermute | solution.py:292
  64.4 12.2 %first_dots.8 = (bf16[2,128,3584]{2,1,0:T(8,128)(2,1)S(1)}, bf16[2,16,3584]{2,1,0:T(8,128)(2,1)S(1)}, bf16[2,16,3584]{2,1,0:T(8,128)(2,1)S(1)}, bf16[2,16,3584]{...) custom-call(bf16[128,2048]{1,0:T(8,128)(2,1)S(1)} %collective-permut, ...), custom_call_target="tpu_custom_call" | custom-call | flops 75161927680 | bytes 293601280 | tf_op jit(solution)/shard_map/first_dots/pallas_call | solution.py:89
  76.6 0.5 collective-permute-start.30
  77.2 0.4 collective-permute-start.32
  77.7 0.5 collective-permute-done.29.refs_1_
  79.3 0.6 activate.6
  79.9 0.6 collective-permute-start.42
  80.5 1.5 collective-permute-start.41
  82.0 0.5 collective-permute-start.40
  82.5 1.0 fold.8
  83.9 0.6 activate.7.refs_3_.refs_0_
  84.6 0.6 collective-permute-start.38
  85.2 3.7 %collective-permute-done.42.refs_5_ = bf16[32,3584]{1,0:T(8,128)(2,1)S(1)} collective-permute-done((bf16[32,3584]{1,0:T(8,128)(2,1)S(1)}, bf16[32,3584]{1,0:T(8,128)(2,1)S(1)}, u32[]{:S(2)}, u32[]{:S(2)}) %collective-permute-start.42) | collective-permute-done | bytes 229408 | tf_op jit(solution)/shard_map/ppermute | solution.py:292
  88.9 0.5 collective-permute-start.47
  89.4 10.4 %first_dots.9 = (bf16[2,64,3584]{2,1,0:T(8,128)(2,1)S(1)}, bf16[2,64,3584]{2,1,0:T(8,128)(2,1)S(1)}) custom-call(bf16[128,2048]{1,0:T(8,128)(2,1)S(1)} %collective-permute-done.23.refs_1_.refs_0_, bf16[2048,7168]{1,0:T(8,128)(2,1)} %refs_1_.3, bf16[2048,7168]{1,0:T(8,128)(2,1)} %refs_2_.9, bf16[64,3584]{1,0:T(8,128)(2,1)S(1)} %activate.7.refs_3_.refs_0_), custom_call_target="tpu_custom_call" | custom-call | flops 37580963840 | bytes 293601280 | tf_op jit(solution)/shard_map/first_dots/pallas_call | solution.py:89
  99.9 0.5 collective-permute-start.44
  100.5 2.2 %collective-permute-done.44.refs_7_ = bf16[32,3584]{1,0:T(8,128)(2,1)S(1)} collective-permute-done((bf16[32,3584]{1,0:T(8,128)(2,1)S(1)}, bf16[32,3584]{1,0:T(8,128)(2,1)S(1)}, u32[]{:S(2)}, u32[]{:S(2)}) %collective-permute-start.44) | collective-permute-done | bytes 229408 | tf_op jit(solution)/shard_map/ppermute | solution.py:292
  103.0 7.8 %last_dot.5 = (f32[128,2048]{1,0:T(8,128)S(1)}, f32[128,2048]{1,0:T(8,128)S(1)}) custom-call(bf16[32,3584]{1,0:T(8,128)(2,1)S(1)} %get-tuple-element.106.refs_9_.refs_0_, bf16[32,3584]{1,0:T(8,128)(2,1)S(1)} %get-tuple-element.108.refs_1_, bf16[32,3584]{1,0:T(8,128)(2,1)S(1)} %collective-permute-done.39.refs_2_, ...), custom_call_target="tpu_custom_call" | custom-call | tf_op jit(solution)/shard_map/last_dot/pallas_call | solution.py:215
  111.1 1.6 collective-permute-done.45.refs_3_
  112.8 6.9 %last_dot.6 = (bf16[128,2048]{1,0:T(8,128)(2,1)S(1)}, f32[128,2048]{1,0:T(8,128)S(1)}) custom-call(bf16[64,3584]{1,0:T(8,128)(2,1)S(1)} %activate.7.refs_3_.refs_0_, bf16[64,3584]{1,0:T(8,128)(2,1)S(1)} %collective-permute-done.37.refs_1_, bf16[64,3584]{1,0:T(8,128)(2,1)S(1)} %collective-permute-done.38.refs_2_, ...), custom_call_target="tpu_custom_call" | custom-call | tf_op jit(solution)/shard_map/last_dot/pallas_call | solution.py:215
  119.7 1.6 collective-permute-start.46
  121.3 1.5 collective-permute-done.47.refs_1_
  122.8 0.6 activate.8
  123.4 0.6 collective-permute-start.51
  124.0 1.5 collective-permute-start.50
  125.5 0.5 fold.9
  126.1 0.6 collective-permute-start.56
  126.7 5.4 %collective-permute-done.51.refs_5_ = bf16[32,3584]{1,0:T(8,128)(2,1)S(1)} collective-permute-done((bf16[32,3584]{1,0:T(8,128)(2,1)S(1)}, bf16[32,3584]{1,0:T(8,128)(2,1)S(1)}, u32[]{:S(2)}, u32[]{:S(2)}) %collective-permute-start.51) | collective-permute-done | bytes 229408 | tf_op jit(solution)/shard_map/ppermute | solution.py:292
  132.0 4.9 %collective-permute-done.50.refs_4_ = bf16[32,3584]{1,0:T(8,128)(2,1)S(1)} collective-permute-done((bf16[32,3584]{1,0:T(8,128)(2,1)S(1)}, bf16[32,3584]{1,0:T(8,128)(2,1)S(1)}, u32[]{:S(2)}, u32[]{:S(2)}) %collective-permute-start.50) | collective-permute-done | bytes 229408 | tf_op jit(solution)/shard_map/ppermute | solution.py:292
  136.9 0.5 collective-permute-start.53
  137.4 1.0 collective-permute-done.54.refs_7_
  138.7 7.8 %last_dot.7 = (bf16[128,2048]{1,0:T(8,128)(2,1)S(1)}, f32[128,2048]{1,0:T(8,128)S(1)}) custom-call(bf16[32,3584]{1,0:T(8,128)(2,1)S(1)} %get-tuple-element.118.refs_2_.refs_0_, bf16[32,3584]{1,0:T(8,128)(2,1)S(1)} %get-tuple-element.119.refs_1_, bf16[32,3584]{1,0:T(8,128)(2,1)S(1)} %collective-permute-done.48.refs_2_, ...), custom_call_target="tpu_custom_call" | custom-call | tf_op jit(solution)/shard_map/last_dot/pallas_call | solution.py:215
  146.9 1.6 collective-permute-start.55
  148.9 0.6 collective-permute-start.58
  149.5 6.1 %last_dot.8.refs_6_.refs_2_ = bf16[128,2048]{1,0:T(8,128)(2,1)S(1)} custom-call(bf16[32,3584]{1,0:T(8,128)(2,1)S(1)} %activate.5.refs_9_.refs_0_, bf16[32,3584]{1,0:T(8,128)(2,1)S(1)} %collective-permute-done.27.refs_6_.refs_1_, bf16[32,3584]{1,0:T(8,128)(2,1)S(1)} %collective-permute-done.24.refs_2_.refs_7_, ...), custom_call_target="tpu_custom_call" | custom-call | tf_op jit(solution)/shard_map/last_dot/pallas_call | solution.py:215
  155.6 0.8 collective-permute-done.58.refs_2_
  156.4 1.5 collective-permute-done.59.refs_3_
  157.9 6.1 %last_dot.9.refs_1_.refs_2_ = bf16[128,2048]{1,0:T(8,128)(2,1)S(1)} custom-call(bf16[32,3584]{1,0:T(8,128)(2,1)S(1)} %activate.9.refs_6_.refs_0_, bf16[32,3584]{1,0:T(8,128)(2,1)S(1)} %collective-permute-done.57.refs_1_, bf16[32,3584]{1,0:T(8,128)(2,1)S(1)} %collective-permute-done.58.refs_2_, bf16[32,3584]{1,0:T(8,128)(2,1)S(1)} %collective-permute-done.59.refs_3_, ...), custom_call_target="tpu_custom_call" | custom-call | tf_op jit(solution)/shard_map/last_dot/pallas_call | solution.py:215
  164.6 15.5 %collective-permute-done.60.refs_1_ = bf16[128,2048]{1,0:T(8,128)(2,1)S(1)} collective-permute-done((bf16[128,2048]{1,0:T(8,128)(2,1)S(1)}, bf16[128,2048]{1,0:T(8,128)(2,1)S(1)}, u32[]{:S(2)}, u32[]{:S(2)}) %collective-permute-start.60) | collective-permute-done | bytes 524320 | tf_op jit(solution)/shard_map/ppermute | solution.py:289
  180.1 1.0 add.5
  (88 shorter events, 9.4 us)
Async XLA Ops:
  0.0 19.3 %collective-permute-start = (bf16[128,2048]{1,0:T(8,128)(2,1)}, bf16[128,2048]{1,0:T(8,128)(2,1)S(1)}, u32[]{:S(2)}, u32[]{:S(2)}) collective-permute-start(bf16[128,2048]{1,0:T(8,128)(2,1)} %refs_0_.5), channel_id=1, source_target_pairs={{0,1},{1,2},{2,3},{3,0},{4,5},{5,6},{6,7},{7,4},{8,9},{9,10},{10,1... | collective-permute-start | bytes 1572872 | tf_op jit(solution)/shard_map/ppermute | solution.py:289
  3.0 1.1 copy-start
  4.1 16.8 %copy-start.1 = (bf16[128,2048]{1,0:T(8,128)(2,1)S(1)}, bf16[128,2048]{1,0:T(8,128)(2,1)}, u32[]{:S(2)}) copy-start(bf16[128,2048]{1,0:T(8,128)(2,1)} %refs_0_.5) | copy-start | bytes 1572868
  14.6 1.6 collective-permute-start.2
  14.7 1.8 collective-permute-start.3
  15.2 1.6 collective-permute-start.4
  15.3 1.9 %collective-permute-start.5 = (bf16[2,16,3584]{2,1,0:T(8,128)(2,1)S(1)}, bf16[2,16,3584]{2,1,0:T(8,128)(2,1)S(1)}, u32[]{:S(2)}, u32[]{:S(2)}) collective-permute-start(bf16[2,16,3584]{2,1,0:T(8,128)(2,1)S(1)} %get-tuple-element.71), channel_id=1, source_target_pairs={{0,4},{4,0},{8,12},{12,8},{1,5},{5,1},{9,13},{13,9},{2,6},{6,2},{1... | collective-permute-start | bytes 688136 | tf_op jit(solution)/shard_map/ppermute | solution.py:292
  17.7 16.1 %collective-permute-start.14 = (bf16[2,32,3584]{2,1,0:T(8,128)(2,1)S(1)}, bf16[2,32,3584]{2,1,0:T(8,128)(2,1)S(1)}, u32[]{:S(2)}, u32[]{:S(2)}) collective-permute-start(bf16[2,32,3584]{2,1,0:T(8,128)(2,1)S(1)} %get-tuple-element.72.refs_4_), channel_id=1, source_target_pairs={{0,8},{4,12},{8,0},{12,4},{1,9},{5,13},{9,1},{13,5},{2,10},{6,14},... | collective-permute-start | bytes 1376264 | tf_op jit(solution)/shard_map/ppermute | solution.py:292
  19.3 20.2 %collective-permute-start.1 = (bf16[128,2048]{1,0:T(8,128)(2,1)S(1)}, bf16[128,2048]{1,0:T(8,128)(2,1)S(1)}, u32[]{:S(2)}, u32[]{:S(2)}) collective-permute-start(bf16[128,2048]{1,0:T(8,128)(2,1)S(1)} %collective-permute-done.refs_1_.refs_0_), channel_id=1, source_target_pairs={{0,1},{1,2},{2,3},{3,0},{4,5},{5,6},{6,7},{7,4},{8,9},{9,10},{10,1... | collective-permute-start | bytes 1572872 | tf_op jit(solution)/shard_map/ppermute | solution.py:289
  33.1 1.6 collective-permute-start.6
  33.2 1.8 collective-permute-start.10
  33.7 1.6 collective-permute-start.11
  33.8 1.9 %collective-permute-start.12 = (bf16[2,16,3584]{2,1,0:T(8,128)(2,1)S(1)}, bf16[2,16,3584]{2,1,0:T(8,128)(2,1)S(1)}, u32[]{:S(2)}, u32[]{:S(2)}) collective-permute-start(bf16[2,16,3584]{2,1,0:T(8,128)(2,1)S(1)} %get-tuple-element.80), channel_id=1, source_target_pairs={{0,4},{4,0},{8,12},{12,8},{1,5},{5,1},{9,13},{13,9},{2,6},{6,2},{1... | collective-permute-start | bytes 688136 | tf_op jit(solution)/shard_map/ppermute | solution.py:292
  34.7 1.5 collective-permute-start.13
  35.0 1.8 %collective-permute-start.7 = (bf16[2,16,3584]{2,1,0:T(8,128)(2,1)S(1)}, bf16[2,16,3584]{2,1,0:T(8,128)(2,1)S(1)}, u32[]{:S(2)}, u32[]{:S(2)}) collective-permute-start(bf16[2,16,3584]{2,1,0:T(8,128)(2,1)S(1)} %get-tuple-element.75), channel_id=1, source_target_pairs={{0,4},{4,0},{8,12},{12,8},{1,5},{5,1},{9,13},{13,9},{2,6},{6,2},{1... | collective-permute-start | bytes 688136 | tf_op jit(solution)/shard_map/ppermute | solution.py:292
  35.4 1.5 collective-permute-start.8
  35.7 1.5 collective-permute-start.9
  36.2 17.7 %collective-permute-start.24 = (bf16[32,3584]{1,0:T(8,128)(2,1)S(1)}, bf16[32,3584]{1,0:T(8,128)(2,1)S(1)}, u32[]{:S(2)}, u32[]{:S(2)}) collective-permute-start(bf16[32,3584]{1,0:T(8,128)(2,1)S(1)} %activate.5.refs_9_.refs_0_), channel_id=1, source_target_pairs={{0,8},{4,12},{8,0},{12,4},{1,9},{5,13},{9,1},{13,5},{2,10},{6,14},... | collective-permute-start | bytes 688136 | tf_op jit(solution)/shard_map/ppermute | solution.py:292
  38.2 26.2 %collective-permute-start.26 = (bf16[2,64,3584]{2,1,0:T(8,128)(2,1)S(1)}, bf16[2,64,3584]{2,1,0:T(8,128)(2,1)S(1)}, u32[]{:S(2)}, u32[]{:S(2)}) collective-permute-start(bf16[2,64,3584]{2,1,0:T(8,128)(2,1)S(1)} %get-tuple-element.83.refs_4_), channel_id=1, source_target_pairs={{0,8},{4,12},{8,0},{12,4},{1,9},{5,13},{9,1},{13,5},{2,10},{6,14},... | collective-permute-start | bytes 2752520 | tf_op jit(solution)/shard_map/ppermute | solution.py:292
  39.5 15.9 %collective-permute-start.23 = (bf16[128,2048]{1,0:T(8,128)(2,1)S(1)}, bf16[128,2048]{1,0:T(8,128)(2,1)S(1)}, u32[]{:S(2)}, u32[]{:S(2)}) collective-permute-start(bf16[128,2048]{1,0:T(8,128)(2,1)S(1)} %collective-permute-done.1.refs_1_.refs_0_), channel_id=1, source_target_pairs={{0,1},{1,2},{2,3},{3,0},{4,5},{5,6},{6,7},{7,4},{8,9},{9,10},{10,1... | collective-permute-start | bytes 1572872 | tf_op jit(solution)/shard_map/ppermute | solution.py:289
  53.3 1.6 collective-permute-start.15
  53.4 1.8 collective-permute-start.16
  53.9 1.8 %collective-permute-start.17 = (bf16[2,16,3584]{2,1,0:T(8,128)(2,1)S(1)}, bf16[2,16,3584]{2,1,0:T(8,128)(2,1)S(1)}, u32[]{:S(2)}, u32[]{:S(2)}) collective-permute-start(bf16[2,16,3584]{2,1,0:T(8,128)(2,1)S(1)} %get-tuple-element.87), channel_id=1, source_target_pairs={{0,4},{4,0},{8,12},{12,8},{1,5},{5,1},{9,13},{13,9},{2,6},{6,2},{1... | collective-permute-start | bytes 688136 | tf_op jit(solution)/shard_map/ppermute | solution.py:292
  54.9 1.5 collective-permute-start.18
  55.2 1.5 collective-permute-start.19
  55.4 1.6 collective-permute-start.20
  55.7 1.6 collective-permute-start.21
  56.4 1.5 collective-permute-start.22
  56.7 3.1 %collective-permute-start.27 = (bf16[32,3584]{1,0:T(8,128)(2,1)S(1)}, bf16[32,3584]{1,0:T(8,128)(2,1)S(1)}, u32[]{:S(2)}, u32[]{:S(2)}) collective-permute-start(bf16[32,3584]{1,0:T(8,128)(2,1)S(1)} %activate.5.refs_9_.refs_0_), channel_id=1, source_target_pairs={{0,4},{4,0},{8,12},{12,8},{1,5},{5,1},{9,13},{13,9},{2,6},{6,2},{1... | collective-permute-start | bytes 688136 | tf_op jit(solution)/shard_map/ppermute | solution.py:292
  57.0 7.4 %collective-permute-start.28 = (bf16[32,3584]{1,0:T(8,128)(2,1)S(1)}, bf16[32,3584]{1,0:T(8,128)(2,1)S(1)}, u32[]{:S(2)}, u32[]{:S(2)}) collective-permute-start(bf16[32,3584]{1,0:T(8,128)(2,1)S(1)} %collective-permute-done.24.refs_2_.refs_7_), channel_id=1, source_target_pairs={{0,4},{4,0},{8,12},{12,8},{1,5},{5,1},{9,13},{13,9},{2,6},{6,2},{1... | collective-permute-start | bytes 688136 | tf_op jit(solution)/shard_map/ppermute | solution.py:292
  58.9 25.1 %collective-permute-start.25 = (bf16[2,64,3584]{2,1,0:T(8,128)(2,1)S(1)}, bf16[2,64,3584]{2,1,0:T(8,128)(2,1)S(1)}, u32[]{:S(2)}, u32[]{:S(2)}) collective-permute-start(bf16[2,64,3584]{2,1,0:T(8,128)(2,1)S(1)} %get-tuple-element.94.refs_4_), channel_id=1, source_target_pairs={{0,8},{4,12},{8,0},{12,4},{1,9},{5,13},{9,1},{13,5},{2,10},{6,14},... | collective-permute-start | bytes 2752520 | tf_op jit(solution)/shard_map/ppermute | solution.py:292
  76.6 1.6 collective-permute-start.29
  76.6 1.8 collective-permute-start.30
  77.1 1.6 collective-permute-start.31
  77.2 1.9 %collective-permute-start.32 = (bf16[2,16,3584]{2,1,0:T(8,128)(2,1)S(1)}, bf16[2,16,3584]{2,1,0:T(8,128)(2,1)S(1)}, u32[]{:S(2)}, u32[]{:S(2)}) collective-permute-start(bf16[2,16,3584]{2,1,0:T(8,128)(2,1)S(1)} %get-tuple-element.100), channel_id=1, source_target_pairs={{0,4},{4,0},{8,12},{12,8},{1,5},{5,1},{9,13},{13,9},{2,6},{6,2},{1... | collective-permute-start | bytes 688136 | tf_op jit(solution)/shard_map/ppermute | solution.py:292
  78.1 1.8 collective-permute-start.33
  78.4 2.1 %collective-permute-start.34 = (bf16[2,16,3584]{2,1,0:T(8,128)(2,1)S(1)}, bf16[2,16,3584]{2,1,0:T(8,128)(2,1)S(1)}, u32[]{:S(2)}, u32[]{:S(2)}) collective-permute-start(bf16[2,16,3584]{2,1,0:T(8,128)(2,1)S(1)} %get-tuple-element.102), channel_id=1, source_target_pairs={{0,4},{4,0},{8,12},{12,8},{1,5},{5,1},{9,13},{13,9},{2,6},{6,2},{1... | collective-permute-start | bytes 688136 | tf_op jit(solution)/shard_map/ppermute | solution.py:292
  78.8 3.3 %collective-permute-start.35 = (bf16[2,16,3584]{2,1,0:T(8,128)(2,1)S(1)}, bf16[2,16,3584]{2,1,0:T(8,128)(2,1)S(1)}, u32[]{:S(2)}, u32[]{:S(2)}) collective-permute-start(bf16[2,16,3584]{2,1,0:T(8,128)(2,1)S(1)} %get-tuple-element.103), channel_id=1, source_target_pairs={{0,4},{4,0},{8,12},{12,8},{1,5},{5,1},{9,13},{13,9},{2,6},{6,2},{1... | collective-permute-start | bytes 688136 | tf_op jit(solution)/shard_map/ppermute | solution.py:292
  79.1 2.9 %collective-permute-start.36 = (bf16[2,16,3584]{2,1,0:T(8,128)(2,1)S(1)}, bf16[2,16,3584]{2,1,0:T(8,128)(2,1)S(1)}, u32[]{:S(2)}, u32[]{:S(2)}) collective-permute-start(bf16[2,16,3584]{2,1,0:T(8,128)(2,1)S(1)} %get-tuple-element.104), channel_id=1, source_target_pairs={{0,4},{4,0},{8,12},{12,8},{1,5},{5,1},{9,13},{13,9},{2,6},{6,2},{1... | collective-permute-start | bytes 688136 | tf_op jit(solution)/shard_map/ppermute | solution.py:292
  79.9 8.9 %collective-permute-start.42 = (bf16[32,3584]{1,0:T(8,128)(2,1)S(1)}, bf16[32,3584]{1,0:T(8,128)(2,1)S(1)}, u32[]{:S(2)}, u32[]{:S(2)}) collective-permute-start(bf16[32,3584]{1,0:T(8,128)(2,1)S(1)} %get-tuple-element.108.refs_1_), channel_id=1, source_target_pairs={{0,8},{4,12},{8,0},{12,4},{1,9},{5,13},{9,1},{13,5},{2,10},{6,14},... | collective-permute-start | bytes 688136 | tf_op jit(solution)/shard_map/ppermute | solution.py:292
  80.5 19.3 %collective-permute-start.41 = (bf16[32,3584]{1,0:T(8,128)(2,1)S(1)}, bf16[32,3584]{1,0:T(8,128)(2,1)S(1)}, u32[]{:S(2)}, u32[]{:S(2)}) collective-permute-start(bf16[32,3584]{1,0:T(8,128)(2,1)S(1)} %get-tuple-element.106.refs_9_.refs_0_), channel_id=1, source_target_pairs={{0,8},{4,12},{8,0},{12,4},{1,9},{5,13},{9,1},{13,5},{2,10},{6,14},... | collective-permute-start | bytes 688136 | tf_op jit(solution)/shard_map/ppermute | solution.py:292
  82.0 17.9 %collective-permute-start.39 = (bf16[32,3584]{1,0:T(8,128)(2,1)S(1)}, bf16[32,3584]{1,0:T(8,128)(2,1)S(1)}, u32[]{:S(2)}, u32[]{:S(2)}) collective-permute-start(bf16[32,3584]{1,0:T(8,128)(2,1)S(1)} %get-tuple-element.106.refs_9_.refs_0_), channel_id=1, source_target_pairs={{0,4},{4,0},{8,12},{12,8},{1,5},{5,1},{9,13},{13,9},{2,6},{6,2},{1... | collective-permute-start | bytes 688136 | tf_op jit(solution)/shard_map/ppermute | solution.py:292
  82.0 18.4 %collective-permute-start.40 = (bf16[32,3584]{1,0:T(8,128)(2,1)S(1)}, bf16[32,3584]{1,0:T(8,128)(2,1)S(1)}, u32[]{:S(2)}, u32[]{:S(2)}) collective-permute-start(bf16[32,3584]{1,0:T(8,128)(2,1)S(1)} %get-tuple-element.108.refs_1_), channel_id=1, source_target_pairs={{0,4},{4,0},{8,12},{12,8},{1,5},{5,1},{9,13},{13,9},{2,6},{6,2},{1... | collective-permute-start | bytes 688136 | tf_op jit(solution)/shard_map/ppermute | solution.py:292
  84.6 26.3 %collective-permute-start.38 = (bf16[64,3584]{1,0:T(8,128)(2,1)S(1)}, bf16[64,3584]{1,0:T(8,128)(2,1)S(1)}, u32[]{:S(2)}, u32[]{:S(2)}) collective-permute-start(bf16[64,3584]{1,0:T(8,128)(2,1)S(1)} %activate.7.refs_3_.refs_0_), channel_id=1, source_target_pairs={{0,8},{4,12},{8,0},{12,4},{1,9},{5,13},{9,1},{13,5},{2,10},{6,14},... | collective-permute-start | bytes 1376264 | tf_op jit(solution)/shard_map/ppermute | solution.py:292
  88.9 33.9 %collective-permute-start.47 = (bf16[2,64,3584]{2,1,0:T(8,128)(2,1)S(1)}, bf16[2,64,3584]{2,1,0:T(8,128)(2,1)S(1)}, u32[]{:S(2)}, u32[]{:S(2)}) collective-permute-start(bf16[2,64,3584]{2,1,0:T(8,128)(2,1)S(1)} %get-tuple-element.117.refs_2_), channel_id=1, source_target_pairs={{0,8},{4,12},{8,0},{12,4},{1,9},{5,13},{9,1},{13,5},{2,10},{6,14},... | collective-permute-start | bytes 2752520 | tf_op jit(solution)/shard_map/ppermute | solution.py:292
  99.8 25.7 %collective-permute-start.52 = (bf16[2,64,3584]{2,1,0:T(8,128)(2,1)S(1)}, bf16[2,64,3584]{2,1,0:T(8,128)(2,1)S(1)}, u32[]{:S(2)}, u32[]{:S(2)}) collective-permute-start(bf16[2,64,3584]{2,1,0:T(8,128)(2,1)S(1)} %get-tuple-element.109.refs_9_), channel_id=1, source_target_pairs={{0,4},{4,0},{8,12},{12,8},{1,5},{5,1},{9,13},{13,9},{2,6},{6,2},{1... | collective-permute-start | bytes 2752520 | tf_op jit(solution)/shard_map/ppermute | solution.py:292
  99.9 2.8 %collective-permute-start.44 = (bf16[32,3584]{1,0:T(8,128)(2,1)S(1)}, bf16[32,3584]{1,0:T(8,128)(2,1)S(1)}, u32[]{:S(2)}, u32[]{:S(2)}) collective-permute-start(bf16[32,3584]{1,0:T(8,128)(2,1)S(1)} %collective-permute-done.42.refs_5_), channel_id=1, source_target_pairs={{0,4},{4,0},{8,12},{12,8},{1,5},{5,1},{9,13},{13,9},{2,6},{6,2},{1... | collective-permute-start | bytes 688136 | tf_op jit(solution)/shard_map/ppermute | solution.py:292
  100.4 2.6 %collective-permute-start.43 = (bf16[32,3584]{1,0:T(8,128)(2,1)S(1)}, bf16[32,3584]{1,0:T(8,128)(2,1)S(1)}, u32[]{:S(2)}, u32[]{:S(2)}) collective-permute-start(bf16[32,3584]{1,0:T(8,128)(2,1)S(1)} %collective-permute-done.41.refs_4_), channel_id=1, source_target_pairs={{0,4},{4,0},{8,12},{12,8},{1,5},{5,1},{9,13},{13,9},{2,6},{6,2},{1... | collective-permute-start | bytes 688136 | tf_op jit(solution)/shard_map/ppermute | solution.py:292
  102.7 8.4 %collective-permute-start.37 = (bf16[64,3584]{1,0:T(8,128)(2,1)S(1)}, bf16[64,3584]{1,0:T(8,128)(2,1)S(1)}, u32[]{:S(2)}, u32[]{:S(2)}) collective-permute-start(bf16[64,3584]{1,0:T(8,128)(2,1)S(1)} %activate.7.refs_3_.refs_0_), channel_id=1, source_target_pairs={{0,4},{4,0},{8,12},{12,8},{1,5},{5,1},{9,13},{13,9},{2,6},{6,2},{1... | collective-permute-start | bytes 1376264 | tf_op jit(solution)/shard_map/ppermute | solution.py:292
  110.9 1.9 %collective-permute-start.45 = (bf16[64,3584]{1,0:T(8,128)(2,1)S(1)}, bf16[64,3584]{1,0:T(8,128)(2,1)S(1)}, u32[]{:S(2)}, u32[]{:S(2)}) collective-permute-start(bf16[64,3584]{1,0:T(8,128)(2,1)S(1)} %collective-permute-done.38.refs_2_), channel_id=1, source_target_pairs={{0,4},{4,0},{8,12},{12,8},{1,5},{5,1},{9,13},{13,9},{2,6},{6,2},{1... | collective-permute-start | bytes 1376264 | tf_op jit(solution)/shard_map/ppermute | solution.py:292
  119.7 26.9 %collective-permute-start.46 = (bf16[128,2048]{1,0:T(8,128)(2,1)S(1)}, bf16[128,2048]{1,0:T(8,128)(2,1)S(1)}, u32[]{:S(2)}, u32[]{:S(2)}) collective-permute-start(bf16[128,2048]{1,0:T(8,128)(2,1)S(1)} %get-tuple-element.115.refs_2_), channel_id=1, source_target_pairs={{0,1},{1,2},{2,3},{3,0},{4,5},{5,6},{6,7},{7,4},{8,9},{9,10},{10,1... | collective-permute-start | bytes 1572872 | tf_op jit(solution)/shard_map/ppermute | solution.py:289
  123.4 8.6 %collective-permute-start.51 = (bf16[32,3584]{1,0:T(8,128)(2,1)S(1)}, bf16[32,3584]{1,0:T(8,128)(2,1)S(1)}, u32[]{:S(2)}, u32[]{:S(2)}) collective-permute-start(bf16[32,3584]{1,0:T(8,128)(2,1)S(1)} %get-tuple-element.119.refs_1_), channel_id=1, source_target_pairs={{0,8},{4,12},{8,0},{12,4},{1,9},{5,13},{9,1},{13,5},{2,10},{6,14},... | collective-permute-start | bytes 688136 | tf_op jit(solution)/shard_map/ppermute | solution.py:292
  124.0 12.9 %collective-permute-start.50 = (bf16[32,3584]{1,0:T(8,128)(2,1)S(1)}, bf16[32,3584]{1,0:T(8,128)(2,1)S(1)}, u32[]{:S(2)}, u32[]{:S(2)}) collective-permute-start(bf16[32,3584]{1,0:T(8,128)(2,1)S(1)} %get-tuple-element.118.refs_2_.refs_0_), channel_id=1, source_target_pairs={{0,8},{4,12},{8,0},{12,4},{1,9},{5,13},{9,1},{13,5},{2,10},{6,14},... | collective-permute-start | bytes 688136 | tf_op jit(solution)/shard_map/ppermute | solution.py:292
  125.5 11.4 %collective-permute-start.48 = (bf16[32,3584]{1,0:T(8,128)(2,1)S(1)}, bf16[32,3584]{1,0:T(8,128)(2,1)S(1)}, u32[]{:S(2)}, u32[]{:S(2)}) collective-permute-start(bf16[32,3584]{1,0:T(8,128)(2,1)S(1)} %get-tuple-element.118.refs_2_.refs_0_), channel_id=1, source_target_pairs={{0,4},{4,0},{8,12},{12,8},{1,5},{5,1},{9,13},{13,9},{2,6},{6,2},{1... | collective-permute-start | bytes 688136 | tf_op jit(solution)/shard_map/ppermute | solution.py:292
  126.1 22.5 %collective-permute-start.56 = (bf16[2,32,3584]{2,1,0:T(8,128)(2,1)S(1)}, bf16[2,32,3584]{2,1,0:T(8,128)(2,1)S(1)}, u32[]{:S(2)}, u32[]{:S(2)}) collective-permute-start(bf16[2,32,3584]{2,1,0:T(8,128)(2,1)S(1)} %get-tuple-element.121.refs_10_), channel_id=1, source_target_pairs={{0,8},{4,12},{8,0},{12,4},{1,9},{5,13},{9,1},{13,5},{2,10},{6,14},... | collective-permute-start | bytes 1376264 | tf_op jit(solution)/shard_map/ppermute | solution.py:292
  132.0 5.4 %collective-permute-start.49 = (bf16[32,3584]{1,0:T(8,128)(2,1)S(1)}, bf16[32,3584]{1,0:T(8,128)(2,1)S(1)}, u32[]{:S(2)}, u32[]{:S(2)}) collective-permute-start(bf16[32,3584]{1,0:T(8,128)(2,1)S(1)} %get-tuple-element.119.refs_1_), channel_id=1, source_target_pairs={{0,4},{4,0},{8,12},{12,8},{1,5},{5,1},{9,13},{13,9},{2,6},{6,2},{1... | collective-permute-start | bytes 688136 | tf_op jit(solution)/shard_map/ppermute | solution.py:292
  136.9 1.5 collective-permute-start.54
  136.9 1.8 collective-permute-start.53
  146.9 17.0 %collective-permute-start.55 = (bf16[128,2048]{1,0:T(8,128)(2,1)S(1)}, bf16[128,2048]{1,0:T(8,128)(2,1)S(1)}, u32[]{:S(2)}, u32[]{:S(2)}) collective-permute-start(bf16[128,2048]{1,0:T(8,128)(2,1)S(1)} %add.3.refs_2_), channel_id=1, source_target_pairs={{0,1},{1,2},{2,3},{3,0},{4,5},{5,6},{6,7},{7,4},{8,9},{9,10},{10,1... | collective-permute-start | bytes 1572872 | tf_op jit(solution)/shard_map/ppermute | solution.py:289
  148.9 31.2 %copy-start.2 = (bf16[128,2048]{1,0:T(8,128)(2,1)S(1)}, bf16[128,2048]{1,0:T(8,128)(2,1)}, u32[]{:S(2)}) copy-start(bf16[128,2048]{1,0:T(8,128)(2,1)} %refs_0_.5) | copy-start | bytes 1572868
  148.9 7.5 %collective-permute-start.58 = (bf16[32,3584]{1,0:T(8,128)(2,1)S(1)}, bf16[32,3584]{1,0:T(8,128)(2,1)S(1)}, u32[]{:S(2)}, u32[]{:S(2)}) collective-permute-start(bf16[32,3584]{1,0:T(8,128)(2,1)S(1)} %activate.9.refs_6_.refs_0_), channel_id=1, source_target_pairs={{0,8},{4,12},{8,0},{12,4},{1,9},{5,13},{9,1},{13,5},{2,10},{6,14},... | collective-permute-start | bytes 688136 | tf_op jit(solution)/shard_map/ppermute | solution.py:292
  149.5 6.9 %collective-permute-start.57 = (bf16[32,3584]{1,0:T(8,128)(2,1)S(1)}, bf16[32,3584]{1,0:T(8,128)(2,1)S(1)}, u32[]{:S(2)}, u32[]{:S(2)}) collective-permute-start(bf16[32,3584]{1,0:T(8,128)(2,1)S(1)} %activate.9.refs_6_.refs_0_), channel_id=1, source_target_pairs={{0,4},{4,0},{8,12},{12,8},{1,5},{5,1},{9,13},{13,9},{2,6},{6,2},{1... | collective-permute-start | bytes 688136 | tf_op jit(solution)/shard_map/ppermute | solution.py:292
  156.4 1.5 collective-permute-start.59
  164.3 15.8 %collective-permute-start.60 = (bf16[128,2048]{1,0:T(8,128)(2,1)S(1)}, bf16[128,2048]{1,0:T(8,128)(2,1)S(1)}, u32[]{:S(2)}, u32[]{:S(2)}) collective-permute-start(bf16[128,2048]{1,0:T(8,128)(2,1)S(1)} %add.4.refs_3_), channel_id=1, source_target_pairs={{0,1},{1,2},{2,3},{3,0},{4,5},{5,6},{6,7},{7,4},{8,9},{9,10},{10,1... | collective-permute-start | bytes 1572872 | tf_op jit(solution)/shard_map/ppermute | solution.py:289
